TPU v7x, 32 devices: a whole 2x2x4 slice. The times are simulated.
32 devices in a mesh: dp: 2 (over x), fsdp: 16 (over z, y, core).
Axes of the slice: x: 2, y: 2, z: 4, core: 2. Of those that a mesh axis runs over, the one named last changes fastest.
Arguments:
- patches: bfloat16 [32, 512, 768], P(('dp', 'fsdp')), may hold values from -6 to 6
- counts: int32 [32], P(('dp', 'fsdp')), may hold values from 128 to 512, as said below
- cotangent: bfloat16 [32, 512, 768], P(('dp', 'fsdp')), may hold values from -6 to 6
- w_attn: float32 [4, 768, 768], P(None, 'fsdp')
- w_in: float32 [2, 768, 2048], P(None, 'fsdp'), may hold values from -0.21875 to 0.21875
- w_down: float32 [2048, 768], P('fsdp'), may hold values from -0.125 to 0.125
- gains: float32 [2, 768], P(None, 'fsdp')
- m_attn: float32 [4, 768, 768], P(None, 'fsdp'), may hold values from -0.00024414062 to 0.00024414062
- m_in: float32 [2, 768, 2048], P(None, 'fsdp'), may hold values from -0.00024414062 to 0.00024414062
- m_down: float32 [2048, 768], P('fsdp'), may hold values from -0.00024414062 to 0.00024414062
- m_gains: float32 [2, 768], P(None, 'fsdp'), may hold values from -0.0007324219 to 0.0007324219
- v_attn: float32 [4, 768, 768], P(None, 'fsdp'), may hold values from 1.4125442e-10 to 5.650177e-10
- v_in: float32 [2, 768, 2048], P(None, 'fsdp'), may hold values from 1.4125443e-11 to 5.6501772e-11
- v_down: float32 [2048, 768], P('fsdp'), may hold values from 1.4125442e-10 to 5.650177e-10
- v_gains: float32 [2, 768], P(None, 'fsdp'), may hold values from 7.062721e-11 to 2.8250885e-10
Outputs:
- output: bfloat16 [32, 512, 768], P(('dp', 'fsdp'))
- input_grad: bfloat16 [32, 512, 768], P(('dp', 'fsdp'))
- grad_norm: float32 [], replicated
- new_attn: float32 [4, 768, 768], P(None, 'fsdp')
- new_in: float32 [2, 768, 2048], P(None, 'fsdp')
- new_down: float32 [2048, 768], P('fsdp')
- new_gains: float32 [2, 768], P(None, 'fsdp')
- first_attn: float32 [4, 768, 768], P(None, 'fsdp')
- first_in: float32 [2, 768, 2048], P(None, 'fsdp')
- first_down: float32 [2048, 768], P('fsdp')
- first_gains: float32 [2, 768], P(None, 'fsdp')
- second_attn: float32 [4, 768, 768], P(None, 'fsdp')
- second_in: float32 [2, 768, 2048], P(None, 'fsdp')
- second_down: float32 [2048, 768], P('fsdp')
- second_gains: float32 [2, 768], P(None, 'fsdp')
Inputs may be any that keep to these rules, and one draw needn't show every extreme that they name: Image i's valid patches are its first counts[i] slots, the others padding; in every draw some image has all 512 slots valid.
All inputs are finite; a program needn't handle non-finite values.
Results may differ from a plain program's by a relative error of at most 0.02.
The roundings to bfloat16 on the way count: a program that leaves them out, or rounds other values in their place, can miss the bound.
Values may be sent and summed in bfloat16 or wider, within the bound.
No kernel may reach another device: no remote copies, remote signals or barrier semaphores. Data moves between devices by JAX's collectives and lax.ppermute only.
A program may use at most 192 MiB of HBM per device.

v0:
```python
import jax
import jax.numpy as jnp
from jax import lax
from jax.sharding import PartitionSpec as P

HD = 64
STEP = 10


NORM_EPS = 1e-06
MASKED = -1000000000.0
BETA_ONE = 0.9
BETA_TWO = 0.999
ADAM_EPS = 1e-08
CLIP_AT = 1.0
MATRIX_RATE = 0.04
MATRIX_DECAY = 0.1
GAIN_RATE = 0.8


def rms_scale(values, gain):
    return values * lax.rsqrt(jnp.mean(values * values, -1, keepdims=True) + NORM_EPS) * gain


def gated_unit(gate, up_part):
    return jax.nn.gelu(gate, approximate=True) * up_part


def split_heads(block, head_size):
    return block.reshape(block.shape[0], block.shape[1] // head_size, head_size)


def head_scores(queries, keys, valid):
    scores = jnp.einsum("qhd,khd->hqk", queries, keys, preferred_element_type=jnp.float32)
    return jnp.where(valid[None, None, :], scores, MASKED)


def attend_forward(qkv, valid, head_size):
    length, width_all = (qkv.shape[1], qkv.shape[2])
    width = 2 * head_size

    def one_pair(index):
        parts = lax.dynamic_slice_in_dim(qkv, index * width, width, 2)
        queries = split_heads(parts[0], head_size)
        keys = split_heads(parts[1], head_size)
        values = split_heads(parts[2], head_size)
        scores = head_scores(queries, keys, valid)
        top = jnp.max(scores, -1, keepdims=True)
        expd = jnp.exp(scores - top)
        total = jnp.sum(expd, -1, keepdims=True)
        probs = (expd / total).astype(jnp.bfloat16)
        context = jnp.einsum("hqk,khd->qhd", probs, values, preferred_element_type=jnp.float32)
        return (context.reshape(length, width), top + jnp.log(total))

    contexts, logsums = lax.map(one_pair, jnp.arange(width_all // width))
    context = jnp.swapaxes(contexts, 0, 1).reshape(length, width_all).astype(jnp.bfloat16)
    return (context, logsums)


def attend_backward(qkv, d_context, logsums, valid, head_size):
    length, width_all = (qkv.shape[1], qkv.shape[2])
    width = 2 * head_size

    def one_pair(item):
        index, logsum = item
        parts = lax.dynamic_slice_in_dim(qkv, index * width, width, 2)
        queries = split_heads(parts[0], head_size)
        keys = split_heads(parts[1], head_size)
        values = split_heads(parts[2], head_size)
        d_out = split_heads(lax.dynamic_slice_in_dim(d_context, index * width, width, 1), head_size)
        probs = jnp.exp(head_scores(queries, keys, valid) - logsum)
        d_probs = jnp.einsum("qhd,khd->hqk", d_out, values, preferred_element_type=jnp.float32)
        d_values = jnp.einsum(
            "hqk,qhd->khd", probs.astype(jnp.bfloat16), d_out, preferred_element_type=jnp.float32
        )
        d_scores = (probs * (d_probs - jnp.sum(probs * d_probs, -1, keepdims=True))).astype(
            jnp.bfloat16
        )
        d_queries = jnp.einsum("hqk,khd->qhd", d_scores, keys, preferred_element_type=jnp.float32)
        d_keys = jnp.einsum("hqk,qhd->khd", d_scores, queries, preferred_element_type=jnp.float32)
        return jnp.stack((d_queries, d_keys, d_values)).reshape(3, length, width)

    pieces = lax.map(one_pair, (jnp.arange(width_all // width), logsums))
    return jnp.transpose(pieces, (1, 2, 0, 3)).reshape(3, length, width_all).astype(jnp.bfloat16)


def adamw(param, first, second, grad, rate, decay):
    first = BETA_ONE * first + (1.0 - BETA_ONE) * grad
    second = BETA_TWO * second + (1.0 - BETA_TWO) * grad * grad
    update = first / (1.0 - BETA_ONE**STEP) / (jnp.sqrt(second / (1.0 - BETA_TWO**STEP)) + ADAM_EPS)
    return (param - rate * (update + decay * param), first, second)


def on_device(
    patches,
    counts,
    cotangent,
    w_attn,
    w_in,
    w_down,
    gains,
    m_attn,
    m_in,
    m_down,
    m_gains,
    v_attn,
    v_in,
    v_down,
    v_gains,
):
    head_size = HD
    inputs = patches[0].astype(jnp.float32)
    length = inputs.shape[0]
    valid = jnp.arange(length) < counts[0]
    row_mask = valid.astype(jnp.float32)[:, None]
    low_attn = w_attn.astype(jnp.bfloat16)
    low_in = w_in.astype(jnp.bfloat16)
    low_down = w_down.astype(jnp.bfloat16)
    low_gains = gains.astype(jnp.bfloat16)
    attn_full, in_full, down_full, gain_full = (
        lax.all_gather(low_attn, "fsdp", axis=1, tiled=True),
        lax.all_gather(low_in, "fsdp", axis=1, tiled=True),
        lax.all_gather(low_down, "fsdp", axis=0, tiled=True),
        lax.all_gather(low_gains, "fsdp", axis=1, tiled=True),
    )
    normed = rms_scale(inputs, gain_full[0].astype(jnp.float32)).astype(jnp.bfloat16)
    qkv = jnp.einsum(
        "sd,jde->jse", normed, attn_full[:3], preferred_element_type=jnp.float32
    ).astype(jnp.bfloat16)
    context, logsums = attend_forward(qkv, valid, head_size)
    attended = inputs + jnp.dot(context, attn_full[3], preferred_element_type=jnp.float32)
    normed_two = rms_scale(attended, gain_full[1].astype(jnp.float32)).astype(jnp.bfloat16)
    gate_up = jnp.einsum("sd,jdf->jsf", normed_two, in_full, preferred_element_type=jnp.float32)
    hidden = gated_unit(gate_up[0], gate_up[1]).astype(jnp.bfloat16)
    result = row_mask * (attended + jnp.dot(hidden, down_full, preferred_element_type=jnp.float32))
    output = result.astype(jnp.bfloat16)[None]
    attn_back, in_back, down_back, gain_back = (
        lax.all_gather(low_attn, "fsdp", axis=1, tiled=True),
        lax.all_gather(low_in, "fsdp", axis=1, tiled=True),
        lax.all_gather(low_down, "fsdp", axis=0, tiled=True),
        lax.all_gather(low_gains, "fsdp", axis=1, tiled=True),
    )
    d_result = (row_mask * cotangent[0].astype(jnp.float32)).astype(jnp.bfloat16)
    g_down = jnp.einsum("sf,sd->fd", hidden, d_result, preferred_element_type=jnp.float32)
    d_hidden = jnp.einsum("sd,fd->sf", d_result, down_back, preferred_element_type=jnp.float32)
    unused, pull_gate = jax.vjp(gated_unit, gate_up[0], gate_up[1])
    d_gate, d_up = pull_gate(d_hidden)
    d_gate_up = jnp.stack((d_gate, d_up)).astype(jnp.bfloat16)
    g_in = jnp.einsum("sd,jsf->jdf", normed_two, d_gate_up, preferred_element_type=jnp.float32)
    d_normed_two = jnp.einsum("jsf,jdf->sd", d_gate_up, in_back, preferred_element_type=jnp.float32)
    unused, pull_two = jax.vjp(rms_scale, attended, gain_back[1].astype(jnp.float32))
    d_norm_two, g_gain_two = pull_two(d_normed_two)
    d_attended = d_result.astype(jnp.float32) + d_norm_two
    d_attended_low = d_attended.astype(jnp.bfloat16)
    g_out = jnp.einsum("sd,se->de", context, d_attended_low, preferred_element_type=jnp.float32)
    d_context = jnp.einsum(
        "se,de->sd", d_attended_low, attn_back[3], preferred_element_type=jnp.float32
    ).astype(jnp.bfloat16)
    d_qkv = attend_backward(qkv, d_context, logsums, valid, head_size)
    g_qkv = jnp.einsum("sd,jse->jde", normed, d_qkv, preferred_element_type=jnp.float32)
    d_normed = jnp.einsum("jse,jde->sd", d_qkv, attn_back[:3], preferred_element_type=jnp.float32)
    unused, pull_one = jax.vjp(rms_scale, inputs, gain_back[0].astype(jnp.float32))
    d_norm_one, g_gain_one = pull_one(d_normed)
    input_grad = (d_attended + d_norm_one).astype(jnp.bfloat16)[None]
    g_attn = jnp.concatenate((g_qkv, g_out[None]), 0)
    g_gains = jnp.stack((g_gain_one, g_gain_two))
    params = (w_attn, w_in, w_down, gains)
    firsts = (m_attn, m_in, m_down, m_gains)
    seconds = (v_attn, v_in, v_down, v_gains)
    rates = (MATRIX_RATE, MATRIX_RATE, MATRIX_RATE, GAIN_RATE)
    decays = (MATRIX_DECAY, MATRIX_DECAY, MATRIX_DECAY, 0.0)
    owned = (
        lax.psum_scatter(g_attn, "fsdp", scatter_dimension=1, tiled=True),
        lax.psum_scatter(g_in, "fsdp", scatter_dimension=1, tiled=True),
        lax.psum_scatter(g_down, "fsdp", scatter_dimension=0, tiled=True),
        lax.psum_scatter(g_gains, "fsdp", scatter_dimension=1, tiled=True),
    )
    owned = (
        lax.psum(owned[0].astype(jnp.bfloat16), "dp").astype(jnp.float32),
        lax.psum(owned[1].astype(jnp.bfloat16), "dp").astype(jnp.float32),
        lax.psum(owned[2].astype(jnp.bfloat16), "dp").astype(jnp.float32),
        lax.psum(owned[3].astype(jnp.bfloat16), "dp").astype(jnp.float32),
    )
    squares = sum((jnp.sum(grad * grad) for grad in owned))
    grad_norm = jnp.sqrt(lax.psum(squares, "fsdp"))
    factor = jnp.minimum(1.0, CLIP_AT / (grad_norm + 1e-06))
    updated = [
        adamw(params[n], firsts[n], seconds[n], owned[n] * factor, rates[n], decays[n])
        for n in range(4)
    ]
    return (
        output,
        input_grad,
        grad_norm,
        updated[0][0],
        updated[1][0],
        updated[2][0],
        updated[3][0],
        updated[0][1],
        updated[1][1],
        updated[2][1],
        updated[3][1],
        updated[0][2],
        updated[1][2],
        updated[2][2],
        updated[3][2],
    )


def solution(mesh):
    placed = (
        P(("dp", "fsdp"), None, None),
        P(("dp", "fsdp")),
        P(("dp", "fsdp"), None, None),
        P(None, "fsdp", None),
        P(None, "fsdp", None),
        P("fsdp", None),
        P(None, "fsdp"),
        P(None, "fsdp", None),
        P(None, "fsdp", None),
        P("fsdp", None),
        P(None, "fsdp"),
        P(None, "fsdp", None),
        P(None, "fsdp", None),
        P("fsdp", None),
        P(None, "fsdp"),
    )
    return jax.shard_map(
        on_device,
        mesh=mesh,
        in_specs=placed,
        out_specs=(
            P(("dp", "fsdp"), None, None),
            P(("dp", "fsdp"), None, None),
            P(),
            P(None, "fsdp", None),
            P(None, "fsdp", None),
            P("fsdp", None),
            P(None, "fsdp"),
            P(None, "fsdp", None),
            P(None, "fsdp", None),
            P("fsdp", None),
            P(None, "fsdp"),
            P(None, "fsdp", None),
            P(None, "fsdp", None),
            P("fsdp", None),
            P(None, "fsdp"),
        ),
        check_vma=False,
    )
```

profile of v0, /device:TPU:0, one launch (start us, length us, event | category | flops | bytes accessed | tf_op | source)
XLA Modules:
  0.0 868.2 jit_solution(1517453956916988980)
XLA Ops:
  7.3 1.9 convert_element_type.152
  9.2 1.9 convert_element_type.159
  13.0 23.1 %all-gather = bf16[16,48,2]{1,2,0:T(2,128)(2,1)S(1)} all-gather(bf16[1,48,2]{1,2,0:T(2,128)(2,1)S(1)} %convert_bitcast_fusion.3), channel_id=1, replica_groups=mesh['dp'=2,'fsdp'=16] {'fsdp'}, dimensions={0}, use_global_device_ids=true | all-gather | bytes 3264 | tf_op jit(solution)/shard_map/all_gather | solution.py:124
  37.5 29.5 %all-gather.5.cloned.1.call-done = bf16[4,768,768]{2,1,0:T(8,128)(2,1)} async-done(((bf16[4,48,768]{2,1,0:T(8,128)(2,1)}), bf16[4,768,768]{2,1,0:T(8,128)(2,1)}) %all-gather.5.cloned.1.call-update) | async-done | bytes 4718608 | tf_op jit(solution)/shard_map/all_gather | solution.py:121
  67.0 5.5 convert_bitcast_fusion
  72.4 2.8 copy.113
  75.3 25.5 %while.24 = (s32[]{:T(128)}, bf16[6,512,128]{1,2,0:T(8,128)(2,1)}, f32[6,2,512,1]{2,1,3,0:T(2,128)S(1)}, s32[6]{0:T(128)S(1)}, bf16[3,512,768]{1,2,0:T(8,128)(2,...) while((s32[]{:T(128)}, bf16[6,512,128]{1,2,0:T(8,128)(2,1)}, ...), condition=%wide.region_4.5_spmd.clone, body=%wide.region_1.4_spmd.clone.sunk | while | flops 138935808 | bytes 7899367 | solution.py:55
  100.9 3.5 multiply_reduce_fusion.2
  104.3 26.0 %all-gather.7.cloned.1.call-done = bf16[2,768,2048]{2,1,0:T(8,128)(2,1)} async-done(((bf16[2,48,2048]{2,1,0:T(8,128)(2,1)}), bf16[2,768,2048]{2,1,0:T(8,128)(2,1)}) %all-gather.7.cloned.1.call-update) | async-done | bytes 6291472 | tf_op jit(solution)/shard_map/all_gather | solution.py:122
  130.4 6.2 convolution_bitcast_fusion.1
  136.5 3.3 copy-done.24
  139.8 4.5 fusion.37
  144.3 32.7 %all-gather.9.cloned.1.call-done = bf16[2048,768]{1,0:T(8,128)(2,1)} async-done(((bf16[128,768]{1,0:T(8,128)(2,1)}), bf16[2048,768]{1,0:T(8,128)(2,1)}) %all-gather.9.cloned.1.call-update) | async-done | bytes 3145744 | tf_op jit(solution)/shard_map/all_gather | solution.py:123
  177.1 8.2 fusion.43
  185.3 9.0 %fusion.65 = (f32[768]{0:T(1024)S(1)}, f32[512]{0:T(512)S(1)}, f32[512,768,1]{1,0,2:T(8,128)}) fusion(f32[512,768]{1,0:T(8,128)S(1)} %copy-done.6, f32[512]{0:T(512)S(1)} %fusion.106, f32[768]{0:T(1024)S(1)} %get-tuple-element.221, bf16[2,768,2048]{2,1,0:T(8,128)(2,1)} %all-gather.7.cloned.1.call-done, bf16[1,512,2048]{2,1,0:T(8,128)(2,1)S(1)} %get-tuple-element.277, ...), kind=kOutput, calls=%fused_computation.102 | convolution fusion | flops 3225680640 | bytes 13641728 | tf_op jit(solution)/shard_map/jsf,jdf->sd/dot_general | solution.py:150
  194.4 2.6 fusion.62
  198.1 3.0 convolution_convert_fusion
  201.2 40.9 %while.25 = (s32[]{:T(128)}, bf16[6,3,512,128]{2,3,0,1:T(8,128)(2,1)}, s32[6]{0:T(128)S(1)}, bf16[3,512,768]{1,2,0:T(8,128)(2,1)S(1)}, f32[6,2,512,1]{2,1,3,0:T(...) while((s32[]{:T(128)}, ...), condition=%wide.region_9.10_spmd.clone, body=%wide.region_7.9_spmd.clone.sunk | while | flops 340917760 | bytes 19158260 | solution.py:83
  242.1 6.3 fusion.54
  251.0 2.1 convolution_bitcast_fusion.2
  253.2 4.2 pad_maximum_fusion
  257.4 12.1 %copy.119 = f32[4,768,768]{2,0,1:T(4,128)} copy(f32[4,768,768]{1,2,0:T(8,128)} %pad_maximum_fusion) | data formatting | bytes 18874368 | tf_op jit(solution)/shard_map/concatenate | solution.py:165
  269.5 10.8 %convolution_bitcast_fusion = f32[2,768,2048]{1,2,0:T(8,128)} fusion(bf16[1,512,2048]{2,1,0:T(8,128)(2,1)} %copy-done.23, bf16[1,512,2048]{2,1,0:T(8,128)(2,1)} %copy-done.22, f32[512,768]{1,0:T(8,128)} %get-tuple-element.279, f32[768]{0:T(1024)S(1)} %get-tuple-element.221, f32[512]{0:T(512)S(1)} %fusion.106), kind=kOutput, calls=%fused_computation.31 | convolution fusion | flops 3224502272 | bytes 18355200 | tf_op jit(solution)/shard_map/sd,jsf->jdf/dot_general | solution.py:149
  280.3 19.4 %copy.122 = f32[2,768,2048]{2,0,1:T(2,128)} copy(f32[2,768,2048]{1,2,0:T(8,128)} %convolution_bitcast_fusion) | data formatting | bytes 25165824 | tf_op jit(solution)/shard_map/sd,jsf->jdf/transpose | solution.py:149
  299.8 455.5 %all-reduce.8 = (bf16[4,768,768]{2,0,1:T(4,128)(2,1)}, bf16[2,768,2048]{2,0,1:T(2,128)(2,1)}) all-reduce(f32[4,768,768]{2,0,1:T(4,128)} %copy.119, f32[2,768,2048]{2,0,1:T(2,128)} %copy.122), channel_id=2, replica_groups=mesh['dp'=2,'fsdp'=16] {'fsdp'}, use_global_device_ids=true, to_apply=%region_11.12.clone | all-reduce | flops 5505024 | bytes 33030144
  761.0 8.3 fusion.68
  770.2 8.7 psum.38
  779.4 28.5 %all-reduce.7.cloned.1.call-done = (bf16[4,48,768]{2,1,0:T(8,128)(2,1)}, bf16[2,48,2048]{2,1,0:T(8,128)(2,1)}, bf16[128,768]{1,0:T(8,128)(2,1)}) async-done(((bf16[4,48,768]{2,1,0:T(8,128)(2,1)}, bf16[2,48,2048]{2,1,0:T(8,128)(2,1)}, bf16[128,768]{1,0:T(8,128)(2,1)}), (bf16[4,48,768]{2,1,0:T(8,128)(2,1)}, bf16[2,48,2048]{2,1,0:T(8,128)(2,1)}, bf16[128,768]{1,0:T(8,128)(2,1)})) %all-reduce.7.cloned.1.call-update) | async-done | bytes 884752 | tf_op jit(solution)/shard_map/psum | solution.py:179
  815.7 2.8 fusion.76
  818.5 33.8 %psum.39 = f32[]{:T(128)} all-reduce(f32[]{:T(128)S(6)} %add.179), channel_id=1, replica_groups=mesh['dp'=2,'fsdp'=16] {'fsdp'}, use_global_device_ids=true, to_apply=%region_25.26 | all-reduce | flops 1 | bytes 8 | tf_op jit(solution)/shard_map/psum | solution.py:185
  853.7 2.3 multiply_subtract_fusion.2
  858.4 1.8 multiply_subtract_fusion
  (223 shorter events, 79.1 us)
Async XLA Ops:
  7.2 29.1 %copy-start.21 = (u32[32]{0:T(128)S(1)}, u32[32]{0:T(128)}, u32[]{:S(2)}) copy-start(u32[32]{0:T(128)} %constant.49) | copy-start | bytes 388
  7.2 4.0 copy-start.7
  7.2 5.5 copy-start.18
  7.2 5.5 copy-start.2
  7.2 59.8 %all-gather.5.cloned.1.call-start = ((), (), s32[]{:S(2)}) async-start(), calls=%async_computation.2 | async-start | bytes 5013504 | tf_op jit(solution)/shard_map/all_gather | solution.py:121
  9.2 121.2 %all-gather.7.cloned.1.call-start = ((), (), s32[]{:S(2)}) async-start(), calls=%async_computation.3 | async-start | bytes 6684672 | tf_op jit(solution)/shard_map/all_gather | solution.py:122
  11.2 165.9 %all-gather.9.cloned.1.call-start = ((), (), s32[]{:S(2)}) async-start(), calls=%async_computation.4 | async-start | bytes 3342336 | tf_op jit(solution)/shard_map/all_gather | solution.py:123
  12.0 747.3 %reduce-scatter.5.cloned.1.call-start = ((), (), s32[]{:S(2)}) async-start(), calls=%async_computation.5 | async-start | bytes 6684672 | tf_op jit(solution)/shard_map/reduce_scatter | solution.py:175
  130.4 9.4 %copy-start.11 = (bf16[1,512,768]{2,1,0:T(8,128)(2,1)S(1)}, bf16[1,512,768]{2,1,0:T(8,128)(2,1)}, u32[]{:S(2)}) copy-start(bf16[1,512,768]{2,1,0:T(8,128)(2,1)} %param.21) | copy-start | bytes 2359300
  136.5 3.3 copy-start.24
  177.1 8.3 copy-start.6
  185.3 9.0 %copy-start.22 = (bf16[1,512,2048]{2,1,0:T(8,128)(2,1)}, bf16[1,512,2048]{2,1,0:T(8,128)(2,1)S(1)}, u32[]{:S(2)}) copy-start(bf16[1,512,2048]{2,1,0:T(8,128)(2,1)S(1)} %get-tuple-element.276) | copy-start | bytes 6291460
  185.3 9.0 %copy-start.23 = (bf16[1,512,2048]{2,1,0:T(8,128)(2,1)}, bf16[1,512,2048]{2,1,0:T(8,128)(2,1)S(1)}, u32[]{:S(2)}) copy-start(bf16[1,512,2048]{2,1,0:T(8,128)(2,1)S(1)} %get-tuple-element.277) | copy-start | bytes 6291460
  194.4 575.0 %reduce-scatter.7.cloned.1.call-start = ((), (), s32[]{:S(2)}) async-start(), calls=%async_computation.6 | async-start | bytes 417792
  197.0 1.2 copy-start
  242.1 7.3 copy-start.1
  242.1 7.3 copy-start.12
  249.4 1.7 copy-start.5
  299.8 508.2 %all-reduce.7.cloned.1.call-start = ((), (), s32[]{:S(2)}) async-start(), calls=%async_computation.7 | async-start | bytes 1769472 | tf_op jit(solution)/shard_map/psum | solution.py:179
  815.7 37.4 %copy-start.19 = (f32[2,48]{1,0:T(2,128)S(1)}, f32[2,48]{1,0:T(2,128)}, u32[]{:S(2)}) copy-start(f32[2,48]{1,0:T(2,128)} %param.29) | copy-start | bytes 1156
  815.7 37.4 %copy-start.20 = (f32[2,48]{1,0:T(2,128)S(1)}, f32[2,48]{1,0:T(2,128)}, u32[]{:S(2)}) copy-start(f32[2,48]{1,0:T(2,128)} %param.33) | copy-start | bytes 1156
  815.7 38.0 %copy-start.8 = (f32[128,768]{1,0:T(8,128)S(1)}, f32[128,768]{1,0:T(8,128)}, u32[]{:S(2)}) copy-start(f32[128,768]{1,0:T(8,128)} %param.24) | copy-start | bytes 1179652
  815.7 38.0 %copy-start.15 = (bf16[128,768]{1,0:T(8,128)(2,1)S(1)}, bf16[128,768]{1,0:T(8,128)(2,1)}, u32[]{:S(2)}) copy-start(bf16[128,768]{1,0:T(8,128)(2,1)} %get-tuple-element.253) | copy-start | bytes 589828
  818.5 37.5 %copy-start.4 = (f32[4,48,768]{2,1,0:T(8,128)S(1)}, f32[4,48,768]{2,1,0:T(8,128)}, u32[]{:S(2)}) copy-start(f32[4,48,768]{2,1,0:T(8,128)} %param.22) | copy-start | bytes 1769476
  818.5 37.5 %copy-start.10 = (bf16[4,48,768]{2,1,0:T(8,128)(2,1)S(1)}, bf16[4,48,768]{2,1,0:T(8,128)(2,1)}, u32[]{:S(2)}) copy-start(bf16[4,48,768]{2,1,0:T(8,128)(2,1)} %get-tuple-element.251) | copy-start | bytes 884740
  818.5 37.5 %copy-start.16 = (f32[4,48,768]{2,1,0:T(8,128)S(1)}, f32[4,48,768]{2,1,0:T(8,128)}, u32[]{:S(2)}) copy-start(f32[4,48,768]{2,1,0:T(8,128)} %param.26) | copy-start | bytes 1769476
  818.5 37.5 %copy-start.17 = (f32[4,48,768]{2,1,0:T(8,128)S(1)}, f32[4,48,768]{2,1,0:T(8,128)}, u32[]{:S(2)}) copy-start(f32[4,48,768]{2,1,0:T(8,128)} %param.30) | copy-start | bytes 1769476
  856.0 1.5 copy-start.3
  856.0 1.5 copy-start.9
  856.1 2.1 copy-start.13
  856.1 2.3 copy-start.14
Sparse Core Ops, SparseCore 0:
  10.9 56.0 all-gather.4
  69.8 60.4 all-gather.6
  133.2 43.8 all-gather.8
  194.5 83.9 reduce-scatter.4
  299.9 71.2 reduce-scatter.6
  761.1 46.7 all-reduce.6
where the time goes:
time: 870 us; the launch traced here: 868 us
  blocking collectives  521 us (60%)
  waiting for transfers between devices  117 us (13%)
  matrix products  89.8 us (10%)
  local copies, waits for them, and re-layouts  64.7 us (7%)
  other arithmetic  46.8 us (5%)
  between operations  20.2 us (2%)
    unnamed x1, blocking collectives  456 us
    psum x1, blocking collectives, on_device(): grad_norm = jnp.sqrt(lax.psum(squares, 'fsdp'))  33.8 us
    all_gather x1, waiting for transfers between devices, on_device(): lax.all_gather(low_down, 'fsdp', axis=0, tiled=True)  32.7 us
    all_gather x1, waiting for transfers between devices, on_device(): lax.all_gather(low_attn, 'fsdp', axis=1, tiled=True)  29.5 us
    psum x1, waiting for transfers between devices, on_device(): lax.psum(owned[0].astype(jnp.bfloat16), 'dp').astype(jnp.float32)  28.5 us
    all_gather x1, waiting for transfers between devices, on_device(): lax.all_gather(low_in, 'fsdp', axis=1, tiled=True)  26 us
    all_gather x1, blocking collectives, on_device(): lax.all_gather(low_gains, 'fsdp', axis=1, tiled=True)  23.1 us
    transpose x1, local copies, waits for them, and re-layouts, on_device(): jnp.einsum('sd,jsf->jdf', normed_two, d_gate_up, preferred_element_type=j...  19.4 us
  transfers between devices with their start and end apart: 6, of which 4 were waited for; matrix products, arithmetic and copies ran while one was open for 19% of the time, Pallas kernels for 0%

commit v1 on v0

--- a/solution.py
+++ b/solution.py
@@ -1,6 +1,10 @@
+import functools
+
 import jax
 import jax.numpy as jnp
 from jax import lax
+from jax.experimental import pallas as pl
+from jax.experimental.pallas import tpu as pltpu
 from jax.sharding import PartitionSpec as P
 
 HD = 64
@@ -91,7 +95,154 @@
     return (param - rate * (update + decay * param), first, second)
 
 
-def on_device(
+EVERY = ("dp", "fsdp")
+
+
+class Grid:
+    def __init__(self, dp, fsdp):
+        self.dp, self.fsdp = dp, fsdp
+        self.nz = fsdp // 4
+        power = self.nz & (self.nz - 1) == 0
+        self.cube = dp == 2 and fsdp % 4 == 0 and self.nz % 2 == 0 and power
+
+    def move(self, step):
+        pairs = []
+        for source in range(self.dp * self.fsdp):
+            x, rest = divmod(source, self.fsdp)
+            z, rest = divmod(rest, 4)
+            y, core = divmod(rest, 2)
+            x, z, y, core = step(x, z, y, core)
+            pairs.append((source, x * self.fsdp + (z * 2 + y) * 2 + core))
+        return pairs
+
+    def flip_x(self, v):
+        return lax.ppermute(v, EVERY, self.move(lambda x, z, y, c: (1 - x, z, y, c)))
+
+    def flip_y(self, v):
+        return lax.ppermute(v, EVERY, self.move(lambda x, z, y, c: (x, z, 1 - y, c)))
+
+    def flip_core(self, v):
+        return lax.ppermute(v, EVERY, self.move(lambda x, z, y, c: (x, z, y, 1 - c)))
+
+    def shift_z(self, v, by):
+        return lax.ppermute(v, EVERY, self.move(lambda x, z, y, c: (x, (z + by) % self.nz, y, c)))
+
+    def swap_z(self, v, bit):
+        return lax.ppermute(v, EVERY, self.move(lambda x, z, y, c: (x, z ^ bit, y, c)))
+
+    def place(self):
+        x, f = lax.axis_index("dp"), lax.axis_index("fsdp")
+        return x, f // 4, f // 2 % 2, f % 2
+
+
+def spread(grid, part):
+    half = grid.nz // 2
+    column = jnp.stack([part] + [grid.shift_z(part, k) for k in range(1, grid.nz)])
+    side = grid.flip_x(column)
+    across = grid.flip_y(column)
+    corner_low = grid.flip_x(across[:half])
+    corner_high = grid.flip_y(side[half:])
+    mine = [column, side, across, corner_low, corner_high]
+    return mine + [grid.flip_core(piece) for piece in mine]
+
+
+def piece_places(grid):
+    nz, half = grid.nz, grid.nz // 2
+    spots = [(0, 0, 0, nz), (1, 0, 0, nz), (0, 1, 0, nz), (1, 1, 0, half), (1, 1, half, nz - half)]
+    return [(dx, dy, dc, low, n) for dc in (0, 1) for dx, dy, low, n in spots]
+
+
+def assemble(grid, pieces):
+    rows, columns = pieces[0].shape[1:]
+    places = piece_places(grid)
+
+    def body(*refs):
+        ins, out, sem = refs[: len(pieces)], refs[len(pieces)], refs[len(pieces) + 1]
+        x, z, y, c = grid.place()
+        for ref, (dx, dy, dc, low, n) in zip(ins, places):
+            for level in range(n):
+                owner_z = lax.rem(z - (low + level) + grid.nz, grid.nz)
+                owner = (owner_z * 2 + lax.rem(y + dy, 2)) * 2 + lax.rem(c + dc, 2)
+                pltpu.make_async_copy(ref.at[level], out.at[lax.rem(x + dx, 2), owner], sem).start()
+        pltpu.make_async_copy(out, out, sem).wait()
+
+    return pl.pallas_call(
+        body,
+        out_shape=jax.ShapeDtypeStruct((2, grid.fsdp, rows, columns), pieces[0].dtype),
+        in_specs=[pl.BlockSpec(memory_space=pl.ANY)] * len(pieces),
+        out_specs=pl.BlockSpec(memory_space=pl.ANY),
+        scratch_shapes=[pltpu.SemaphoreType.DMA],
+        name="assemble",
+    )(*pieces)
+
+
+def reduce_group(grid, grads):
+    if not grid.cube:
+        owned = lax.psum_scatter(grads.astype(jnp.float32), "fsdp", scatter_dimension=1)
+        return lax.psum(owned.astype(jnp.bfloat16), "dp")
+    x, z, y, c = grid.place()
+    half = grid.nz // 2
+    grads = grads.reshape((2, grid.nz, 2, 2) + grads.shape[2:])
+    got = grid.flip_core(lax.dynamic_index_in_dim(grads, 1 - c, 3, False))
+    keep = lax.dynamic_index_in_dim(grads, c, 3, False)
+
+    def block(h, at_y, low, n):
+        total = 0.0
+        for array in (keep, got):
+            part = lax.dynamic_index_in_dim(array, h, 0, False)[low : low + n]
+            total = total + lax.dynamic_index_in_dim(part, at_y, 1, False).astype(jnp.float32)
+        return total
+
+    def low(v):
+        return v.astype(jnp.bfloat16)
+
+    nz = grid.nz
+    in_x = grid.flip_x(low(block(1 - x, 1 - y, 0, half)))
+    in_y = grid.flip_y(low(block(1 - x, 1 - y, half, nz - half)))
+    to_x = jnp.concatenate(
+        [block(1 - x, y, 0, half), block(1 - x, y, half, nz - half) + in_y.astype(jnp.float32)]
+    )
+    to_y = jnp.concatenate(
+        [block(x, 1 - y, 0, half) + in_x.astype(jnp.float32), block(x, 1 - y, half, nz - half)]
+    )
+    got_x, got_y = grid.flip_x(low(to_x)), grid.flip_y(low(to_y))
+    column = low(block(x, y, 0, nz) + got_x.astype(jnp.float32) + got_y.astype(jnp.float32))
+    total = lax.dynamic_index_in_dim(column, z, 0, False).astype(jnp.float32)
+    for k in range(1, nz):
+        out = lax.dynamic_index_in_dim(column, lax.rem(z + k, nz), 0, False)
+        total = total + grid.shift_z(out, k).astype(jnp.float32)
+    return low(total)
+
+
+def both_halves(grid, total):
+    x = lax.axis_index("dp")
+    other = grid.flip_x(total)
+    return jnp.stack([jnp.where(x == 0, total, other), jnp.where(x == 0, other, total)])
+
+
+def total_of(grid, value):
+    if not grid.cube:
+        return lax.psum(value, "fsdp")
+    value = grid.flip_core(value) + value
+    value = grid.flip_x(value) + value
+    value = grid.flip_y(value) + value
+    bit = 1
+    while bit < grid.nz:
+        value = grid.swap_z(value, bit) + value
+        bit *= 2
+    return value
+
+
+def split_columns(v):
+    return jnp.moveaxis(v.reshape(v.shape[:-1] + (2, v.shape[-1] // 2)), -2, 0)
+
+
+def join_columns(v):
+    moved = jnp.moveaxis(v, 0, -2)
+    return moved.reshape(moved.shape[:-2] + (2 * v.shape[-1],))
+
+
+def on_device(grid,
     patches,
     counts,
     cotangent,
@@ -117,12 +268,40 @@
     low_in = w_in.astype(jnp.bfloat16)
     low_down = w_down.astype(jnp.bfloat16)
     low_gains = gains.astype(jnp.bfloat16)
-    attn_full, in_full, down_full, gain_full = (
-        lax.all_gather(low_attn, "fsdp", axis=1, tiled=True),
-        lax.all_gather(low_in, "fsdp", axis=1, tiled=True),
-        lax.all_gather(low_down, "fsdp", axis=0, tiled=True),
-        lax.all_gather(low_gains, "fsdp", axis=1, tiled=True),
-    )
+    x = lax.axis_index("dp")
+    rows = low_attn.shape[1]
+    wide = low_down.shape[0]
+    ups = low_in.shape[2] // 2
+    columns = inputs.shape[1] // 2
+    gain_rows = jnp.pad(low_gains, ((0, 14), (0, 2 * columns - rows)))
+    first_part = jnp.concatenate([low_attn[0], low_attn[1], low_attn[2], gain_rows], 0)
+    second_part = jnp.concatenate([low_attn[3], low_down], 0)
+    third_part = jnp.concatenate([low_in[0], low_in[1]], 0)
+    first_part, second_part, third_part = (
+        split_columns(p) for p in (first_part, second_part, third_part)
+    )
+    if grid.cube:
+        first_pieces = spread(grid, lax.dynamic_index_in_dim(first_part, x, 0, False))
+        second_part, first_pieces[0] = lax.optimization_barrier((second_part, first_pieces[0]))
+        second_pieces = spread(grid, lax.dynamic_index_in_dim(second_part, x, 0, False))
+        third_part, second_pieces[0] = lax.optimization_barrier((third_part, second_pieces[0]))
+        third_pieces = spread(grid, lax.dynamic_index_in_dim(third_part, x, 0, False))
+        first_full = assemble(grid, first_pieces)
+        second_full = assemble(grid, second_pieces)
+        third_full = assemble(grid, third_pieces)
+    else:
+        first_full, second_full, third_full = (
+            lax.all_gather(p, "fsdp", axis=1) for p in (first_part, second_part, third_part)
+        )
+
+    def whole(full, low, n):
+        return join_columns(full[:, :, low : low + n].reshape(2, grid.fsdp * n, full.shape[3]))
+
+    qkv_full = [whole(first_full, j * rows, rows) for j in range(3)]
+    attn_full = jnp.stack(qkv_full + [whole(second_full, 0, rows)])
+    down_full = whole(second_full, rows, wide)
+    in_full = jnp.stack([whole(third_full, j * rows, rows) for j in range(2)])
+    gain_full = jnp.swapaxes(first_full[0, :, 3 * rows : 3 * rows + 2, :rows], 0, 1).reshape(2, -1)
     normed = rms_scale(inputs, gain_full[0].astype(jnp.float32)).astype(jnp.bfloat16)
     qkv = jnp.einsum(
         "sd,jde->jse", normed, attn_full[:3], preferred_element_type=jnp.float32
@@ -134,12 +313,7 @@
     hidden = gated_unit(gate_up[0], gate_up[1]).astype(jnp.bfloat16)
     result = row_mask * (attended + jnp.dot(hidden, down_full, preferred_element_type=jnp.float32))
     output = result.astype(jnp.bfloat16)[None]
-    attn_back, in_back, down_back, gain_back = (
-        lax.all_gather(low_attn, "fsdp", axis=1, tiled=True),
-        lax.all_gather(low_in, "fsdp", axis=1, tiled=True),
-        lax.all_gather(low_down, "fsdp", axis=0, tiled=True),
-        lax.all_gather(low_gains, "fsdp", axis=1, tiled=True),
-    )
+    attn_back, in_back, down_back, gain_back = attn_full, in_full, down_full, gain_full
     d_result = (row_mask * cotangent[0].astype(jnp.float32)).astype(jnp.bfloat16)
     g_down = jnp.einsum("sf,sd->fd", hidden, d_result, preferred_element_type=jnp.float32)
     d_hidden = jnp.einsum("sd,fd->sf", d_result, down_back, preferred_element_type=jnp.float32)
@@ -162,27 +336,35 @@
     unused, pull_one = jax.vjp(rms_scale, inputs, gain_back[0].astype(jnp.float32))
     d_norm_one, g_gain_one = pull_one(d_normed)
     input_grad = (d_attended + d_norm_one).astype(jnp.bfloat16)[None]
-    g_attn = jnp.concatenate((g_qkv, g_out[None]), 0)
     g_gains = jnp.stack((g_gain_one, g_gain_two))
     params = (w_attn, w_in, w_down, gains)
     firsts = (m_attn, m_in, m_down, m_gains)
     seconds = (v_attn, v_in, v_down, v_gains)
     rates = (MATRIX_RATE, MATRIX_RATE, MATRIX_RATE, GAIN_RATE)
     decays = (MATRIX_DECAY, MATRIX_DECAY, MATRIX_DECAY, 0.0)
+    def parts(g, n):
+        return split_columns(g.astype(jnp.bfloat16).reshape(grid.fsdp, n, g.shape[1]))
+
+    gain_slab = jnp.swapaxes(g_gains.astype(jnp.bfloat16).reshape(2, grid.fsdp, rows), 0, 1)
+    gain_slab = jnp.pad(gain_slab, ((0, 0), (0, 14), (0, columns - rows)))
+    gain_slab = jnp.stack([gain_slab, jnp.zeros_like(gain_slab)])
+    first = jnp.concatenate([parts(g_qkv[j], rows) for j in range(3)] + [gain_slab], 2)
+    second = jnp.concatenate([parts(g_out, rows), parts(g_down, wide)], 2)
+    third = jnp.concatenate([parts(g_in[j], rows) for j in range(2)], 2)
+    third = reduce_group(grid, third)
+    second = reduce_group(grid, second)
+    first = reduce_group(grid, first)
+    squares = sum((jnp.sum(jnp.square(g.astype(jnp.float32))) for g in (first, second, third)))
+    grad_norm = jnp.sqrt(total_of(grid, squares))
+    if grid.cube:
+        first, second, third = (both_halves(grid, g) for g in (first, second, third))
+    first, second, third = (join_columns(g).astype(jnp.float32) for g in (first, second, third))
     owned = (
-        lax.psum_scatter(g_attn, "fsdp", scatter_dimension=1, tiled=True),
-        lax.psum_scatter(g_in, "fsdp", scatter_dimension=1, tiled=True),
-        lax.psum_scatter(g_down, "fsdp", scatter_dimension=0, tiled=True),
-        lax.psum_scatter(g_gains, "fsdp", scatter_dimension=1, tiled=True),
-    )
-    owned = (
-        lax.psum(owned[0].astype(jnp.bfloat16), "dp").astype(jnp.float32),
-        lax.psum(owned[1].astype(jnp.bfloat16), "dp").astype(jnp.float32),
-        lax.psum(owned[2].astype(jnp.bfloat16), "dp").astype(jnp.float32),
-        lax.psum(owned[3].astype(jnp.bfloat16), "dp").astype(jnp.float32),
-    )
-    squares = sum((jnp.sum(grad * grad) for grad in owned))
-    grad_norm = jnp.sqrt(lax.psum(squares, "fsdp"))
+        jnp.stack([first[j * rows : (j + 1) * rows] for j in range(3)] + [second[:rows]]),
+        jnp.stack([third[j * rows : (j + 1) * rows] for j in range(2)]),
+        second[rows:],
+        first[3 * rows : 3 * rows + 2, :rows],
+    )
     factor = jnp.minimum(1.0, CLIP_AT / (grad_norm + 1e-06))
     updated = [
         adamw(params[n], firsts[n], seconds[n], owned[n] * factor, rates[n], decays[n])
@@ -225,8 +407,9 @@
         P("fsdp", None),
         P(None, "fsdp"),
     )
+    grid = Grid(mesh.shape["dp"], mesh.shape["fsdp"])
     return jax.shard_map(
-        on_device,
+        functools.partial(on_device, grid),
         mesh=mesh,
         in_specs=placed,
         out_specs=(

time: 870 us -> 936 us (1.076)
  blocking collectives: 521 us -> 0 us
  Pallas kernels: 0 us -> 444 us
  local copies, waits for them, and re-layouts: 64.7 us -> 164 us
  starting transfers between devices: 0.25 us -> 73.4 us
  waiting for transfers between devices: 117 us -> 75.6 us
  other arithmetic: 46.8 us -> 86.7 us
  matrix products: 89.8 us -> 67.2 us
  between operations: 20.2 us -> 9.66 us
    unnamed x1 -> x0, blocking collectives: 456 us -> none
    pallas_call x0 -> x3, Pallas kernels: none -> 444 us  [assemble(): pl.pallas_call(body, out_shape=jax.ShapeDtypeStruct((2, grid.fsdp, rows,...]
    all_gather x3 -> x0, waiting for transfers between devices: 88.2 us -> none  [the longest x1 32.7 us: on_device(): lax.all_gather(low_down, 'fsdp', axis=0, tiled=True)]
    ppermute x0 -> x68, waiting for transfers between devices: none -> 75.6 us  [the longest x18 47.2 us: shift_z(): lax.ppermute(v, EVERY, self.move(lambda x, z, y, c: (x, (z + by) % self.n...]
    ppermute x0 -> x68, starting transfers between devices: none -> 73.4 us  [the longest x18 26.2 us: shift_z(): lax.ppermute(v, EVERY, self.move(lambda x, z, y, c: (x, (z + by) % self.n...]
    slice x0 -> x29, local copies, waits for them, and re-layouts: none -> 48.5 us  [the longest x3 12.4 us: on_device(): third = jnp.concatenate([parts(g_in[j], rows) for j in range(2)], 2)]
    psum x2 -> x0, blocking collectives: 42.5 us -> none  [the longest x1 33.8 us: on_device(): grad_norm = jnp.sqrt(lax.psum(squares, 'fsdp'))]
    psum x1 -> x0, waiting for transfers between devices: 28.5 us -> none  [on_device(): lax.psum(owned[0].astype(jnp.bfloat16), 'dp').astype(jnp.float32)]
  transfers between devices with their start and end apart: 6 -> 68, of which waited for: 4 -> 20; matrix products, arithmetic and copies ran while one was open for 19% -> 20% of each run, Pallas kernels for 0% -> 27%
where the time goes in v1:
time: 936 us; the launch traced here: 929 us
  Pallas kernels  444 us (47%)
  local copies, waits for them, and re-layouts  164 us (18%)
  other arithmetic  86.7 us (9%)
  waiting for transfers between devices  75.6 us (8%)
  starting transfers between devices  73.4 us (8%)
  matrix products  67.2 us (7%)
  between operations  9.66 us (1%)
    pallas_call x3, Pallas kernels, assemble(): pl.pallas_call(body, out_shape=jax.ShapeDtypeStruct((2, grid.fsdp, rows,...  444 us
    ppermute x18, waiting for transfers between devices, shift_z(): lax.ppermute(v, EVERY, self.move(lambda x, z, y, c: (x, (z + by) % self.n...  47.2 us
    ppermute x18, starting transfers between devices, shift_z(): lax.ppermute(v, EVERY, self.move(lambda x, z, y, c: (x, (z + by) % self.n...  26.2 us
    convert_element_type x5, local copies, waits for them, and re-layouts, parts(): g.astype(jnp.bfloat16).reshape(grid.fsdp, n, g.shape[1])  23 us
    ppermute x16, starting transfers between devices, flip_x(): lax.ppermute(v, EVERY, self.move(lambda x, z, y, c: (1 - x, z, y, c)))  22.1 us
  transfers between devices with their start and end apart: 68, of which 20 were waited for; matrix products, arithmetic and copies ran while one was open for 20% of the time, Pallas kernels for 27%

profile of v1, /device:TPU:0, one launch (start us, length us, event | category | flops | bytes accessed | tf_op | source)
XLA Modules:
  0.0 929.2 jit_solution(11117454927181906638)
XLA Ops:
  2.1 5.1 collective-permute-start.2
  10.9 6.9 collective-permute-done.1
  27.9 7.7 collective-permute-done.13
  45.2 11.3 %collective-permute-done.25 = bf16[96,1024]{1,0:T(8,128)(2,1)} collective-permute-done((bf16[96,1024]{1,0:T(8,128)(2,1)S(1)}, bf16[96,1024]{1,0:T(8,128)(2,1)}, u32[]{:S(2)}, u32[]{:S(2)}) %collective-permute-start.25) | collective-permute-done | bytes 196640 | tf_op jit(solution)/shard_map/ppermute | solution.py:128
  75.1 120.3 %assemble.3 = bf16[2,16,160,384]{3,2,1,0:T(8,128)(2,1)} custom-call(bf16[4,160,384]{2,1,0:T(8,128)(2,1)} %copy-done.20, bf16[4,160,384]{2,1,0:T(8,128)(2,1)} %copy-done.29, bf16[4,160,384]{2,1,0:T(8,128)(2,1)} %copy-done.30, bf16[2,160,384]{2,1,0:T(8,128)(2,1)} %copy-done.47, bf16[2,160,384]{2,1,0:T(8,128)(2,1)} %collective-permute-done.6.refs_4_, ...), custom_call_target="tpu_custom_call" | custom-call | tf_op jit(solution)/shard_map/assemble/pallas_call | solution.py:169
  214.5 29.0 %while.24 = (s32[]{:T(128)}, bf16[6,512,128]{1,2,0:T(8,128)(2,1)}, f32[6,2,512,1]{2,1,3,0:T(2,128)}, s32[6]{0:T(128)S(1)}, bf16[3,512,768]{1,2,0:T(8,128)(2,1)S(...) while((s32[]{:T(128)}, bf16[6,512,128]{1,2,0:T(8,128)(2,1)}, ...), condition=%wide.region_4.5_spmd.clone, body=%wide.region_1.4_spmd.clone.sunk | while | flops 138935808 | bytes 7899367 | solution.py:59
  243.6 132.1 %assemble.4 = bf16[2,16,176,384]{3,2,1,0:T(8,128)(2,1)} custom-call(bf16[4,176,384]{2,1,0:T(8,128)(2,1)} %pad_maximum_fusion.14.refs_0_, bf16[4,176,384]{2,1,0:T(8,128)(2,1)} %collective-permute-done.15.refs_1_, bf16[4,176,384]{2,1,0:T(8,128)(2,1)} %collective-permute-done.16.refs_2_, bf16[2,176,384]{2,1,0:T(8,128)(2,1)} %collective-permute-done.17.refs_3_, ...), custom_call_target="tpu_custom_call" | custom-call | tf_op jit(solution)/shard_map/assemble/pallas_call | solution.py:169
  380.7 5.2 copy.128
  389.2 191.7 %assemble.5 = bf16[2,16,96,1024]{3,2,1,0:T(8,128)(2,1)} custom-call(bf16[4,96,1024]{2,1,0:T(8,128)(2,1)} %pad_maximum_fusion.11.refs_0_, bf16[4,96,1024]{2,1,0:T(8,128)(2,1)} %collective-permute-done.27.refs_1_, bf16[4,96,1024]{2,1,0:T(8,128)(2,1)} %collective-permute-done.28.refs_2_, bf16[2,96,1024]{2,1,0:T(8,128)(2,1)} %copy-done.44, ...), custom_call_target="tpu_custom_call" | custom-call | tf_op jit(solution)/shard_map/assemble/pallas_call | solution.py:169
  580.9 5.6 fusion.150
  586.5 4.6 copy.127
  594.0 6.3 convolution_bitcast_fusion
  602.9 5.9 fusion.36
  614.8 45.9 %while.25 = (s32[]{:T(128)}, bf16[6,3,512,128]{2,3,0,1:T(8,128)(2,1)}, s32[6]{0:T(128)S(1)}, bf16[3,512,768]{1,2,0:T(8,128)(2,1)}, f32[6,2,512,1]{2,1,3,0:T(2,12...) while((s32[]{:T(128)}, ...), condition=%wide.region_9.10_spmd.clone, body=%wide.region_7.9_spmd.clone.sunk | while | flops 340917760 | bytes 19158260 | solution.py:87
  660.7 6.2 fusion.45
  672.3 5.5 convert_bitcast_fusion
  700.0 5.2 fusion.31
  713.1 7.0 reshape_reshape.5
  720.1 4.3 copy.260
  735.8 4.7 copy.154
  740.5 6.2 convert_element_type.711
  746.7 4.7 copy.153
  751.4 6.1 convert_element_type.710
  757.6 18.2 %pad_maximum_fusion.1 = bf16[2,16,96,1024]{3,0,2,1:T(2,128)(2,1)S(1)} fusion(bf16[2,16,48,1024]{3,0,2,1:T(2,128)(2,1)} %bitcast.636, bf16[2,16,48,1024]{3,0,2,1:T(2,128)(2,1)} %bitcast.639), kind=kLoop, calls=%fused_computation.29 | loop fusion | flops 3145728 | bytes 12582912 | tf_op jit(solution)/shard_map/concatenate | solution.py:353
  796.4 4.9 constant_dynamic-slice_fusion.14
  804.6 4.4 collective-permute-done.40
  810.7 4.8 collective-permute-start.42
  817.2 7.9 collective-permute-done.42
  832.1 8.3 collective-permute-done.55
  847.0 5.0 collective-permute-done.46
  882.1 6.4 collective-permute-done.58
  895.0 4.5 collective-permute-start.61
  (540 shorter events, 293.5 us)
Async XLA Ops:
  17.9 20.3 %collective-permute-start.3 = (bf16[4,160,384]{2,1,0:T(8,128)(2,1)S(1)}, bf16[4,160,384]{2,1,0:T(8,128)(2,1)S(1)}, u32[]{:S(2)}, u32[]{:S(2)}) collective-permute-start(bf16[4,160,384]{2,1,0:T(8,128)(2,1)S(1)} %pad_maximum_fusion.17.refs_0_), channel_id=1, source_target_pairs={{0,16},{1,17},{2,18},{3,19},{4,20},{5,21},{6,22},{7,23},{8,24},{9,... | collective-permute-start | bytes 1474568 | tf_op jit(solution)/shard_map/ppermute | solution.py:119
  19.4 20.1 %collective-permute-start.4 = (bf16[4,160,384]{2,1,0:T(8,128)(2,1)S(1)}, bf16[4,160,384]{2,1,0:T(8,128)(2,1)S(1)}, u32[]{:S(2)}, u32[]{:S(2)}) collective-permute-start(bf16[4,160,384]{2,1,0:T(8,128)(2,1)S(1)} %pad_maximum_fusion.17.refs_0_), channel_id=1, source_target_pairs={{0,2},{1,3},{2,0},{3,1},{4,6},{5,7},{6,4},{7,5},{8,10},{9,11},{10,... | collective-permute-start | bytes 1474568 | tf_op jit(solution)/shard_map/ppermute | solution.py:122
  23.3 12.3 %collective-permute-start.13 = (bf16[176,384]{1,0:T(8,128)(2,1)}, bf16[176,384]{1,0:T(8,128)(2,1)}, u32[]{:S(2)}, u32[]{:S(2)}) collective-permute-start(bf16[176,384]{1,0:T(8,128)(2,1)} %fusion.183), channel_id=1, source_target_pairs={{0,8},{1,9},{2,10},{3,11},{4,12},{5,13},{6,14},{7,15},{8,0},{9,1},... | collective-permute-start | bytes 405512 | tf_op jit(solution)/shard_map/ppermute | solution.py:128
  27.9 30.6 %collective-permute-start.7 = (bf16[4,160,384]{2,1,0:T(8,128)(2,1)S(1)}, bf16[4,160,384]{2,1,0:T(8,128)(2,1)S(1)}, u32[]{:S(2)}, u32[]{:S(2)}) collective-permute-start(bf16[4,160,384]{2,1,0:T(8,128)(2,1)S(1)} %pad_maximum_fusion.17.refs_0_), channel_id=1, source_target_pairs={{0,1},{1,0},{2,3},{3,2},{4,5},{5,4},{6,7},{7,6},{8,9},{9,8},{10,11... | collective-permute-start | bytes 1474568 | tf_op jit(solution)/shard_map/ppermute | solution.py:125
  37.5 26.1 %collective-permute-start.15 = (bf16[4,176,384]{2,1,0:T(8,128)(2,1)}, bf16[4,176,384]{2,1,0:T(8,128)(2,1)}, u32[]{:S(2)}, u32[]{:S(2)}) collective-permute-start(bf16[4,176,384]{2,1,0:T(8,128)(2,1)} %pad_maximum_fusion.14.refs_0_), channel_id=1, source_target_pairs={{0,16},{1,17},{2,18},{3,19},{4,20},{5,21},{6,22},{7,23},{8,24},{9,... | collective-permute-start | bytes 1622024 | tf_op jit(solution)/shard_map/ppermute | solution.py:119
  38.2 18.3 %collective-permute-start.25 = (bf16[96,1024]{1,0:T(8,128)(2,1)S(1)}, bf16[96,1024]{1,0:T(8,128)(2,1)}, u32[]{:S(2)}, u32[]{:S(2)}) collective-permute-start(bf16[96,1024]{1,0:T(8,128)(2,1)S(1)} %fusion.182), channel_id=1, source_target_pairs={{0,8},{1,9},{2,10},{3,11},{4,12},{5,13},{6,14},{7,15},{8,0},{9,1},... | collective-permute-start | bytes 589832 | tf_op jit(solution)/shard_map/ppermute | solution.py:128
  39.5 18.5 %collective-permute-start.24 = (bf16[96,1024]{1,0:T(8,128)(2,1)S(1)}, bf16[96,1024]{1,0:T(8,128)(2,1)S(1)}, u32[]{:S(2)}, u32[]{:S(2)}) collective-permute-start(bf16[96,1024]{1,0:T(8,128)(2,1)S(1)} %fusion.182), channel_id=1, source_target_pairs={{0,4},{1,5},{2,6},{3,7},{4,8},{5,9},{6,10},{7,11},{8,12},{9,13},{1... | collective-permute-start | bytes 589832 | tf_op jit(solution)/shard_map/ppermute | solution.py:128
  44.5 22.4 %collective-permute-start.16 = (bf16[4,176,384]{2,1,0:T(8,128)(2,1)}, bf16[4,176,384]{2,1,0:T(8,128)(2,1)}, u32[]{:S(2)}, u32[]{:S(2)}) collective-permute-start(bf16[4,176,384]{2,1,0:T(8,128)(2,1)} %pad_maximum_fusion.14.refs_0_), channel_id=1, source_target_pairs={{0,2},{1,3},{2,0},{3,1},{4,6},{5,7},{6,4},{7,5},{8,10},{9,11},{10,... | collective-permute-start | bytes 1622024 | tf_op jit(solution)/shard_map/ppermute | solution.py:122
  66.9 136.9 %collective-permute-start.27 = (bf16[4,96,1024]{2,1,0:T(8,128)(2,1)}, bf16[4,96,1024]{2,1,0:T(8,128)(2,1)}, u32[]{:S(2)}, u32[]{:S(2)}) collective-permute-start(bf16[4,96,1024]{2,1,0:T(8,128)(2,1)} %pad_maximum_fusion.11.refs_0_), channel_id=1, source_target_pairs={{0,16},{1,17},{2,18},{3,19},{4,20},{5,21},{6,22},{7,23},{8,24},{9,... | collective-permute-start | bytes 2359304 | tf_op jit(solution)/shard_map/ppermute | solution.py:119
  67.5 136.4 %collective-permute-start.28 = (bf16[4,96,1024]{2,1,0:T(8,128)(2,1)}, bf16[4,96,1024]{2,1,0:T(8,128)(2,1)}, u32[]{:S(2)}, u32[]{:S(2)}) collective-permute-start(bf16[4,96,1024]{2,1,0:T(8,128)(2,1)} %pad_maximum_fusion.11.refs_0_), channel_id=1, source_target_pairs={{0,2},{1,3},{2,0},{3,1},{4,6},{5,7},{6,4},{7,5},{8,10},{9,11},{10,... | collective-permute-start | bytes 2359304 | tf_op jit(solution)/shard_map/ppermute | solution.py:122
  72.8 139.1 %collective-permute-start.19 = (bf16[4,176,384]{2,1,0:T(8,128)(2,1)}, bf16[4,176,384]{2,1,0:T(8,128)(2,1)}, u32[]{:S(2)}, u32[]{:S(2)}) collective-permute-start(bf16[4,176,384]{2,1,0:T(8,128)(2,1)} %pad_maximum_fusion.14.refs_0_), channel_id=1, source_target_pairs={{0,1},{1,0},{2,3},{3,2},{4,5},{5,4},{6,7},{7,6},{8,9},{9,8},{10,11... | collective-permute-start | bytes 1622024 | tf_op jit(solution)/shard_map/ppermute | solution.py:125
  72.9 130.3 %collective-permute-start.17 = (bf16[2,176,384]{2,1,0:T(8,128)(2,1)}, bf16[2,176,384]{2,1,0:T(8,128)(2,1)}, u32[]{:S(2)}, u32[]{:S(2)}) collective-permute-start(bf16[2,176,384]{2,1,0:T(8,128)(2,1)} %slice.338), channel_id=1, source_target_pairs={{0,16},{1,17},{2,18},{3,19},{4,20},{5,21},{6,22},{7,23},{8,24},{9,... | collective-permute-start | bytes 811016 | tf_op jit(solution)/shard_map/ppermute | solution.py:119
  74.4 128.9 %collective-permute-start.18 = (bf16[2,176,384]{2,1,0:T(8,128)(2,1)}, bf16[2,176,384]{2,1,0:T(8,128)(2,1)}, u32[]{:S(2)}, u32[]{:S(2)}) collective-permute-start(bf16[2,176,384]{2,1,0:T(8,128)(2,1)} %slice.339), channel_id=1, source_target_pairs={{0,2},{1,3},{2,0},{3,1},{4,6},{5,7},{6,4},{7,5},{8,10},{9,11},{10,... | collective-permute-start | bytes 811016 | tf_op jit(solution)/shard_map/ppermute | solution.py:122
  212.0 176.4 %collective-permute-start.31 = (bf16[4,96,1024]{2,1,0:T(8,128)(2,1)}, bf16[4,96,1024]{2,1,0:T(8,128)(2,1)}, u32[]{:S(2)}, u32[]{:S(2)}) collective-permute-start(bf16[4,96,1024]{2,1,0:T(8,128)(2,1)} %pad_maximum_fusion.11.refs_0_), channel_id=1, source_target_pairs={{0,1},{1,0},{2,3},{3,2},{4,5},{5,4},{6,7},{7,6},{8,9},{9,8},{10,11... | collective-permute-start | bytes 2359304 | tf_op jit(solution)/shard_map/ppermute | solution.py:125
  212.1 173.8 %collective-permute-start.29 = (bf16[2,96,1024]{2,1,0:T(8,128)(2,1)}, bf16[2,96,1024]{2,1,0:T(8,128)(2,1)S(1)}, u32[]{:S(2)}, u32[]{:S(2)}) collective-permute-start(bf16[2,96,1024]{2,1,0:T(8,128)(2,1)} %slice.341), channel_id=1, source_target_pairs={{0,16},{1,17},{2,18},{3,19},{4,20},{5,21},{6,22},{7,23},{8,24},{9,... | collective-permute-start | bytes 1179656 | tf_op jit(solution)/shard_map/ppermute | solution.py:119
  212.6 173.4 %collective-permute-start.30 = (bf16[2,96,1024]{2,1,0:T(8,128)(2,1)}, bf16[2,96,1024]{2,1,0:T(8,128)(2,1)}, u32[]{:S(2)}, u32[]{:S(2)}) collective-permute-start(bf16[2,96,1024]{2,1,0:T(8,128)(2,1)} %slice.342), channel_id=1, source_target_pairs={{0,2},{1,3},{2,0},{3,1},{4,6},{5,7},{6,4},{7,5},{8,10},{9,11},{10,... | collective-permute-start | bytes 1179656 | tf_op jit(solution)/shard_map/ppermute | solution.py:122
  214.0 174.4 %collective-permute-start.32 = (bf16[4,96,1024]{2,1,0:T(8,128)(2,1)}, bf16[4,96,1024]{2,1,0:T(8,128)(2,1)}, u32[]{:S(2)}, u32[]{:S(2)}) collective-permute-start(bf16[4,96,1024]{2,1,0:T(8,128)(2,1)} %collective-permute-done.27.refs_1_), channel_id=1, source_target_pairs={{0,1},{1,0},{2,3},{3,2},{4,5},{5,4},{6,7},{7,6},{8,9},{9,8},{10,11... | collective-permute-start | bytes 2359304 | tf_op jit(solution)/shard_map/ppermute | solution.py:125
  214.0 174.4 %collective-permute-start.33 = (bf16[4,96,1024]{2,1,0:T(8,128)(2,1)}, bf16[4,96,1024]{2,1,0:T(8,128)(2,1)}, u32[]{:S(2)}, u32[]{:S(2)}) collective-permute-start(bf16[4,96,1024]{2,1,0:T(8,128)(2,1)} %collective-permute-done.28.refs_2_), channel_id=1, source_target_pairs={{0,1},{1,0},{2,3},{3,2},{4,5},{5,4},{6,7},{7,6},{8,9},{9,8},{10,11... | collective-permute-start | bytes 2359304 | tf_op jit(solution)/shard_map/ppermute | solution.py:125
  709.3 73.0 %collective-permute-start.36 = (bf16[2,4,2,160,384]{4,3,1,2,0:T(8,128)(2,1)}, bf16[2,4,2,160,384]{4,3,1,2,0:T(8,128)(2,1)}, u32[]{:S(2)}, u32[]{:S(2)}) collective-permute-start(bf16[2,4,2,160,384]{4,3,1,2,0:T(8,128)(2,1)} %copy_bitcast_fusion.3), channel_id=1, source_target_pairs={{0,1},{1,0},{2,3},{3,2},{4,5},{5,4},{6,7},{7,6},{8,9},{9,8},{10,11... | collective-permute-start | bytes 5898248 | tf_op jit(solution)/shard_map/ppermute | solution.py:125
  732.3 54.7 %collective-permute-start.44 = (bf16[2,4,2,176,384]{4,3,1,2,0:T(8,128)(2,1)}, bf16[2,4,2,176,384]{4,3,1,2,0:T(8,128)(2,1)}, u32[]{:S(2)}, u32[]{:S(2)}) collective-permute-start(bf16[2,4,2,176,384]{4,3,1,2,0:T(8,128)(2,1)} %copy_bitcast_fusion.2), channel_id=1, source_target_pairs={{0,1},{1,0},{2,3},{3,2},{4,5},{5,4},{6,7},{7,6},{8,9},{9,8},{10,11... | collective-permute-start | bytes 6488072 | tf_op jit(solution)/shard_map/ppermute | solution.py:125
  779.0 48.9 %collective-permute-start.52 = (bf16[2,4,2,96,1024]{4,3,1,2,0:T(8,128)(2,1)S(1)}, bf16[2,4,2,96,1024]{4,3,1,2,0:T(8,128)(2,1)S(1)}, u32[]{:S(2)}, u32[]{:S(2)}) collective-permute-start(bf16[2,4,2,96,1024]{4,3,1,2,0:T(8,128)(2,1)S(1)} %bitcast.653), channel_id=1, source_target_pairs={{0,1},{1,0},{2,3},{3,2},{4,5},{5,4},{6,7},{7,6},{8,9},{9,8},{10,11... | collective-permute-start | bytes 9437192 | tf_op jit(solution)/shard_map/ppermute | solution.py:125
  788.2 14.8 %collective-permute-start.47 = (bf16[2,176,384]{2,1,0:T(8,128)(2,1)S(1)}, bf16[2,176,384]{2,1,0:T(8,128)(2,1)S(1)}, u32[]{:S(2)}, u32[]{:S(2)}) collective-permute-start(bf16[2,176,384]{2,1,0:T(8,128)(2,1)S(1)} %get-tuple-element.231), channel_id=1, source_target_pairs={{0,16},{1,17},{2,18},{3,19},{4,20},{5,21},{6,22},{7,23},{8,24},{9,... | collective-permute-start | bytes 811016 | tf_op jit(solution)/shard_map/ppermute | solution.py:119
  788.8 14.2 %collective-permute-start.45 = (bf16[2,176,384]{2,1,0:T(8,128)(2,1)S(1)}, bf16[2,176,384]{2,1,0:T(8,128)(2,1)S(1)}, u32[]{:S(2)}, u32[]{:S(2)}) collective-permute-start(bf16[2,176,384]{2,1,0:T(8,128)(2,1)S(1)} %get-tuple-element.230), channel_id=1, source_target_pairs={{0,2},{1,3},{2,0},{3,1},{4,6},{5,7},{6,4},{7,5},{8,10},{9,11},{10,... | collective-permute-start | bytes 811016 | tf_op jit(solution)/shard_map/ppermute | solution.py:122
  795.6 13.4 %collective-permute-start.40 = (bf16[4,160,384]{2,1,0:T(8,128)(2,1)S(1)}, bf16[4,160,384]{2,1,0:T(8,128)(2,1)S(1)}, u32[]{:S(2)}, u32[]{:S(2)}) collective-permute-start(bf16[4,160,384]{2,1,0:T(8,128)(2,1)S(1)} %pad_maximum_fusion.19), channel_id=1, source_target_pairs={{0,2},{1,3},{2,0},{3,1},{4,6},{5,7},{6,4},{7,5},{8,10},{9,11},{10,... | collective-permute-start | bytes 1474568 | tf_op jit(solution)/shard_map/ppermute | solution.py:122
  796.4 12.7 %collective-permute-start.38 = (bf16[4,160,384]{2,1,0:T(8,128)(2,1)S(1)}, bf16[4,160,384]{2,1,0:T(8,128)(2,1)S(1)}, u32[]{:S(2)}, u32[]{:S(2)}) collective-permute-start(bf16[4,160,384]{2,1,0:T(8,128)(2,1)S(1)} %pad_maximum_fusion.18), channel_id=1, source_target_pairs={{0,16},{1,17},{2,18},{3,19},{4,20},{5,21},{6,22},{7,23},{8,24},{9,... | collective-permute-start | bytes 1474568 | tf_op jit(solution)/shard_map/ppermute | solution.py:119
  810.7 14.5 %collective-permute-start.42 = (bf16[160,384]{1,0:T(8,128)(2,1)S(1)}, bf16[160,384]{1,0:T(8,128)(2,1)S(1)}, u32[]{:S(2)}, u32[]{:S(2)}) collective-permute-start(bf16[160,384]{1,0:T(8,128)(2,1)S(1)} %get-tuple-element.273), channel_id=1, source_target_pairs={{0,8},{1,9},{2,10},{3,11},{4,12},{5,13},{6,14},{7,15},{8,0},{9,1},... | collective-permute-start | bytes 368648 | tf_op jit(solution)/shard_map/ppermute | solution.py:128
  815.6 31.3 %collective-permute-start.48 = (bf16[4,176,384]{2,1,0:T(8,128)(2,1)S(1)}, bf16[4,176,384]{2,1,0:T(8,128)(2,1)S(1)}, u32[]{:S(2)}, u32[]{:S(2)}) collective-permute-start(bf16[4,176,384]{2,1,0:T(8,128)(2,1)S(1)} %pad_maximum_fusion.16), channel_id=1, source_target_pairs={{0,2},{1,3},{2,0},{3,1},{4,6},{5,7},{6,4},{7,5},{8,10},{9,11},{10,... | collective-permute-start | bytes 1622024 | tf_op jit(solution)/shard_map/ppermute | solution.py:122
  830.4 21.6 %collective-permute-start.46 = (bf16[4,176,384]{2,1,0:T(8,128)(2,1)S(1)}, bf16[4,176,384]{2,1,0:T(8,128)(2,1)S(1)}, u32[]{:S(2)}, u32[]{:S(2)}) collective-permute-start(bf16[4,176,384]{2,1,0:T(8,128)(2,1)S(1)} %pad_maximum_fusion.15), channel_id=1, source_target_pairs={{0,16},{1,17},{2,18},{3,19},{4,20},{5,21},{6,22},{7,23},{8,24},{9,... | collective-permute-start | bytes 1622024 | tf_op jit(solution)/shard_map/ppermute | solution.py:119
  842.5 28.6 %collective-permute-start.56 = (bf16[4,96,1024]{2,1,0:T(8,128)(2,1)}, bf16[4,96,1024]{2,1,0:T(8,128)(2,1)S(1)}, u32[]{:S(2)}, u32[]{:S(2)}) collective-permute-start(bf16[4,96,1024]{2,1,0:T(8,128)(2,1)} %pad_maximum_fusion.13), channel_id=1, source_target_pairs={{0,2},{1,3},{2,0},{3,1},{4,6},{5,7},{6,4},{7,5},{8,10},{9,11},{10,... | collective-permute-start | bytes 2359304 | tf_op jit(solution)/shard_map/ppermute | solution.py:122
  845.4 25.7 %collective-permute-start.54 = (bf16[4,96,1024]{2,1,0:T(8,128)(2,1)}, bf16[4,96,1024]{2,1,0:T(8,128)(2,1)}, u32[]{:S(2)}, u32[]{:S(2)}) collective-permute-start(bf16[4,96,1024]{2,1,0:T(8,128)(2,1)} %pad_maximum_fusion.12), channel_id=1, source_target_pairs={{0,16},{1,17},{2,18},{3,19},{4,20},{5,21},{6,22},{7,23},{8,24},{9,... | collective-permute-start | bytes 2359304 | tf_op jit(solution)/shard_map/ppermute | solution.py:119
  875.9 12.6 %collective-permute-start.58 = (bf16[96,1024]{1,0:T(8,128)(2,1)S(1)}, bf16[96,1024]{1,0:T(8,128)(2,1)}, u32[]{:S(2)}, u32[]{:S(2)}) collective-permute-start(bf16[96,1024]{1,0:T(8,128)(2,1)S(1)} %get-tuple-element.264), channel_id=1, source_target_pairs={{0,8},{1,9},{2,10},{3,11},{4,12},{5,13},{6,14},{7,15},{8,0},{9,1},... | collective-permute-start | bytes 589832 | tf_op jit(solution)/shard_map/ppermute | solution.py:128
  892.6 29.5 %collective-permute-start.67 = (bf16[96,1024]{1,0:T(8,128)(2,1)}, bf16[96,1024]{1,0:T(8,128)(2,1)}, u32[]{:S(2)}, u32[]{:S(2)}) collective-permute-start(bf16[96,1024]{1,0:T(8,128)(2,1)} %get-tuple-element.209), channel_id=1, source_target_pairs={{0,16},{1,17},{2,18},{3,19},{4,20},{5,21},{6,22},{7,23},{8,24},{9,... | collective-permute-start | bytes 589832 | tf_op jit(solution)/shard_map/ppermute | solution.py:119
  (106 other events, 1138.7 us)

commit v2 on v0

v2 whole, which is shorter than its diff:
```python
import functools
import math

import jax
import jax.numpy as jnp
from jax import lax
from jax.experimental import pallas as pl
from jax.experimental.pallas import tpu as pltpu
from jax.sharding import PartitionSpec as P

HD = 64
STEP = 10


NORM_EPS = 1e-06
MASKED = -1000000000.0
BETA_ONE = 0.9
BETA_TWO = 0.999
ADAM_EPS = 1e-08
CLIP_AT = 1.0
MATRIX_RATE = 0.04
MATRIX_DECAY = 0.1
GAIN_RATE = 0.8

EVERY = ("dp", "fsdp")
LOW = jnp.bfloat16
WIDE = jnp.float32
SLAB = 16
VMEM_LIMIT = 56 * 1024 * 1024
ANYWHERE = pl.BlockSpec(memory_space=pl.ANY)


class Grid:
    def __init__(self, dp, fsdp):
        self.dp, self.fsdp = dp, fsdp
        self.nz = fsdp // 4
        power = self.nz & (self.nz - 1) == 0
        self.cube = dp == 2 and fsdp % 4 == 0 and self.nz % 2 == 0 and power

    def move(self, step):
        pairs = []
        for source in range(self.dp * self.fsdp):
            x, rest = divmod(source, self.fsdp)
            z, rest = divmod(rest, 4)
            y, core = divmod(rest, 2)
            x, z, y, core = step(x, z, y, core)
            pairs.append((source, x * self.fsdp + (z * 2 + y) * 2 + core))
        return pairs

    def flip_x(self, v):
        return lax.ppermute(v, EVERY, self.move(lambda x, z, y, c: (1 - x, z, y, c)))

    def flip_y(self, v):
        return lax.ppermute(v, EVERY, self.move(lambda x, z, y, c: (x, z, 1 - y, c)))

    def flip_core(self, v):
        return lax.ppermute(v, EVERY, self.move(lambda x, z, y, c: (x, z, y, 1 - c)))

    def shift_z(self, v, by):
        return lax.ppermute(v, EVERY, self.move(lambda x, z, y, c: (x, (z + by) % self.nz, y, c)))

    def swap_z(self, v, bit):
        return lax.ppermute(v, EVERY, self.move(lambda x, z, y, c: (x, z ^ bit, y, c)))

    def place(self):
        x, f = lax.axis_index("dp"), lax.axis_index("fsdp")
        return x, f // 4, lax.rem(f // 2, 2), lax.rem(f, 2)


def spread(grid, part):
    half = grid.nz // 2
    column = jnp.stack([part] + [grid.shift_z(part, k) for k in range(1, grid.nz)])
    side = grid.flip_x(column)
    across = grid.flip_y(column)
    corner_low = grid.flip_x(across[:half])
    corner_high = grid.flip_y(side[half:])
    mine = [column, side, across, corner_low, corner_high]
    return mine + [grid.flip_core(piece) for piece in mine]


def piece_places(grid):
    nz, half = grid.nz, grid.nz // 2
    spots = [(0, 0, 0, nz), (1, 0, 0, nz), (0, 1, 0, nz), (1, 1, 0, half), (1, 1, half, nz - half)]
    return [(dx, dy, dc, low, n) for dc in (0, 1) for dx, dy, low, n in spots]


def gather_groups(grid, groups):
    if not grid.cube:
        return [lax.all_gather(split_columns(g), "fsdp", axis=1) for g in groups]
    x = lax.axis_index("dp")
    parts = [lax.dynamic_index_in_dim(split_columns(g), x, 0, False) for g in groups]
    pieces = []
    for n, part in enumerate(parts):
        if n:
            part, pieces[-1][0] = lax.optimization_barrier((part, pieces[-1][0]))
        pieces.append(spread(grid, part))
    return pieces


def reduce_group(grid, keep, sent):
    x, z, y, c = grid.place()
    nz, half = grid.nz, grid.nz // 2
    got = grid.flip_core(sent)
    keep, got = (v.reshape((2, nz, 2) + v.shape[2:]) for v in (keep, got))

    def block(h, at_y, low, n):
        total = 0.0
        for array in (keep, got):
            part = lax.dynamic_index_in_dim(array, h, 0, False)[low : low + n]
            total = total + lax.dynamic_index_in_dim(part, at_y, 1, False).astype(WIDE)
        return total

    def low(v):
        return v.astype(LOW)

    in_x = grid.flip_x(low(block(1 - x, 1 - y, 0, half)))
    in_y = grid.flip_y(low(block(1 - x, 1 - y, half, nz - half)))
    to_x = jnp.concatenate(
        [block(1 - x, y, 0, half), block(1 - x, y, half, nz - half) + in_y.astype(WIDE)]
    )
    to_y = jnp.concatenate(
        [block(x, 1 - y, 0, half) + in_x.astype(WIDE), block(x, 1 - y, half, nz - half)]
    )
    got_x, got_y = grid.flip_x(low(to_x)), grid.flip_y(low(to_y))
    column = low(block(x, y, 0, nz) + got_x.astype(WIDE) + got_y.astype(WIDE))
    total = lax.dynamic_index_in_dim(column, z, 0, False).astype(WIDE)
    for k in range(1, nz):
        out = lax.dynamic_index_in_dim(column, lax.rem(z + k, nz), 0, False)
        total = total + grid.shift_z(out, k).astype(WIDE)
    return low(total)


def both_halves(grid, total):
    x = lax.axis_index("dp")
    other = grid.flip_x(total)
    first = jnp.where(x == 0, total, other)
    return jnp.concatenate([first, jnp.where(x == 0, other, total)], -1)


def total_of(grid, value):
    if not grid.cube:
        return lax.psum(value, "fsdp")
    value = grid.flip_core(value) + value
    value = grid.flip_x(value) + value
    value = grid.flip_y(value) + value
    bit = 1
    while bit < grid.nz:
        value = grid.swap_z(value, bit) + value
        bit *= 2
    return value


def split_columns(v):
    return jnp.stack(jnp.split(v, 2, -1))


def params(semantics=None):
    return pltpu.CompilerParams(vmem_limit_bytes=VMEM_LIMIT, dimension_semantics=semantics)


def cost(flops, moved, hard=0):
    return pl.CostEstimate(flops=int(flops), bytes_accessed=int(moved), transcendentals=int(hard))


def dot(a, b):
    return jnp.dot(a, b, preferred_element_type=WIDE)


def dot_nt(a, b):
    return lax.dot_general(a, b, (((1,), (1,)), ((), ())), preferred_element_type=WIDE)


def dot_tn(a, b):
    return lax.dot_general(a, b, (((0,), (0,)), ((), ())), preferred_element_type=WIDE)


class Source:
    def __init__(self, grid, arrays):
        self.grid, self.arrays = grid, arrays
        self.specs = [ANYWHERE] * len(arrays)

    def copy(self, refs, low, rows, target, sem):
        grid = self.grid
        x, z, y, c = grid.place()
        for ref, (dx, dy, dc, first, n) in zip(refs, piece_places(grid)):
            half = lax.rem(x + dx, 2)
            for level in range(n):
                owner_z = lax.rem(z - (first + level) + grid.nz, grid.nz)
                shard = (owner_z * 2 + lax.rem(y + dy, 2)) * 2 + lax.rem(c + dc, 2)
                source = ref.at[level, pl.ds(low, rows)]
                pltpu.make_async_copy(source, target(half, shard), sem).start()


def wait_all(ref, sem):
    pltpu.make_async_copy(ref, ref, sem).wait()


def shard_target(matrix, rows):
    n = matrix.shape[-1] // 2

    def target(half, shard):
        return matrix.at[
            pl.ds(pl.multiple_of(shard * rows, 16), rows), pl.ds(pl.multiple_of(half * n, 128), n)
        ]

    return target


def start_load(source, refs, low, rows, matrix, sem, whole=0):
    if source.grid.cube:
        source.copy(refs, low, rows, shard_target(matrix, rows), sem)
    else:
        pltpu.make_async_copy(refs[whole], matrix, sem).start()


def store_grad(grid, refs, index, low, rows, value):
    lead, columns = index
    if not grid.cube:
        refs[0][lead, :, low : low + rows, columns] = value.astype(LOW).reshape(grid.fsdp, rows, -1)
        return
    c = lax.rem(lax.axis_index("fsdp"), 2)
    value = value.astype(LOW).reshape(grid.fsdp // 2, 2, rows, value.shape[-1])
    even, odd = value[:, 0], value[:, 1]
    refs[0][lead, :, low : low + rows, columns] = jnp.where(c == 0, even, odd)
    refs[1][lead, :, low : low + rows, columns] = jnp.where(c == 0, odd, even)


def grad_shapes(grid, rows, columns):
    if not grid.cube:
        return [jax.ShapeDtypeStruct((2, grid.fsdp, rows, columns // 2), LOW)]
    return [jax.ShapeDtypeStruct((2, grid.fsdp // 2, rows, columns // 2), LOW)] * 2


def norm_rows(values):
    return lax.rsqrt(jnp.mean(values * values, -1, keepdims=True) + NORM_EPS)


def norm_back(values, scale, gain, grad):
    y = values * scale
    c = grad * gain
    back = scale * (c - y * jnp.mean(c * y, -1, keepdims=True))
    return back, jnp.sum(grad * y, 0, keepdims=True)


def project_in(grid, source, image, gains):
    length, width = image.shape
    rows = width // grid.fsdp
    count = len(source.arrays)

    def body(*refs):
        image_ref, gains_ref, pieces = refs[0], refs[1], refs[2 : 2 + count]
        normed_ref, qkv_ref, gains_out, weights, slabs, sems = refs[2 + count :]
        for j in range(3):
            start_load(source, pieces, j * rows, rows, weights.at[j], sems.at[j], j)
        if grid.cube:
            source.copy(pieces, 3 * rows, SLAB, lambda h, f: slabs.at[h, f], sems.at[3])
        values = image_ref[...].astype(WIDE)
        scaled = values * norm_rows(values)
        if grid.cube:
            wait_all(slabs, sems.at[3])
            found = jnp.sum(slabs[...].astype(WIDE), 1)
            gain = jnp.concatenate([found[0], found[1]], -1)
        else:
            gain = gains_ref[...].astype(WIDE)
        gains_out[...] = gain
        normed = (scaled * gain[0:1]).astype(LOW)
        normed_ref[...] = normed
        for j in range(3):
            wait_all(weights.at[j], sems.at[j])
            qkv_ref[j] = dot(normed, weights[j]).astype(LOW)

    vmem = pl.BlockSpec(memory_space=pltpu.VMEM)
    return pl.pallas_call(
        body,
        out_shape=[
            jax.ShapeDtypeStruct((length, width), LOW),
            jax.ShapeDtypeStruct((3, length, width), LOW),
            jax.ShapeDtypeStruct((SLAB, width), WIDE),
        ],
        in_specs=[vmem, vmem] + source.specs,
        out_specs=[vmem] * 3,
        scratch_shapes=[
            pltpu.VMEM((3, width, width), LOW),
            pltpu.VMEM((2, grid.fsdp, SLAB, width // 2), LOW),
            pltpu.SemaphoreType.DMA((4,)),
        ],
        compiler_params=params(),
        cost_estimate=cost(6 * length * width * width, 8 * width * width + 10 * length * width),
        name="project_in",
    )(image, gains, *source.arrays)


def attend(qkv, counts):
    length, width = qkv.shape[1:]
    pair = 2 * HD

    def body(counts_ref, qkv_ref, context_ref):
        seen = lax.broadcasted_iota(jnp.int32, (1, length), 1) < counts_ref[0]
        first = lax.broadcasted_iota(jnp.int32, (1, pair), 1) < HD
        q, k, v = qkv_ref[0], qkv_ref[1], qkv_ref[2]
        found = []
        for head in range(2):
            own = first if head == 0 else jnp.logical_not(first)
            scores = dot_nt(jnp.where(own, q, jnp.zeros_like(q)), k)
            scores = jnp.where(seen, scores, MASKED)
            probs = jnp.exp(scores - jnp.max(scores, -1, keepdims=True))
            summed = dot(probs.astype(LOW), jnp.where(own, v, jnp.ones_like(v)))
            found.append(summed / pltpu.roll(summed, HD, 1))
        context_ref[...] = jnp.where(first, found[0], found[1]).astype(LOW)

    return pl.pallas_call(
        body,
        grid=(width // pair,),
        out_shape=jax.ShapeDtypeStruct((length, width), LOW),
        in_specs=[
            pl.BlockSpec(memory_space=pltpu.SMEM),
            pl.BlockSpec((3, length, pair), lambda i: (0, 0, i)),
        ],
        out_specs=pl.BlockSpec((length, pair), lambda i: (0, i)),
        compiler_params=params(("arbitrary",)),
        cost_estimate=cost(
            4 * length * length * width, 8 * length * width, length * length * width // HD
        ),
        name="attend",
    )(counts, qkv)


def attend_back(qkv, d_context, counts):
    length, width = qkv.shape[1:]
    pair = 2 * HD

    def body(counts_ref, qkv_ref, d_ref, out_ref):
        seen = lax.broadcasted_iota(jnp.int32, (length, 1), 0) < counts_ref[0]
        first = lax.broadcasted_iota(jnp.int32, (1, pair), 1) < HD
        q, k, v, d = qkv_ref[0], qkv_ref[1], qkv_ref[2], d_ref[...]
        found = []
        for head in range(2):
            own = first if head == 0 else jnp.logical_not(first)
            scores = dot_nt(k, jnp.where(own, q, jnp.zeros_like(q)))
            scores = jnp.where(seen, scores, MASKED)
            probs = jnp.exp(scores - jnp.max(scores, 0, keepdims=True))
            probs = probs * (1.0 / jnp.sum(probs, 0, keepdims=True))
            d_probs = dot_nt(v, jnp.where(own, d, jnp.zeros_like(d)))
            weighed = probs * d_probs
            d_scores = (weighed - probs * jnp.sum(weighed, 0, keepdims=True)).astype(LOW)
            found.append((dot_tn(d_scores, k), dot(d_scores, q), dot(probs.astype(LOW), d)))
        for j in range(3):
            out_ref[j] = jnp.where(first, found[0][j], found[1][j]).astype(LOW)

    return pl.pallas_call(
        body,
        grid=(width // pair,),
        out_shape=jax.ShapeDtypeStruct((3, length, width), LOW),
        in_specs=[
            pl.BlockSpec(memory_space=pltpu.SMEM),
            pl.BlockSpec((3, length, pair), lambda i: (0, 0, i)),
            pl.BlockSpec((length, pair), lambda i: (0, i)),
        ],
        out_specs=pl.BlockSpec((3, length, pair), lambda i: (0, 0, i)),
        compiler_params=params(("arbitrary",)),
        cost_estimate=cost(
            10 * length * length * width, 14 * length * width, length * length * width // HD
        ),
        name="attend_back",
    )(counts, qkv, d_context)


def feed_forward(grid, second, third, image, context, cotangent, counts, gains):
    length, width = image.shape
    rows = width // grid.fsdp
    down_rows = second.down_rows
    hidden_width = down_rows * grid.fsdp
    steps = 4
    chunk = hidden_width // steps
    n_second, n_third = len(second.arrays), len(third.arrays)
    n_refs = len(grad_shapes(grid, rows, width))

    def body(*refs):
        counts_ref, image_ref, context_ref, cotangent_ref, gains_ref = refs[:5]
        seconds, refs = refs[5 : 5 + n_second], refs[5 + n_second :]
        thirds, refs = refs[:n_third], refs[n_third:]
        output_ref, d_attended_ref, d_context_ref, d_gain_ref = refs[:4]
        out_grads, refs = refs[4 : 4 + n_refs], refs[4 + n_refs :]
        in_grads, refs = refs[:n_refs], refs[n_refs:]
        w_out, w_down, w_gate, w_up, attended, normed, normed_t, e_ref, total, d_normed, sems = refs
        step = pl.program_id(0)
        seen = lax.broadcasted_iota(jnp.int32, (length, 1), 0) < counts_ref[0]

        @pl.when(step == 0)
        def _():
            start_load(second, seconds, 0, rows, w_out, sems.at[0], 0)
            start_load(third, thirds, 0, rows, w_gate, sems.at[1], 0)
            start_load(third, thirds, rows, rows, w_up, sems.at[2], 1)
            start_load(second, seconds, rows, down_rows, w_down, sems.at[3], 1)
            e = cotangent_ref[...]
            e_ref[...] = jnp.where(seen, e, jnp.zeros_like(e))
            wait_all(w_out, sems.at[0])
            values = image_ref[...].astype(WIDE) + dot(context_ref[...], w_out[...])
            attended[...] = values
            low = (values * norm_rows(values) * gains_ref[1:2]).astype(LOW)
            normed[...] = low
            normed_t[...] = low.T
            total[...] = values
            d_normed[...] = jnp.zeros_like(d_normed)
            wait_all(w_gate, sems.at[1])
            wait_all(w_up, sems.at[2])
            wait_all(w_down, sems.at[3])

        columns = pl.ds(pl.multiple_of(step * chunk, chunk), chunk)
        gate_w, up_w, down_w = w_gate[:, columns], w_up[:, columns], w_down[columns]
        e = e_ref[...]
        gate, up = dot(normed[...], gate_w), dot(normed[...], up_w)
        square = gate * gate
        bend = jnp.tanh(0.7978845608 * (gate + 0.044715 * square * gate))
        half_up = 0.5 * (1.0 + bend)
        gelu = gate * half_up
        slope = half_up + 0.5 * gate * (1.0 - bend * bend) * (
            0.7978845608 * (1.0 + 3.0 * 0.044715 * square)
        )
        hidden = (gelu * up).astype(LOW)
        total[...] += dot(hidden, down_w)
        d_hidden = dot_nt(e, down_w)
        d_gate = (d_hidden * up * slope).astype(LOW)
        d_up = (d_hidden * gelu).astype(LOW)
        g_down = dot_tn(hidden, e)
        shards = chunk // down_rows
        if grid.cube:
            c = lax.rem(lax.axis_index("fsdp"), 2)
            g_down = g_down.astype(LOW).reshape(shards // 2, 2, down_rows, width)
            even, odd = g_down[:, 0], g_down[:, 1]
            g_down = [jnp.where(c == 0, even, odd), jnp.where(c == 0, odd, even)]
            lead = pl.ds(step * (shards // 2), shards // 2)
        else:
            g_down = [g_down.astype(LOW).reshape(shards, down_rows, width)]
            lead = pl.ds(step * shards, shards)
        for ref, value in zip(out_grads, g_down):
            for h in range(2):
                ref[h, lead, rows:] = value[:, :, h * (width // 2) : (h + 1) * (width // 2)]
        everything = (0, slice(None))
        store_grad(grid, in_grads, everything, 0, rows, dot(normed_t[...], d_gate))
        store_grad(grid, in_grads, everything, rows, rows, dot(normed_t[...], d_up))
        d_normed[...] += dot_nt(d_gate, gate_w) + dot_nt(d_up, up_w)

        @pl.when(step == steps - 1)
        def _():
            output_ref[...] = jnp.where(seen, total[...], 0.0).astype(LOW)
            values = attended[...]
            back, d_gain = norm_back(values, norm_rows(values), gains_ref[1:2], d_normed[...])
            d_gain_ref[...] = jnp.broadcast_to(d_gain, d_gain_ref.shape)
            d_attended = e_ref[...].astype(WIDE) + back
            d_attended_ref[...] = d_attended
            low = d_attended.astype(LOW)
            d_context_ref[...] = dot_nt(low, w_out[...]).astype(LOW)
            g_out = dot_tn(context_ref[...], low)
            for h in range(2):
                part = g_out[:, h * (width // 2) : (h + 1) * (width // 2)]
                store_grad(grid, out_grads, (h, slice(None)), 0, rows, part)

    vmem = pl.BlockSpec(memory_space=pltpu.VMEM)
    per_half = steps // 2
    out_grads = grad_shapes(grid, rows + down_rows, width)
    in_grads = grad_shapes(grid, 2 * rows, hidden_width)
    block = (1,) + in_grads[0].shape[1:3] + (chunk,)
    in_block = pl.BlockSpec(block, lambda i: (i // per_half, 0, 0, lax.rem(i, per_half)))
    results = pl.pallas_call(
        body,
        grid=(steps,),
        out_shape=[
            jax.ShapeDtypeStruct((length, width), LOW),
            jax.ShapeDtypeStruct((length, width), WIDE),
            jax.ShapeDtypeStruct((length, width), LOW),
            jax.ShapeDtypeStruct((8, width), WIDE),
        ]
        + out_grads
        + in_grads,
        in_specs=[pl.BlockSpec(memory_space=pltpu.SMEM)] + [vmem] * 4 + second.specs + third.specs,
        out_specs=[vmem] * (4 + n_refs) + [in_block] * n_refs,
        scratch_shapes=[
            pltpu.VMEM((width, width), LOW),
            pltpu.VMEM((hidden_width, width), LOW),
            pltpu.VMEM((width, hidden_width), LOW),
            pltpu.VMEM((width, hidden_width), LOW),
            pltpu.VMEM((length, width), WIDE),
            pltpu.VMEM((length, width), LOW),
            pltpu.VMEM((width, length), LOW),
            pltpu.VMEM((length, width), LOW),
            pltpu.VMEM((length, width), WIDE),
            pltpu.VMEM((length, width), WIDE),
            pltpu.SemaphoreType.DMA((4,)),
        ],
        compiler_params=params(("arbitrary",)),
        cost_estimate=cost(
            6 * length * width * (3 * hidden_width + width),
            8 * width * (3 * hidden_width + width),
            length * hidden_width,
        ),
        name="feed_forward",
    )(counts, image, context, cotangent, gains, *second.arrays, *third.arrays)
    return results[:4], results[4 : 4 + n_refs], results[4 + n_refs :]


def project_back(grid, source, image, normed, d_qkv, d_attended, gains, d_gain_two):
    length, width = image.shape
    rows = width // grid.fsdp
    count = len(source.arrays)
    n_refs = len(grad_shapes(grid, rows, width))

    def body(*refs):
        image_ref, normed_ref, d_qkv_ref, d_attended_ref, gains_ref, d_gain_ref = refs[:6]
        pieces, refs = refs[6 : 6 + count], refs[6 + count :]
        input_grad_ref, grads, weights, sems = refs[0], refs[1 : 1 + n_refs], refs[-2], refs[-1]
        for j in range(3):
            start_load(source, pieces, j * rows, rows, weights.at[j], sems.at[j], j)
        normed_t = normed_ref[...].T
        for j in range(3):
            g = dot(normed_t, d_qkv_ref[j])
            for h in range(2):
                part = g[:, h * (width // 2) : (h + 1) * (width // 2)]
                store_grad(grid, grads, (h, slice(None)), j * rows, rows, part)
        d_normed = jnp.zeros((length, width), WIDE)
        for j in range(3):
            wait_all(weights.at[j], sems.at[j])
            d_normed = d_normed + dot_nt(d_qkv_ref[j], weights[j])
        values = image_ref[...].astype(WIDE)
        back, d_gain = norm_back(values, norm_rows(values), gains_ref[0:1], d_normed)
        input_grad_ref[...] = (d_attended_ref[...] + back).astype(LOW)
        slab = jnp.concatenate(
            [d_gain, d_gain_ref[0:1], jnp.zeros((SLAB - 2, width), WIDE)], 0
        ).astype(LOW)
        for h in range(2):
            part = slab[:, h * (width // 2) : (h + 1) * (width // 2)]
            for ref in grads:
                ref[h, :, 3 * rows :] = jnp.broadcast_to(part[None], (ref.shape[1],) + part.shape)

    vmem = pl.BlockSpec(memory_space=pltpu.VMEM)
    results = pl.pallas_call(
        body,
        out_shape=[jax.ShapeDtypeStruct((length, width), LOW)]
        + grad_shapes(grid, 3 * rows + SLAB, width),
        in_specs=[vmem] * 6 + source.specs,
        out_specs=[vmem] * (1 + n_refs),
        scratch_shapes=[
            pltpu.VMEM((3, width, width), LOW),
            pltpu.SemaphoreType.DMA((3,)),
        ],
        compiler_params=params(),
        cost_estimate=cost(12 * length * width * width, 18 * width * width + 14 * length * width),
        name="project_back",
    )(image, normed, d_qkv, d_attended, gains, d_gain_two, *source.arrays)
    return results[0], results[1:]


def adamw(param, first, second, grad, rate, decay):
    first = BETA_ONE * first + (1.0 - BETA_ONE) * grad
    second = BETA_TWO * second + (1.0 - BETA_TWO) * grad * grad
    update = first / (1.0 - BETA_ONE**STEP) / (jnp.sqrt(second / (1.0 - BETA_TWO**STEP)) + ADAM_EPS)
    return (param - rate * (update + decay * param), first, second)


def on_device(
    grid,
    patches,
    counts,
    cotangent,
    w_attn,
    w_in,
    w_down,
    gains,
    m_attn,
    m_in,
    m_down,
    m_gains,
    v_attn,
    v_in,
    v_down,
    v_gains,
):
    image, e = patches[0], cotangent[0]
    width = image.shape[1]
    rows, down_rows = w_attn.shape[1], w_down.shape[0]
    shard = lax.axis_index("fsdp")
    low_attn, low_in, low_down, low_gains = (
        w.astype(LOW) for w in (w_attn, w_in, w_down, gains)
    )
    owned = lax.broadcasted_iota(jnp.int32, (1, width), 1) // rows == shard
    slab = jnp.where(owned, jnp.tile(low_gains, (1, grid.fsdp)), jnp.zeros((), LOW))
    slab = jnp.pad(slab, ((0, SLAB - 2), (0, 0)))
    groups = gather_groups(
        grid,
        [
            jnp.concatenate([low_attn[0], low_attn[1], low_attn[2], slab], 0),
            jnp.concatenate([low_attn[3], low_down], 0),
            jnp.concatenate([low_in[0], low_in[1]], 0),
        ],
    )
    whole_gains = jnp.zeros((SLAB, width), WIDE)
    if not grid.cube:

        def whole(full, low, n):
            full = full[:, :, low : low + n].reshape(2, grid.fsdp * n, full.shape[3])
            return jnp.concatenate([full[0], full[1]], -1)

        first_full, second_full, third_full = groups
        slabs = jnp.sum(first_full[:, :, 3 * rows :].astype(WIDE), 1)
        whole_gains = jnp.concatenate([slabs[0], slabs[1]], -1)
        groups = [
            [whole(first_full, j * rows, rows) for j in range(3)],
            [whole(second_full, 0, rows), whole(second_full, rows, down_rows)],
            [whole(third_full, j * rows, rows) for j in range(2)],
        ]
    first, second, third = (Source(grid, g) for g in groups)
    second.down_rows = down_rows

    normed, qkv, full_gains = project_in(grid, first, image, whole_gains)
    context = attend(qkv, counts)
    (output, d_attended, d_context, d_gain_two), out_grads, in_grads = feed_forward(
        grid, second, third, image, context, e, counts, full_gains
    )
    d_qkv = attend_back(qkv, d_context, counts)
    input_grad, qkv_grads = project_back(
        grid, first, image, normed, d_qkv, d_attended, full_gains, d_gain_two
    )

    if grid.cube:
        third, second, first = (
            reduce_group(grid, *g) for g in (in_grads, out_grads, qkv_grads)
        )
        x = lax.axis_index("dp")
        half = width // 2
        mine = lax.dynamic_slice_in_dim(owned, x * half, half, 1)
    else:

        def reduce_whole(g):
            total = lax.psum_scatter(g.astype(WIDE), "fsdp", scatter_dimension=1)
            total = lax.psum(total.astype(LOW), "dp")
            return jnp.concatenate([total[0], total[1]], -1)

        third, second, first = (reduce_whole(g[0]) for g in (in_grads, out_grads, qkv_grads))
        mine = owned

    def squares(v):
        return jnp.sum(jnp.square(v.astype(WIDE)))

    squared = squares(first[: 3 * rows]) + squares(second) + squares(third)
    squared = squared + squares(jnp.where(mine, first[3 * rows :], jnp.zeros((), LOW)))
    grad_norm = jnp.sqrt(total_of(grid, squared))
    if grid.cube:
        first, second, third = (both_halves(grid, g) for g in (first, second, third))
    first, second, third = (g.astype(WIDE) for g in (first, second, third))
    own_gains = lax.dynamic_slice_in_dim(first[3 * rows : 3 * rows + 2], shard * rows, rows, 1)
    factor = jnp.minimum(1.0, CLIP_AT / (grad_norm + 1e-06))
    owned_grads = (
        jnp.stack([first[j * rows : (j + 1) * rows] for j in range(3)] + [second[:rows]]),
        jnp.stack([third[:rows], third[rows:]]),
        second[rows:],
        own_gains,
    )
    weights = (w_attn, w_in, w_down, gains)
    firsts = (m_attn, m_in, m_down, m_gains)
    seconds = (v_attn, v_in, v_down, v_gains)
    rates = (MATRIX_RATE, MATRIX_RATE, MATRIX_RATE, GAIN_RATE)
    decays = (MATRIX_DECAY, MATRIX_DECAY, MATRIX_DECAY, 0.0)
    updated = [
        adamw(weights[n], firsts[n], seconds[n], owned_grads[n] * factor, rates[n], decays[n])
        for n in range(4)
    ]
    return (
        output[None],
        input_grad[None],
        grad_norm,
        updated[0][0],
        updated[1][0],
        updated[2][0],
        updated[3][0],
        updated[0][1],
        updated[1][1],
        updated[2][1],
        updated[3][1],
        updated[0][2],
        updated[1][2],
        updated[2][2],
        updated[3][2],
    )


def solution(mesh):
    placed = (
        P(("dp", "fsdp"), None, None),
        P(("dp", "fsdp")),
        P(("dp", "fsdp"), None, None),
        P(None, "fsdp", None),
        P(None, "fsdp", None),
        P("fsdp", None),
        P(None, "fsdp"),
        P(None, "fsdp", None),
        P(None, "fsdp", None),
        P("fsdp", None),
        P(None, "fsdp"),
        P(None, "fsdp", None),
        P(None, "fsdp", None),
        P("fsdp", None),
        P(None, "fsdp"),
    )
    grid = Grid(mesh.shape["dp"], mesh.shape["fsdp"])
    return jax.shard_map(
        functools.partial(on_device, grid),
        mesh=mesh,
        in_specs=placed,
        out_specs=(
            P(("dp", "fsdp"), None, None),
            P(("dp", "fsdp"), None, None),
            P(),
            P(None, "fsdp", None),
            P(None, "fsdp", None),
            P("fsdp", None),
            P(None, "fsdp"),
            P(None, "fsdp", None),
            P(None, "fsdp", None),
            P("fsdp", None),
            P(None, "fsdp"),
            P(None, "fsdp", None),
            P(None, "fsdp", None),
            P("fsdp", None),
            P(None, "fsdp"),
        ),
        check_vma=False,
    )
```

time: 870 us -> 312 us (0.36)
  blocking collectives: 521 us -> 0 us
  matrix products: 89.8 us -> 0 us
  starting transfers between devices: 0.25 us -> 84.1 us
  Pallas kernels: 0 us -> 71 us
  local copies, waits for them, and re-layouts: 64.7 us -> 5.17 us
  other arithmetic: 46.8 us -> 33.1 us
  between operations: 20.2 us -> 9.07 us
    unnamed x1 -> x0, blocking collectives: 456 us -> none
    ppermute x0 -> x68, waiting for transfers between devices: none -> 109 us  [the longest x18 39.8 us: shift_z(): lax.ppermute(v, EVERY, self.move(lambda x, z, y, c: (x, (z + by) % self.n...]
    dot_general x54 -> x0, matrix products: 89.8 us -> none  [the longest x1 10.8 us: on_device(): jnp.einsum('sd,jsf->jdf', normed_two, d_gate_up, preferred_element_type=j...]
    all_gather x3 -> x0, waiting for transfers between devices: 88.2 us -> none  [the longest x1 32.7 us: on_device(): lax.all_gather(low_down, 'fsdp', axis=0, tiled=True)]
    ppermute x0 -> x68, starting transfers between devices: none -> 84.1 us  [the longest x18 34.1 us: shift_z(): lax.ppermute(v, EVERY, self.move(lambda x, z, y, c: (x, (z + by) % self.n...]
    pallas_call x0 -> x5, Pallas kernels: none -> 71 us  [the longest x1 28 us: feed_forward(): pl.pallas_call(body, grid=(steps,), out_shape=[jax.ShapeDtypeStruct((leng...]
    psum x2 -> x0, blocking collectives: 42.5 us -> none  [the longest x1 33.8 us: on_device(): grad_norm = jnp.sqrt(lax.psum(squares, 'fsdp'))]
    psum x1 -> x0, waiting for transfers between devices: 28.5 us -> none  [on_device(): lax.psum(owned[0].astype(jnp.bfloat16), 'dp').astype(jnp.float32)]
  transfers between devices with their start and end apart: 6 -> 68, of which waited for: 4 -> 31; matrix products, arithmetic and copies ran while one was open for 19% -> 10% of each run, Pallas kernels for 0% -> 5%
where the time goes in v2:
time: 312 us; the launch traced here: 311 us
  waiting for transfers between devices  109 us (35%)
  starting transfers between devices  84.1 us (27%)
  Pallas kernels  71 us (23%)
  other arithmetic  33.1 us (11%)
  between operations  9.07 us (3%)
  local copies, waits for them, and re-layouts  5.17 us (2%)
    ppermute x18, waiting for transfers between devices, shift_z(): lax.ppermute(v, EVERY, self.move(lambda x, z, y, c: (x, (z + by) % self.n...  39.8 us
    ppermute x18, starting transfers between devices, shift_z(): lax.ppermute(v, EVERY, self.move(lambda x, z, y, c: (x, (z + by) % self.n...  34.1 us
    ppermute x16, waiting for transfers between devices, flip_x(): lax.ppermute(v, EVERY, self.move(lambda x, z, y, c: (1 - x, z, y, c)))  31 us
    ppermute x13, waiting for transfers between devices, flip_y(): lax.ppermute(v, EVERY, self.move(lambda x, z, y, c: (x, z, 1 - y, c)))  30.9 us
    pallas_call x1, Pallas kernels, feed_forward(): pl.pallas_call(body, grid=(steps,), out_shape=[jax.ShapeDtypeStruct((leng...  28 us
    ppermute x16, starting transfers between devices, flip_x(): lax.ppermute(v, EVERY, self.move(lambda x, z, y, c: (1 - x, z, y, c)))  21.1 us
    pallas_call x1, Pallas kernels, attend_back(): pl.pallas_call(body, grid=(width // pair,), out_shape=jax.ShapeDtypeStruc...  16.1 us
    ppermute x13, starting transfers between devices, flip_y(): lax.ppermute(v, EVERY, self.move(lambda x, z, y, c: (x, z, 1 - y, c)))  14.5 us
  transfers between devices with their start and end apart: 68, of which 31 were waited for; matrix products, arithmetic and copies ran while one was open for 10% of the time, Pallas kernels for 5%

profile of v2, /device:TPU:0, one launch (start us, length us, event | category | flops | bytes accessed | tf_op | source)
XLA Modules:
  0.0 311.1 jit_solution(12488959104701275223)
XLA Ops:
  2.9 3.1 collective-permute-start
  5.9 2.6 collective-permute-start.1
  12.2 4.4 %collective-permute-done.1 = bf16[160,384]{1,0:T(8,128)(2,1)S(1)} collective-permute-done((bf16[160,384]{1,0:T(8,128)(2,1)S(1)}, bf16[160,384]{1,0:T(8,128)(2,1)S(1)}, u32[]{:S(2)}, u32[]{:S(2)}) %collective-permute-start.1) | collective-permute-done | bytes 122912 | tf_op jit(solution)/shard_map/ppermute | solution.py:60
  16.7 3.2 %collective-permute-start.12 = (bf16[176,384]{1,0:T(8,128)(2,1)S(1)}, bf16[176,384]{1,0:T(8,128)(2,1)S(1)}, u32[]{:S(2)}, u32[]{:S(2)}) collective-permute-start(bf16[176,384]{1,0:T(8,128)(2,1)S(1)} %fusion.44), channel_id=1, source_target_pairs={{0,4},{1,5},{2,6},{3,7},{4,8},{5,9},{6,10},{7,11},{8,12},{9,13},{1... | collective-permute-start | bytes 405512 | tf_op jit(solution)/shard_map/ppermute | solution.py:60
  25.3 4.6 %collective-permute-done.13 = bf16[176,384]{1,0:T(8,128)(2,1)S(1)} collective-permute-done((bf16[176,384]{1,0:T(8,128)(2,1)S(1)}, bf16[176,384]{1,0:T(8,128)(2,1)S(1)}, u32[]{:S(2)}, u32[]{:S(2)}) %collective-permute-start.13) | collective-permute-done | bytes 135200 | tf_op jit(solution)/shard_map/ppermute | solution.py:60
  30.0 3.4 %collective-permute-start.24 = (bf16[96,1024]{1,0:T(8,128)(2,1)S(1)}, bf16[96,1024]{1,0:T(8,128)(2,1)S(1)}, u32[]{:S(2)}, u32[]{:S(2)}) collective-permute-start(bf16[96,1024]{1,0:T(8,128)(2,1)S(1)} %fusion.39), channel_id=1, source_target_pairs={{0,4},{1,5},{2,6},{3,7},{4,8},{5,9},{6,10},{7,11},{8,12},{9,13},{1... | collective-permute-start | bytes 589832 | tf_op jit(solution)/shard_map/ppermute | solution.py:60
  38.4 2.3 collective-permute-done.24
  42.2 5.6 %collective-permute-done.25 = bf16[96,1024]{1,0:T(8,128)(2,1)S(1)} collective-permute-done((bf16[96,1024]{1,0:T(8,128)(2,1)S(1)}, bf16[96,1024]{1,0:T(8,128)(2,1)S(1)}, u32[]{:S(2)}, u32[]{:S(2)}) %collective-permute-start.25) | collective-permute-done | bytes 196640 | tf_op jit(solution)/shard_map/ppermute | solution.py:60
  51.4 7.7 %collective-permute-done.15.refs_6_ = bf16[4,176,384]{2,1,0:T(8,128)(2,1)S(1)} collective-permute-done((bf16[4,176,384]{2,1,0:T(8,128)(2,1)S(1)}, bf16[4,176,384]{2,1,0:T(8,128)(2,1)S(1)}, u32[]{:S(2)}, u32[]{:S(2)}) %collective-permute-start.15) | collective-permute-done | bytes 540704 | tf_op jit(solution)/shard_map/ppermute | solution.py:51
  70.2 3.6 %collective-permute-done.18.refs_9_ = bf16[2,176,384]{2,1,0:T(8,128)(2,1)S(1)} collective-permute-done((bf16[2,176,384]{2,1,0:T(8,128)(2,1)S(1)}, bf16[2,176,384]{2,1,0:T(8,128)(2,1)S(1)}, u32[]{:S(2)}, u32[]{:S(2)}) %collective-permute-start.18) | collective-permute-done | bytes 270368 | tf_op jit(solution)/shard_map/ppermute | solution.py:54
  76.6 10.6 %collective-permute-done.28.refs_17_ = bf16[4,96,1024]{2,1,0:T(8,128)(2,1)S(1)} collective-permute-done((bf16[4,96,1024]{2,1,0:T(8,128)(2,1)S(1)}, bf16[4,96,1024]{2,1,0:T(8,128)(2,1)S(1)}, u32[]{:S(2)}, u32[]{:S(2)}) %collective-permute-start.28) | collective-permute-done | bytes 786464 | tf_op jit(solution)/shard_map/ppermute | solution.py:54
  93.4 7.0 %collective-permute-done.29.refs_18_ = bf16[2,96,1024]{2,1,0:T(8,128)(2,1)} collective-permute-done((bf16[2,96,1024]{2,1,0:T(8,128)(2,1)S(1)}, bf16[2,96,1024]{2,1,0:T(8,128)(2,1)}, u32[]{:S(2)}, u32[]{:S(2)}) %collective-permute-start.29) | collective-permute-done | bytes 393248 | tf_op jit(solution)/shard_map/ppermute | solution.py:51
  103.0 7.6 %project_in.1 = (bf16[512,768]{1,0:T(8,128)(2,1)}, bf16[3,512,768]{2,1,0:T(8,128)(2,1)}, f32[16,768]{1,0:T(8,128)}) custom-call(bf16[512,768]{1,0:T(8,128)(2,1)} %bitcast.337, f32[16,768]{1,0:T(8,128)} %broadcast_in_dim.35.refs_1_, bf16[4,160,384]{2,1,0:T(8,128)(2,1)} %copy-done.20, bf16[4,160,384]{2,1,0:T(8,128)(2,1)} %copy-done.26, ...), custom_call_target="tpu_custom_call" | custom-call | flops 1811939328 | bytes 8650752 | tf_op jit(solution)/shard_map/project_in/pallas_call | solution.py:273
  110.6 8.7 %attend.1.refs_2_ = bf16[512,768]{1,0:T(8,128)(2,1)} custom-call(s32[1]{0:T(128)S(6)} %copy.126.counts_ref.refs_0_, bf16[3,512,768]{2,1,0:T(8,128)(2,1)} %get-tuple-element.34.qkv_ref), custom_call_target="tpu_custom_call" | custom-call | flops 805306368 | bytes 3145728 | tf_op jit(solution)/shard_map/attend/pallas_call | solution.py:311
  120.6 28.0 %feed_forward.1 = (bf16[512,768]{1,0:T(8,128)(2,1)}, f32[512,768]{1,0:T(8,128)}, bf16[512,768]{1,0:T(8,128)(2,1)}, f32[8,768]{1,0:T(8,128)}, bf16[2,8,176,384]{3...) custom-call(s32[1]{0:T(128)S(6)} %copy.126.counts_ref.refs_0_, ...), custom_call_target="tpu_custom_call" | custom-call | flops 16307453952 | bytes 42467328 | tf_op jit(solution)/shard_map/feed_forward/pallas_call | solution.py:465
  148.6 16.1 %attend_back.1.refs_2_ = bf16[3,512,768]{2,1,0:T(8,128)(2,1)} custom-call(s32[1]{0:T(128)S(6)} %copy.126.counts_ref.refs_0_, bf16[3,512,768]{2,1,0:T(8,128)(2,1)} %get-tuple-element.34.qkv_ref, bf16[512,768]{1,0:T(8,128)(2,1)} %get-tuple-element.41.d_ref), custom_call_target="tpu_custom_call" | custom-call | flops 2013265920 | bytes 5505024 | tf_op jit(solution)/shard_map/attend_back/pallas_call | solution.py:350
  164.8 10.6 %project_back.1 = (bf16[512,768]{1,0:T(8,128)(2,1)}, bf16[2,8,160,384]{3,2,1,0:T(8,128)(2,1)}, bf16[2,8,160,384]{3,2,1,0:T(8,128)(2,1)}) custom-call(bf16[512,768]{1,0:T(8,128)(2,1)} %bitcast.339, bf16[512,768]{1,0:T(8,128)(2,1)} %get-tuple-element.40.refs_1_, bf16[3,512,768]{2,1,0:T(8,128)(2,1)} %attend_back.1.refs_2_, ...), custom_call_target="tpu_custom_call" | custom-call | flops 3623878656 | bytes 16121856 | tf_op jit(solution)/shard_map/project_back/pallas_call | solution.py:536
  176.5 3.4 %collective-permute-done.36 = bf16[2,8,160,384]{3,2,1,0:T(8,128)(2,1)} collective-permute-done((bf16[2,8,160,384]{3,2,1,0:T(8,128)(2,1)}, bf16[2,8,160,384]{3,2,1,0:T(8,128)(2,1)}, u32[]{:S(2)}, u32[]{:S(2)}) %collective-permute-start.36) | collective-permute-done | bytes 1966112 | tf_op jit(solution)/shard_map/ppermute | solution.py:57
  188.1 2.5 collective-permute-done.37
  200.3 8.7 %collective-permute-done.38 = bf16[4,160,384]{2,1,0:T(8,128)(2,1)} collective-permute-done((bf16[4,160,384]{2,1,0:T(8,128)(2,1)}, bf16[4,160,384]{2,1,0:T(8,128)(2,1)}, u32[]{:S(2)}, u32[]{:S(2)}) %collective-permute-start.38) | collective-permute-done | bytes 491552 | tf_op jit(solution)/shard_map/ppermute | solution.py:51
  214.8 3.5 %collective-permute-done.41 = bf16[160,384]{1,0:T(8,128)(2,1)S(1)} collective-permute-done((bf16[160,384]{1,0:T(8,128)(2,1)S(1)}, bf16[160,384]{1,0:T(8,128)(2,1)S(1)}, u32[]{:S(2)}, u32[]{:S(2)}) %collective-permute-start.41) | collective-permute-done | bytes 122912 | tf_op jit(solution)/shard_map/ppermute | solution.py:60
  218.8 2.5 collective-permute-done.42
  227.4 9.3 %collective-permute-done.53 = bf16[2,96,1024]{2,1,0:T(8,128)(2,1)S(1)} collective-permute-done((bf16[2,96,1024]{2,1,0:T(8,128)(2,1)S(1)}, bf16[2,96,1024]{2,1,0:T(8,128)(2,1)S(1)}, u32[]{:S(2)}, u32[]{:S(2)}) %collective-permute-start.53) | collective-permute-done | bytes 393248 | tf_op jit(solution)/shard_map/ppermute | solution.py:54
  246.2 2.8 collective-permute-start.51
  250.2 4.1 %collective-permute-done.50 = bf16[176,384]{1,0:T(8,128)(2,1)S(1)} collective-permute-done((bf16[176,384]{1,0:T(8,128)(2,1)S(1)}, bf16[176,384]{1,0:T(8,128)(2,1)S(1)}, u32[]{:S(2)}, u32[]{:S(2)}) %collective-permute-start.50) | collective-permute-done | bytes 135200 | tf_op jit(solution)/shard_map/ppermute | solution.py:60
  260.6 2.4 collective-permute-start.57
  266.6 3.8 %collective-permute-done.57 = bf16[96,1024]{1,0:T(8,128)(2,1)S(1)} collective-permute-done((bf16[96,1024]{1,0:T(8,128)(2,1)S(1)}, bf16[96,1024]{1,0:T(8,128)(2,1)S(1)}, u32[]{:S(2)}, u32[]{:S(2)}) %collective-permute-start.57) | collective-permute-done | bytes 196640 | tf_op jit(solution)/shard_map/ppermute | solution.py:60
  270.4 5.2 %collective-permute-done.58 = bf16[96,1024]{1,0:T(8,128)(2,1)S(1)} collective-permute-done((bf16[96,1024]{1,0:T(8,128)(2,1)S(1)}, bf16[96,1024]{1,0:T(8,128)(2,1)S(1)}, u32[]{:S(2)}, u32[]{:S(2)}) %collective-permute-start.58) | collective-permute-done | bytes 196640 | tf_op jit(solution)/shard_map/ppermute | solution.py:60
  279.6 4.3 %collective-permute-start.61 = (f32[]{:T(128)}, f32[]{:T(128)}, u32[]{:S(2)}, u32[]{:S(2)}) collective-permute-start(f32[]{:T(128)} %add.533), channel_id=1, source_target_pairs={{0,16},{1,17},{2,18},{3,19},{4,20},{5,21},{6,22},{7,23},{8,24},{9,... | collective-permute-start | bytes 20 | tf_op jit(solution)/shard_map/ppermute | solution.py:51
  290.6 6.0 %collective-permute-start.63 = (f32[]{:T(128)}, f32[]{:T(128)}, u32[]{:S(2)}, u32[]{:S(2)}) collective-permute-start(f32[]{:T(128)} %add.535), channel_id=1, source_target_pairs={{0,4},{1,5},{2,6},{3,7},{4,0},{5,1},{6,2},{7,3},{8,12},{9,13},{10,... | collective-permute-start | bytes 20 | tf_op jit(solution)/shard_map/ppermute | solution.py:63
  297.4 3.7 %collective-permute-start.64 = (f32[]{:T(128)}, f32[]{:T(128)}, u32[]{:S(2)}, u32[]{:S(2)}) collective-permute-start(f32[]{:T(128)} %add.536), channel_id=1, source_target_pairs={{0,8},{1,9},{2,10},{3,11},{4,12},{5,13},{6,14},{7,15},{8,0},{9,1},... | collective-permute-start | bytes 20 | tf_op jit(solution)/shard_map/ppermute | solution.py:63
  302.6 2.3 multiply_subtract_fusion.2
  (266 shorter events, 108.2 us)
Async XLA Ops:
  22.5 25.4 %collective-permute-start.4 = (bf16[4,160,384]{2,1,0:T(8,128)(2,1)S(1)}, bf16[4,160,384]{2,1,0:T(8,128)(2,1)S(1)}, u32[]{:S(2)}, u32[]{:S(2)}) collective-permute-start(bf16[4,160,384]{2,1,0:T(8,128)(2,1)S(1)} %pad_maximum_fusion.6.refs_2_.refs_6_), channel_id=1, source_target_pairs={{0,2},{1,3},{2,0},{3,1},{4,6},{5,7},{6,4},{7,5},{8,10},{9,11},{10,... | collective-permute-start | bytes 1474568 | tf_op jit(solution)/shard_map/ppermute | solution.py:54
  33.4 15.0 %collective-permute-start.3 = (bf16[4,160,384]{2,1,0:T(8,128)(2,1)S(1)}, bf16[4,160,384]{2,1,0:T(8,128)(2,1)S(1)}, u32[]{:S(2)}, u32[]{:S(2)}) collective-permute-start(bf16[4,160,384]{2,1,0:T(8,128)(2,1)S(1)} %pad_maximum_fusion.6.refs_2_.refs_6_), channel_id=1, source_target_pairs={{0,16},{1,17},{2,18},{3,19},{4,20},{5,21},{6,22},{7,23},{8,24},{9,... | collective-permute-start | bytes 1474568 | tf_op jit(solution)/shard_map/ppermute | solution.py:51
  34.9 12.9 %collective-permute-start.25 = (bf16[96,1024]{1,0:T(8,128)(2,1)S(1)}, bf16[96,1024]{1,0:T(8,128)(2,1)S(1)}, u32[]{:S(2)}, u32[]{:S(2)}) collective-permute-start(bf16[96,1024]{1,0:T(8,128)(2,1)S(1)} %fusion.39), channel_id=1, source_target_pairs={{0,8},{1,9},{2,10},{3,11},{4,12},{5,13},{6,14},{7,15},{8,0},{9,1},... | collective-permute-start | bytes 589832 | tf_op jit(solution)/shard_map/ppermute | solution.py:60
  36.9 12.9 %collective-permute-start.16 = (bf16[4,176,384]{2,1,0:T(8,128)(2,1)S(1)}, bf16[4,176,384]{2,1,0:T(8,128)(2,1)S(1)}, u32[]{:S(2)}, u32[]{:S(2)}) collective-permute-start(bf16[4,176,384]{2,1,0:T(8,128)(2,1)S(1)} %pad_maximum_fusion.3.refs_5_), channel_id=1, source_target_pairs={{0,2},{1,3},{2,0},{3,1},{4,6},{5,7},{6,4},{7,5},{8,10},{9,11},{10,... | collective-permute-start | bytes 1622024 | tf_op jit(solution)/shard_map/ppermute | solution.py:54
  40.7 18.4 %collective-permute-start.15 = (bf16[4,176,384]{2,1,0:T(8,128)(2,1)S(1)}, bf16[4,176,384]{2,1,0:T(8,128)(2,1)S(1)}, u32[]{:S(2)}, u32[]{:S(2)}) collective-permute-start(bf16[4,176,384]{2,1,0:T(8,128)(2,1)S(1)} %pad_maximum_fusion.3.refs_5_), channel_id=1, source_target_pairs={{0,16},{1,17},{2,18},{3,19},{4,20},{5,21},{6,22},{7,23},{8,24},{9,... | collective-permute-start | bytes 1622024 | tf_op jit(solution)/shard_map/ppermute | solution.py:51
  47.8 14.4 %collective-permute-start.7 = (bf16[4,160,384]{2,1,0:T(8,128)(2,1)S(1)}, bf16[4,160,384]{2,1,0:T(8,128)(2,1)S(1)}, u32[]{:S(2)}, u32[]{:S(2)}) collective-permute-start(bf16[4,160,384]{2,1,0:T(8,128)(2,1)S(1)} %pad_maximum_fusion.6.refs_2_.refs_6_), channel_id=1, source_target_pairs={{0,1},{1,0},{2,3},{3,2},{4,5},{5,4},{6,7},{7,6},{8,9},{9,8},{10,11... | collective-permute-start | bytes 1474568 | tf_op jit(solution)/shard_map/ppermute | solution.py:57
  47.9 15.0 %collective-permute-start.19 = (bf16[4,176,384]{2,1,0:T(8,128)(2,1)S(1)}, bf16[4,176,384]{2,1,0:T(8,128)(2,1)S(1)}, u32[]{:S(2)}, u32[]{:S(2)}) collective-permute-start(bf16[4,176,384]{2,1,0:T(8,128)(2,1)S(1)} %pad_maximum_fusion.3.refs_5_), channel_id=1, source_target_pairs={{0,1},{1,0},{2,3},{3,2},{4,5},{5,4},{6,7},{7,6},{8,9},{9,8},{10,11... | collective-permute-start | bytes 1622024 | tf_op jit(solution)/shard_map/ppermute | solution.py:57
  48.4 12.4 %collective-permute-start.26 = (bf16[96,1024]{1,0:T(8,128)(2,1)S(1)}, bf16[96,1024]{1,0:T(8,128)(2,1)S(1)}, u32[]{:S(2)}, u32[]{:S(2)}) collective-permute-start(bf16[96,1024]{1,0:T(8,128)(2,1)S(1)} %fusion.39), channel_id=1, source_target_pairs={{0,12},{1,13},{2,14},{3,15},{4,0},{5,1},{6,2},{7,3},{8,4},{9,5},{1... | collective-permute-start | bytes 589832 | tf_op jit(solution)/shard_map/ppermute | solution.py:60
  49.9 14.7 %collective-permute-start.5 = (bf16[2,160,384]{2,1,0:T(8,128)(2,1)S(1)}, bf16[2,160,384]{2,1,0:T(8,128)(2,1)S(1)}, u32[]{:S(2)}, u32[]{:S(2)}) collective-permute-start(bf16[2,160,384]{2,1,0:T(8,128)(2,1)S(1)} %slice.224), channel_id=1, source_target_pairs={{0,16},{1,17},{2,18},{3,19},{4,20},{5,21},{6,22},{7,23},{8,24},{9,... | collective-permute-start | bytes 737288 | tf_op jit(solution)/shard_map/ppermute | solution.py:51
  62.3 11.5 %collective-permute-start.18 = (bf16[2,176,384]{2,1,0:T(8,128)(2,1)S(1)}, bf16[2,176,384]{2,1,0:T(8,128)(2,1)S(1)}, u32[]{:S(2)}, u32[]{:S(2)}) collective-permute-start(bf16[2,176,384]{2,1,0:T(8,128)(2,1)S(1)} %slice.229), channel_id=1, source_target_pairs={{0,2},{1,3},{2,0},{3,1},{4,6},{5,7},{6,4},{7,5},{8,10},{9,11},{10,... | collective-permute-start | bytes 811016 | tf_op jit(solution)/shard_map/ppermute | solution.py:54
  62.9 24.3 %collective-permute-start.28 = (bf16[4,96,1024]{2,1,0:T(8,128)(2,1)S(1)}, bf16[4,96,1024]{2,1,0:T(8,128)(2,1)S(1)}, u32[]{:S(2)}, u32[]{:S(2)}) collective-permute-start(bf16[4,96,1024]{2,1,0:T(8,128)(2,1)S(1)} %pad_maximum_fusion.refs_15_), channel_id=1, source_target_pairs={{0,2},{1,3},{2,0},{3,1},{4,6},{5,7},{6,4},{7,5},{8,10},{9,11},{10,... | collective-permute-start | bytes 2359304 | tf_op jit(solution)/shard_map/ppermute | solution.py:54
  64.5 22.7 %collective-permute-start.27 = (bf16[4,96,1024]{2,1,0:T(8,128)(2,1)S(1)}, bf16[4,96,1024]{2,1,0:T(8,128)(2,1)S(1)}, u32[]{:S(2)}, u32[]{:S(2)}) collective-permute-start(bf16[4,96,1024]{2,1,0:T(8,128)(2,1)S(1)} %pad_maximum_fusion.refs_15_), channel_id=1, source_target_pairs={{0,16},{1,17},{2,18},{3,19},{4,20},{5,21},{6,22},{7,23},{8,24},{9,... | collective-permute-start | bytes 2359304 | tf_op jit(solution)/shard_map/ppermute | solution.py:51
  73.8 16.8 %collective-permute-start.31 = (bf16[4,96,1024]{2,1,0:T(8,128)(2,1)S(1)}, bf16[4,96,1024]{2,1,0:T(8,128)(2,1)S(1)}, u32[]{:S(2)}, u32[]{:S(2)}) collective-permute-start(bf16[4,96,1024]{2,1,0:T(8,128)(2,1)S(1)} %pad_maximum_fusion.refs_15_), channel_id=1, source_target_pairs={{0,1},{1,0},{2,3},{3,2},{4,5},{5,4},{6,7},{7,6},{8,9},{9,8},{10,11... | collective-permute-start | bytes 2359304 | tf_op jit(solution)/shard_map/ppermute | solution.py:57
  74.6 18.2 %collective-permute-start.20 = (bf16[4,176,384]{2,1,0:T(8,128)(2,1)S(1)}, bf16[4,176,384]{2,1,0:T(8,128)(2,1)S(1)}, u32[]{:S(2)}, u32[]{:S(2)}) collective-permute-start(bf16[4,176,384]{2,1,0:T(8,128)(2,1)S(1)} %collective-permute-done.15.refs_6_), channel_id=1, source_target_pairs={{0,1},{1,0},{2,3},{3,2},{4,5},{5,4},{6,7},{7,6},{8,9},{9,8},{10,11... | collective-permute-start | bytes 1622024 | tf_op jit(solution)/shard_map/ppermute | solution.py:57
  76.4 15.7 %collective-permute-start.22 = (bf16[2,176,384]{2,1,0:T(8,128)(2,1)S(1)}, bf16[2,176,384]{2,1,0:T(8,128)(2,1)S(1)}, u32[]{:S(2)}, u32[]{:S(2)}) collective-permute-start(bf16[2,176,384]{2,1,0:T(8,128)(2,1)S(1)} %collective-permute-done.17.refs_8_), channel_id=1, source_target_pairs={{0,1},{1,0},{2,3},{3,2},{4,5},{5,4},{6,7},{7,6},{8,9},{9,8},{10,11... | collective-permute-start | bytes 811016 | tf_op jit(solution)/shard_map/ppermute | solution.py:57
  92.1 27.1 %collective-permute-start.32 = (bf16[4,96,1024]{2,1,0:T(8,128)(2,1)S(1)}, bf16[4,96,1024]{2,1,0:T(8,128)(2,1)S(1)}, u32[]{:S(2)}, u32[]{:S(2)}) collective-permute-start(bf16[4,96,1024]{2,1,0:T(8,128)(2,1)S(1)} %collective-permute-done.27.refs_16_), channel_id=1, source_target_pairs={{0,1},{1,0},{2,3},{3,2},{4,5},{5,4},{6,7},{7,6},{8,9},{9,8},{10,11... | collective-permute-start | bytes 2359304 | tf_op jit(solution)/shard_map/ppermute | solution.py:57
  92.8 26.5 %collective-permute-start.33 = (bf16[4,96,1024]{2,1,0:T(8,128)(2,1)S(1)}, bf16[4,96,1024]{2,1,0:T(8,128)(2,1)S(1)}, u32[]{:S(2)}, u32[]{:S(2)}) collective-permute-start(bf16[4,96,1024]{2,1,0:T(8,128)(2,1)S(1)} %collective-permute-done.28.refs_17_), channel_id=1, source_target_pairs={{0,1},{1,0},{2,3},{3,2},{4,5},{5,4},{6,7},{7,6},{8,9},{9,8},{10,11... | collective-permute-start | bytes 2359304 | tf_op jit(solution)/shard_map/ppermute | solution.py:57
  92.9 26.4 %collective-permute-start.21 = (bf16[4,176,384]{2,1,0:T(8,128)(2,1)S(1)}, bf16[4,176,384]{2,1,0:T(8,128)(2,1)S(1)}, u32[]{:S(2)}, u32[]{:S(2)}) collective-permute-start(bf16[4,176,384]{2,1,0:T(8,128)(2,1)S(1)} %collective-permute-done.16.refs_7_), channel_id=1, source_target_pairs={{0,1},{1,0},{2,3},{3,2},{4,5},{5,4},{6,7},{7,6},{8,9},{9,8},{10,11... | collective-permute-start | bytes 1622024 | tf_op jit(solution)/shard_map/ppermute | solution.py:57
  100.4 18.8 %collective-permute-start.34 = (bf16[2,96,1024]{2,1,0:T(8,128)(2,1)}, bf16[2,96,1024]{2,1,0:T(8,128)(2,1)}, u32[]{:S(2)}, u32[]{:S(2)}) collective-permute-start(bf16[2,96,1024]{2,1,0:T(8,128)(2,1)} %collective-permute-done.29.refs_18_), channel_id=1, source_target_pairs={{0,1},{1,0},{2,3},{3,2},{4,5},{5,4},{6,7},{7,6},{8,9},{9,8},{10,11... | collective-permute-start | bytes 1179656 | tf_op jit(solution)/shard_map/ppermute | solution.py:57
  101.7 17.6 %collective-permute-start.35 = (bf16[2,96,1024]{2,1,0:T(8,128)(2,1)}, bf16[2,96,1024]{2,1,0:T(8,128)(2,1)}, u32[]{:S(2)}, u32[]{:S(2)}) collective-permute-start(bf16[2,96,1024]{2,1,0:T(8,128)(2,1)} %collective-permute-done.30.refs_19_), channel_id=1, source_target_pairs={{0,1},{1,0},{2,3},{3,2},{4,5},{5,4},{6,7},{7,6},{8,9},{9,8},{10,11... | collective-permute-start | bytes 1179656 | tf_op jit(solution)/shard_map/ppermute | solution.py:57
  176.0 46.7 %collective-permute-start.52 = (bf16[2,8,96,1024]{3,2,1,0:T(8,128)(2,1)}, bf16[2,8,96,1024]{3,2,1,0:T(8,128)(2,1)}, u32[]{:S(2)}, u32[]{:S(2)}) collective-permute-start(bf16[2,8,96,1024]{3,2,1,0:T(8,128)(2,1)} %get-tuple-element.50), channel_id=1, source_target_pairs={{0,1},{1,0},{2,3},{3,2},{4,5},{5,4},{6,7},{7,6},{8,9},{9,8},{10,11... | collective-permute-start | bytes 9437192 | tf_op jit(solution)/shard_map/ppermute | solution.py:57
  186.7 11.4 %collective-permute-start.47 = (bf16[2,176,384]{2,1,0:T(8,128)(2,1)S(1)}, bf16[2,176,384]{2,1,0:T(8,128)(2,1)}, u32[]{:S(2)}, u32[]{:S(2)}) collective-permute-start(bf16[2,176,384]{2,1,0:T(8,128)(2,1)S(1)} %get-tuple-element.74), channel_id=1, source_target_pairs={{0,16},{1,17},{2,18},{3,19},{4,20},{5,21},{6,22},{7,23},{8,24},{9,... | collective-permute-start | bytes 811016 | tf_op jit(solution)/shard_map/ppermute | solution.py:51
  194.5 14.5 %collective-permute-start.38 = (bf16[4,160,384]{2,1,0:T(8,128)(2,1)}, bf16[4,160,384]{2,1,0:T(8,128)(2,1)}, u32[]{:S(2)}, u32[]{:S(2)}) collective-permute-start(bf16[4,160,384]{2,1,0:T(8,128)(2,1)} %pad_maximum_fusion.7), channel_id=1, source_target_pairs={{0,16},{1,17},{2,18},{3,19},{4,20},{5,21},{6,22},{7,23},{8,24},{9,... | collective-permute-start | bytes 1474568 | tf_op jit(solution)/shard_map/ppermute | solution.py:51
  196.0 13.0 %collective-permute-start.40 = (bf16[4,160,384]{2,1,0:T(8,128)(2,1)}, bf16[4,160,384]{2,1,0:T(8,128)(2,1)}, u32[]{:S(2)}, u32[]{:S(2)}) collective-permute-start(bf16[4,160,384]{2,1,0:T(8,128)(2,1)} %pad_maximum_fusion.8), channel_id=1, source_target_pairs={{0,2},{1,3},{2,0},{3,1},{4,6},{5,7},{6,4},{7,5},{8,10},{9,11},{10,... | collective-permute-start | bytes 1474568 | tf_op jit(solution)/shard_map/ppermute | solution.py:54
  199.6 42.0 %collective-permute-start.46 = (bf16[4,176,384]{2,1,0:T(8,128)(2,1)S(1)}, bf16[4,176,384]{2,1,0:T(8,128)(2,1)S(1)}, u32[]{:S(2)}, u32[]{:S(2)}) collective-permute-start(bf16[4,176,384]{2,1,0:T(8,128)(2,1)S(1)} %pad_maximum_fusion.4), channel_id=1, source_target_pairs={{0,16},{1,17},{2,18},{3,19},{4,20},{5,21},{6,22},{7,23},{8,24},{9,... | collective-permute-start | bytes 1622024 | tf_op jit(solution)/shard_map/ppermute | solution.py:51
  218.3 23.3 %collective-permute-start.48 = (bf16[4,176,384]{2,1,0:T(8,128)(2,1)S(1)}, bf16[4,176,384]{2,1,0:T(8,128)(2,1)S(1)}, u32[]{:S(2)}, u32[]{:S(2)}) collective-permute-start(bf16[4,176,384]{2,1,0:T(8,128)(2,1)S(1)} %pad_maximum_fusion.5), channel_id=1, source_target_pairs={{0,2},{1,3},{2,0},{3,1},{4,6},{5,7},{6,4},{7,5},{8,10},{9,11},{10,... | collective-permute-start | bytes 1622024 | tf_op jit(solution)/shard_map/ppermute | solution.py:54
  224.7 12.0 %collective-permute-start.53 = (bf16[2,96,1024]{2,1,0:T(8,128)(2,1)S(1)}, bf16[2,96,1024]{2,1,0:T(8,128)(2,1)S(1)}, u32[]{:S(2)}, u32[]{:S(2)}) collective-permute-start(bf16[2,96,1024]{2,1,0:T(8,128)(2,1)S(1)} %get-tuple-element.69), channel_id=1, source_target_pairs={{0,2},{1,3},{2,0},{3,1},{4,6},{5,7},{6,4},{7,5},{8,10},{9,11},{10,... | collective-permute-start | bytes 1179656 | tf_op jit(solution)/shard_map/ppermute | solution.py:54
  225.2 11.6 %collective-permute-start.55 = (bf16[2,96,1024]{2,1,0:T(8,128)(2,1)S(1)}, bf16[2,96,1024]{2,1,0:T(8,128)(2,1)S(1)}, u32[]{:S(2)}, u32[]{:S(2)}) collective-permute-start(bf16[2,96,1024]{2,1,0:T(8,128)(2,1)S(1)} %get-tuple-element.68), channel_id=1, source_target_pairs={{0,16},{1,17},{2,18},{3,19},{4,20},{5,21},{6,22},{7,23},{8,24},{9,... | collective-permute-start | bytes 1179656 | tf_op jit(solution)/shard_map/ppermute | solution.py:51
  239.3 19.0 %collective-permute-start.54 = (bf16[4,96,1024]{2,1,0:T(8,128)(2,1)}, bf16[4,96,1024]{2,1,0:T(8,128)(2,1)}, u32[]{:S(2)}, u32[]{:S(2)}) collective-permute-start(bf16[4,96,1024]{2,1,0:T(8,128)(2,1)} %pad_maximum_fusion.1), channel_id=1, source_target_pairs={{0,16},{1,17},{2,18},{3,19},{4,20},{5,21},{6,22},{7,23},{8,24},{9,... | collective-permute-start | bytes 2359304 | tf_op jit(solution)/shard_map/ppermute | solution.py:51
  240.7 17.6 %collective-permute-start.56 = (bf16[4,96,1024]{2,1,0:T(8,128)(2,1)}, bf16[4,96,1024]{2,1,0:T(8,128)(2,1)}, u32[]{:S(2)}, u32[]{:S(2)}) collective-permute-start(bf16[4,96,1024]{2,1,0:T(8,128)(2,1)} %pad_maximum_fusion.2), channel_id=1, source_target_pairs={{0,2},{1,3},{2,0},{3,1},{4,6},{5,7},{6,4},{7,5},{8,10},{9,11},{10,... | collective-permute-start | bytes 2359304 | tf_op jit(solution)/shard_map/ppermute | solution.py:54
  263.0 12.5 %collective-permute-start.58 = (bf16[96,1024]{1,0:T(8,128)(2,1)S(1)}, bf16[96,1024]{1,0:T(8,128)(2,1)S(1)}, u32[]{:S(2)}, u32[]{:S(2)}) collective-permute-start(bf16[96,1024]{1,0:T(8,128)(2,1)S(1)} %get-tuple-element.89), channel_id=1, source_target_pairs={{0,8},{1,9},{2,10},{3,11},{4,12},{5,13},{6,14},{7,15},{8,0},{9,1},... | collective-permute-start | bytes 589832 | tf_op jit(solution)/shard_map/ppermute | solution.py:60
  278.5 28.8 %collective-permute-start.67 = (bf16[96,1024]{1,0:T(8,128)(2,1)S(1)}, bf16[96,1024]{1,0:T(8,128)(2,1)S(1)}, u32[]{:S(2)}, u32[]{:S(2)}) collective-permute-start(bf16[96,1024]{1,0:T(8,128)(2,1)S(1)} %get-tuple-element.64), channel_id=1, source_target_pairs={{0,16},{1,17},{2,18},{3,19},{4,20},{5,21},{6,22},{7,23},{8,24},{9,... | collective-permute-start | bytes 589832 | tf_op jit(solution)/shard_map/ppermute | solution.py:51
  (83 other events, 1242.6 us)

commit v3 on v2

v3 whole, which is shorter than its diff:
```python
import functools
import math

import jax
import jax.numpy as jnp
from jax import lax
from jax.experimental import pallas as pl
from jax.experimental.pallas import tpu as pltpu
from jax.sharding import PartitionSpec as P

HD = 64
STEP = 10


NORM_EPS = 1e-06
MASKED = -1000000000.0
BETA_ONE = 0.9
BETA_TWO = 0.999
ADAM_EPS = 1e-08
CLIP_AT = 1.0
MATRIX_RATE = 0.04
MATRIX_DECAY = 0.1
GAIN_RATE = 0.8

EVERY = ("dp", "fsdp")
LOW = jnp.bfloat16
WIDE = jnp.float32
SLAB = 16
VMEM_LIMIT = 56 * 1024 * 1024
ANYWHERE = pl.BlockSpec(memory_space=pl.ANY)


class Grid:
    def __init__(self, dp, fsdp):
        self.dp, self.fsdp = dp, fsdp
        self.nz = fsdp // 4
        power = self.nz & (self.nz - 1) == 0
        self.cube = dp == 2 and fsdp % 4 == 0 and self.nz % 2 == 0 and power

    def move(self, step):
        pairs = []
        for source in range(self.dp * self.fsdp):
            x, rest = divmod(source, self.fsdp)
            z, rest = divmod(rest, 4)
            y, core = divmod(rest, 2)
            x, z, y, core = step(x, z, y, core)
            pairs.append((source, x * self.fsdp + (z * 2 + y) * 2 + core))
        return pairs

    def flip_x(self, v):
        return lax.ppermute(v, EVERY, self.move(lambda x, z, y, c: (1 - x, z, y, c)))

    def flip_y(self, v):
        return lax.ppermute(v, EVERY, self.move(lambda x, z, y, c: (x, z, 1 - y, c)))

    def flip_xy(self, v):
        return lax.ppermute(v, EVERY, self.move(lambda x, z, y, c: (1 - x, z, 1 - y, c)))

    def flip_core(self, v):
        return lax.ppermute(v, EVERY, self.move(lambda x, z, y, c: (x, z, y, 1 - c)))

    def swap_z(self, v, bit):
        return lax.ppermute(v, EVERY, self.move(lambda x, z, y, c: (x, z ^ bit, y, c)))

    def place(self):
        x, f = lax.axis_index("dp"), lax.axis_index("fsdp")
        return x, f // 4, lax.rem(f // 2, 2), lax.rem(f, 2)


def after(first, then):
    return lax.optimization_barrier((first, then))


class Spread:
    def __init__(self, grid, part):
        self.grid, self.part = grid, part
        self.half = grid.nz // 2

    def send_levels(self):
        self.levels = [self.grid.swap_z(self.part, k) for k in range(1, self.grid.nz)]

    def load_column(self):
        self.column = jnp.stack([self.part] + self.levels)

    def send_sides(self):
        self.side = self.grid.flip_x(self.column)
        self.across = self.grid.flip_y(self.column)

    def send_corners(self):
        self.low = self.grid.flip_x(self.across[: self.half])
        self.high = self.grid.flip_y(self.side[self.half :])
        self.most = jnp.concatenate([self.column, self.side, self.across])
        self.other_most = self.grid.flip_core(self.most)

    def finish(self):
        self.rest = jnp.concatenate([self.low, self.high])
        self.other_rest = self.grid.flip_core(self.rest)

    @property
    def pieces(self):
        return [self.most, self.rest, self.other_most, self.other_rest]


def piece_places(grid):
    nz = grid.nz
    most = [(x, y, level) for x, y in ((0, 0), (1, 0), (0, 1)) for level in range(nz)]
    rest = [(1, 1, level) for level in range(nz)]
    return [[(x, y, core, n) for x, y, n in spots] for core in (0, 1) for spots in (most, rest)]


class Reduce:
    def __init__(self, grid, keep, sent):
        self.grid, self.keep, self.sent = grid, keep, sent
        self.half = grid.nz // 2
        self.in_x = self.in_y = None

    def send_core(self):
        self.got = self.grid.flip_core(self.sent)

    def block(self, h, at_y, low=0, n=None):
        n = self.grid.nz if n is None else n
        total = 0.0
        for array in (self.keep, self.got):
            array = array.reshape((2, self.grid.nz, 2) + array.shape[2:])
            part = lax.dynamic_index_in_dim(array, h, 0, False)[low : low + n]
            total = total + lax.dynamic_index_in_dim(part, at_y, 1, False).astype(WIDE)
        return total

    def load_corners(self):
        x, z, y, c = self.grid.place()
        low = self.block(1 - x, 1 - y, 0, self.half)
        high = self.block(1 - x, 1 - y, self.half, self.grid.nz - self.half)
        return low.astype(LOW), high.astype(LOW)

    def send_corners(self, corners):
        self.in_x, self.in_y = self.grid.flip_x(corners[0]), self.grid.flip_y(corners[1])

    def load_sides(self):
        x, z, y, c = self.grid.place()
        half, rest = self.half, self.grid.nz - self.half
        if self.in_x is None:
            to_x, to_y = self.block(1 - x, y), self.block(x, 1 - y)
            return [v.astype(LOW) for v in (to_x, to_y, self.block(1 - x, 1 - y))]
        high = self.block(1 - x, y, half, rest) + self.in_y.astype(WIDE)
        low = self.block(x, 1 - y, 0, half) + self.in_x.astype(WIDE)
        to_x = jnp.concatenate([self.block(1 - x, y, 0, half), high])
        to_y = jnp.concatenate([low, self.block(x, 1 - y, half, rest)])
        return [to_x.astype(LOW), to_y.astype(LOW)]

    def send_sides(self, sides):
        sends = (self.grid.flip_x, self.grid.flip_y, self.grid.flip_xy)
        self.sides = [send(v) for send, v in zip(sends, sides)]

    def load_levels(self):
        x, z, y, c = self.grid.place()
        column = self.block(x, y) + sum(v.astype(WIDE) for v in self.sides)
        column = column.astype(LOW)
        self.own = lax.dynamic_index_in_dim(column, z, 0, False)
        self.leave = [
            lax.dynamic_index_in_dim(column, z ^ k, 0, False) for k in range(1, self.grid.nz)
        ]

    def send_levels(self):
        self.arrive = [self.grid.swap_z(v, k) for k, v in enumerate(self.leave, 1)]

    def load_total(self):
        self.total = sum((v.astype(WIDE) for v in self.arrive), self.own.astype(WIDE)).astype(LOW)

    def send_total(self):
        self.other = self.grid.flip_x(self.total)


def total_of(grid, value):
    if not grid.cube:
        return lax.psum(value, "fsdp")
    value = value + grid.flip_core(value)
    value = value + grid.flip_x(value)
    value = value + grid.flip_y(value)
    bit = 1
    while bit < grid.nz:
        value = value + grid.swap_z(value, bit)
        bit *= 2
    return value


def split_columns(v):
    return jnp.stack(jnp.split(v, 2, -1))


def params(semantics=None):
    return pltpu.CompilerParams(vmem_limit_bytes=VMEM_LIMIT, dimension_semantics=semantics)


def cost(microseconds):
    return pl.CostEstimate(flops=int(microseconds * 1e6), bytes_accessed=0, transcendentals=0)


def dot(a, b):
    return jnp.dot(a, b, preferred_element_type=WIDE)


def dot_nt(a, b):
    return lax.dot_general(a, b, (((1,), (1,)), ((), ())), preferred_element_type=WIDE)


def dot_tn(a, b):
    return lax.dot_general(a, b, (((0,), (0,)), ((), ())), preferred_element_type=WIDE)


class Source:
    def __init__(self, grid, arrays, whole=False):
        self.grid, self.arrays, self.whole = grid, arrays, whole
        self.specs = [ANYWHERE] * len(arrays)

    def copy(self, refs, low, rows, target, sem):
        grid = self.grid
        x, z, y, c = grid.place()
        for ref, spots in zip(refs, piece_places(grid)):
            for entry, (dx, dy, dc, level) in enumerate(spots):
                half = lax.rem(x + dx, 2)
                shard = ((z ^ level) * 2 + lax.rem(y + dy, 2)) * 2 + lax.rem(c + dc, 2)
                source = ref.at[entry, pl.ds(low, rows)]
                pltpu.make_async_copy(source, target(half, shard), sem).start()


def wait_all(ref, sem):
    pltpu.make_async_copy(ref, ref, sem).wait()


def shard_target(matrix, rows):
    n = matrix.shape[-1] // 2

    def target(half, shard):
        return matrix.at[
            pl.ds(pl.multiple_of(shard * rows, 16), rows), pl.ds(pl.multiple_of(half * n, 128), n)
        ]

    return target


def start_load(source, refs, low, rows, matrix, sem, whole=0):
    if not source.whole:
        source.copy(refs, low, rows, shard_target(matrix, rows), sem)
    else:
        pltpu.make_async_copy(refs[whole], matrix, sem).start()


def load_rows(grid, refs, which, low, target, sem):
    source = refs[0].at[:, pl.ds(low, target.shape[1])] if grid.cube else refs[which]
    pltpu.make_async_copy(source, target, sem).start()


def store_grad(grid, refs, index, low, rows, value):
    lead, columns = index
    if not grid.cube:
        refs[0][lead, :, low : low + rows, columns] = value.astype(LOW).reshape(grid.fsdp, rows, -1)
        return
    c = lax.rem(lax.axis_index("fsdp"), 2)
    value = value.astype(LOW).reshape(grid.fsdp // 2, 2, rows, value.shape[-1])
    even, odd = value[:, 0], value[:, 1]
    refs[0][lead, :, low : low + rows, columns] = jnp.where(c == 0, even, odd)
    refs[1][lead, :, low : low + rows, columns] = jnp.where(c == 0, odd, even)


def grad_shapes(grid, rows, columns):
    if not grid.cube:
        return [jax.ShapeDtypeStruct((2, grid.fsdp, rows, columns // 2), LOW)]
    return [jax.ShapeDtypeStruct((2, grid.fsdp // 2, rows, columns // 2), LOW)] * 2


def norm_rows(values):
    return lax.rsqrt(jnp.mean(values * values, -1, keepdims=True) + NORM_EPS)


def norm_back(values, scale, gain, grad):
    y = values * scale
    c = grad * gain
    back = scale * (c - y * jnp.mean(c * y, -1, keepdims=True))
    return back, jnp.sum(grad * y, 0, keepdims=True)


def project_in(grid, source, image, gains):
    length, width = image.shape
    rows = width // grid.fsdp
    count = len(source.arrays)

    def body(*refs):
        image_ref, gains_ref, pieces = refs[0], refs[1], refs[2 : 2 + count]
        normed_ref, qkv_ref, gains_out, weights, slabs, sems = refs[2 + count :]
        for j in range(3):
            start_load(source, pieces, j * rows, rows, weights.at[j], sems.at[j], j)
        if grid.cube:
            source.copy(pieces, 3 * rows, SLAB, lambda h, f: slabs.at[h, f], sems.at[3])
        values = image_ref[...].astype(WIDE)
        scaled = values * norm_rows(values)
        if grid.cube:
            wait_all(slabs, sems.at[3])
            found = jnp.sum(slabs[...].astype(WIDE), 1)
            gain = jnp.concatenate([found[0], found[1]], -1)
        else:
            gain = gains_ref[...].astype(WIDE)
        gains_out[...] = gain
        normed = (scaled * gain[0:1]).astype(LOW)
        normed_ref[...] = normed
        for j in range(3):
            wait_all(weights.at[j], sems.at[j])
            qkv_ref[j] = dot(normed, weights[j]).astype(LOW)

    vmem = pl.BlockSpec(memory_space=pltpu.VMEM)
    return pl.pallas_call(
        body,
        out_shape=[
            jax.ShapeDtypeStruct((length, width), LOW),
            jax.ShapeDtypeStruct((3, length, width), LOW),
            jax.ShapeDtypeStruct((SLAB, width), WIDE),
        ],
        in_specs=[vmem, vmem] + source.specs,
        out_specs=[vmem] * 3,
        scratch_shapes=[
            pltpu.VMEM((3, width, width), LOW),
            pltpu.VMEM((2, grid.fsdp, SLAB, width // 2), LOW),
            pltpu.SemaphoreType.DMA((4,)),
        ],
        compiler_params=params(),
        cost_estimate=cost(8),
        name="project_in",
    )(image, gains, *source.arrays)


def attend(qkv, counts):
    length, width = qkv.shape[1:]
    pair = 2 * HD

    def body(counts_ref, qkv_ref, context_ref):
        seen = lax.broadcasted_iota(jnp.int32, (1, length), 1) < counts_ref[0]
        first = lax.broadcasted_iota(jnp.int32, (1, pair), 1) < HD
        q, k, v = qkv_ref[0], qkv_ref[1], qkv_ref[2]
        found = []
        for head in range(2):
            own = first if head == 0 else jnp.logical_not(first)
            scores = dot_nt(jnp.where(own, q, jnp.zeros_like(q)), k)
            scores = jnp.where(seen, scores, MASKED)
            probs = jnp.exp(scores - jnp.max(scores, -1, keepdims=True))
            summed = dot(probs.astype(LOW), jnp.where(own, v, jnp.ones_like(v)))
            found.append(summed / pltpu.roll(summed, HD, 1))
        context_ref[...] = jnp.where(first, found[0], found[1]).astype(LOW)

    return pl.pallas_call(
        body,
        grid=(width // pair,),
        out_shape=jax.ShapeDtypeStruct((length, width), LOW),
        in_specs=[
            pl.BlockSpec(memory_space=pltpu.SMEM),
            pl.BlockSpec((3, length, pair), lambda i: (0, 0, i)),
        ],
        out_specs=pl.BlockSpec((length, pair), lambda i: (0, i)),
        compiler_params=params(("arbitrary",)),
        cost_estimate=cost(9),
        name="attend",
    )(counts, qkv)


def attend_back(qkv, d_context, counts, low, steps):
    length = qkv.shape[1]
    pair = 2 * HD
    width = steps * pair

    def body(counts_ref, qkv_ref, d_ref, out_ref):
        seen = lax.broadcasted_iota(jnp.int32, (length, 1), 0) < counts_ref[0]
        first = lax.broadcasted_iota(jnp.int32, (1, pair), 1) < HD
        q, k, v, d = qkv_ref[0], qkv_ref[1], qkv_ref[2], d_ref[...]
        found = []
        for head in range(2):
            own = first if head == 0 else jnp.logical_not(first)
            scores = dot_nt(k, jnp.where(own, q, jnp.zeros_like(q)))
            scores = jnp.where(seen, scores, MASKED)
            probs = jnp.exp(scores - jnp.max(scores, 0, keepdims=True))
            probs = probs * (1.0 / jnp.sum(probs, 0, keepdims=True))
            d_probs = dot_nt(v, jnp.where(own, d, jnp.zeros_like(d)))
            weighed = probs * d_probs
            d_scores = (weighed - probs * jnp.sum(weighed, 0, keepdims=True)).astype(LOW)
            found.append((dot_tn(d_scores, k), dot(d_scores, q), dot(probs.astype(LOW), d)))
        for j in range(3):
            out_ref[j] = jnp.where(first, found[0][j], found[1][j]).astype(LOW)

    return pl.pallas_call(
        body,
        grid=(width // pair,),
        out_shape=jax.ShapeDtypeStruct((3, length, width), LOW),
        in_specs=[
            pl.BlockSpec(memory_space=pltpu.SMEM),
            pl.BlockSpec((3, length, pair), lambda i: (0, 0, low + i)),
            pl.BlockSpec((length, pair), lambda i: (0, low + i)),
        ],
        out_specs=pl.BlockSpec((3, length, pair), lambda i: (0, 0, i)),
        compiler_params=params(("arbitrary",)),
        cost_estimate=cost(2.3 * steps + 2),
        name="attend_back",
    )(counts, qkv, d_context)


def feed_forward(grid, second, third, image, context, cotangent, counts, gains):
    length, width = image.shape
    rows = width // grid.fsdp
    down_rows = second.down_rows
    hidden_width = down_rows * grid.fsdp
    steps = 4
    chunk = hidden_width // steps
    n_second, n_third = len(second.arrays), len(third.arrays)
    n_refs = len(grad_shapes(grid, rows, width))

    def body(*refs):
        counts_ref, image_ref, context_ref, cotangent_ref, gains_ref = refs[:5]
        seconds, refs = refs[5 : 5 + n_second], refs[5 + n_second :]
        thirds, refs = refs[:n_third], refs[n_third:]
        output_ref, attended, d_normed, hidden_ref = refs[:4]
        in_grads, refs = refs[4 : 4 + n_refs], refs[4 + n_refs :]
        w_out, w_down, w_gate, w_up, normed, normed_t, e_ref, total, sems = refs
        step = pl.program_id(0)
        seen = lax.broadcasted_iota(jnp.int32, (length, 1), 0) < counts_ref[0]

        @pl.when(step == 0)
        def _():
            start_load(second, seconds, 0, rows, w_out, sems.at[0], 0)
            load_rows(grid, thirds, 0, 0, w_gate, sems.at[1])
            load_rows(grid, thirds, 1, rows, w_up, sems.at[2])
            start_load(second, seconds, rows, down_rows, w_down, sems.at[3], 1)
            e = cotangent_ref[...]
            e_ref[...] = jnp.where(seen, e, jnp.zeros_like(e))
            wait_all(w_out, sems.at[0])
            values = image_ref[...].astype(WIDE) + dot(context_ref[...], w_out[...])
            attended[...] = values
            low = (values * norm_rows(values) * gains_ref[1:2]).astype(LOW)
            normed[...] = low
            normed_t[...] = low.T
            total[...] = values
            d_normed[...] = jnp.zeros_like(d_normed)
            wait_all(w_gate, sems.at[1])
            wait_all(w_up, sems.at[2])
            wait_all(w_down, sems.at[3])

        columns = pl.ds(pl.multiple_of(step * chunk, chunk), chunk)
        gate_w, up_w = (w[:, :, columns].reshape(width, chunk) for w in (w_gate, w_up))
        down_w = w_down[columns]
        e = e_ref[...]
        gate, up = dot(normed[...], gate_w), dot(normed[...], up_w)
        square = gate * gate
        bend = jnp.tanh(0.7978845608 * (gate + 0.044715 * square * gate))
        half_up = 0.5 * (1.0 + bend)
        gelu = gate * half_up
        slope = half_up + 0.5 * gate * (1.0 - bend * bend) * (
            0.7978845608 * (1.0 + 3.0 * 0.044715 * square)
        )
        hidden = (gelu * up).astype(LOW)
        hidden_ref[...] = hidden
        total[...] += dot(hidden, down_w)
        d_hidden = dot_nt(e, down_w)
        d_gate = (d_hidden * up * slope).astype(LOW)
        d_up = (d_hidden * gelu).astype(LOW)
        everything = (0, slice(None))
        store_grad(grid, in_grads, everything, 0, rows, dot(normed_t[...], d_gate))
        store_grad(grid, in_grads, everything, rows, rows, dot(normed_t[...], d_up))
        d_normed[...] += dot_nt(d_gate, gate_w) + dot_nt(d_up, up_w)

        @pl.when(step == steps - 1)
        def _():
            output_ref[...] = jnp.where(seen, total[...], 0.0).astype(LOW)

    vmem = pl.BlockSpec(memory_space=pltpu.VMEM)
    per_half = steps // 2
    in_grads = grad_shapes(grid, 2 * rows, hidden_width)
    block = (1,) + in_grads[0].shape[1:3] + (chunk,)
    in_block = pl.BlockSpec(block, lambda i: (i // per_half, 0, 0, lax.rem(i, per_half)))
    results = pl.pallas_call(
        body,
        grid=(steps,),
        out_shape=[
            jax.ShapeDtypeStruct((length, width), LOW),
            jax.ShapeDtypeStruct((length, width), WIDE),
            jax.ShapeDtypeStruct((length, width), WIDE),
            jax.ShapeDtypeStruct((length, hidden_width), LOW),
        ]
        + in_grads,
        in_specs=[pl.BlockSpec(memory_space=pltpu.SMEM)] + [vmem] * 4 + second.specs + third.specs,
        out_specs=[vmem] * 3
        + [pl.BlockSpec((length, chunk), lambda i: (0, i))]
        + [in_block] * n_refs,
        scratch_shapes=[
            pltpu.VMEM((width, width), LOW),
            pltpu.VMEM((hidden_width, width), LOW),
            pltpu.VMEM((grid.fsdp, rows, hidden_width), LOW),
            pltpu.VMEM((grid.fsdp, rows, hidden_width), LOW),
            pltpu.VMEM((length, width), LOW),
            pltpu.VMEM((width, length), LOW),
            pltpu.VMEM((length, width), LOW),
            pltpu.VMEM((length, width), WIDE),
            pltpu.SemaphoreType.DMA((4,)),
        ],
        compiler_params=params(("arbitrary",)),
        cost_estimate=cost(25),
        name="feed_forward",
    )(counts, image, context, cotangent, gains, *second.arrays, *third.arrays)
    return results[:4], results[4:]


def feed_forward_back(grid, second, context, cotangent, counts, gains, attended, d_normed, hidden):
    length, width = context.shape
    rows, down_rows = width // grid.fsdp, second.down_rows
    n_second = len(second.arrays)

    def body(*refs):
        counts_ref, context_ref, cotangent_ref, gains_ref = refs[:4]
        attended_ref, d_normed_ref, hidden_ref = refs[4:7]
        seconds, refs = refs[7 : 7 + n_second], refs[7 + n_second :]
        d_attended_ref, d_context_ref, d_gain_ref, grads, w_out, sem = refs
        start_load(second, seconds, 0, rows, w_out, sem, 0)
        seen = lax.broadcasted_iota(jnp.int32, (length, 1), 0) < counts_ref[0]
        e = cotangent_ref[...]
        e = jnp.where(seen, e, jnp.zeros_like(e))
        values = attended_ref[...]
        back, d_gain = norm_back(values, norm_rows(values), gains_ref[1:2], d_normed_ref[...])
        d_gain_ref[...] = jnp.broadcast_to(d_gain, d_gain_ref.shape)
        d_attended = e.astype(WIDE) + back
        d_attended_ref[...] = d_attended
        low = d_attended.astype(LOW)
        wait_all(w_out, sem)
        d_context_ref[...] = dot_nt(low, w_out[...]).astype(LOW)
        g_out = dot_tn(context_ref[...], low).astype(LOW)
        grads[:, :rows] = g_out.reshape(grid.fsdp, rows, width)
        g_down = dot_tn(hidden_ref[...], e).astype(LOW)
        grads[:, rows:] = g_down.reshape(grid.fsdp, down_rows, width)

    vmem = pl.BlockSpec(memory_space=pltpu.VMEM)
    return pl.pallas_call(
        body,
        out_shape=[
            jax.ShapeDtypeStruct((length, width), WIDE),
            jax.ShapeDtypeStruct((length, width), LOW),
            jax.ShapeDtypeStruct((8, width), WIDE),
            jax.ShapeDtypeStruct((grid.fsdp, rows + down_rows, width), LOW),
        ],
        in_specs=[pl.BlockSpec(memory_space=pltpu.SMEM)] + [vmem] * 6 + second.specs,
        out_specs=[vmem] * 4,
        scratch_shapes=[pltpu.VMEM((width, width), LOW), pltpu.SemaphoreType.DMA],
        compiler_params=params(),
        cost_estimate=cost(10),
        name="feed_forward_back",
    )(counts, context, cotangent, gains, attended, d_normed, hidden, *second.arrays)


def project_back(grid, source, image, normed, d_qkv, d_attended, gains, d_gain_two):
    length, width = image.shape
    rows = width // grid.fsdp
    count, parts = len(source.arrays), len(d_qkv)
    shapes = grad_shapes(grid, 3 * rows + SLAB, width)

    def body(*refs):
        image_ref, normed_ref, d_attended_ref, gains_ref, d_gain_ref = refs[:5]
        d_refs, refs = refs[5 : 5 + parts], refs[5 + parts :]
        pieces, refs = refs[:count], refs[count:]
        input_grad_ref, grads, (weights, sems) = refs[0], refs[1 : 1 + len(shapes)], refs[-2:]
        for j in range(3):
            start_load(source, pieces, j * rows, rows, weights.at[j], sems.at[j], j)
        normed_t = normed_ref[...].T
        d_parts = [jnp.concatenate([d_ref[j] for d_ref in d_refs], -1) for j in range(3)]
        for j in range(3):
            g = dot(normed_t, d_parts[j])
            for h in range(2):
                part = g[:, h * (width // 2) : (h + 1) * (width // 2)]
                store_grad(grid, grads, (h, slice(None)), j * rows, rows, part)
        d_normed = jnp.zeros((length, width), WIDE)
        for j in range(3):
            wait_all(weights.at[j], sems.at[j])
            d_normed = d_normed + dot_nt(d_parts[j], weights[j])
        values = image_ref[...].astype(WIDE)
        back, d_gain = norm_back(values, norm_rows(values), gains_ref[0:1], d_normed)
        input_grad_ref[...] = (d_attended_ref[...] + back).astype(LOW)
        slab = jnp.concatenate(
            [d_gain, d_gain_ref[0:1], jnp.zeros((SLAB - 2, width), WIDE)], 0
        ).astype(LOW)
        for h in range(2):
            part = slab[:, h * (width // 2) : (h + 1) * (width // 2)]
            for ref in grads:
                ref[h, :, 3 * rows :] = jnp.broadcast_to(part[None], (ref.shape[1],) + part.shape)

    vmem = pl.BlockSpec(memory_space=pltpu.VMEM)
    results = pl.pallas_call(
        body,
        out_shape=[jax.ShapeDtypeStruct((length, width), LOW)] + shapes,
        in_specs=[vmem] * (5 + parts) + source.specs,
        out_specs=[vmem] * (1 + len(shapes)),
        scratch_shapes=[
            pltpu.VMEM((3, width, width), LOW),
            pltpu.SemaphoreType.DMA((3,)),
        ],
        compiler_params=params(),
        cost_estimate=cost(11),
        name="project_back",
    )(image, normed, d_attended, gains, d_gain_two, *d_qkv, *source.arrays)
    return results[0], results[1:]


def adamw(param, first, second, grad, rate, decay):
    first = BETA_ONE * first + (1.0 - BETA_ONE) * grad
    second = BETA_TWO * second + (1.0 - BETA_TWO) * grad * grad
    update = first / (1.0 - BETA_ONE**STEP) / (jnp.sqrt(second / (1.0 - BETA_TWO**STEP)) + ADAM_EPS)
    return (param - rate * (update + decay * param), first, second)


def update(grad_norm, weights, firsts, seconds, first, second, third, own_gains):
    rows = weights[0].shape[1]
    rates = (MATRIX_RATE, MATRIX_RATE, MATRIX_RATE, GAIN_RATE)
    decays = (MATRIX_DECAY, MATRIX_DECAY, MATRIX_DECAY, 0.0)

    def body(*refs):
        norm_ref, first_ref, second_ref, third_ref, gains_ref = refs[:5]
        weight_refs, first_refs, second_refs = refs[5:9], refs[9:13], refs[13:17]
        outs = refs[17:]
        factor = jnp.minimum(1.0, CLIP_AT / (norm_ref[0] + 1e-06))

        def one(n, index, grad):
            taken = [r[n][index] for r in (weight_refs, first_refs, second_refs)]
            results = adamw(*taken, grad.astype(WIDE) * factor, rates[n], decays[n])
            for k, value in enumerate(results):
                outs[4 * k + n][index] = value

        for j in range(3):
            one(0, j, first_ref[0, j * rows : (j + 1) * rows])
        one(0, 3, second_ref[:rows])
        for j in range(2):
            one(1, j, third_ref[0, j * rows : (j + 1) * rows])
        one(2, slice(None), second_ref[rows:])
        one(3, slice(None), gains_ref[...])

    def halves(shape):
        block = shape[:-1] + (shape[-1] // 2,)
        return pl.BlockSpec(block, lambda i: (0,) * (len(shape) - 1) + (i,))

    whole = pl.BlockSpec(own_gains.shape, lambda i: (0, 0))
    own = [halves(w.shape) for w in weights[:3]] + [whole]
    outer = [pl.BlockSpec((1,) + v.shape[1:], lambda i: (i, 0, 0)) for v in (first, third)]
    results = pl.pallas_call(
        body,
        grid=(2,),
        out_shape=[jax.ShapeDtypeStruct(w.shape, WIDE) for w in weights] * 3,
        in_specs=[pl.BlockSpec(memory_space=pltpu.SMEM), outer[0], halves(second.shape), outer[1]]
        + [whole]
        + own * 3,
        out_specs=own * 3,
        compiler_params=params(("arbitrary",)),
        cost_estimate=cost(4),
        name="update",
    )(grad_norm.reshape(1), first, second, third, own_gains, *weights, *firsts, *seconds)
    return results


def on_device(
    grid,
    patches,
    counts,
    cotangent,
    w_attn,
    w_in,
    w_down,
    gains,
    m_attn,
    m_in,
    m_down,
    m_gains,
    v_attn,
    v_in,
    v_down,
    v_gains,
):
    image, e = patches[0], cotangent[0]
    width = image.shape[1]
    rows, down_rows = w_attn.shape[1], w_down.shape[0]
    shard = lax.axis_index("fsdp")
    low_attn, low_in, low_down, low_gains = (
        w.astype(LOW) for w in (w_attn, w_in, w_down, gains)
    )
    owned = lax.broadcasted_iota(jnp.int32, (1, width), 1) // rows == shard
    slab = jnp.where(owned, jnp.tile(low_gains, (1, grid.fsdp)), jnp.zeros((), LOW))
    slab = jnp.pad(slab, ((0, SLAB - 2), (0, 0)))
    groups = [
        split_columns(g)
        for g in (
            jnp.concatenate([low_attn[0], low_attn[1], low_attn[2], slab], 0),
            jnp.concatenate([low_attn[3], low_down], 0),
        )
    ]
    pairs = width // (2 * HD)
    in_full = lax.all_gather(low_in.reshape(2 * rows, -1), "fsdp")
    in_full = [in_full] if grid.cube else [in_full[:, :rows], in_full[:, rows:]]
    third = Source(grid, in_full, True)

    if grid.cube:
        x = lax.axis_index("dp")
        parts = [lax.dynamic_index_in_dim(g, x, 0, False) for g in groups]
        one, two = Spread(grid, parts[0]), Spread(grid, parts[1])
        one.send_levels()
        one.levels, two.part = after(one.levels, two.part)
        one.load_column()
        one.send_sides()
        two.send_levels()
        (one.side, one.across), two.levels = after((one.side, one.across), two.levels)
        one.send_corners()
        two.load_column()
        two.send_sides()
        one.finish()
        first = Source(grid, one.pieces)
        normed, qkv, full_gains = project_in(grid, first, image, jnp.zeros((SLAB, width), WIDE))
        qkv, two.side, two.across = lax.optimization_barrier((qkv, two.side, two.across))
        two.send_corners()
        context = attend(qkv, counts)
        context, two.low, two.high = lax.optimization_barrier((context, two.low, two.high))
        two.finish()
        second = Source(grid, two.pieces)
        second.down_rows = down_rows

        (output, attended, d_normed, hidden), in_grads = feed_forward(
            grid, second, third, image, context, e, counts, full_gains
        )
        three = Reduce(grid, *in_grads)
        three.send_core()
        d_attended, d_context, d_gain_two, out_grads = feed_forward_back(
            grid, second, context, e, counts, full_gains, attended, d_normed, hidden
        )
        out_total = lax.psum_scatter(out_grads, "fsdp", scatter_dimension=0)
        three.got, d_context = after(three.got, d_context)
        corners, d_context = after(three.load_corners(), d_context)
        three.send_corners(corners)
        low = pairs // 2
        d_qkv = [attend_back(qkv, d_context, counts, 0, low)]
        d_qkv, three.in_x, three.in_y = lax.optimization_barrier((d_qkv, three.in_x, three.in_y))
        sides, d_context = after(three.load_sides(), d_context)
        three.send_sides(sides)
        d_qkv.append(attend_back(qkv, d_context, counts, low, pairs - low))
        input_grad, grads = project_back(
            grid, first, image, normed, d_qkv, d_attended, full_gains, d_gain_two
        )
        one = Reduce(grid, *grads)
        three.sides, one.sent = after(three.sides, one.sent)
        one.send_core()
        three.load_levels()
        three.leave, one.got = after(three.leave, one.got)
        three.send_levels()
        one.send_sides(one.load_sides())
        one.sides, three.arrive, out_total = lax.optimization_barrier(
            (one.sides, three.arrive, out_total)
        )
        one.load_levels()
        one.send_levels()
        three.load_total()
        three.send_total()
        out_other = grid.flip_x(out_total)
        one.load_total()
        one.send_total()
        second = (out_total.astype(WIDE) + out_other.astype(WIDE)).astype(LOW)
        first, third = (
            jnp.stack([jnp.where(x == 0, g.total, g.other), jnp.where(x == 0, g.other, g.total)])
            for g in (one, three)
        )
        mine = lax.dynamic_slice_in_dim(owned, x * (width // 2), width // 2, 1)
        counted = (one.total, three.total)
    else:
        groups = [lax.all_gather(g, "fsdp", axis=1) for g in groups]

        def whole(full, low, n):
            full = full[:, :, low : low + n].reshape(2, grid.fsdp * n, full.shape[3])
            return jnp.concatenate([full[0], full[1]], -1)

        slabs = jnp.sum(groups[0][:, :, 3 * rows :].astype(WIDE), 1)
        first = Source(grid, [whole(groups[0], j * rows, rows) for j in range(3)], True)
        second = Source(
            grid, [whole(groups[1], 0, rows), whole(groups[1], rows, down_rows)], True
        )
        second.down_rows = down_rows
        normed, qkv, full_gains = project_in(
            grid, first, image, jnp.concatenate([slabs[0], slabs[1]], -1)
        )
        context = attend(qkv, counts)
        (output, attended, d_normed, hidden), in_grads = feed_forward(
            grid, second, third, image, context, e, counts, full_gains
        )
        d_attended, d_context, d_gain_two, out_grads = feed_forward_back(
            grid, second, context, e, counts, full_gains, attended, d_normed, hidden
        )
        d_qkv = [attend_back(qkv, d_context, counts, 0, pairs)]
        input_grad, grads = project_back(
            grid, first, image, normed, d_qkv, d_attended, full_gains, d_gain_two
        )

        def reduce_whole(g, dim):
            total = lax.psum_scatter(g.astype(WIDE), "fsdp", scatter_dimension=dim)
            return lax.psum(total.astype(LOW), "dp")

        first, third = reduce_whole(grads[0], 1), reduce_whole(in_grads[0], 1)
        second = reduce_whole(out_grads, 0)
        mine = owned.reshape(2, 1, width // 2)
        counted = (first, third)

    def squares(v):
        return jnp.sum(jnp.square(v.astype(WIDE)))

    squared = squares(counted[0][..., : 3 * rows, :]) + squares(counted[1])
    squared = squared + squares(jnp.where(mine, counted[0][..., 3 * rows :, :], jnp.zeros((), LOW)))
    squared = squared + squares(second) * (0.5 if grid.cube else 1.0)
    grad_norm = jnp.sqrt(total_of(grid, squared))
    own_gains = jnp.concatenate([first[0, 3 * rows : 3 * rows + 2], first[1, 3 * rows : 3 * rows + 2]], -1)
    own_gains = lax.dynamic_slice_in_dim(own_gains, shard * rows, rows, 1)
    updated = update(
        grad_norm,
        (w_attn, w_in, w_down, gains),
        (m_attn, m_in, m_down, m_gains),
        (v_attn, v_in, v_down, v_gains),
        first,
        second,
        third,
        own_gains,
    )
    return (output[None], input_grad[None], grad_norm, *updated)


def solution(mesh):
    placed = (
        P(("dp", "fsdp"), None, None),
        P(("dp", "fsdp")),
        P(("dp", "fsdp"), None, None),
        P(None, "fsdp", None),
        P(None, "fsdp", None),
        P("fsdp", None),
        P(None, "fsdp"),
        P(None, "fsdp", None),
        P(None, "fsdp", None),
        P("fsdp", None),
        P(None, "fsdp"),
        P(None, "fsdp", None),
        P(None, "fsdp", None),
        P("fsdp", None),
        P(None, "fsdp"),
    )
    grid = Grid(mesh.shape["dp"], mesh.shape["fsdp"])
    return jax.shard_map(
        functools.partial(on_device, grid),
        mesh=mesh,
        in_specs=placed,
        out_specs=(
            P(("dp", "fsdp"), None, None),
            P(("dp", "fsdp"), None, None),
            P(),
            P(None, "fsdp", None),
            P(None, "fsdp", None),
            P("fsdp", None),
            P(None, "fsdp"),
            P(None, "fsdp", None),
            P(None, "fsdp", None),
            P("fsdp", None),
            P(None, "fsdp"),
            P(None, "fsdp", None),
            P(None, "fsdp", None),
            P("fsdp", None),
            P(None, "fsdp"),
        ),
        check_vma=False,
    )
```

time: 312 us -> 286 us (0.917)
  starting transfers between devices: 84.1 us -> 55 us
  Pallas kernels: 71 us -> 84.9 us
  waiting for transfers between devices: 109 us -> 95.1 us
  between operations: 9.07 us -> 22.2 us
  other arithmetic: 33.1 us -> 20.3 us
    ppermute x18 -> x1, waiting for transfers between devices: 39.8 us -> 0.01 us  [flip_xy(): lax.ppermute(v, EVERY, self.move(lambda x, z, y, c: (1 - x, z, 1 - y, c)))]
    ppermute x2 -> x14, waiting for transfers between devices: 0.95 us -> 37.7 us  [swap_z(): lax.ppermute(v, EVERY, self.move(lambda x, z, y, c: (x, z ^ bit, y, c)))]
    ppermute x18 -> x1, starting transfers between devices: 34.1 us -> 1.6 us  [flip_xy(): lax.ppermute(v, EVERY, self.move(lambda x, z, y, c: (1 - x, z, 1 - y, c)))]
    ppermute x16 -> x11, waiting for transfers between devices: 31 us -> 6.3 us  [flip_x(): lax.ppermute(v, EVERY, self.move(lambda x, z, y, c: (1 - x, z, y, c)))]
    reduce_scatter x0 -> x1, waiting for transfers between devices: none -> 19.8 us  [on_device(): out_total = lax.psum_scatter(out_grads, 'fsdp', scatter_dimension=0)]
    ppermute x2 -> x14, starting transfers between devices: 9.72 us -> 29.2 us  [swap_z(): lax.ppermute(v, EVERY, self.move(lambda x, z, y, c: (x, z ^ bit, y, c)))]
    pallas_call x0 -> x2, Pallas kernels: none -> 15.3 us  [the longest x1 9.87 us: feed_forward_back(): pl.pallas_call(body, out_shape=[jax.ShapeDtypeStruct((length, width), WID...]
    ppermute x16 -> x11, starting transfers between devices: 21.1 us -> 12.3 us  [flip_x(): lax.ppermute(v, EVERY, self.move(lambda x, z, y, c: (1 - x, z, y, c)))]
  transfers between devices with their start and end apart: 68 -> 43, of which waited for: 31 -> 21; matrix products, arithmetic and copies ran while one was open for 10% -> 6% of each run, Pallas kernels for 5% -> 19%
where the time goes in v3:
time: 286 us; the launch traced here: 285 us
  waiting for transfers between devices  95.1 us (33%)
  Pallas kernels  84.9 us (30%)
  starting transfers between devices  55 us (19%)
  between operations  22.2 us (8%)
  other arithmetic  20.3 us (7%)
  local copies, waits for them, and re-layouts  7.54 us (3%)
    ppermute x14, waiting for transfers between devices, swap_z(): lax.ppermute(v, EVERY, self.move(lambda x, z, y, c: (x, z ^ bit, y, c)))  37.7 us
    ppermute x14, starting transfers between devices, swap_z(): lax.ppermute(v, EVERY, self.move(lambda x, z, y, c: (x, z ^ bit, y, c)))  29.2 us
    ppermute x8, waiting for transfers between devices, flip_y(): lax.ppermute(v, EVERY, self.move(lambda x, z, y, c: (x, z, 1 - y, c)))  26.5 us
    pallas_call x1, Pallas kernels, feed_forward(): pl.pallas_call(body, grid=(steps,), out_shape=[jax.ShapeDtypeStruct((leng...  24.2 us
    reduce_scatter x1, waiting for transfers between devices, on_device(): out_total = lax.psum_scatter(out_grads, 'fsdp', scatter_dimension=0)  19.8 us
    pallas_call x2, Pallas kernels, attend_back(): pl.pallas_call(body, grid=(width // pair,), out_shape=jax.ShapeDtypeStruc...  18 us
    ppermute x11, starting transfers between devices, flip_x(): lax.ppermute(v, EVERY, self.move(lambda x, z, y, c: (1 - x, z, y, c)))  12.3 us
    pallas_call x1, Pallas kernels, project_back(): pl.pallas_call(body, out_shape=[jax.ShapeDtypeStruct((length, width), LOW...  11.1 us
  transfers between devices with their start and end apart: 43, of which 21 were waited for; matrix products, arithmetic and copies ran while one was open for 6% of the time, Pallas kernels for 19%

profile of v3, /device:TPU:0, one launch (start us, length us, event | category | flops | bytes accessed | tf_op | source)
XLA Modules:
  0.0 285.0 jit_solution(13648389598890140837)
XLA Ops:
  7.2 2.0 convert_element_type.221
  10.4 3.1 %collective-permute-start = (bf16[160,384]{1,0:T(8,128)(2,1)S(1)}, bf16[160,384]{1,0:T(8,128)(2,1)S(1)}, u32[]{:S(2)}, u32[]{:S(2)}) collective-permute-start(bf16[160,384]{1,0:T(8,128)(2,1)S(1)} %bitcast.191), channel_id=1, source_target_pairs={{0,4},{1,5},{2,6},{3,7},{4,0},{5,1},{6,2},{7,3},{8,12},{9,13},{10,... | collective-permute-start | bytes 368648 | tf_op jit(solution)/shard_map/ppermute | solution.py:63
  13.5 2.6 collective-permute-start.1
  16.2 1.9 collective-permute-done
  18.1 7.7 %collective-permute-done.1 = bf16[160,384]{1,0:T(8,128)(2,1)S(1)} collective-permute-done((bf16[160,384]{1,0:T(8,128)(2,1)S(1)}, bf16[160,384]{1,0:T(8,128)(2,1)S(1)}, u32[]{:S(2)}, u32[]{:S(2)}) %collective-permute-start.1) | collective-permute-done | bytes 122912 | tf_op jit(solution)/shard_map/ppermute | solution.py:63
  29.0 8.5 %collective-permute-start.5 = (bf16[176,384]{1,0:T(8,128)(2,1)S(1)}, bf16[176,384]{1,0:T(8,128)(2,1)S(1)}, u32[]{:S(2)}, u32[]{:S(2)}) collective-permute-start(bf16[176,384]{1,0:T(8,128)(2,1)S(1)} %fusion.20), channel_id=1, source_target_pairs={{0,4},{1,5},{2,6},{3,7},{4,0},{5,1},{6,2},{7,3},{8,12},{9,13},{10,... | collective-permute-start | bytes 405512 | tf_op jit(solution)/shard_map/ppermute | solution.py:63
  37.5 2.3 collective-permute-start.6
  43.3 6.6 %collective-permute-done.6 = bf16[176,384]{1,0:T(8,128)(2,1)S(1)} collective-permute-done((bf16[176,384]{1,0:T(8,128)(2,1)S(1)}, bf16[176,384]{1,0:T(8,128)(2,1)S(1)}, u32[]{:S(2)}, u32[]{:S(2)}) %collective-permute-start.6) | collective-permute-done | bytes 135200 | tf_op jit(solution)/shard_map/ppermute | solution.py:63
  54.5 4.5 %collective-permute-done.8 = bf16[2,160,384]{2,1,0:T(8,128)(2,1)S(1)} collective-permute-done((bf16[2,160,384]{2,1,0:T(8,128)(2,1)S(1)}, bf16[2,160,384]{2,1,0:T(8,128)(2,1)S(1)}, u32[]{:S(2)}, u32[]{:S(2)}) %collective-permute-start.8) | collective-permute-done | bytes 245792 | tf_op jit(solution)/shard_map/ppermute | solution.py:51
  59.1 6.6 %collective-permute-done.9 = bf16[2,160,384]{2,1,0:T(8,128)(2,1)S(1)} collective-permute-done((bf16[2,160,384]{2,1,0:T(8,128)(2,1)S(1)}, bf16[2,160,384]{2,1,0:T(8,128)(2,1)S(1)}, u32[]{:S(2)}, u32[]{:S(2)}) %collective-permute-start.9) | collective-permute-done | bytes 245792 | tf_op jit(solution)/shard_map/ppermute | solution.py:54
  69.0 7.6 %project_in.1 = (bf16[512,768]{1,0:T(8,128)(2,1)}, bf16[3,512,768]{2,1,0:T(8,128)(2,1)}, f32[16,768]{1,0:T(8,128)}) custom-call(bf16[512,768]{1,0:T(8,128)(2,1)} %bitcast.173, f32[16,768]{1,0:T(8,128)} %broadcast_in_dim.35.refs_1_, bf16[12,160,384]{2,1,0:T(8,128)(2,1)} %copy-done.2, bf16[4,160,384]{2,1,0:T(8,128)(2,1)} %copy-done.6, ...), custom_call_target="tpu_custom_call" | custom-call | flops 8000000 | tf_op jit(solution)/shard_map/project_in/pallas_call | solution.py:310
  76.5 11.6 %collective-permute-done.13 = bf16[4,176,384]{2,1,0:T(8,128)(2,1)S(1)} collective-permute-done((bf16[4,176,384]{2,1,0:T(8,128)(2,1)S(1)}, bf16[4,176,384]{2,1,0:T(8,128)(2,1)S(1)}, u32[]{:S(2)}, u32[]{:S(2)}) %collective-permute-start.13) | collective-permute-done | bytes 540704 | tf_op jit(solution)/shard_map/ppermute | solution.py:54
  88.6 2.0 collective-permute-start.15
  91.3 8.7 %attend.1.refs_2_.refs_1_ = bf16[512,768]{1,0:T(8,128)(2,1)} custom-call(s32[1]{0:T(128)S(6)} %copy.104.counts_ref.refs_0_, bf16[3,512,768]{2,1,0:T(8,128)(2,1)} %get-tuple-element.93.qkv_ref), custom_call_target="tpu_custom_call" | custom-call | flops 9000000 | tf_op jit(solution)/shard_map/attend/pallas_call | solution.py:348
  103.7 24.2 %feed_forward.1 = (bf16[512,768]{1,0:T(8,128)(2,1)}, f32[512,768]{1,0:T(8,128)}, f32[512,768]{1,0:T(8,128)}, bf16[512,2048]{1,0:T(8,128)(2,1)}, bf16[2,8,96,1024...) custom-call(s32[1]{0:T(128)S(6)} %copy.104.counts_ref.refs_0_, bf16[512,768]{1,0:T(8,128)(2,1)} %bitcast.174, ...), custom_call_target="tpu_custom_call" | custom-call | flops 25000000 | tf_op jit(solution)/shard_map/feed_forward/pallas_call | solution.py:474
  128.1 9.9 %feed_forward_back.1 = (f32[512,768]{1,0:T(8,128)}, bf16[512,768]{1,0:T(8,128)(2,1)}, f32[8,768]{1,0:T(8,128)}, bf16[16,176,768]{2,1,0:T(8,128)(2,1)}) custom-call(s32[1]{0:T(128)S(6)} %copy.104.counts_ref.refs_0_, bf16[512,768]{1,0:T(8,128)(2,1)} %attend.1.refs_2_.refs_1_, bf16[512,768]{1,0:T(8,128)(2,1)} %bitcast.177, ...), custom_call_target="tpu_custom_call" | custom-call | flops 10000000 | tf_op jit(solution)/shard_map/feed_forward_back/pallas_call | solution.py:534
  139.9 2.0 fusion.11
  144.0 9.0 %attend_back.2.refs_5_ = bf16[3,512,384]{2,1,0:T(8,128)(2,1)} custom-call(s32[1]{0:T(128)S(6)} %copy.104.counts_ref.refs_0_, bf16[3,512,768]{2,1,0:T(8,128)(2,1)} %get-tuple-element.93.qkv_ref, bf16[512,768]{1,0:T(8,128)(2,1)} %get-tuple-element.118.d_ref), custom_call_target="tpu_custom_call" | custom-call | flops 8899999 | tf_op jit(solution)/shard_map/attend_back/pallas_call | solution.py:386
  157.3 9.0 %attend_back.3.refs_6_ = bf16[3,512,384]{2,1,0:T(8,128)(2,1)} custom-call(s32[1]{0:T(128)S(6)} %copy.104.counts_ref.refs_0_, bf16[3,512,768]{2,1,0:T(8,128)(2,1)} %get-tuple-element.93.qkv_ref, bf16[512,768]{1,0:T(8,128)(2,1)} %get-tuple-element.118.d_ref), custom_call_target="tpu_custom_call" | custom-call | flops 8899999 | tf_op jit(solution)/shard_map/attend_back/pallas_call | solution.py:386
  166.3 11.1 %project_back.1 = (bf16[512,768]{1,0:T(8,128)(2,1)}, bf16[2,8,160,384]{3,2,1,0:T(8,128)(2,1)}, bf16[2,8,160,384]{3,2,1,0:T(8,128)(2,1)}) custom-call(bf16[512,768]{1,0:T(8,128)(2,1)} %bitcast.175, bf16[512,768]{1,0:T(8,128)(2,1)} %get-tuple-element.101.refs_1_, f32[512,768]{1,0:T(8,128)} %get-tuple-element.105.refs_2_, ...), custom_call_target="tpu_custom_call" | custom-call | flops 11000000 | tf_op jit(solution)/shard_map/project_back/pallas_call | solution.py:587
  177.4 5.9 %collective-permute-done.22 = bf16[4,96,1024]{2,1,0:T(8,128)(2,1)} collective-permute-done((bf16[4,96,1024]{2,1,0:T(8,128)(2,1)S(1)}, bf16[4,96,1024]{2,1,0:T(8,128)(2,1)}, u32[]{:S(2)}, u32[]{:S(2)}) %collective-permute-start.22) | collective-permute-done | bytes 786464 | tf_op jit(solution)/shard_map/ppermute | solution.py:54
  183.3 2.4 fusion
  187.6 2.7 fusion.6
  193.7 2.3 collective-permute-start.27
  197.4 9.2 %collective-permute-done.27 = bf16[96,1024]{1,0:T(8,128)(2,1)S(1)} collective-permute-done((bf16[96,1024]{1,0:T(8,128)(2,1)S(1)}, bf16[96,1024]{1,0:T(8,128)(2,1)S(1)}, u32[]{:S(2)}, u32[]{:S(2)}) %collective-permute-start.27) | collective-permute-done | bytes 196640 | tf_op jit(solution)/shard_map/ppermute | solution.py:63
  207.3 19.8 %reduce-scatter.2.cloned.1.call-done = bf16[1,176,768]{2,1,0:T(8,128)(2,1)} async-done(((bf16[16,176,768]{2,1,0:T(8,128)(2,1)}), bf16[1,176,768]{2,1,0:T(8,128)(2,1)}) %reduce-scatter.2.cloned.1.call-update) | async-done | bytes 270352 | tf_op jit(solution)/shard_map/reduce_scatter | solution.py:729
  228.9 2.4 collective-permute-start.32
  237.2 5.6 %collective-permute-done.31 = bf16[160,384]{1,0:T(8,128)(2,1)S(1)} collective-permute-done((bf16[160,384]{1,0:T(8,128)(2,1)S(1)}, bf16[160,384]{1,0:T(8,128)(2,1)S(1)}, u32[]{:S(2)}, u32[]{:S(2)}) %collective-permute-start.31) | collective-permute-done | bytes 122912 | tf_op jit(solution)/shard_map/ppermute | solution.py:63
  253.9 2.2 collective-permute-start.35
  263.7 2.2 collective-permute-done.37
  268.3 2.6 collective-permute-done.38
  271.6 5.5 %update.1 = (f32[4,48,768]{2,1,0:T(8,128)}, f32[2,48,2048]{2,1,0:T(8,128)}, f32[128,768]{1,0:T(8,128)}, f32[2,48]{1,0:T(2,128)}, f32[4,48,768]{2,1,0:T(8,128)}, ...) custom-call(f32[1]{0:T(128)} %bitcast.46.refs_0_, ...), custom_call_target="tpu_custom_call" | custom-call | flops 4000000 | tf_op jit(solution)/shard_map/update/pallas_call | solution.py:642
  (151 shorter events, 59.3 us)
Async XLA Ops:
  7.2 95.1 %all-gather.2.cloned.1.call-start = ((), (), s32[]{:S(2)}) async-start(), calls=%async_computation.1 | async-start | bytes 6684672 | tf_op jit(solution)/shard_map/all_gather | solution.py:693
  9.2 217.9 %reduce-scatter.2.cloned.1.call-start = ((), (), s32[]{:S(2)}) async-start(), calls=%async_computation.2 | async-start | bytes 4595712 | tf_op jit(solution)/shard_map/reduce_scatter | solution.py:729
  13.5 12.4 %collective-permute-start.1 = (bf16[160,384]{1,0:T(8,128)(2,1)S(1)}, bf16[160,384]{1,0:T(8,128)(2,1)S(1)}, u32[]{:S(2)}, u32[]{:S(2)}) collective-permute-start(bf16[160,384]{1,0:T(8,128)(2,1)S(1)} %bitcast.192), channel_id=1, source_target_pairs={{0,8},{1,9},{2,10},{3,11},{4,12},{5,13},{6,14},{7,15},{8,0},{9,1},... | collective-permute-start | bytes 368648 | tf_op jit(solution)/shard_map/ppermute | solution.py:63
  16.1 9.8 %collective-permute-start.2 = (bf16[160,384]{1,0:T(8,128)(2,1)S(1)}, bf16[160,384]{1,0:T(8,128)(2,1)S(1)}, u32[]{:S(2)}, u32[]{:S(2)}) collective-permute-start(bf16[160,384]{1,0:T(8,128)(2,1)S(1)} %bitcast.193), channel_id=1, source_target_pairs={{0,12},{1,13},{2,14},{3,15},{4,8},{5,9},{6,10},{7,11},{8,4},{9,5},... | collective-permute-start | bytes 368648 | tf_op jit(solution)/shard_map/ppermute | solution.py:63
  25.9 23.9 %collective-permute-start.3 = (bf16[4,160,384]{2,1,0:T(8,128)(2,1)S(1)}, bf16[4,160,384]{2,1,0:T(8,128)(2,1)S(1)}, u32[]{:S(2)}, u32[]{:S(2)}) collective-permute-start(bf16[4,160,384]{2,1,0:T(8,128)(2,1)S(1)} %pad_maximum_fusion.3), channel_id=1, source_target_pairs={{0,16},{1,17},{2,18},{3,19},{4,20},{5,21},{6,22},{7,23},{8,24},{9,... | collective-permute-start | bytes 1474568 | tf_op jit(solution)/shard_map/ppermute | solution.py:51
  27.5 22.4 %collective-permute-start.4 = (bf16[4,160,384]{2,1,0:T(8,128)(2,1)S(1)}, bf16[4,160,384]{2,1,0:T(8,128)(2,1)S(1)}, u32[]{:S(2)}, u32[]{:S(2)}) collective-permute-start(bf16[4,160,384]{2,1,0:T(8,128)(2,1)S(1)} %pad_maximum_fusion.3), channel_id=1, source_target_pairs={{0,2},{1,3},{2,0},{3,1},{4,6},{5,7},{6,4},{7,5},{8,10},{9,11},{10,... | collective-permute-start | bytes 1474568 | tf_op jit(solution)/shard_map/ppermute | solution.py:54
  29.0 14.3 %collective-permute-start.5 = (bf16[176,384]{1,0:T(8,128)(2,1)S(1)}, bf16[176,384]{1,0:T(8,128)(2,1)S(1)}, u32[]{:S(2)}, u32[]{:S(2)}) collective-permute-start(bf16[176,384]{1,0:T(8,128)(2,1)S(1)} %fusion.20), channel_id=1, source_target_pairs={{0,4},{1,5},{2,6},{3,7},{4,0},{5,1},{6,2},{7,3},{8,12},{9,13},{10,... | collective-permute-start | bytes 405512 | tf_op jit(solution)/shard_map/ppermute | solution.py:63
  37.5 12.4 %collective-permute-start.6 = (bf16[176,384]{1,0:T(8,128)(2,1)S(1)}, bf16[176,384]{1,0:T(8,128)(2,1)S(1)}, u32[]{:S(2)}, u32[]{:S(2)}) collective-permute-start(bf16[176,384]{1,0:T(8,128)(2,1)S(1)} %fusion.20), channel_id=1, source_target_pairs={{0,8},{1,9},{2,10},{3,11},{4,12},{5,13},{6,14},{7,15},{8,0},{9,1},... | collective-permute-start | bytes 405512 | tf_op jit(solution)/shard_map/ppermute | solution.py:63
  39.8 10.0 %collective-permute-start.7 = (bf16[176,384]{1,0:T(8,128)(2,1)S(1)}, bf16[176,384]{1,0:T(8,128)(2,1)S(1)}, u32[]{:S(2)}, u32[]{:S(2)}) collective-permute-start(bf16[176,384]{1,0:T(8,128)(2,1)S(1)} %fusion.20), channel_id=1, source_target_pairs={{0,12},{1,13},{2,14},{3,15},{4,8},{5,9},{6,10},{7,11},{8,4},{9,5},... | collective-permute-start | bytes 405512 | tf_op jit(solution)/shard_map/ppermute | solution.py:63
  50.1 17.6 %collective-permute-start.10 = (bf16[12,160,384]{2,1,0:T(8,128)(2,1)S(1)}, bf16[12,160,384]{2,1,0:T(8,128)(2,1)S(1)}, u32[]{:S(2)}, u32[]{:S(2)}) collective-permute-start(bf16[12,160,384]{2,1,0:T(8,128)(2,1)S(1)} %constant_dynamic-update-slice_fusion.refs_2_.refs_7_), channel_id=1, source_target_pairs={{0,1},{1,0},{2,3},{3,2},{4,5},{5,4},{6,7},{7,6},{8,9},{9,8},{10,11... | collective-permute-start | bytes 4423688 | tf_op jit(solution)/shard_map/ppermute | solution.py:60
  50.2 8.8 %collective-permute-start.8 = (bf16[2,160,384]{2,1,0:T(8,128)(2,1)S(1)}, bf16[2,160,384]{2,1,0:T(8,128)(2,1)S(1)}, u32[]{:S(2)}, u32[]{:S(2)}) collective-permute-start(bf16[2,160,384]{2,1,0:T(8,128)(2,1)S(1)} %slice.76), channel_id=1, source_target_pairs={{0,16},{1,17},{2,18},{3,19},{4,20},{5,21},{6,22},{7,23},{8,24},{9,... | collective-permute-start | bytes 737288 | tf_op jit(solution)/shard_map/ppermute | solution.py:51
  51.7 14.0 %collective-permute-start.9 = (bf16[2,160,384]{2,1,0:T(8,128)(2,1)S(1)}, bf16[2,160,384]{2,1,0:T(8,128)(2,1)S(1)}, u32[]{:S(2)}, u32[]{:S(2)}) collective-permute-start(bf16[2,160,384]{2,1,0:T(8,128)(2,1)S(1)} %slice.77), channel_id=1, source_target_pairs={{0,2},{1,3},{2,0},{3,1},{4,6},{5,7},{6,4},{7,5},{8,10},{9,11},{10,... | collective-permute-start | bytes 737288 | tf_op jit(solution)/shard_map/ppermute | solution.py:54
  53.3 23.2 %collective-permute-start.12 = (bf16[4,176,384]{2,1,0:T(8,128)(2,1)S(1)}, bf16[4,176,384]{2,1,0:T(8,128)(2,1)S(1)}, u32[]{:S(2)}, u32[]{:S(2)}) collective-permute-start(bf16[4,176,384]{2,1,0:T(8,128)(2,1)S(1)} %pad_maximum_fusion.2), channel_id=1, source_target_pairs={{0,16},{1,17},{2,18},{3,19},{4,20},{5,21},{6,22},{7,23},{8,24},{9,... | collective-permute-start | bytes 1622024 | tf_op jit(solution)/shard_map/ppermute | solution.py:51
  53.9 34.3 %collective-permute-start.13 = (bf16[4,176,384]{2,1,0:T(8,128)(2,1)S(1)}, bf16[4,176,384]{2,1,0:T(8,128)(2,1)S(1)}, u32[]{:S(2)}, u32[]{:S(2)}) collective-permute-start(bf16[4,176,384]{2,1,0:T(8,128)(2,1)S(1)} %pad_maximum_fusion.2), channel_id=1, source_target_pairs={{0,2},{1,3},{2,0},{3,1},{4,6},{5,7},{6,4},{7,5},{8,10},{9,11},{10,... | collective-permute-start | bytes 1622024 | tf_op jit(solution)/shard_map/ppermute | solution.py:54
  88.4 13.9 %collective-permute-start.16 = (bf16[12,176,384]{2,1,0:T(8,128)(2,1)S(1)}, bf16[12,176,384]{2,1,0:T(8,128)(2,1)S(1)}, u32[]{:S(2)}, u32[]{:S(2)}) collective-permute-start(bf16[12,176,384]{2,1,0:T(8,128)(2,1)S(1)} %constant_dynamic-update-slice_fusion.8.refs_5_.refs_7_), channel_id=1, source_target_pairs={{0,1},{1,0},{2,3},{3,2},{4,5},{5,4},{6,7},{7,6},{8,9},{9,8},{10,11... | collective-permute-start | bytes 4866056 | tf_op jit(solution)/shard_map/ppermute | solution.py:60
  88.5 11.4 %collective-permute-start.14 = (bf16[2,176,384]{2,1,0:T(8,128)(2,1)S(1)}, bf16[2,176,384]{2,1,0:T(8,128)(2,1)S(1)}, u32[]{:S(2)}, u32[]{:S(2)}) collective-permute-start(bf16[2,176,384]{2,1,0:T(8,128)(2,1)S(1)} %slice.78), channel_id=1, source_target_pairs={{0,16},{1,17},{2,18},{3,19},{4,20},{5,21},{6,22},{7,23},{8,24},{9,... | collective-permute-start | bytes 811016 | tf_op jit(solution)/shard_map/ppermute | solution.py:51
  88.6 11.4 %collective-permute-start.15 = (bf16[2,176,384]{2,1,0:T(8,128)(2,1)S(1)}, bf16[2,176,384]{2,1,0:T(8,128)(2,1)S(1)}, u32[]{:S(2)}, u32[]{:S(2)}) collective-permute-start(bf16[2,176,384]{2,1,0:T(8,128)(2,1)S(1)} %slice.79), channel_id=1, source_target_pairs={{0,2},{1,3},{2,0},{3,1},{4,6},{5,7},{6,4},{7,5},{8,10},{9,11},{10,... | collective-permute-start | bytes 811016 | tf_op jit(solution)/shard_map/ppermute | solution.py:54
  127.9 10.2 %collective-permute-start.18 = (bf16[2,8,96,1024]{3,2,1,0:T(8,128)(2,1)}, bf16[2,8,96,1024]{3,2,1,0:T(8,128)(2,1)}, u32[]{:S(2)}, u32[]{:S(2)}) collective-permute-start(bf16[2,8,96,1024]{3,2,1,0:T(8,128)(2,1)} %get-tuple-element.108), channel_id=1, source_target_pairs={{0,1},{1,0},{2,3},{3,2},{4,5},{5,4},{6,7},{7,6},{8,9},{9,8},{10,11... | collective-permute-start | bytes 9437192 | tf_op jit(solution)/shard_map/ppermute | solution.py:60
  141.9 11.5 %collective-permute-start.19 = (bf16[2,96,1024]{2,1,0:T(8,128)(2,1)S(1)}, bf16[2,96,1024]{2,1,0:T(8,128)(2,1)S(1)}, u32[]{:S(2)}, u32[]{:S(2)}) collective-permute-start(bf16[2,96,1024]{2,1,0:T(8,128)(2,1)S(1)} %get-tuple-element.113), channel_id=1, source_target_pairs={{0,16},{1,17},{2,18},{3,19},{4,20},{5,21},{6,22},{7,23},{8,24},{9,... | collective-permute-start | bytes 1179656 | tf_op jit(solution)/shard_map/ppermute | solution.py:51
  143.0 11.1 %collective-permute-start.20 = (bf16[2,96,1024]{2,1,0:T(8,128)(2,1)S(1)}, bf16[2,96,1024]{2,1,0:T(8,128)(2,1)S(1)}, u32[]{:S(2)}, u32[]{:S(2)}) collective-permute-start(bf16[2,96,1024]{2,1,0:T(8,128)(2,1)S(1)} %get-tuple-element.114), channel_id=1, source_target_pairs={{0,2},{1,3},{2,0},{3,1},{4,6},{5,7},{6,4},{7,5},{8,10},{9,11},{10,... | collective-permute-start | bytes 1179656 | tf_op jit(solution)/shard_map/ppermute | solution.py:54
  155.8 21.5 %collective-permute-start.21 = (bf16[4,96,1024]{2,1,0:T(8,128)(2,1)S(1)}, bf16[4,96,1024]{2,1,0:T(8,128)(2,1)S(1)}, u32[]{:S(2)}, u32[]{:S(2)}) collective-permute-start(bf16[4,96,1024]{2,1,0:T(8,128)(2,1)S(1)} %get-tuple-element.121), channel_id=1, source_target_pairs={{0,16},{1,17},{2,18},{3,19},{4,20},{5,21},{6,22},{7,23},{8,24},{9,... | collective-permute-start | bytes 2359304 | tf_op jit(solution)/shard_map/ppermute | solution.py:51
  156.9 26.3 %collective-permute-start.22 = (bf16[4,96,1024]{2,1,0:T(8,128)(2,1)S(1)}, bf16[4,96,1024]{2,1,0:T(8,128)(2,1)}, u32[]{:S(2)}, u32[]{:S(2)}) collective-permute-start(bf16[4,96,1024]{2,1,0:T(8,128)(2,1)S(1)} %get-tuple-element.122), channel_id=1, source_target_pairs={{0,2},{1,3},{2,0},{3,1},{4,6},{5,7},{6,4},{7,5},{8,10},{9,11},{10,... | collective-permute-start | bytes 2359304 | tf_op jit(solution)/shard_map/ppermute | solution.py:54
  190.3 36.9 %collective-permute-start.24 = (bf16[4,160,384]{2,1,0:T(8,128)(2,1)}, bf16[4,160,384]{2,1,0:T(8,128)(2,1)S(1)}, u32[]{:S(2)}, u32[]{:S(2)}) collective-permute-start(bf16[4,160,384]{2,1,0:T(8,128)(2,1)} %get-tuple-element.165), channel_id=1, source_target_pairs={{0,16},{1,17},{2,18},{3,19},{4,20},{5,21},{6,22},{7,23},{8,24},{9,... | collective-permute-start | bytes 1474568 | tf_op jit(solution)/shard_map/ppermute | solution.py:51
  190.7 36.4 %collective-permute-start.25 = (bf16[4,160,384]{2,1,0:T(8,128)(2,1)}, bf16[4,160,384]{2,1,0:T(8,128)(2,1)}, u32[]{:S(2)}, u32[]{:S(2)}) collective-permute-start(bf16[4,160,384]{2,1,0:T(8,128)(2,1)} %get-tuple-element.164), channel_id=1, source_target_pairs={{0,2},{1,3},{2,0},{3,1},{4,6},{5,7},{6,4},{7,5},{8,10},{9,11},{10,... | collective-permute-start | bytes 1474568 | tf_op jit(solution)/shard_map/ppermute | solution.py:54
  192.2 35.0 %collective-permute-start.26 = (bf16[4,160,384]{2,1,0:T(8,128)(2,1)}, bf16[4,160,384]{2,1,0:T(8,128)(2,1)}, u32[]{:S(2)}, u32[]{:S(2)}) collective-permute-start(bf16[4,160,384]{2,1,0:T(8,128)(2,1)} %get-tuple-element.163), channel_id=1, source_target_pairs={{0,18},{1,19},{2,16},{3,17},{4,22},{5,23},{6,20},{7,21},{8,26},{9,... | collective-permute-start | bytes 1474568 | tf_op jit(solution)/shard_map/ppermute | solution.py:57
  193.7 12.8 %collective-permute-start.27 = (bf16[96,1024]{1,0:T(8,128)(2,1)S(1)}, bf16[96,1024]{1,0:T(8,128)(2,1)S(1)}, u32[]{:S(2)}, u32[]{:S(2)}) collective-permute-start(bf16[96,1024]{1,0:T(8,128)(2,1)S(1)} %get-tuple-element.128), channel_id=1, source_target_pairs={{0,4},{1,5},{2,6},{3,7},{4,0},{5,1},{6,2},{7,3},{8,12},{9,13},{10,... | collective-permute-start | bytes 589832 | tf_op jit(solution)/shard_map/ppermute | solution.py:63
  196.0 31.1 %collective-permute-start.28 = (bf16[96,1024]{1,0:T(8,128)(2,1)}, bf16[96,1024]{1,0:T(8,128)(2,1)}, u32[]{:S(2)}, u32[]{:S(2)}) collective-permute-start(bf16[96,1024]{1,0:T(8,128)(2,1)} %get-tuple-element.129), channel_id=1, source_target_pairs={{0,8},{1,9},{2,10},{3,11},{4,12},{5,13},{6,14},{7,15},{8,0},{9,1},... | collective-permute-start | bytes 589832 | tf_op jit(solution)/shard_map/ppermute | solution.py:63
  207.3 19.8 %collective-permute-start.29 = (bf16[96,1024]{1,0:T(8,128)(2,1)S(1)}, bf16[96,1024]{1,0:T(8,128)(2,1)}, u32[]{:S(2)}, u32[]{:S(2)}) collective-permute-start(bf16[96,1024]{1,0:T(8,128)(2,1)S(1)} %get-tuple-element.130), channel_id=1, source_target_pairs={{0,12},{1,13},{2,14},{3,15},{4,8},{5,9},{6,10},{7,11},{8,4},{9,5},... | collective-permute-start | bytes 589832 | tf_op jit(solution)/shard_map/ppermute | solution.py:63
  231.3 11.4 %collective-permute-start.31 = (bf16[160,384]{1,0:T(8,128)(2,1)S(1)}, bf16[160,384]{1,0:T(8,128)(2,1)S(1)}, u32[]{:S(2)}, u32[]{:S(2)}) collective-permute-start(bf16[160,384]{1,0:T(8,128)(2,1)S(1)} %get-tuple-element.171), channel_id=1, source_target_pairs={{0,8},{1,9},{2,10},{3,11},{4,12},{5,13},{6,14},{7,15},{8,0},{9,1},... | collective-permute-start | bytes 368648 | tf_op jit(solution)/shard_map/ppermute | solution.py:63
  233.2 9.5 %collective-permute-start.30 = (bf16[160,384]{1,0:T(8,128)(2,1)S(1)}, bf16[160,384]{1,0:T(8,128)(2,1)S(1)}, u32[]{:S(2)}, u32[]{:S(2)}) collective-permute-start(bf16[160,384]{1,0:T(8,128)(2,1)S(1)} %get-tuple-element.169), channel_id=1, source_target_pairs={{0,4},{1,5},{2,6},{3,7},{4,0},{5,1},{6,2},{7,3},{8,12},{9,13},{10,... | collective-permute-start | bytes 368648 | tf_op jit(solution)/shard_map/ppermute | solution.py:63
  233.4 16.7 %collective-permute-start.33 = (bf16[176,768]{1,0:T(8,128)(2,1)S(1)}, bf16[176,768]{1,0:T(8,128)(2,1)S(1)}, u32[]{:S(2)}, u32[]{:S(2)}) collective-permute-start(bf16[176,768]{1,0:T(8,128)(2,1)S(1)} %bitcast.194), channel_id=1, source_target_pairs={{0,16},{1,17},{2,18},{3,19},{4,20},{5,21},{6,22},{7,23},{8,24},{9,... | collective-permute-start | bytes 811016 | tf_op jit(solution)/shard_map/ppermute | solution.py:51
  236.7 11.1 %collective-permute-start.40 = (bf16[96,1024]{1,0:T(8,128)(2,1)S(1)}, bf16[96,1024]{1,0:T(8,128)(2,1)S(1)}, u32[]{:S(2)}, u32[]{:S(2)}) collective-permute-start(bf16[96,1024]{1,0:T(8,128)(2,1)S(1)} %get-tuple-element.154), channel_id=1, source_target_pairs={{0,16},{1,17},{2,18},{3,19},{4,20},{5,21},{6,22},{7,23},{8,24},{9,... | collective-permute-start | bytes 589832 | tf_op jit(solution)/shard_map/ppermute | solution.py:51
  (26 other events, 112.3 us)
Sparse Core Ops, SparseCore 0:
  10.9 91.4 all-gather.1
  138.2 88.8 reduce-scatter.1

commit v4 on v3

--- a/solution.py
+++ b/solution.py
@@ -26,7 +26,7 @@
 LOW = jnp.bfloat16
 WIDE = jnp.float32
 SLAB = 16
-VMEM_LIMIT = 56 * 1024 * 1024
+MIB = 1024 * 1024
 ANYWHERE = pl.BlockSpec(memory_space=pl.ANY)
 
 
@@ -111,41 +111,22 @@
 class Reduce:
     def __init__(self, grid, keep, sent):
         self.grid, self.keep, self.sent = grid, keep, sent
-        self.half = grid.nz // 2
-        self.in_x = self.in_y = None
 
     def send_core(self):
         self.got = self.grid.flip_core(self.sent)
 
-    def block(self, h, at_y, low=0, n=None):
-        n = self.grid.nz if n is None else n
+    def block(self, h, at_y):
         total = 0.0
         for array in (self.keep, self.got):
             array = array.reshape((2, self.grid.nz, 2) + array.shape[2:])
-            part = lax.dynamic_index_in_dim(array, h, 0, False)[low : low + n]
+            part = lax.dynamic_index_in_dim(array, h, 0, False)
             total = total + lax.dynamic_index_in_dim(part, at_y, 1, False).astype(WIDE)
         return total
 
-    def load_corners(self):
-        x, z, y, c = self.grid.place()
-        low = self.block(1 - x, 1 - y, 0, self.half)
-        high = self.block(1 - x, 1 - y, self.half, self.grid.nz - self.half)
-        return low.astype(LOW), high.astype(LOW)
-
-    def send_corners(self, corners):
-        self.in_x, self.in_y = self.grid.flip_x(corners[0]), self.grid.flip_y(corners[1])
-
     def load_sides(self):
         x, z, y, c = self.grid.place()
-        half, rest = self.half, self.grid.nz - self.half
-        if self.in_x is None:
-            to_x, to_y = self.block(1 - x, y), self.block(x, 1 - y)
-            return [v.astype(LOW) for v in (to_x, to_y, self.block(1 - x, 1 - y))]
-        high = self.block(1 - x, y, half, rest) + self.in_y.astype(WIDE)
-        low = self.block(x, 1 - y, 0, half) + self.in_x.astype(WIDE)
-        to_x = jnp.concatenate([self.block(1 - x, y, 0, half), high])
-        to_y = jnp.concatenate([low, self.block(x, 1 - y, half, rest)])
-        return [to_x.astype(LOW), to_y.astype(LOW)]
+        places = ((1 - x, y), (x, 1 - y), (1 - x, 1 - y))
+        return [self.block(h, at_y).astype(LOW) for h, at_y in places]
 
     def send_sides(self, sides):
         sends = (self.grid.flip_x, self.grid.flip_y, self.grid.flip_xy)
@@ -168,6 +149,24 @@
 
     def send_total(self):
         self.other = self.grid.flip_x(self.total)
+
+
+class Fold:
+    def __init__(self, grid, parts):
+        self.grid, self.parts = grid, parts
+
+    def by_bits(self, dim):
+        count = self.parts[0].shape[dim].bit_length() - 1
+        self.parts = [v.reshape(v.shape[:dim] + (2,) * count + v.shape[dim + 1 :]) for v in self.parts]
+        return count
+
+    def leave(self, dim, mine):
+        leave = sum(lax.dynamic_index_in_dim(v, 1 - mine, dim, False).astype(WIDE) for v in self.parts)
+        self.parts = [lax.dynamic_index_in_dim(v, mine, dim, False) for v in self.parts]
+        return leave.astype(LOW)
+
+    def total(self):
+        return sum(v.astype(WIDE) for v in self.parts).astype(LOW)
 
 
 def total_of(grid, value):
@@ -187,8 +186,8 @@
     return jnp.stack(jnp.split(v, 2, -1))
 
 
-def params(semantics=None):
-    return pltpu.CompilerParams(vmem_limit_bytes=VMEM_LIMIT, dimension_semantics=semantics)
+def params(mib, semantics=None):
+    return pltpu.CompilerParams(vmem_limit_bytes=mib * MIB, dimension_semantics=semantics)
 
 
 def cost(microseconds):
@@ -321,7 +320,7 @@
             pltpu.VMEM((2, grid.fsdp, SLAB, width // 2), LOW),
             pltpu.SemaphoreType.DMA((4,)),
         ],
-        compiler_params=params(),
+        compiler_params=params(12),
         cost_estimate=cost(8),
         name="project_in",
     )(image, gains, *source.arrays)
@@ -354,7 +353,7 @@
             pl.BlockSpec((3, length, pair), lambda i: (0, 0, i)),
         ],
         out_specs=pl.BlockSpec((length, pair), lambda i: (0, i)),
-        compiler_params=params(("arbitrary",)),
+        compiler_params=params(8, ("arbitrary",)),
         cost_estimate=cost(9),
         name="attend",
     )(counts, qkv)
@@ -393,7 +392,7 @@
             pl.BlockSpec((length, pair), lambda i: (0, low + i)),
         ],
         out_specs=pl.BlockSpec((3, length, pair), lambda i: (0, 0, i)),
-        compiler_params=params(("arbitrary",)),
+        compiler_params=params(8, ("arbitrary",)),
         cost_estimate=cost(2.3 * steps + 2),
         name="attend_back",
     )(counts, qkv, d_context)
@@ -413,9 +412,10 @@
         counts_ref, image_ref, context_ref, cotangent_ref, gains_ref = refs[:5]
         seconds, refs = refs[5 : 5 + n_second], refs[5 + n_second :]
         thirds, refs = refs[:n_third], refs[n_third:]
-        output_ref, attended, d_normed, hidden_ref = refs[:4]
-        in_grads, refs = refs[4 : 4 + n_refs], refs[4 + n_refs :]
-        w_out, w_down, w_gate, w_up, normed, normed_t, e_ref, total, sems = refs
+        output_ref, d_attended_ref, d_context_ref, d_gain_ref = refs[:4]
+        out_grads, refs = refs[4 : 4 + n_refs], refs[4 + n_refs :]
+        in_grads, refs = refs[:n_refs], refs[n_refs:]
+        w_out, w_down, w_gate, w_up, attended, normed, normed_t, e_ref, total, d_normed, sems = refs
         step = pl.program_id(0)
         seen = lax.broadcasted_iota(jnp.int32, (length, 1), 0) < counts_ref[0]
 
@@ -452,11 +452,24 @@
             0.7978845608 * (1.0 + 3.0 * 0.044715 * square)
         )
         hidden = (gelu * up).astype(LOW)
-        hidden_ref[...] = hidden
         total[...] += dot(hidden, down_w)
         d_hidden = dot_nt(e, down_w)
         d_gate = (d_hidden * up * slope).astype(LOW)
         d_up = (d_hidden * gelu).astype(LOW)
+        g_down = dot_tn(hidden, e)
+        shards = chunk // down_rows
+        if grid.cube:
+            c = lax.rem(lax.axis_index("fsdp"), 2)
+            g_down = g_down.astype(LOW).reshape(shards // 2, 2, down_rows, width)
+            even, odd = g_down[:, 0], g_down[:, 1]
+            g_down = [jnp.where(c == 0, even, odd), jnp.where(c == 0, odd, even)]
+            lead = pl.ds(step * (shards // 2), shards // 2)
+        else:
+            g_down = [g_down.astype(LOW).reshape(shards, down_rows, width)]
+            lead = pl.ds(step * shards, shards)
+        for ref, value in zip(out_grads, g_down):
+            for h in range(2):
+                ref[h, lead, rows:] = value[:, :, h * (width // 2) : (h + 1) * (width // 2)]
         everything = (0, slice(None))
         store_grad(grid, in_grads, everything, 0, rows, dot(normed_t[...], d_gate))
         store_grad(grid, in_grads, everything, rows, rows, dot(normed_t[...], d_up))
@@ -465,9 +478,21 @@
         @pl.when(step == steps - 1)
         def _():
             output_ref[...] = jnp.where(seen, total[...], 0.0).astype(LOW)
+            values = attended[...]
+            back, d_gain = norm_back(values, norm_rows(values), gains_ref[1:2], d_normed[...])
+            d_gain_ref[...] = jnp.broadcast_to(d_gain, d_gain_ref.shape)
+            d_attended = e_ref[...].astype(WIDE) + back
+            d_attended_ref[...] = d_attended
+            low = d_attended.astype(LOW)
+            d_context_ref[...] = dot_nt(low, w_out[...]).astype(LOW)
+            g_out = dot_tn(context_ref[...], low)
+            for h in range(2):
+                part = g_out[:, h * (width // 2) : (h + 1) * (width // 2)]
+                store_grad(grid, out_grads, (h, slice(None)), 0, rows, part)
 
     vmem = pl.BlockSpec(memory_space=pltpu.VMEM)
     per_half = steps // 2
+    out_grads = grad_shapes(grid, rows + down_rows, width)
     in_grads = grad_shapes(grid, 2 * rows, hidden_width)
     block = (1,) + in_grads[0].shape[1:3] + (chunk,)
     in_block = pl.BlockSpec(block, lambda i: (i // per_half, 0, 0, lax.rem(i, per_half)))
@@ -477,75 +502,31 @@
         out_shape=[
             jax.ShapeDtypeStruct((length, width), LOW),
             jax.ShapeDtypeStruct((length, width), WIDE),
-            jax.ShapeDtypeStruct((length, width), WIDE),
-            jax.ShapeDtypeStruct((length, hidden_width), LOW),
+            jax.ShapeDtypeStruct((length, width), LOW),
+            jax.ShapeDtypeStruct((8, width), WIDE),
         ]
+        + out_grads
         + in_grads,
         in_specs=[pl.BlockSpec(memory_space=pltpu.SMEM)] + [vmem] * 4 + second.specs + third.specs,
-        out_specs=[vmem] * 3
-        + [pl.BlockSpec((length, chunk), lambda i: (0, i))]
-        + [in_block] * n_refs,
+        out_specs=[vmem] * (4 + n_refs) + [in_block] * n_refs,
         scratch_shapes=[
             pltpu.VMEM((width, width), LOW),
             pltpu.VMEM((hidden_width, width), LOW),
             pltpu.VMEM((grid.fsdp, rows, hidden_width), LOW),
             pltpu.VMEM((grid.fsdp, rows, hidden_width), LOW),
+            pltpu.VMEM((length, width), WIDE),
             pltpu.VMEM((length, width), LOW),
             pltpu.VMEM((width, length), LOW),
             pltpu.VMEM((length, width), LOW),
             pltpu.VMEM((length, width), WIDE),
+            pltpu.VMEM((length, width), WIDE),
             pltpu.SemaphoreType.DMA((4,)),
         ],
-        compiler_params=params(("arbitrary",)),
-        cost_estimate=cost(25),
+        compiler_params=params(56, ("arbitrary",)),
+        cost_estimate=cost(28),
         name="feed_forward",
     )(counts, image, context, cotangent, gains, *second.arrays, *third.arrays)
-    return results[:4], results[4:]
-
-
-def feed_forward_back(grid, second, context, cotangent, counts, gains, attended, d_normed, hidden):
-    length, width = context.shape
-    rows, down_rows = width // grid.fsdp, second.down_rows
-    n_second = len(second.arrays)
-
-    def body(*refs):
-        counts_ref, context_ref, cotangent_ref, gains_ref = refs[:4]
-        attended_ref, d_normed_ref, hidden_ref = refs[4:7]
-        seconds, refs = refs[7 : 7 + n_second], refs[7 + n_second :]
-        d_attended_ref, d_context_ref, d_gain_ref, grads, w_out, sem = refs
-        start_load(second, seconds, 0, rows, w_out, sem, 0)
-        seen = lax.broadcasted_iota(jnp.int32, (length, 1), 0) < counts_ref[0]
-        e = cotangent_ref[...]
-        e = jnp.where(seen, e, jnp.zeros_like(e))
-        values = attended_ref[...]
-        back, d_gain = norm_back(values, norm_rows(values), gains_ref[1:2], d_normed_ref[...])
-        d_gain_ref[...] = jnp.broadcast_to(d_gain, d_gain_ref.shape)
-        d_attended = e.astype(WIDE) + back
-        d_attended_ref[...] = d_attended
-        low = d_attended.astype(LOW)
-        wait_all(w_out, sem)
-        d_context_ref[...] = dot_nt(low, w_out[...]).astype(LOW)
-        g_out = dot_tn(context_ref[...], low).astype(LOW)
-        grads[:, :rows] = g_out.reshape(grid.fsdp, rows, width)
-        g_down = dot_tn(hidden_ref[...], e).astype(LOW)
-        grads[:, rows:] = g_down.reshape(grid.fsdp, down_rows, width)
-
-    vmem = pl.BlockSpec(memory_space=pltpu.VMEM)
-    return pl.pallas_call(
-        body,
-        out_shape=[
-            jax.ShapeDtypeStruct((length, width), WIDE),
-            jax.ShapeDtypeStruct((length, width), LOW),
-            jax.ShapeDtypeStruct((8, width), WIDE),
-            jax.ShapeDtypeStruct((grid.fsdp, rows + down_rows, width), LOW),
-        ],
-        in_specs=[pl.BlockSpec(memory_space=pltpu.SMEM)] + [vmem] * 6 + second.specs,
-        out_specs=[vmem] * 4,
-        scratch_shapes=[pltpu.VMEM((width, width), LOW), pltpu.SemaphoreType.DMA],
-        compiler_params=params(),
-        cost_estimate=cost(10),
-        name="feed_forward_back",
-    )(counts, context, cotangent, gains, attended, d_normed, hidden, *second.arrays)
+    return results[:4], results[4 : 4 + n_refs], results[4 + n_refs :]
 
 
 def project_back(grid, source, image, normed, d_qkv, d_attended, gains, d_gain_two):
@@ -593,11 +574,60 @@
             pltpu.VMEM((3, width, width), LOW),
             pltpu.SemaphoreType.DMA((3,)),
         ],
-        compiler_params=params(),
+        compiler_params=params(12),
         cost_estimate=cost(11),
         name="project_back",
     )(image, normed, d_attended, gains, d_gain_two, *d_qkv, *source.arrays)
     return results[0], results[1:]
+
+
+def fold_column(reduce):
+    grid = reduce.grid
+    rows, columns = reduce.keep.shape[2:]
+    half = grid.nz // 2
+
+    def level(i):
+        return jnp.where(i < half, 2 * i + 1, 2 * (i - half))
+
+    def body(place_ref, keep_ref, got_ref, *refs):
+        sides, (leave_ref, rest_ref) = refs[:-2], refs[-2:]
+        total = keep_ref[0, 0].astype(WIDE) + got_ref[0, 0].astype(WIDE)
+        for ref in sides:
+            total = total + ref[0].astype(WIDE)
+        total = total.astype(LOW)
+
+        @pl.when(pl.program_id(0) < half)
+        def _():
+            leave_ref[0] = total
+
+        @pl.when(pl.program_id(0) >= half)
+        def _():
+            rest_ref[0] = total
+
+    def own(i, place):
+        return place[0], (place[1] ^ level(i)) * 2 + place[2], 0, 0
+
+    block = (1, rows, columns)
+    whole = pl.BlockSpec((1,) + block, own)
+    side = pl.BlockSpec(block, lambda i, place: (place[1] ^ level(i), 0, 0))
+    shape = jax.ShapeDtypeStruct((half, rows, columns), LOW)
+    x, z, y, _ = grid.place()
+    return pl.pallas_call(
+        body,
+        grid_spec=pltpu.PrefetchScalarGridSpec(
+            num_scalar_prefetch=1,
+            grid=(grid.nz,),
+            in_specs=[whole, whole] + [side] * len(reduce.sides),
+            out_specs=[
+                pl.BlockSpec(block, lambda i, place: (jnp.minimum(i, half - 1), 0, 0)),
+                pl.BlockSpec(block, lambda i, place: (jnp.maximum(i - half, 0), 0, 0)),
+            ],
+        ),
+        out_shape=[shape, shape],
+        compiler_params=params(16, ("arbitrary",)),
+        cost_estimate=cost(6e7),
+        name="fold_column",
+    )(jnp.stack([x, z, y]).astype(jnp.int32), reduce.keep, reduce.got, *reduce.sides)
 
 
 def adamw(param, first, second, grad, rate, decay):
@@ -607,16 +637,53 @@
     return (param - rate * (update + decay * param), first, second)
 
 
-def update(grad_norm, weights, firsts, seconds, first, second, third, own_gains):
+def finish(grid, own, arrive, squared, slab_rows):
+    rows, columns = own.shape
+    per_shard = 2 * columns // grid.fsdp
+
+    def body(*refs):
+        squared_ref, total_ref, sum_ref = refs[0], refs[-2], refs[-1]
+        total = refs[1][...].astype(WIDE)
+        for ref in refs[2:-2]:
+            total = total + ref[...].astype(WIDE)
+        total = total.astype(LOW)
+        total_ref[...] = total
+        column = lax.broadcasted_iota(jnp.int32, (rows, columns), 1) + lax.axis_index("dp") * columns
+        row = lax.broadcasted_iota(jnp.int32, (rows, columns), 0)
+        first = lax.axis_index("fsdp") * per_shard
+        mine = jnp.logical_and(column >= first, column < first + per_shard)
+        counted = jnp.where(jnp.logical_or(row < rows - slab_rows, mine), total.astype(WIDE), 0.0)
+        sum_ref[0] = squared_ref[0] + jnp.sum(counted * counted)
+
+    vmem, smem = (pl.BlockSpec(memory_space=m) for m in (pltpu.VMEM, pltpu.SMEM))
+    return pl.pallas_call(
+        body,
+        out_shape=[jax.ShapeDtypeStruct((rows, columns), LOW), jax.ShapeDtypeStruct((1,), WIDE)],
+        in_specs=[smem] + [vmem] * (1 + len(arrive)),
+        out_specs=[vmem, smem],
+        compiler_params=params(8),
+        cost_estimate=cost(1),
+        name="finish",
+    )(squared.reshape(1), own, *arrive)
+
+
+def update(grid, grad_norm, x, weights, firsts, seconds, grads):
     rows = weights[0].shape[1]
+    per_half = grid.fsdp // 2
+    columns = weights[0].shape[2] // 2
     rates = (MATRIX_RATE, MATRIX_RATE, MATRIX_RATE, GAIN_RATE)
     decays = (MATRIX_DECAY, MATRIX_DECAY, MATRIX_DECAY, 0.0)
 
     def body(*refs):
-        norm_ref, first_ref, second_ref, third_ref, gains_ref = refs[:5]
-        weight_refs, first_refs, second_refs = refs[5:9], refs[9:13], refs[13:17]
-        outs = refs[17:]
+        norm_ref, x_ref = refs[:2]
+        weight_refs, first_refs, second_refs = refs[8:12], refs[12:16], refs[16:20]
+        outs = refs[20:]
+        half = pl.program_id(0)
         factor = jnp.minimum(1.0, CLIP_AT / (norm_ref[0] + 1e-06))
+        group_one, group_two, group_three = (
+            jnp.where(x_ref[0] == half, mine[...], other[...])
+            for mine, other in zip(refs[2:8:2], refs[3:8:2])
+        )
 
         def one(n, index, grad):
             taken = [r[n][index] for r in (weight_refs, first_refs, second_refs)]
@@ -625,33 +692,41 @@
                 outs[4 * k + n][index] = value
 
         for j in range(3):
-            one(0, j, first_ref[0, j * rows : (j + 1) * rows])
-        one(0, 3, second_ref[:rows])
+            one(0, j, group_one[j * rows : (j + 1) * rows])
+        one(0, 3, group_two[:rows])
         for j in range(2):
-            one(1, j, third_ref[0, j * rows : (j + 1) * rows])
-        one(2, slice(None), second_ref[rows:])
-        one(3, slice(None), gains_ref[...])
+            one(1, j, group_three[j * rows : (j + 1) * rows])
+        one(2, slice(None), group_two[rows:])
+        shard = lax.axis_index("fsdp")
+
+        @pl.when(shard // per_half == half)
+        def _():
+            shape = (columns, rows)
+            place = lax.broadcasted_iota(jnp.int32, shape, 0) - lax.rem(shard, per_half) * rows
+            pick = (place == lax.broadcasted_iota(jnp.int32, shape, 1)).astype(WIDE).astype(LOW)
+            one(3, slice(None), dot(group_one[3 * rows :], pick)[:2])
 
     def halves(shape):
         block = shape[:-1] + (shape[-1] // 2,)
         return pl.BlockSpec(block, lambda i: (0,) * (len(shape) - 1) + (i,))
 
-    whole = pl.BlockSpec(own_gains.shape, lambda i: (0, 0))
-    own = [halves(w.shape) for w in weights[:3]] + [whole]
-    outer = [pl.BlockSpec((1,) + v.shape[1:], lambda i: (i, 0, 0)) for v in (first, third)]
-    results = pl.pallas_call(
+    smem, vmem = (pl.BlockSpec(memory_space=m) for m in (pltpu.SMEM, pltpu.VMEM))
+    own = [halves(w.shape) for w in weights[:3]]
+    own.append(pl.BlockSpec(weights[3].shape, lambda i: (0, 0)))
+    return pl.pallas_call(
         body,
         grid=(2,),
         out_shape=[jax.ShapeDtypeStruct(w.shape, WIDE) for w in weights] * 3,
-        in_specs=[pl.BlockSpec(memory_space=pltpu.SMEM), outer[0], halves(second.shape), outer[1]]
-        + [whole]
-        + own * 3,
+        in_specs=[smem, smem] + [vmem] * 6 + own * 3,
         out_specs=own * 3,
-        compiler_params=params(("arbitrary",)),
+        compiler_params=params(56, ("arbitrary",)),
         cost_estimate=cost(4),
         name="update",
-    )(grad_norm.reshape(1), first, second, third, own_gains, *weights, *firsts, *seconds)
-    return results
+    )(grad_norm.reshape(1), x.reshape(1), *(v for g in grads for v in g), *weights, *firsts, *seconds)
+
+
+def squares(v):
+    return jnp.sum(jnp.square(v.astype(WIDE)))
 
 
 def on_device(
@@ -710,59 +785,75 @@
         one.finish()
         first = Source(grid, one.pieces)
         normed, qkv, full_gains = project_in(grid, first, image, jnp.zeros((SLAB, width), WIDE))
-        qkv, two.side, two.across = lax.optimization_barrier((qkv, two.side, two.across))
+        context = attend(qkv, counts)
+        context, two.side, two.across = lax.optimization_barrier((context, two.side, two.across))
         two.send_corners()
-        context = attend(qkv, counts)
-        context, two.low, two.high = lax.optimization_barrier((context, two.low, two.high))
         two.finish()
         second = Source(grid, two.pieces)
         second.down_rows = down_rows
 
-        (output, attended, d_normed, hidden), in_grads = feed_forward(
+        (output, d_attended, d_context, d_gain_two), out_grads, in_grads = feed_forward(
             grid, second, third, image, context, e, counts, full_gains
         )
         three = Reduce(grid, *in_grads)
         three.send_core()
-        d_attended, d_context, d_gain_two, out_grads = feed_forward_back(
-            grid, second, context, e, counts, full_gains, attended, d_normed, hidden
-        )
-        out_total = lax.psum_scatter(out_grads, "fsdp", scatter_dimension=0)
-        three.got, d_context = after(three.got, d_context)
-        corners, d_context = after(three.load_corners(), d_context)
-        three.send_corners(corners)
-        low = pairs // 2
-        d_qkv = [attend_back(qkv, d_context, counts, 0, low)]
-        d_qkv, three.in_x, three.in_y = lax.optimization_barrier((d_qkv, three.in_x, three.in_y))
-        sides, d_context = after(three.load_sides(), d_context)
+        two_keep, two_sent = out_grads
+        two_got = grid.flip_core(two_sent)
+        cut = pairs // 3
+        d_qkv = [attend_back(qkv, d_context, counts, 0, cut)]
+        three.got, d_qkv = after(three.got, d_qkv)
+        sides = three.load_sides()
         three.send_sides(sides)
-        d_qkv.append(attend_back(qkv, d_context, counts, low, pairs - low))
+        _, (two_got, d_context) = after(sides, (two_got, d_context))
+        shape = (2, grid.nz, 2) + two_keep.shape[2:]
+        two = Fold(grid, [two_keep.reshape(shape), two_got.reshape(shape)])
+        bits = two.by_bits(1)
+        x, z, y, c = grid.place()
+        leave, d_context = after(two.leave(bits, lax.rem(z, 2)), d_context)
+        arrived = grid.swap_z(leave, 1)
+        d_qkv.append(attend_back(qkv, d_context, counts, cut, pairs - cut))
         input_grad, grads = project_back(
             grid, first, image, normed, d_qkv, d_attended, full_gains, d_gain_two
         )
+        for bit in range(1, bits):
+            grads, arrived = after(grads, arrived)
+            two.parts.append(arrived)
+            leave, three.sides = after(two.leave(bits - bit, lax.rem(z >> bit, 2)), three.sides)
+            arrived = grid.swap_z(leave, 1 << bit)
         one = Reduce(grid, *grads)
-        three.sides, one.sent = after(three.sides, one.sent)
         one.send_core()
-        three.load_levels()
-        three.leave, one.got = after(three.leave, one.got)
-        three.send_levels()
-        one.send_sides(one.load_sides())
-        one.sides, three.arrive, out_total = lax.optimization_barrier(
-            (one.sides, three.arrive, out_total)
-        )
+        leave, rest = fold_column(three)
+        in_three = grid.swap_z(leave, 1)
+        leave, one.got = after(leave, one.got)
+        sides = one.load_sides()
+        one.send_sides(sides)
+        _, (arrived, in_three) = after(sides, (arrived, in_three))
+        two.parts.append(arrived)
+        arrived = grid.flip_y(two.leave(1, y))
+        three = Fold(grid, [rest, in_three])
+        bits = three.by_bits(0)
+        for bit in range(1, bits + 1):
+            in_three = grid.swap_z(three.leave(bits - bit, 0), 1 << bit)
+            three.parts.append(in_three)
         one.load_levels()
         one.send_levels()
-        three.load_total()
-        three.send_total()
-        out_other = grid.flip_x(out_total)
-        one.load_total()
+        _, arrived = after(one.leave, arrived)
+        two.parts.append(arrived)
+        leave = two.leave(0, x)
+        arrived = grid.flip_x(leave)
+        two.parts.append(arrived)
+        _, in_three = after(leave, in_three)
+        three.parts[-1] = in_three
+        three.total = three.total()
+        three.other = grid.flip_x(three.total)
+        two.total = two.total()
+        two.other = grid.flip_x(two.total)
+        squared = squares(three.total) + squares(two.total)
+        squared, one.arrive = after(squared, one.arrive)
+        one.total, squared = finish(grid, one.own, one.arrive, squared, SLAB)
         one.send_total()
-        second = (out_total.astype(WIDE) + out_other.astype(WIDE)).astype(LOW)
-        first, third = (
-            jnp.stack([jnp.where(x == 0, g.total, g.other), jnp.where(x == 0, g.other, g.total)])
-            for g in (one, three)
-        )
-        mine = lax.dynamic_slice_in_dim(owned, x * (width // 2), width // 2, 1)
-        counted = (one.total, three.total)
+        grad_norm = jnp.sqrt(total_of(grid, squared[0]))
+        reduced = [(g.total, g.other) for g in (one, two, three)]
     else:
         groups = [lax.all_gather(g, "fsdp", axis=1) for g in groups]
 
@@ -780,44 +871,33 @@
             grid, first, image, jnp.concatenate([slabs[0], slabs[1]], -1)
         )
         context = attend(qkv, counts)
-        (output, attended, d_normed, hidden), in_grads = feed_forward(
+        (output, d_attended, d_context, d_gain_two), out_grads, in_grads = feed_forward(
             grid, second, third, image, context, e, counts, full_gains
-        )
-        d_attended, d_context, d_gain_two, out_grads = feed_forward_back(
-            grid, second, context, e, counts, full_gains, attended, d_normed, hidden
         )
         d_qkv = [attend_back(qkv, d_context, counts, 0, pairs)]
         input_grad, grads = project_back(
             grid, first, image, normed, d_qkv, d_attended, full_gains, d_gain_two
         )
 
-        def reduce_whole(g, dim):
-            total = lax.psum_scatter(g.astype(WIDE), "fsdp", scatter_dimension=dim)
-            return lax.psum(total.astype(LOW), "dp")
-
-        first, third = reduce_whole(grads[0], 1), reduce_whole(in_grads[0], 1)
-        second = reduce_whole(out_grads, 0)
+        reduced = []
+        for (g,) in (grads, out_grads, in_grads):
+            total = lax.psum_scatter(g.astype(WIDE), "fsdp", scatter_dimension=1)
+            reduced.append(lax.psum(total.astype(LOW), "dp"))
+        x = jnp.int32(0)
         mine = owned.reshape(2, 1, width // 2)
-        counted = (first, third)
-
-    def squares(v):
-        return jnp.sum(jnp.square(v.astype(WIDE)))
-
-    squared = squares(counted[0][..., : 3 * rows, :]) + squares(counted[1])
-    squared = squared + squares(jnp.where(mine, counted[0][..., 3 * rows :, :], jnp.zeros((), LOW)))
-    squared = squared + squares(second) * (0.5 if grid.cube else 1.0)
-    grad_norm = jnp.sqrt(total_of(grid, squared))
-    own_gains = jnp.concatenate([first[0, 3 * rows : 3 * rows + 2], first[1, 3 * rows : 3 * rows + 2]], -1)
-    own_gains = lax.dynamic_slice_in_dim(own_gains, shard * rows, rows, 1)
+        slabs = jnp.where(mine, reduced[0][:, 3 * rows :], jnp.zeros((), LOW))
+        squared = squares(reduced[0][:, : 3 * rows]) + squares(slabs)
+        squared = squared + squares(reduced[1]) + squares(reduced[2])
+        grad_norm = jnp.sqrt(total_of(grid, squared))
+
     updated = update(
+        grid,
         grad_norm,
+        x,
         (w_attn, w_in, w_down, gains),
         (m_attn, m_in, m_down, m_gains),
         (v_attn, v_in, v_down, v_gains),
-        first,
-        second,
-        third,
-        own_gains,
+        reduced,
     )
     return (output[None], input_grad[None], grad_norm, *updated)
 

time: 286 us -> 277 us (0.969)
  Pallas kernels: 84.9 us -> 74.8 us
  waiting for transfers between devices: 95.1 us -> 89.4 us
  local copies, waits for them, and re-layouts: 7.54 us -> 11.5 us
    reduce_scatter x1 -> x0, waiting for transfers between devices: 19.8 us -> none  [on_device(): out_total = lax.psum_scatter(out_grads, 'fsdp', scatter_dimension=0)]
    convert_element_type x2 -> x7, other arithmetic: 2.73 us -> 13.9 us  [the longest x5 7.41 us: leave(): return leave.astype(LOW)]
    ppermute x11, waiting for transfers between devices: 6.3 us -> 12.6 us  [flip_x(): lax.ppermute(v, EVERY, self.move(lambda x, z, y, c: (1 - x, z, y, c)))]
    ppermute x14 -> x15, waiting for transfers between devices: 37.7 us -> 43.4 us  [swap_z(): lax.ppermute(v, EVERY, self.move(lambda x, z, y, c: (x, z ^ bit, y, c)))]
    pallas_call x1 -> x2, Pallas kernels: 9.87 us -> 4.49 us  [the longest x1 3.7 us: fold_column(): pl.pallas_call(body, grid_spec=pltpu.PrefetchScalarGridSpec(num_scalar_pr...]
    unnamed x41 -> x83, local copies, waits for them, and re-layouts: 5.56 us -> 9.85 us
    pallas_call x1, Pallas kernels: 24.2 us -> 28.2 us  [feed_forward(): pl.pallas_call(body, grid=(steps,), out_shape=[jax.ShapeDtypeStruct((leng...]
    another operation x5 -> x1, other arithmetic: 3.15 us -> 0.08 us  [fold_column(): jnp.stack([x, z, y]).astype(jnp.int32)]
  transfers between devices with their start and end apart: 43 -> 45, of which waited for: 21 -> 22; matrix products, arithmetic and copies ran while one was open for 6% -> 7% of each run, Pallas kernels for 19% -> 14%
where the time goes in v4:
time: 277 us; the launch traced here: 276 us
  waiting for transfers between devices  89.4 us (32%)
  Pallas kernels  74.8 us (27%)
  starting transfers between devices  56.6 us (20%)
  between operations  22.1 us (8%)
  other arithmetic  21.5 us (8%)
  local copies, waits for them, and re-layouts  11.5 us (4%)
    ppermute x15, waiting for transfers between devices, swap_z(): lax.ppermute(v, EVERY, self.move(lambda x, z, y, c: (x, z ^ bit, y, c)))  43.4 us
    ppermute x15, starting transfers between devices, swap_z(): lax.ppermute(v, EVERY, self.move(lambda x, z, y, c: (x, z ^ bit, y, c)))  29.4 us
    pallas_call x1, Pallas kernels, feed_forward(): pl.pallas_call(body, grid=(steps,), out_shape=[jax.ShapeDtypeStruct((leng...  28.2 us
    ppermute x8, waiting for transfers between devices, flip_y(): lax.ppermute(v, EVERY, self.move(lambda x, z, y, c: (x, z, 1 - y, c)))  25.8 us
    pallas_call x2, Pallas kernels, attend_back(): pl.pallas_call(body, grid=(width // pair,), out_shape=jax.ShapeDtypeStruc...  15.4 us
    ppermute x11, starting transfers between devices, flip_x(): lax.ppermute(v, EVERY, self.move(lambda x, z, y, c: (1 - x, z, y, c)))  13 us
    ppermute x11, waiting for transfers between devices, flip_x(): lax.ppermute(v, EVERY, self.move(lambda x, z, y, c: (1 - x, z, y, c)))  12.6 us
    ppermute x8, starting transfers between devices, flip_y(): lax.ppermute(v, EVERY, self.move(lambda x, z, y, c: (x, z, 1 - y, c)))  11.1 us
  transfers between devices with their start and end apart: 45, of which 22 were waited for; matrix products, arithmetic and copies ran while one was open for 7% of the time, Pallas kernels for 14%

profile of v4, /device:TPU:0, one launch (start us, length us, event | category | flops | bytes accessed | tf_op | source)
XLA Modules:
  0.0 275.9 jit_solution(17986810794394352944)
XLA Ops:
  9.6 3.1 %collective-permute-start = (bf16[160,384]{1,0:T(8,128)(2,1)S(1)}, bf16[160,384]{1,0:T(8,128)(2,1)S(1)}, u32[]{:S(2)}, u32[]{:S(2)}) collective-permute-start(bf16[160,384]{1,0:T(8,128)(2,1)S(1)} %bitcast.170), channel_id=1, source_target_pairs={{0,4},{1,5},{2,6},{3,7},{4,0},{5,1},{6,2},{7,3},{8,12},{9,13},{10,... | collective-permute-start | bytes 368648 | tf_op jit(solution)/shard_map/ppermute | solution.py:63
  12.7 2.6 collective-permute-start.1
  17.4 7.7 %collective-permute-done.1 = bf16[160,384]{1,0:T(8,128)(2,1)S(1)} collective-permute-done((bf16[160,384]{1,0:T(8,128)(2,1)S(1)}, bf16[160,384]{1,0:T(8,128)(2,1)S(1)}, u32[]{:S(2)}, u32[]{:S(2)}) %collective-permute-start.1) | collective-permute-done | bytes 122912 | tf_op jit(solution)/shard_map/ppermute | solution.py:63
  28.2 7.2 %collective-permute-start.5 = (bf16[176,384]{1,0:T(8,128)(2,1)S(1)}, bf16[176,384]{1,0:T(8,128)(2,1)S(1)}, u32[]{:S(2)}, u32[]{:S(2)}) collective-permute-start(bf16[176,384]{1,0:T(8,128)(2,1)S(1)} %fusion.18), channel_id=1, source_target_pairs={{0,4},{1,5},{2,6},{3,7},{4,0},{5,1},{6,2},{7,3},{8,12},{9,13},{10,... | collective-permute-start | bytes 405512 | tf_op jit(solution)/shard_map/ppermute | solution.py:63
  35.4 3.3 %collective-permute-start.6 = (bf16[176,384]{1,0:T(8,128)(2,1)S(1)}, bf16[176,384]{1,0:T(8,128)(2,1)S(1)}, u32[]{:S(2)}, u32[]{:S(2)}) collective-permute-start(bf16[176,384]{1,0:T(8,128)(2,1)S(1)} %fusion.18), channel_id=1, source_target_pairs={{0,8},{1,9},{2,10},{3,11},{4,12},{5,13},{6,14},{7,15},{8,0},{9,1},... | collective-permute-start | bytes 405512 | tf_op jit(solution)/shard_map/ppermute | solution.py:63
  40.2 3.3 %collective-permute-done.5 = bf16[176,384]{1,0:T(8,128)(2,1)S(1)} collective-permute-done((bf16[176,384]{1,0:T(8,128)(2,1)S(1)}, bf16[176,384]{1,0:T(8,128)(2,1)S(1)}, u32[]{:S(2)}, u32[]{:S(2)}) %collective-permute-start.5) | collective-permute-done | bytes 135200 | tf_op jit(solution)/shard_map/ppermute | solution.py:63
  43.6 5.6 %collective-permute-done.6 = bf16[176,384]{1,0:T(8,128)(2,1)S(1)} collective-permute-done((bf16[176,384]{1,0:T(8,128)(2,1)S(1)}, bf16[176,384]{1,0:T(8,128)(2,1)S(1)}, u32[]{:S(2)}, u32[]{:S(2)}) %collective-permute-start.6) | collective-permute-done | bytes 135200 | tf_op jit(solution)/shard_map/ppermute | solution.py:63
  54.5 4.5 %collective-permute-done.8 = bf16[2,160,384]{2,1,0:T(8,128)(2,1)S(1)} collective-permute-done((bf16[2,160,384]{2,1,0:T(8,128)(2,1)S(1)}, bf16[2,160,384]{2,1,0:T(8,128)(2,1)S(1)}, u32[]{:S(2)}, u32[]{:S(2)}) %collective-permute-start.8) | collective-permute-done | bytes 245792 | tf_op jit(solution)/shard_map/ppermute | solution.py:51
  59.0 6.5 %collective-permute-done.9 = bf16[2,160,384]{2,1,0:T(8,128)(2,1)S(1)} collective-permute-done((bf16[2,160,384]{2,1,0:T(8,128)(2,1)S(1)}, bf16[2,160,384]{2,1,0:T(8,128)(2,1)S(1)}, u32[]{:S(2)}, u32[]{:S(2)}) %collective-permute-start.9) | collective-permute-done | bytes 245792 | tf_op jit(solution)/shard_map/ppermute | solution.py:54
  67.5 4.8 %project_in.1 = (bf16[512,768]{1,0:T(8,128)(2,1)S(1)}, bf16[3,512,768]{2,1,0:T(8,128)(2,1)S(1)}, f32[16,768]{1,0:T(8,128)S(1)}) custom-call(bf16[512,768]{1,0:T(8,128)(2,1)S(1)} %bitcast.151, f32[16,768]{1,0:T(8,128)S(1)} %broadcast_in_dim.21.refs_1_, bf16[12,160,384]{2,1,0:T(8,128)(2,1)S(1)} %constant_dynamic-update-slice_fusion.refs_2_.refs_7_, ...), custom_call_target="tpu_custom_call" | custom-call | flops 8000000 | tf_op jit(solution)/shard_map/project_in/pallas_call | solution.py:309
  72.4 7.3 %attend.1.refs_2_ = bf16[512,768]{1,0:T(8,128)(2,1)S(1)} custom-call(s32[1]{0:T(128)S(6)} %copy.105.counts_ref.refs_0_, bf16[3,512,768]{2,1,0:T(8,128)(2,1)S(1)} %get-tuple-element.85.qkv_ref), custom_call_target="tpu_custom_call" | custom-call | flops 9000000 | tf_op jit(solution)/shard_map/attend/pallas_call | solution.py:347
  80.6 7.4 %collective-permute-done.13 = bf16[4,176,384]{2,1,0:T(8,128)(2,1)S(1)} collective-permute-done((bf16[4,176,384]{2,1,0:T(8,128)(2,1)S(1)}, bf16[4,176,384]{2,1,0:T(8,128)(2,1)S(1)}, u32[]{:S(2)}, u32[]{:S(2)}) %collective-permute-start.13) | collective-permute-done | bytes 540704 | tf_op jit(solution)/shard_map/ppermute | solution.py:54
  89.5 2.1 collective-permute-start.15
  91.6 6.7 %collective-permute-done.14 = bf16[2,176,384]{2,1,0:T(8,128)(2,1)S(1)} collective-permute-done((bf16[2,176,384]{2,1,0:T(8,128)(2,1)S(1)}, bf16[2,176,384]{2,1,0:T(8,128)(2,1)S(1)}, u32[]{:S(2)}, u32[]{:S(2)}) %collective-permute-start.14) | collective-permute-done | bytes 270368 | tf_op jit(solution)/shard_map/ppermute | solution.py:51
  98.6 2.0 collective-permute-done.17.refs_8_
  102.1 28.2 %feed_forward.1 = (bf16[512,768]{1,0:T(8,128)(2,1)}, f32[512,768]{1,0:T(8,128)}, bf16[512,768]{1,0:T(8,128)(2,1)}, f32[8,768]{1,0:T(8,128)}, bf16[2,8,176,384]{3...) custom-call(s32[1]{0:T(128)S(6)} %copy.105.counts_ref.refs_0_, ...), custom_call_target="tpu_custom_call" | custom-call | flops 28000000 | tf_op jit(solution)/shard_map/feed_forward/pallas_call | solution.py:499
  132.0 5.1 %attend_back.2.refs_5_ = bf16[3,512,256]{2,1,0:T(8,128)(2,1)S(1)} custom-call(s32[1]{0:T(128)S(6)} %copy.105.counts_ref.refs_0_, bf16[3,512,768]{2,1,0:T(8,128)(2,1)S(1)} %get-tuple-element.85.qkv_ref, bf16[512,768]{1,0:T(8,128)(2,1)S(1)} %copy-done.6), custom_call_target="tpu_custom_call" | custom-call | flops 6600000 | tf_op jit(solution)/shard_map/attend_back/pallas_call | solution.py:385
  138.0 3.9 %fusion.5 = (bf16[4,96,1024]{2,1,0:T(8,128)(2,1)}, bf16[4,96,1024]{2,1,0:T(8,128)(2,1)}, bf16[4,96,1024]{2,1,0:T(8,128)(2,1)}) fusion(bf16[2,4,2,96,1024]{4,3,2,1,0:T(8,128)(2,1)} %bitcast.23, s32[]{:T(128)S(6)} %select_n.149, s32[]{:T(128)S(6)} %select_n.155, bf16[2,4,2,96,1024]{4,3,2,1,0:T(8,128)(2,1)S(1)} %bitcast.155, s32[]{:T(128)S(6)} %select_n.153, ...), kind=kLoop, calls=%fused_computation.14 | loop fusion | flops 4718592 | bytes 7077904 | tf_op jit(solution)/shard_map/convert_element_type | solution.py:129
  149.4 10.3 %attend_back.3.refs_6_ = bf16[3,512,512]{2,1,0:T(8,128)(2,1)S(1)} custom-call(s32[1]{0:T(128)S(6)} %copy.105.counts_ref.refs_0_, bf16[3,512,768]{2,1,0:T(8,128)(2,1)S(1)} %get-tuple-element.85.qkv_ref, bf16[512,768]{1,0:T(8,128)(2,1)S(1)} %copy-done.7), custom_call_target="tpu_custom_call" | custom-call | flops 11200000 | tf_op jit(solution)/shard_map/attend_back/pallas_call | solution.py:385
  164.4 8.0 %project_back.1 = (bf16[512,768]{1,0:T(8,128)(2,1)}, bf16[2,8,160,384]{3,2,1,0:T(8,128)(2,1)S(1)}, bf16[2,8,160,384]{3,2,1,0:T(8,128)(2,1)}) custom-call(bf16[512,768]{1,0:T(8,128)(2,1)S(1)} %bitcast.152, bf16[512,768]{1,0:T(8,128)(2,1)S(1)} %copy-done.19, f32[512,768]{1,0:T(8,128)S(1)} %copy-done.17, f32[16,768]{1,0:T(8,128)S(1)} %copy-done.21, ...), custom_call_target="tpu_custom_call" | custom-call | flops 11000000 | tf_op jit(solution)/shard_map/project_back/pallas_call | solution.py:568
  172.5 2.4 fusion.1
  174.9 8.8 %collective-permute-done.22.refs_1_ = bf16[4,96,1024]{2,1,0:T(8,128)(2,1)} collective-permute-done((bf16[4,96,1024]{2,1,0:T(8,128)(2,1)}, bf16[4,96,1024]{2,1,0:T(8,128)(2,1)}, u32[]{:S(2)}, u32[]{:S(2)}) %collective-permute-start.22) | collective-permute-done | bytes 786464 | tf_op jit(solution)/shard_map/ppermute | solution.py:54
  185.0 3.7 %fold_column.1 = (bf16[2,96,1024]{2,1,0:T(8,128)(2,1)S(1)}, bf16[2,96,1024]{2,1,0:T(8,128)(2,1)S(1)}) custom-call(s32[3]{0:T(128)S(1)} %pad_add_fusion.place_ref, bf16[2,8,96,1024]{3,2,1,0:T(8,128)(2,1)S(1)} %copy-done.16, bf16[2,8,96,1024]{3,2,1,0:T(8,128)(2,1)} %collective-permute-done.18.got_ref, bf16[4,96,1024]{2,1,0:T(8,128)(2,1)} %collective-permute-done.21.refs_0_, ...), custom_call_target="tpu_custom_call" | custom-call | flops 60000001064960 | tf_op jit(solution)/shard_map/fold_column/pallas_call | solution.py:615
  190.5 2.6 fusion.7
  196.6 15.0 %collective-permute-done.26 = bf16[2,96,1024]{2,1,0:T(8,128)(2,1)} collective-permute-done((bf16[2,96,1024]{2,1,0:T(8,128)(2,1)S(1)}, bf16[2,96,1024]{2,1,0:T(8,128)(2,1)}, u32[]{:S(2)}, u32[]{:S(2)}) %collective-permute-start.26) | collective-permute-done | bytes 393248 | tf_op jit(solution)/shard_map/ppermute | solution.py:63
  221.2 2.4 collective-permute-start.35
  226.3 4.8 %collective-permute-done.31 = bf16[96,1024]{1,0:T(8,128)(2,1)S(1)} collective-permute-done((bf16[96,1024]{1,0:T(8,128)(2,1)S(1)}, bf16[96,1024]{1,0:T(8,128)(2,1)S(1)}, u32[]{:S(2)}, u32[]{:S(2)}) %collective-permute-start.31) | collective-permute-done | bytes 196640 | tf_op jit(solution)/shard_map/ppermute | solution.py:63
  242.6 2.2 collective-permute-start.37
  246.8 2.0 collective-permute-start.38
  252.5 2.2 collective-permute-done.39
  256.9 3.0 %collective-permute-done.40 = f32[]{:T(128)} collective-permute-done((f32[]{:T(128)}, f32[]{:T(128)}, u32[]{:S(2)}, u32[]{:S(2)}) %collective-permute-start.40) | collective-permute-done | bytes 36 | tf_op jit(solution)/shard_map/ppermute | solution.py:63
  261.3 6.6 %update.1 = (f32[4,48,768]{2,1,0:T(8,128)}, f32[2,48,2048]{2,1,0:T(8,128)}, f32[128,768]{1,0:T(8,128)}, f32[2,48]{1,0:T(2,128)}, f32[4,48,768]{2,1,0:T(8,128)}, ...) custom-call(f32[1]{0:T(128)} %bitcast.60.refs_0_, ...), custom_call_target="tpu_custom_call" | custom-call | flops 4000000 | tf_op jit(solution)/shard_map/update/pallas_call | solution.py:716
  (189 shorter events, 68.6 us)
Async XLA Ops:
  7.2 94.9 %all-gather.2.cloned.1.call-start = ((), (), s32[]{:S(2)}) async-start(), calls=%async_computation | async-start | bytes 6684672 | tf_op jit(solution)/shard_map/all_gather | solution.py:768
  12.7 12.3 %collective-permute-start.1 = (bf16[160,384]{1,0:T(8,128)(2,1)S(1)}, bf16[160,384]{1,0:T(8,128)(2,1)S(1)}, u32[]{:S(2)}, u32[]{:S(2)}) collective-permute-start(bf16[160,384]{1,0:T(8,128)(2,1)S(1)} %bitcast.171), channel_id=1, source_target_pairs={{0,8},{1,9},{2,10},{3,11},{4,12},{5,13},{6,14},{7,15},{8,0},{9,1},... | collective-permute-start | bytes 368648 | tf_op jit(solution)/shard_map/ppermute | solution.py:63
  15.3 9.7 %collective-permute-start.2 = (bf16[160,384]{1,0:T(8,128)(2,1)S(1)}, bf16[160,384]{1,0:T(8,128)(2,1)S(1)}, u32[]{:S(2)}, u32[]{:S(2)}) collective-permute-start(bf16[160,384]{1,0:T(8,128)(2,1)S(1)} %bitcast.172), channel_id=1, source_target_pairs={{0,12},{1,13},{2,14},{3,15},{4,8},{5,9},{6,10},{7,11},{8,4},{9,5},... | collective-permute-start | bytes 368648 | tf_op jit(solution)/shard_map/ppermute | solution.py:63
  25.1 24.0 %collective-permute-start.3 = (bf16[4,160,384]{2,1,0:T(8,128)(2,1)S(1)}, bf16[4,160,384]{2,1,0:T(8,128)(2,1)S(1)}, u32[]{:S(2)}, u32[]{:S(2)}) collective-permute-start(bf16[4,160,384]{2,1,0:T(8,128)(2,1)S(1)} %pad_maximum_fusion.1), channel_id=1, source_target_pairs={{0,16},{1,17},{2,18},{3,19},{4,20},{5,21},{6,22},{7,23},{8,24},{9,... | collective-permute-start | bytes 1474568 | tf_op jit(solution)/shard_map/ppermute | solution.py:51
  26.7 22.5 %collective-permute-start.4 = (bf16[4,160,384]{2,1,0:T(8,128)(2,1)S(1)}, bf16[4,160,384]{2,1,0:T(8,128)(2,1)S(1)}, u32[]{:S(2)}, u32[]{:S(2)}) collective-permute-start(bf16[4,160,384]{2,1,0:T(8,128)(2,1)S(1)} %pad_maximum_fusion.1), channel_id=1, source_target_pairs={{0,2},{1,3},{2,0},{3,1},{4,6},{5,7},{6,4},{7,5},{8,10},{9,11},{10,... | collective-permute-start | bytes 1474568 | tf_op jit(solution)/shard_map/ppermute | solution.py:54
  28.2 15.3 %collective-permute-start.5 = (bf16[176,384]{1,0:T(8,128)(2,1)S(1)}, bf16[176,384]{1,0:T(8,128)(2,1)S(1)}, u32[]{:S(2)}, u32[]{:S(2)}) collective-permute-start(bf16[176,384]{1,0:T(8,128)(2,1)S(1)} %fusion.18), channel_id=1, source_target_pairs={{0,4},{1,5},{2,6},{3,7},{4,0},{5,1},{6,2},{7,3},{8,12},{9,13},{10,... | collective-permute-start | bytes 405512 | tf_op jit(solution)/shard_map/ppermute | solution.py:63
  35.4 13.8 %collective-permute-start.6 = (bf16[176,384]{1,0:T(8,128)(2,1)S(1)}, bf16[176,384]{1,0:T(8,128)(2,1)S(1)}, u32[]{:S(2)}, u32[]{:S(2)}) collective-permute-start(bf16[176,384]{1,0:T(8,128)(2,1)S(1)} %fusion.18), channel_id=1, source_target_pairs={{0,8},{1,9},{2,10},{3,11},{4,12},{5,13},{6,14},{7,15},{8,0},{9,1},... | collective-permute-start | bytes 405512 | tf_op jit(solution)/shard_map/ppermute | solution.py:63
  38.7 10.4 %collective-permute-start.7 = (bf16[176,384]{1,0:T(8,128)(2,1)S(1)}, bf16[176,384]{1,0:T(8,128)(2,1)S(1)}, u32[]{:S(2)}, u32[]{:S(2)}) collective-permute-start(bf16[176,384]{1,0:T(8,128)(2,1)S(1)} %fusion.18), channel_id=1, source_target_pairs={{0,12},{1,13},{2,14},{3,15},{4,8},{5,9},{6,10},{7,11},{8,4},{9,5},... | collective-permute-start | bytes 405512 | tf_op jit(solution)/shard_map/ppermute | solution.py:63
  49.3 18.2 %collective-permute-start.10 = (bf16[12,160,384]{2,1,0:T(8,128)(2,1)S(1)}, bf16[12,160,384]{2,1,0:T(8,128)(2,1)S(1)}, u32[]{:S(2)}, u32[]{:S(2)}) collective-permute-start(bf16[12,160,384]{2,1,0:T(8,128)(2,1)S(1)} %constant_dynamic-update-slice_fusion.refs_2_.refs_7_), channel_id=1, source_target_pairs={{0,1},{1,0},{2,3},{3,2},{4,5},{5,4},{6,7},{7,6},{8,9},{9,8},{10,11... | collective-permute-start | bytes 4423688 | tf_op jit(solution)/shard_map/ppermute | solution.py:60
  51.7 13.8 %collective-permute-start.9 = (bf16[2,160,384]{2,1,0:T(8,128)(2,1)S(1)}, bf16[2,160,384]{2,1,0:T(8,128)(2,1)S(1)}, u32[]{:S(2)}, u32[]{:S(2)}) collective-permute-start(bf16[2,160,384]{2,1,0:T(8,128)(2,1)S(1)} %slice.33), channel_id=1, source_target_pairs={{0,2},{1,3},{2,0},{3,1},{4,6},{5,7},{6,4},{7,5},{8,10},{9,11},{10,... | collective-permute-start | bytes 737288 | tf_op jit(solution)/shard_map/ppermute | solution.py:54
  53.3 27.3 %collective-permute-start.12 = (bf16[4,176,384]{2,1,0:T(8,128)(2,1)S(1)}, bf16[4,176,384]{2,1,0:T(8,128)(2,1)S(1)}, u32[]{:S(2)}, u32[]{:S(2)}) collective-permute-start(bf16[4,176,384]{2,1,0:T(8,128)(2,1)S(1)} %pad_maximum_fusion), channel_id=1, source_target_pairs={{0,16},{1,17},{2,18},{3,19},{4,20},{5,21},{6,22},{7,23},{8,24},{9,... | collective-permute-start | bytes 1622024 | tf_op jit(solution)/shard_map/ppermute | solution.py:51
  53.9 34.0 %collective-permute-start.13 = (bf16[4,176,384]{2,1,0:T(8,128)(2,1)S(1)}, bf16[4,176,384]{2,1,0:T(8,128)(2,1)S(1)}, u32[]{:S(2)}, u32[]{:S(2)}) collective-permute-start(bf16[4,176,384]{2,1,0:T(8,128)(2,1)S(1)} %pad_maximum_fusion), channel_id=1, source_target_pairs={{0,2},{1,3},{2,0},{3,1},{4,6},{5,7},{6,4},{7,5},{8,10},{9,11},{10,... | collective-permute-start | bytes 1622024 | tf_op jit(solution)/shard_map/ppermute | solution.py:54
  89.3 11.3 %collective-permute-start.16 = (bf16[12,176,384]{2,1,0:T(8,128)(2,1)S(1)}, bf16[12,176,384]{2,1,0:T(8,128)(2,1)}, u32[]{:S(2)}, u32[]{:S(2)}) collective-permute-start(bf16[12,176,384]{2,1,0:T(8,128)(2,1)S(1)} %constant_dynamic-update-slice_fusion.8.refs_5_), channel_id=1, source_target_pairs={{0,1},{1,0},{2,3},{3,2},{4,5},{5,4},{6,7},{7,6},{8,9},{9,8},{10,11... | collective-permute-start | bytes 4866056 | tf_op jit(solution)/shard_map/ppermute | solution.py:60
  130.7 11.2 %collective-permute-start.19 = (bf16[2,8,176,384]{3,2,1,0:T(8,128)(2,1)}, bf16[2,8,176,384]{3,2,1,0:T(8,128)(2,1)}, u32[]{:S(2)}, u32[]{:S(2)}) collective-permute-start(bf16[2,8,176,384]{3,2,1,0:T(8,128)(2,1)} %get-tuple-element.103), channel_id=1, source_target_pairs={{0,1},{1,0},{2,3},{3,2},{4,5},{5,4},{6,7},{7,6},{8,9},{9,8},{10,11... | collective-permute-start | bytes 6488072 | tf_op jit(solution)/shard_map/ppermute | solution.py:60
  144.5 27.9 %collective-permute-start.20 = (bf16[2,2,2,176,384]{4,3,0,2,1:T(8,128)(2,1)}, bf16[2,2,2,176,384]{4,3,0,2,1:T(8,128)(2,1)}, u32[]{:S(2)}, u32[]{:S(2)}) collective-permute-start(bf16[2,2,2,176,384]{4,3,0,2,1:T(8,128)(2,1)} %copy.64), channel_id=1, source_target_pairs={{0,4},{1,5},{2,6},{3,7},{4,0},{5,1},{6,2},{7,3},{8,12},{9,13},{10,... | collective-permute-start | bytes 3244040 | tf_op jit(solution)/shard_map/ppermute | solution.py:63
  145.8 29.1 %collective-permute-start.21 = (bf16[4,96,1024]{2,1,0:T(8,128)(2,1)}, bf16[4,96,1024]{2,1,0:T(8,128)(2,1)}, u32[]{:S(2)}, u32[]{:S(2)}) collective-permute-start(bf16[4,96,1024]{2,1,0:T(8,128)(2,1)} %get-tuple-element.151), channel_id=1, source_target_pairs={{0,16},{1,17},{2,18},{3,19},{4,20},{5,21},{6,22},{7,23},{8,24},{9,... | collective-permute-start | bytes 2359304 | tf_op jit(solution)/shard_map/ppermute | solution.py:51
  147.5 36.2 %collective-permute-start.22 = (bf16[4,96,1024]{2,1,0:T(8,128)(2,1)}, bf16[4,96,1024]{2,1,0:T(8,128)(2,1)}, u32[]{:S(2)}, u32[]{:S(2)}) collective-permute-start(bf16[4,96,1024]{2,1,0:T(8,128)(2,1)} %get-tuple-element.150), channel_id=1, source_target_pairs={{0,2},{1,3},{2,0},{3,1},{4,6},{5,7},{6,4},{7,5},{8,10},{9,11},{10,... | collective-permute-start | bytes 2359304 | tf_op jit(solution)/shard_map/ppermute | solution.py:54
  148.5 35.2 %collective-permute-start.23 = (bf16[4,96,1024]{2,1,0:T(8,128)(2,1)}, bf16[4,96,1024]{2,1,0:T(8,128)(2,1)}, u32[]{:S(2)}, u32[]{:S(2)}) collective-permute-start(bf16[4,96,1024]{2,1,0:T(8,128)(2,1)} %get-tuple-element.149), channel_id=1, source_target_pairs={{0,18},{1,19},{2,16},{3,17},{4,22},{5,23},{6,20},{7,21},{8,26},{9,... | collective-permute-start | bytes 2359304 | tf_op jit(solution)/shard_map/ppermute | solution.py:57
  183.7 27.9 %collective-permute-start.25 = (bf16[2,2,176,384]{3,2,1,0:T(8,128)(2,1)}, bf16[2,2,176,384]{3,2,1,0:T(8,128)(2,1)}, u32[]{:S(2)}, u32[]{:S(2)}) collective-permute-start(bf16[2,2,176,384]{3,2,1,0:T(8,128)(2,1)} %fusion.1), channel_id=1, source_target_pairs={{0,8},{1,9},{2,10},{3,11},{4,12},{5,13},{6,14},{7,15},{8,0},{9,1},... | collective-permute-start | bytes 1622024 | tf_op jit(solution)/shard_map/ppermute | solution.py:63
  188.7 22.9 %collective-permute-start.26 = (bf16[2,96,1024]{2,1,0:T(8,128)(2,1)S(1)}, bf16[2,96,1024]{2,1,0:T(8,128)(2,1)}, u32[]{:S(2)}, u32[]{:S(2)}) collective-permute-start(bf16[2,96,1024]{2,1,0:T(8,128)(2,1)S(1)} %get-tuple-element.117), channel_id=1, source_target_pairs={{0,4},{1,5},{2,6},{3,7},{4,0},{5,1},{6,2},{7,3},{8,12},{9,13},{10,... | collective-permute-start | bytes 1179656 | tf_op jit(solution)/shard_map/ppermute | solution.py:63
  193.1 21.8 %collective-permute-start.27 = (bf16[4,160,384]{2,1,0:T(8,128)(2,1)}, bf16[4,160,384]{2,1,0:T(8,128)(2,1)S(1)}, u32[]{:S(2)}, u32[]{:S(2)}) collective-permute-start(bf16[4,160,384]{2,1,0:T(8,128)(2,1)} %get-tuple-element.152), channel_id=1, source_target_pairs={{0,16},{1,17},{2,18},{3,19},{4,20},{5,21},{6,22},{7,23},{8,24},{9,... | collective-permute-start | bytes 1474568 | tf_op jit(solution)/shard_map/ppermute | solution.py:51
  193.7 22.7 %collective-permute-start.28 = (bf16[4,160,384]{2,1,0:T(8,128)(2,1)}, bf16[4,160,384]{2,1,0:T(8,128)(2,1)}, u32[]{:S(2)}, u32[]{:S(2)}) collective-permute-start(bf16[4,160,384]{2,1,0:T(8,128)(2,1)} %get-tuple-element.154), channel_id=1, source_target_pairs={{0,2},{1,3},{2,0},{3,1},{4,6},{5,7},{6,4},{7,5},{8,10},{9,11},{10,... | collective-permute-start | bytes 1474568 | tf_op jit(solution)/shard_map/ppermute | solution.py:54
  195.2 22.3 %collective-permute-start.29 = (bf16[4,160,384]{2,1,0:T(8,128)(2,1)}, bf16[4,160,384]{2,1,0:T(8,128)(2,1)}, u32[]{:S(2)}, u32[]{:S(2)}) collective-permute-start(bf16[4,160,384]{2,1,0:T(8,128)(2,1)} %get-tuple-element.153), channel_id=1, source_target_pairs={{0,18},{1,19},{2,16},{3,17},{4,22},{5,23},{6,20},{7,21},{8,26},{9,... | collective-permute-start | bytes 1474568 | tf_op jit(solution)/shard_map/ppermute | solution.py:57
  213.0 10.7 %collective-permute-start.30 = (bf16[2,176,384]{2,1,0:T(8,128)(2,1)S(1)}, bf16[2,176,384]{2,1,0:T(8,128)(2,1)S(1)}, u32[]{:S(2)}, u32[]{:S(2)}) collective-permute-start(bf16[2,176,384]{2,1,0:T(8,128)(2,1)S(1)} %fusion.6), channel_id=1, source_target_pairs={{0,2},{1,3},{2,0},{3,1},{4,6},{5,7},{6,4},{7,5},{8,10},{9,11},{10,... | collective-permute-start | bytes 811016 | tf_op jit(solution)/shard_map/ppermute | solution.py:54
  214.9 16.3 %collective-permute-start.31 = (bf16[96,1024]{1,0:T(8,128)(2,1)S(1)}, bf16[96,1024]{1,0:T(8,128)(2,1)S(1)}, u32[]{:S(2)}, u32[]{:S(2)}) collective-permute-start(bf16[96,1024]{1,0:T(8,128)(2,1)S(1)} %fusion.16), channel_id=1, source_target_pairs={{0,8},{1,9},{2,10},{3,11},{4,12},{5,13},{6,14},{7,15},{8,0},{9,1},... | collective-permute-start | bytes 589832 | tf_op jit(solution)/shard_map/ppermute | solution.py:63
  219.2 18.8 %collective-permute-start.33 = (bf16[160,384]{1,0:T(8,128)(2,1)S(1)}, bf16[160,384]{1,0:T(8,128)(2,1)S(1)}, u32[]{:S(2)}, u32[]{:S(2)}) collective-permute-start(bf16[160,384]{1,0:T(8,128)(2,1)S(1)} %get-tuple-element.158), channel_id=1, source_target_pairs={{0,4},{1,5},{2,6},{3,7},{4,0},{5,1},{6,2},{7,3},{8,12},{9,13},{10,... | collective-permute-start | bytes 368648 | tf_op jit(solution)/shard_map/ppermute | solution.py:63
  219.6 18.4 %collective-permute-start.34 = (bf16[160,384]{1,0:T(8,128)(2,1)S(1)}, bf16[160,384]{1,0:T(8,128)(2,1)S(1)}, u32[]{:S(2)}, u32[]{:S(2)}) collective-permute-start(bf16[160,384]{1,0:T(8,128)(2,1)S(1)} %get-tuple-element.157), channel_id=1, source_target_pairs={{0,8},{1,9},{2,10},{3,11},{4,12},{5,13},{6,14},{7,15},{8,0},{9,1},... | collective-permute-start | bytes 368648 | tf_op jit(solution)/shard_map/ppermute | solution.py:63
  221.2 16.7 %collective-permute-start.35 = (bf16[160,384]{1,0:T(8,128)(2,1)S(1)}, bf16[160,384]{1,0:T(8,128)(2,1)S(1)}, u32[]{:S(2)}, u32[]{:S(2)}) collective-permute-start(bf16[160,384]{1,0:T(8,128)(2,1)S(1)} %get-tuple-element.156), channel_id=1, source_target_pairs={{0,12},{1,13},{2,14},{3,15},{4,8},{5,9},{6,10},{7,11},{8,4},{9,5},... | collective-permute-start | bytes 368648 | tf_op jit(solution)/shard_map/ppermute | solution.py:63
  224.8 9.1 %collective-permute-start.32 = (bf16[176,384]{1,0:T(8,128)(2,1)S(1)}, bf16[176,384]{1,0:T(8,128)(2,1)S(1)}, u32[]{:S(2)}, u32[]{:S(2)}) collective-permute-start(bf16[176,384]{1,0:T(8,128)(2,1)S(1)} %fusion.14), channel_id=1, source_target_pairs={{0,16},{1,17},{2,18},{3,19},{4,20},{5,21},{6,22},{7,23},{8,24},{9,... | collective-permute-start | bytes 405512 | tf_op jit(solution)/shard_map/ppermute | solution.py:51
  232.8 27.8 %collective-permute-start.43 = (bf16[96,1024]{1,0:T(8,128)(2,1)S(1)}, bf16[96,1024]{1,0:T(8,128)(2,1)S(1)}, u32[]{:S(2)}, u32[]{:S(2)}) collective-permute-start(bf16[96,1024]{1,0:T(8,128)(2,1)S(1)} %get-tuple-element.146.refs_6_), channel_id=1, source_target_pairs={{0,16},{1,17},{2,18},{3,19},{4,20},{5,21},{6,22},{7,23},{8,24},{9,... | collective-permute-start | bytes 589832 | tf_op jit(solution)/shard_map/ppermute | solution.py:51
  235.8 24.8 %collective-permute-start.42 = (bf16[176,384]{1,0:T(8,128)(2,1)S(1)}, bf16[176,384]{1,0:T(8,128)(2,1)S(1)}, u32[]{:S(2)}, u32[]{:S(2)}) collective-permute-start(bf16[176,384]{1,0:T(8,128)(2,1)S(1)} %get-tuple-element.144.refs_4_), channel_id=1, source_target_pairs={{0,16},{1,17},{2,18},{3,19},{4,20},{5,21},{6,22},{7,23},{8,24},{9,... | collective-permute-start | bytes 405512 | tf_op jit(solution)/shard_map/ppermute | solution.py:51
  238.8 21.8 %collective-permute-start.41 = (bf16[160,384]{1,0:T(8,128)(2,1)S(1)}, bf16[160,384]{1,0:T(8,128)(2,1)S(1)}, u32[]{:S(2)}, u32[]{:S(2)}) collective-permute-start(bf16[160,384]{1,0:T(8,128)(2,1)S(1)} %get-tuple-element.130.refs_2_), channel_id=1, source_target_pairs={{0,16},{1,17},{2,18},{3,19},{4,20},{5,21},{6,22},{7,23},{8,24},{9,... | collective-permute-start | bytes 368648 | tf_op jit(solution)/shard_map/ppermute | solution.py:51
  (49 other events, 335.6 us)
Sparse Core Ops, SparseCore 0:
  10.9 91.1 all-gather.1

commit v5 on v4

--- a/solution.py
+++ b/solution.py
@@ -637,15 +637,13 @@
     return (param - rate * (update + decay * param), first, second)
 
 
-def finish(grid, own, arrive, squared, slab_rows):
+def finish(grid, own, arrive, totals, slab_rows):
     rows, columns = own.shape
     per_shard = 2 * columns // grid.fsdp
 
     def body(*refs):
-        squared_ref, total_ref, sum_ref = refs[0], refs[-2], refs[-1]
-        total = refs[1][...].astype(WIDE)
-        for ref in refs[2:-2]:
-            total = total + ref[...].astype(WIDE)
+        others, refs, (total_ref, sum_ref) = refs[: len(totals)], refs[len(totals) : -2], refs[-2:]
+        total = sum(ref[...].astype(WIDE) for ref in refs)
         total = total.astype(LOW)
         total_ref[...] = total
         column = lax.broadcasted_iota(jnp.int32, (rows, columns), 1) + lax.axis_index("dp") * columns
@@ -653,18 +651,22 @@
         first = lax.axis_index("fsdp") * per_shard
         mine = jnp.logical_and(column >= first, column < first + per_shard)
         counted = jnp.where(jnp.logical_or(row < rows - slab_rows, mine), total.astype(WIDE), 0.0)
-        sum_ref[0] = squared_ref[0] + jnp.sum(counted * counted)
+        squared = jnp.sum(counted * counted)
+        for ref in others:
+            value = ref[...].astype(WIDE)
+            squared = squared + jnp.sum(value * value)
+        sum_ref[0] = squared
 
     vmem, smem = (pl.BlockSpec(memory_space=m) for m in (pltpu.VMEM, pltpu.SMEM))
     return pl.pallas_call(
         body,
         out_shape=[jax.ShapeDtypeStruct((rows, columns), LOW), jax.ShapeDtypeStruct((1,), WIDE)],
-        in_specs=[smem] + [vmem] * (1 + len(arrive)),
+        in_specs=[vmem] * (1 + len(arrive) + len(totals)),
         out_specs=[vmem, smem],
         compiler_params=params(8),
         cost_estimate=cost(1),
         name="finish",
-    )(squared.reshape(1), own, *arrive)
+    )(*totals, own, *arrive)
 
 
 def update(grid, grad_norm, x, weights, firsts, seconds, grads):
@@ -809,15 +811,16 @@
         two = Fold(grid, [two_keep.reshape(shape), two_got.reshape(shape)])
         bits = two.by_bits(1)
         x, z, y, c = grid.place()
-        leave, d_context = after(two.leave(bits, lax.rem(z, 2)), d_context)
-        arrived = grid.swap_z(leave, 1)
+        leave = two.leave(bits, lax.rem(z, 2))
+        leave, d_context = after([leave[0], leave[1]], d_context)
+        arrived = [grid.swap_z(v, 1) for v in leave]
         d_qkv.append(attend_back(qkv, d_context, counts, cut, pairs - cut))
         input_grad, grads = project_back(
             grid, first, image, normed, d_qkv, d_attended, full_gains, d_gain_two
         )
         for bit in range(1, bits):
             grads, arrived = after(grads, arrived)
-            two.parts.append(arrived)
+            two.parts.append(jnp.stack(arrived) if bit == 1 else arrived)
             leave, three.sides = after(two.leave(bits - bit, lax.rem(z >> bit, 2)), three.sides)
             arrived = grid.swap_z(leave, 1 << bit)
         one = Reduce(grid, *grads)
@@ -848,9 +851,8 @@
         three.other = grid.flip_x(three.total)
         two.total = two.total()
         two.other = grid.flip_x(two.total)
-        squared = squares(three.total) + squares(two.total)
-        squared, one.arrive = after(squared, one.arrive)
-        one.total, squared = finish(grid, one.own, one.arrive, squared, SLAB)
+        totals = (three.total, two.total)
+        one.total, squared = finish(grid, one.own, one.arrive, totals, SLAB)
         one.send_total()
         grad_norm = jnp.sqrt(total_of(grid, squared[0]))
         reduced = [(g.total, g.other) for g in (one, two, three)]

time: 277 us -> 269 us (0.971)
  waiting for transfers between devices: 89.4 us -> 82 us
    ppermute x8, waiting for transfers between devices: 25.8 us -> 22 us  [flip_y(): lax.ppermute(v, EVERY, self.move(lambda x, z, y, c: (x, z, 1 - y, c)))]
    reduce_sum x2 -> x0, other arithmetic: 3.47 us -> none  [squares(): return jnp.sum(jnp.square(v.astype(WIDE)))]
    ppermute x15 -> x16, waiting for transfers between devices: 43.4 us -> 41.2 us  [swap_z(): lax.ppermute(v, EVERY, self.move(lambda x, z, y, c: (x, z ^ bit, y, c)))]
    ppermute x15 -> x16, starting transfers between devices: 29.4 us -> 31.1 us  [swap_z(): lax.ppermute(v, EVERY, self.move(lambda x, z, y, c: (x, z ^ bit, y, c)))]
    unnamed x83 -> x81, local copies, waits for them, and re-layouts: 9.85 us -> 10.2 us
  transfers between devices with their start and end apart: 45 -> 46, of which waited for: 22 -> 22; matrix products, arithmetic and copies ran while one was open for 7% -> 8% of each run, Pallas kernels for 14% -> 15%
where the time goes in v5:
time: 269 us
  waiting for transfers between devices  82 us (30%)
  Pallas kernels  74.6 us (28%)
  starting transfers between devices  58.6 us (22%)
  other arithmetic  21.1 us (8%)
  between operations  20.4 us (8%)
  local copies, waits for them, and re-layouts  11.8 us (4%)
    ppermute x16, waiting for transfers between devices, swap_z(): lax.ppermute(v, EVERY, self.move(lambda x, z, y, c: (x, z ^ bit, y, c)))  41.2 us
    ppermute x16, starting transfers between devices, swap_z(): lax.ppermute(v, EVERY, self.move(lambda x, z, y, c: (x, z ^ bit, y, c)))  31.1 us
    pallas_call x1, Pallas kernels, feed_forward(): pl.pallas_call(body, grid=(steps,), out_shape=[jax.ShapeDtypeStruct((leng...  28 us
    ppermute x8, waiting for transfers between devices, flip_y(): lax.ppermute(v, EVERY, self.move(lambda x, z, y, c: (x, z, 1 - y, c)))  22 us
    pallas_call x2, Pallas kernels, attend_back(): pl.pallas_call(body, grid=(width // pair,), out_shape=jax.ShapeDtypeStruc...  15.4 us
    ppermute x11, starting transfers between devices, flip_x(): lax.ppermute(v, EVERY, self.move(lambda x, z, y, c: (1 - x, z, y, c)))  13.5 us
    ppermute x11, waiting for transfers between devices, flip_x(): lax.ppermute(v, EVERY, self.move(lambda x, z, y, c: (1 - x, z, y, c)))  13.1 us
    ppermute x8, starting transfers between devices, flip_y(): lax.ppermute(v, EVERY, self.move(lambda x, z, y, c: (x, z, 1 - y, c)))  10.3 us
  transfers between devices with their start and end apart: 46, of which 22 were waited for; matrix products, arithmetic and copies ran while one was open for 8% of the time, Pallas kernels for 15%

profile of v5, /device:TPU:0, one launch (start us, length us, event | category | flops | bytes accessed | tf_op | source)
XLA Modules:
  0.0 268.6 jit_solution(8967035596325720495)
XLA Ops:
  10.3 3.1 %collective-permute-start = (bf16[160,384]{1,0:T(8,128)(2,1)S(1)}, bf16[160,384]{1,0:T(8,128)(2,1)S(1)}, u32[]{:S(2)}, u32[]{:S(2)}) collective-permute-start(bf16[160,384]{1,0:T(8,128)(2,1)S(1)} %bitcast.178), channel_id=1, source_target_pairs={{0,4},{1,5},{2,6},{3,7},{4,0},{5,1},{6,2},{7,3},{8,12},{9,13},{10,... | collective-permute-start | bytes 368648 | tf_op jit(solution)/shard_map/ppermute | solution.py:63
  13.4 2.6 collective-permute-start.1
  18.1 7.7 %collective-permute-done.1 = bf16[160,384]{1,0:T(8,128)(2,1)S(1)} collective-permute-done((bf16[160,384]{1,0:T(8,128)(2,1)S(1)}, bf16[160,384]{1,0:T(8,128)(2,1)S(1)}, u32[]{:S(2)}, u32[]{:S(2)}) %collective-permute-start.1) | collective-permute-done | bytes 122912 | tf_op jit(solution)/shard_map/ppermute | solution.py:63
  29.0 8.4 %collective-permute-start.5 = (bf16[176,384]{1,0:T(8,128)(2,1)S(1)}, bf16[176,384]{1,0:T(8,128)(2,1)S(1)}, u32[]{:S(2)}, u32[]{:S(2)}) collective-permute-start(bf16[176,384]{1,0:T(8,128)(2,1)S(1)} %fusion.22), channel_id=1, source_target_pairs={{0,4},{1,5},{2,6},{3,7},{4,0},{5,1},{6,2},{7,3},{8,12},{9,13},{10,... | collective-permute-start | bytes 405512 | tf_op jit(solution)/shard_map/ppermute | solution.py:63
  37.4 2.3 collective-permute-start.6
  43.3 6.5 %collective-permute-done.6 = bf16[176,384]{1,0:T(8,128)(2,1)S(1)} collective-permute-done((bf16[176,384]{1,0:T(8,128)(2,1)S(1)}, bf16[176,384]{1,0:T(8,128)(2,1)S(1)}, u32[]{:S(2)}, u32[]{:S(2)}) %collective-permute-start.6) | collective-permute-done | bytes 135200 | tf_op jit(solution)/shard_map/ppermute | solution.py:63
  55.2 4.5 %collective-permute-done.8 = bf16[2,160,384]{2,1,0:T(8,128)(2,1)S(1)} collective-permute-done((bf16[2,160,384]{2,1,0:T(8,128)(2,1)S(1)}, bf16[2,160,384]{2,1,0:T(8,128)(2,1)S(1)}, u32[]{:S(2)}, u32[]{:S(2)}) %collective-permute-start.8) | collective-permute-done | bytes 245792 | tf_op jit(solution)/shard_map/ppermute | solution.py:51
  59.7 6.1 %collective-permute-done.9 = bf16[2,160,384]{2,1,0:T(8,128)(2,1)S(1)} collective-permute-done((bf16[2,160,384]{2,1,0:T(8,128)(2,1)S(1)}, bf16[2,160,384]{2,1,0:T(8,128)(2,1)S(1)}, u32[]{:S(2)}, u32[]{:S(2)}) %collective-permute-start.9) | collective-permute-done | bytes 245792 | tf_op jit(solution)/shard_map/ppermute | solution.py:54
  67.8 4.8 %project_in.1 = (bf16[512,768]{1,0:T(8,128)(2,1)S(1)}, bf16[3,512,768]{2,1,0:T(8,128)(2,1)S(1)}, f32[16,768]{1,0:T(8,128)S(1)}) custom-call(bf16[512,768]{1,0:T(8,128)(2,1)S(1)} %bitcast.159, f32[16,768]{1,0:T(8,128)S(1)} %broadcast_in_dim.21.refs_1_, bf16[12,160,384]{2,1,0:T(8,128)(2,1)S(1)} %constant_dynamic-update-slice_fusion.refs_2_.refs_7_, ...), custom_call_target="tpu_custom_call" | custom-call | flops 8000000 | tf_op jit(solution)/shard_map/project_in/pallas_call | solution.py:309
  72.7 7.3 %attend.1.refs_2_ = bf16[512,768]{1,0:T(8,128)(2,1)S(1)} custom-call(s32[1]{0:T(128)S(6)} %copy.109.counts_ref.refs_0_, bf16[3,512,768]{2,1,0:T(8,128)(2,1)S(1)} %get-tuple-element.83.qkv_ref), custom_call_target="tpu_custom_call" | custom-call | flops 9000000 | tf_op jit(solution)/shard_map/attend/pallas_call | solution.py:347
  80.8 7.9 %collective-permute-done.13 = bf16[4,176,384]{2,1,0:T(8,128)(2,1)S(1)} collective-permute-done((bf16[4,176,384]{2,1,0:T(8,128)(2,1)S(1)}, bf16[4,176,384]{2,1,0:T(8,128)(2,1)S(1)}, u32[]{:S(2)}, u32[]{:S(2)}) %collective-permute-start.13) | collective-permute-done | bytes 540704 | tf_op jit(solution)/shard_map/ppermute | solution.py:54
  92.4 6.7 %collective-permute-done.14 = bf16[2,176,384]{2,1,0:T(8,128)(2,1)S(1)} collective-permute-done((bf16[2,176,384]{2,1,0:T(8,128)(2,1)S(1)}, bf16[2,176,384]{2,1,0:T(8,128)(2,1)S(1)}, u32[]{:S(2)}, u32[]{:S(2)}) %collective-permute-start.14) | collective-permute-done | bytes 270368 | tf_op jit(solution)/shard_map/ppermute | solution.py:51
  99.6 2.1 collective-permute-done.17.refs_8_
  102.5 28.0 %feed_forward.1 = (bf16[512,768]{1,0:T(8,128)(2,1)}, f32[512,768]{1,0:T(8,128)}, bf16[512,768]{1,0:T(8,128)(2,1)}, f32[8,768]{1,0:T(8,128)}, bf16[2,8,176,384]{3...) custom-call(s32[1]{0:T(128)S(6)} %copy.109.counts_ref.refs_0_, ...), custom_call_target="tpu_custom_call" | custom-call | flops 28000000 | tf_op jit(solution)/shard_map/feed_forward/pallas_call | solution.py:499
  132.2 5.1 %attend_back.2.refs_5_ = bf16[3,512,256]{2,1,0:T(8,128)(2,1)S(1)} custom-call(s32[1]{0:T(128)S(6)} %copy.109.counts_ref.refs_0_, bf16[3,512,768]{2,1,0:T(8,128)(2,1)S(1)} %get-tuple-element.83.qkv_ref, bf16[512,768]{1,0:T(8,128)(2,1)S(1)} %copy-done.6), custom_call_target="tpu_custom_call" | custom-call | flops 6600000 | tf_op jit(solution)/shard_map/attend_back/pallas_call | solution.py:385
  138.1 3.9 %fusion.4 = (bf16[4,96,1024]{2,1,0:T(8,128)(2,1)}, bf16[4,96,1024]{2,1,0:T(8,128)(2,1)}, bf16[4,96,1024]{2,1,0:T(8,128)(2,1)}) fusion(bf16[2,4,2,96,1024]{4,3,2,1,0:T(8,128)(2,1)} %bitcast.23, s32[]{:T(128)S(6)} %select_n.149, s32[]{:T(128)S(6)} %select_n.155, bf16[2,4,2,96,1024]{4,3,2,1,0:T(8,128)(2,1)S(1)} %bitcast.163, s32[]{:T(128)S(6)} %select_n.153, ...), kind=kLoop, calls=%fused_computation.21 | loop fusion | flops 4718592 | bytes 7077904 | tf_op jit(solution)/shard_map/convert_element_type | solution.py:129
  150.3 10.3 %attend_back.3.refs_6_ = bf16[3,512,512]{2,1,0:T(8,128)(2,1)S(1)} custom-call(s32[1]{0:T(128)S(6)} %copy.109.counts_ref.refs_0_, bf16[3,512,768]{2,1,0:T(8,128)(2,1)S(1)} %get-tuple-element.83.qkv_ref, bf16[512,768]{1,0:T(8,128)(2,1)S(1)} %copy-done.7), custom_call_target="tpu_custom_call" | custom-call | flops 11200000 | tf_op jit(solution)/shard_map/attend_back/pallas_call | solution.py:385
  165.3 8.0 %project_back.1 = (bf16[512,768]{1,0:T(8,128)(2,1)}, bf16[2,8,160,384]{3,2,1,0:T(8,128)(2,1)S(1)}, bf16[2,8,160,384]{3,2,1,0:T(8,128)(2,1)}) custom-call(bf16[512,768]{1,0:T(8,128)(2,1)S(1)} %bitcast.160, bf16[512,768]{1,0:T(8,128)(2,1)S(1)} %copy-done.21, f32[512,768]{1,0:T(8,128)S(1)} %copy-done.18, f32[16,768]{1,0:T(8,128)S(1)} %copy-done.23, ...), custom_call_target="tpu_custom_call" | custom-call | flops 11000000 | tf_op jit(solution)/shard_map/project_back/pallas_call | solution.py:568
  173.8 2.4 fusion
  176.2 3.8 %collective-permute-done.23.refs_1_ = bf16[4,96,1024]{2,1,0:T(8,128)(2,1)} collective-permute-done((bf16[4,96,1024]{2,1,0:T(8,128)(2,1)}, bf16[4,96,1024]{2,1,0:T(8,128)(2,1)}, u32[]{:S(2)}, u32[]{:S(2)}) %collective-permute-start.23) | collective-permute-done | bytes 786464 | tf_op jit(solution)/shard_map/ppermute | solution.py:54
  180.0 2.5 collective-permute-start.26
  182.5 3.7 %fold_column.1 = (bf16[2,96,1024]{2,1,0:T(8,128)(2,1)S(1)}, bf16[2,96,1024]{2,1,0:T(8,128)(2,1)S(1)}) custom-call(s32[3]{0:T(128)S(1)} %pad_add_fusion.place_ref, bf16[2,8,96,1024]{3,2,1,0:T(8,128)(2,1)S(1)} %copy-done.16, bf16[2,8,96,1024]{3,2,1,0:T(8,128)(2,1)} %collective-permute-done.18.got_ref, bf16[4,96,1024]{2,1,0:T(8,128)(2,1)} %collective-permute-done.22.refs_0_, ...), custom_call_target="tpu_custom_call" | custom-call | flops 60000001064960 | tf_op jit(solution)/shard_map/fold_column/pallas_call | solution.py:615
  186.3 2.6 fusion.7
  192.4 14.2 %collective-permute-done.27 = bf16[2,96,1024]{2,1,0:T(8,128)(2,1)} collective-permute-done((bf16[2,96,1024]{2,1,0:T(8,128)(2,1)S(1)}, bf16[2,96,1024]{2,1,0:T(8,128)(2,1)}, u32[]{:S(2)}, u32[]{:S(2)}) %collective-permute-start.27) | collective-permute-done | bytes 393248 | tf_op jit(solution)/shard_map/ppermute | solution.py:63
  210.2 2.5 collective-permute-done.29
  216.1 2.8 %collective-permute-start.36 = (bf16[160,384]{1,0:T(8,128)(2,1)S(1)}, bf16[160,384]{1,0:T(8,128)(2,1)S(1)}, u32[]{:S(2)}, u32[]{:S(2)}) collective-permute-start(bf16[160,384]{1,0:T(8,128)(2,1)S(1)} %get-tuple-element.150), channel_id=1, source_target_pairs={{0,12},{1,13},{2,14},{3,15},{4,8},{5,9},{6,10},{7,11},{8,4},{9,5},... | collective-permute-start | bytes 368648 | tf_op jit(solution)/shard_map/ppermute | solution.py:63
  221.1 4.1 %collective-permute-done.32 = bf16[96,1024]{1,0:T(8,128)(2,1)S(1)} collective-permute-done((bf16[96,1024]{1,0:T(8,128)(2,1)S(1)}, bf16[96,1024]{1,0:T(8,128)(2,1)S(1)}, u32[]{:S(2)}, u32[]{:S(2)}) %collective-permute-start.32) | collective-permute-done | bytes 196640 | tf_op jit(solution)/shard_map/ppermute | solution.py:63
  234.3 2.6 collective-permute-start.38
  239.3 2.3 collective-permute-start.39
  248.0 2.2 collective-permute-start.41
  250.2 2.4 collective-permute-done.41
  254.0 6.6 %update.1 = (f32[4,48,768]{2,1,0:T(8,128)}, f32[2,48,2048]{2,1,0:T(8,128)}, f32[128,768]{1,0:T(8,128)}, f32[2,48]{1,0:T(2,128)}, f32[4,48,768]{2,1,0:T(8,128)}, ...) custom-call(f32[1]{0:T(128)} %bitcast.64.refs_0_, ...), custom_call_target="tpu_custom_call" | custom-call | flops 4000000 | tf_op jit(solution)/shard_map/update/pallas_call | solution.py:718
  (189 shorter events, 68.1 us)
Async XLA Ops:
  7.2 95.0 %all-gather.2.cloned.1.call-start = ((), (), s32[]{:S(2)}) async-start(), calls=%async_computation | async-start | bytes 6684672 | tf_op jit(solution)/shard_map/all_gather | solution.py:770
  13.4 12.4 %collective-permute-start.1 = (bf16[160,384]{1,0:T(8,128)(2,1)S(1)}, bf16[160,384]{1,0:T(8,128)(2,1)S(1)}, u32[]{:S(2)}, u32[]{:S(2)}) collective-permute-start(bf16[160,384]{1,0:T(8,128)(2,1)S(1)} %bitcast.179), channel_id=1, source_target_pairs={{0,8},{1,9},{2,10},{3,11},{4,12},{5,13},{6,14},{7,15},{8,0},{9,1},... | collective-permute-start | bytes 368648 | tf_op jit(solution)/shard_map/ppermute | solution.py:63
  25.9 24.0 %collective-permute-start.3 = (bf16[4,160,384]{2,1,0:T(8,128)(2,1)S(1)}, bf16[4,160,384]{2,1,0:T(8,128)(2,1)S(1)}, u32[]{:S(2)}, u32[]{:S(2)}) collective-permute-start(bf16[4,160,384]{2,1,0:T(8,128)(2,1)S(1)} %pad_maximum_fusion.1), channel_id=1, source_target_pairs={{0,16},{1,17},{2,18},{3,19},{4,20},{5,21},{6,22},{7,23},{8,24},{9,... | collective-permute-start | bytes 1474568 | tf_op jit(solution)/shard_map/ppermute | solution.py:51
  27.4 22.4 %collective-permute-start.4 = (bf16[4,160,384]{2,1,0:T(8,128)(2,1)S(1)}, bf16[4,160,384]{2,1,0:T(8,128)(2,1)S(1)}, u32[]{:S(2)}, u32[]{:S(2)}) collective-permute-start(bf16[4,160,384]{2,1,0:T(8,128)(2,1)S(1)} %pad_maximum_fusion.1), channel_id=1, source_target_pairs={{0,2},{1,3},{2,0},{3,1},{4,6},{5,7},{6,4},{7,5},{8,10},{9,11},{10,... | collective-permute-start | bytes 1474568 | tf_op jit(solution)/shard_map/ppermute | solution.py:54
  29.0 14.3 %collective-permute-start.5 = (bf16[176,384]{1,0:T(8,128)(2,1)S(1)}, bf16[176,384]{1,0:T(8,128)(2,1)S(1)}, u32[]{:S(2)}, u32[]{:S(2)}) collective-permute-start(bf16[176,384]{1,0:T(8,128)(2,1)S(1)} %fusion.22), channel_id=1, source_target_pairs={{0,4},{1,5},{2,6},{3,7},{4,0},{5,1},{6,2},{7,3},{8,12},{9,13},{10,... | collective-permute-start | bytes 405512 | tf_op jit(solution)/shard_map/ppermute | solution.py:63
  37.4 12.4 %collective-permute-start.6 = (bf16[176,384]{1,0:T(8,128)(2,1)S(1)}, bf16[176,384]{1,0:T(8,128)(2,1)S(1)}, u32[]{:S(2)}, u32[]{:S(2)}) collective-permute-start(bf16[176,384]{1,0:T(8,128)(2,1)S(1)} %fusion.22), channel_id=1, source_target_pairs={{0,8},{1,9},{2,10},{3,11},{4,12},{5,13},{6,14},{7,15},{8,0},{9,1},... | collective-permute-start | bytes 405512 | tf_op jit(solution)/shard_map/ppermute | solution.py:63
  39.7 10.1 %collective-permute-start.7 = (bf16[176,384]{1,0:T(8,128)(2,1)S(1)}, bf16[176,384]{1,0:T(8,128)(2,1)S(1)}, u32[]{:S(2)}, u32[]{:S(2)}) collective-permute-start(bf16[176,384]{1,0:T(8,128)(2,1)S(1)} %fusion.22), channel_id=1, source_target_pairs={{0,12},{1,13},{2,14},{3,15},{4,8},{5,9},{6,10},{7,11},{8,4},{9,5},... | collective-permute-start | bytes 405512 | tf_op jit(solution)/shard_map/ppermute | solution.py:63
  50.0 17.8 %collective-permute-start.10 = (bf16[12,160,384]{2,1,0:T(8,128)(2,1)S(1)}, bf16[12,160,384]{2,1,0:T(8,128)(2,1)S(1)}, u32[]{:S(2)}, u32[]{:S(2)}) collective-permute-start(bf16[12,160,384]{2,1,0:T(8,128)(2,1)S(1)} %constant_dynamic-update-slice_fusion.refs_2_.refs_7_), channel_id=1, source_target_pairs={{0,1},{1,0},{2,3},{3,2},{4,5},{5,4},{6,7},{7,6},{8,9},{9,8},{10,11... | collective-permute-start | bytes 4423688 | tf_op jit(solution)/shard_map/ppermute | solution.py:60
  52.3 13.5 %collective-permute-start.9 = (bf16[2,160,384]{2,1,0:T(8,128)(2,1)S(1)}, bf16[2,160,384]{2,1,0:T(8,128)(2,1)S(1)}, u32[]{:S(2)}, u32[]{:S(2)}) collective-permute-start(bf16[2,160,384]{2,1,0:T(8,128)(2,1)S(1)} %slice.41), channel_id=1, source_target_pairs={{0,2},{1,3},{2,0},{3,1},{4,6},{5,7},{6,4},{7,5},{8,10},{9,11},{10,... | collective-permute-start | bytes 737288 | tf_op jit(solution)/shard_map/ppermute | solution.py:54
  53.9 26.9 %collective-permute-start.12 = (bf16[4,176,384]{2,1,0:T(8,128)(2,1)S(1)}, bf16[4,176,384]{2,1,0:T(8,128)(2,1)S(1)}, u32[]{:S(2)}, u32[]{:S(2)}) collective-permute-start(bf16[4,176,384]{2,1,0:T(8,128)(2,1)S(1)} %pad_maximum_fusion), channel_id=1, source_target_pairs={{0,16},{1,17},{2,18},{3,19},{4,20},{5,21},{6,22},{7,23},{8,24},{9,... | collective-permute-start | bytes 1622024 | tf_op jit(solution)/shard_map/ppermute | solution.py:51
  54.5 34.3 %collective-permute-start.13 = (bf16[4,176,384]{2,1,0:T(8,128)(2,1)S(1)}, bf16[4,176,384]{2,1,0:T(8,128)(2,1)S(1)}, u32[]{:S(2)}, u32[]{:S(2)}) collective-permute-start(bf16[4,176,384]{2,1,0:T(8,128)(2,1)S(1)} %pad_maximum_fusion), channel_id=1, source_target_pairs={{0,2},{1,3},{2,0},{3,1},{4,6},{5,7},{6,4},{7,5},{8,10},{9,11},{10,... | collective-permute-start | bytes 1622024 | tf_op jit(solution)/shard_map/ppermute | solution.py:54
  90.1 11.6 %collective-permute-start.16 = (bf16[12,176,384]{2,1,0:T(8,128)(2,1)S(1)}, bf16[12,176,384]{2,1,0:T(8,128)(2,1)}, u32[]{:S(2)}, u32[]{:S(2)}) collective-permute-start(bf16[12,176,384]{2,1,0:T(8,128)(2,1)S(1)} %constant_dynamic-update-slice_fusion.8.refs_5_), channel_id=1, source_target_pairs={{0,1},{1,0},{2,3},{3,2},{4,5},{5,4},{6,7},{7,6},{8,9},{9,8},{10,11... | collective-permute-start | bytes 4866056 | tf_op jit(solution)/shard_map/ppermute | solution.py:60
  130.7 14.8 %collective-permute-start.19 = (bf16[2,8,176,384]{3,2,1,0:T(8,128)(2,1)}, bf16[2,8,176,384]{3,2,1,0:T(8,128)(2,1)}, u32[]{:S(2)}, u32[]{:S(2)}) collective-permute-start(bf16[2,8,176,384]{3,2,1,0:T(8,128)(2,1)} %get-tuple-element.101), channel_id=1, source_target_pairs={{0,1},{1,0},{2,3},{3,2},{4,5},{5,4},{6,7},{7,6},{8,9},{9,8},{10,11... | collective-permute-start | bytes 6488072 | tf_op jit(solution)/shard_map/ppermute | solution.py:60
  142.1 34.1 %collective-permute-start.22 = (bf16[4,96,1024]{2,1,0:T(8,128)(2,1)}, bf16[4,96,1024]{2,1,0:T(8,128)(2,1)}, u32[]{:S(2)}, u32[]{:S(2)}) collective-permute-start(bf16[4,96,1024]{2,1,0:T(8,128)(2,1)} %get-tuple-element.143), channel_id=1, source_target_pairs={{0,16},{1,17},{2,18},{3,19},{4,20},{5,21},{6,22},{7,23},{8,24},{9,... | collective-permute-start | bytes 2359304 | tf_op jit(solution)/shard_map/ppermute | solution.py:51
  143.4 36.6 %collective-permute-start.23 = (bf16[4,96,1024]{2,1,0:T(8,128)(2,1)}, bf16[4,96,1024]{2,1,0:T(8,128)(2,1)}, u32[]{:S(2)}, u32[]{:S(2)}) collective-permute-start(bf16[4,96,1024]{2,1,0:T(8,128)(2,1)} %get-tuple-element.142), channel_id=1, source_target_pairs={{0,2},{1,3},{2,0},{3,1},{4,6},{5,7},{6,4},{7,5},{8,10},{9,11},{10,... | collective-permute-start | bytes 2359304 | tf_op jit(solution)/shard_map/ppermute | solution.py:54
  144.1 35.9 %collective-permute-start.24 = (bf16[4,96,1024]{2,1,0:T(8,128)(2,1)}, bf16[4,96,1024]{2,1,0:T(8,128)(2,1)}, u32[]{:S(2)}, u32[]{:S(2)}) collective-permute-start(bf16[4,96,1024]{2,1,0:T(8,128)(2,1)} %get-tuple-element.141), channel_id=1, source_target_pairs={{0,18},{1,19},{2,16},{3,17},{4,22},{5,23},{6,20},{7,21},{8,26},{9,... | collective-permute-start | bytes 2359304 | tf_op jit(solution)/shard_map/ppermute | solution.py:57
  148.2 25.2 %collective-permute-start.20 = (bf16[2,2,176,384]{3,2,1,0:T(8,128)(2,1)}, bf16[2,2,176,384]{3,2,1,0:T(8,128)(2,1)}, u32[]{:S(2)}, u32[]{:S(2)}) collective-permute-start(bf16[2,2,176,384]{3,2,1,0:T(8,128)(2,1)} %get-tuple-element.108), channel_id=1, source_target_pairs={{0,4},{1,5},{2,6},{3,7},{4,0},{5,1},{6,2},{7,3},{8,12},{9,13},{10,... | collective-permute-start | bytes 1622024 | tf_op jit(solution)/shard_map/ppermute | solution.py:63
  150.2 23.6 %collective-permute-start.21 = (bf16[2,2,176,384]{3,2,1,0:T(8,128)(2,1)}, bf16[2,2,176,384]{3,2,1,0:T(8,128)(2,1)}, u32[]{:S(2)}, u32[]{:S(2)}) collective-permute-start(bf16[2,2,176,384]{3,2,1,0:T(8,128)(2,1)} %get-tuple-element.109), channel_id=1, source_target_pairs={{0,4},{1,5},{2,6},{3,7},{4,0},{5,1},{6,2},{7,3},{8,12},{9,13},{10,... | collective-permute-start | bytes 1622024 | tf_op jit(solution)/shard_map/ppermute | solution.py:63
  173.8 12.5 %collective-permute-start.25 = (bf16[2,8,160,384]{3,2,1,0:T(8,128)(2,1)}, bf16[2,8,160,384]{3,2,1,0:T(8,128)(2,1)}, u32[]{:S(2)}, u32[]{:S(2)}) collective-permute-start(bf16[2,8,160,384]{3,2,1,0:T(8,128)(2,1)} %get-tuple-element.118), channel_id=1, source_target_pairs={{0,1},{1,0},{2,3},{3,2},{4,5},{5,4},{6,7},{7,6},{8,9},{9,8},{10,11... | collective-permute-start | bytes 5898248 | tf_op jit(solution)/shard_map/ppermute | solution.py:60
  180.0 26.6 %collective-permute-start.26 = (bf16[2,2,176,384]{3,2,1,0:T(8,128)(2,1)}, bf16[2,2,176,384]{3,2,1,0:T(8,128)(2,1)}, u32[]{:S(2)}, u32[]{:S(2)}) collective-permute-start(bf16[2,2,176,384]{3,2,1,0:T(8,128)(2,1)} %fusion), channel_id=1, source_target_pairs={{0,8},{1,9},{2,10},{3,11},{4,12},{5,13},{6,14},{7,15},{8,0},{9,1},... | collective-permute-start | bytes 1622024 | tf_op jit(solution)/shard_map/ppermute | solution.py:63
  186.2 20.4 %collective-permute-start.27 = (bf16[2,96,1024]{2,1,0:T(8,128)(2,1)S(1)}, bf16[2,96,1024]{2,1,0:T(8,128)(2,1)}, u32[]{:S(2)}, u32[]{:S(2)}) collective-permute-start(bf16[2,96,1024]{2,1,0:T(8,128)(2,1)S(1)} %get-tuple-element.117), channel_id=1, source_target_pairs={{0,4},{1,5},{2,6},{3,7},{4,0},{5,1},{6,2},{7,3},{8,12},{9,13},{10,... | collective-permute-start | bytes 1179656 | tf_op jit(solution)/shard_map/ppermute | solution.py:63
  188.9 21.3 %collective-permute-start.28 = (bf16[4,160,384]{2,1,0:T(8,128)(2,1)}, bf16[4,160,384]{2,1,0:T(8,128)(2,1)S(1)}, u32[]{:S(2)}, u32[]{:S(2)}) collective-permute-start(bf16[4,160,384]{2,1,0:T(8,128)(2,1)} %get-tuple-element.144), channel_id=1, source_target_pairs={{0,16},{1,17},{2,18},{3,19},{4,20},{5,21},{6,22},{7,23},{8,24},{9,... | collective-permute-start | bytes 1474568 | tf_op jit(solution)/shard_map/ppermute | solution.py:51
  190.1 22.6 %collective-permute-start.29 = (bf16[4,160,384]{2,1,0:T(8,128)(2,1)}, bf16[4,160,384]{2,1,0:T(8,128)(2,1)}, u32[]{:S(2)}, u32[]{:S(2)}) collective-permute-start(bf16[4,160,384]{2,1,0:T(8,128)(2,1)} %get-tuple-element.146), channel_id=1, source_target_pairs={{0,2},{1,3},{2,0},{3,1},{4,6},{5,7},{6,4},{7,5},{8,10},{9,11},{10,... | collective-permute-start | bytes 1474568 | tf_op jit(solution)/shard_map/ppermute | solution.py:54
  190.9 21.8 %collective-permute-start.30 = (bf16[4,160,384]{2,1,0:T(8,128)(2,1)}, bf16[4,160,384]{2,1,0:T(8,128)(2,1)}, u32[]{:S(2)}, u32[]{:S(2)}) collective-permute-start(bf16[4,160,384]{2,1,0:T(8,128)(2,1)} %get-tuple-element.145), channel_id=1, source_target_pairs={{0,18},{1,19},{2,16},{3,17},{4,22},{5,23},{6,20},{7,21},{8,26},{9,... | collective-permute-start | bytes 1474568 | tf_op jit(solution)/shard_map/ppermute | solution.py:57
  208.0 10.9 %collective-permute-start.31 = (bf16[2,176,384]{2,1,0:T(8,128)(2,1)S(1)}, bf16[2,176,384]{2,1,0:T(8,128)(2,1)S(1)}, u32[]{:S(2)}, u32[]{:S(2)}) collective-permute-start(bf16[2,176,384]{2,1,0:T(8,128)(2,1)S(1)} %fusion.6), channel_id=1, source_target_pairs={{0,2},{1,3},{2,0},{3,1},{4,6},{5,7},{6,4},{7,5},{8,10},{9,11},{10,... | collective-permute-start | bytes 811016 | tf_op jit(solution)/shard_map/ppermute | solution.py:54
  210.1 15.1 %collective-permute-start.32 = (bf16[96,1024]{1,0:T(8,128)(2,1)S(1)}, bf16[96,1024]{1,0:T(8,128)(2,1)S(1)}, u32[]{:S(2)}, u32[]{:S(2)}) collective-permute-start(bf16[96,1024]{1,0:T(8,128)(2,1)S(1)} %fusion.18), channel_id=1, source_target_pairs={{0,8},{1,9},{2,10},{3,11},{4,12},{5,13},{6,14},{7,15},{8,0},{9,1},... | collective-permute-start | bytes 589832 | tf_op jit(solution)/shard_map/ppermute | solution.py:63
  214.4 15.2 %collective-permute-start.34 = (bf16[160,384]{1,0:T(8,128)(2,1)S(1)}, bf16[160,384]{1,0:T(8,128)(2,1)S(1)}, u32[]{:S(2)}, u32[]{:S(2)}) collective-permute-start(bf16[160,384]{1,0:T(8,128)(2,1)S(1)} %get-tuple-element.152), channel_id=1, source_target_pairs={{0,4},{1,5},{2,6},{3,7},{4,0},{5,1},{6,2},{7,3},{8,12},{9,13},{10,... | collective-permute-start | bytes 368648 | tf_op jit(solution)/shard_map/ppermute | solution.py:63
  215.8 13.9 %collective-permute-start.35 = (bf16[160,384]{1,0:T(8,128)(2,1)S(1)}, bf16[160,384]{1,0:T(8,128)(2,1)S(1)}, u32[]{:S(2)}, u32[]{:S(2)}) collective-permute-start(bf16[160,384]{1,0:T(8,128)(2,1)S(1)} %get-tuple-element.151), channel_id=1, source_target_pairs={{0,8},{1,9},{2,10},{3,11},{4,12},{5,13},{6,14},{7,15},{8,0},{9,1},... | collective-permute-start | bytes 368648 | tf_op jit(solution)/shard_map/ppermute | solution.py:63
  216.1 13.6 %collective-permute-start.36 = (bf16[160,384]{1,0:T(8,128)(2,1)S(1)}, bf16[160,384]{1,0:T(8,128)(2,1)S(1)}, u32[]{:S(2)}, u32[]{:S(2)}) collective-permute-start(bf16[160,384]{1,0:T(8,128)(2,1)S(1)} %get-tuple-element.150), channel_id=1, source_target_pairs={{0,12},{1,13},{2,14},{3,15},{4,8},{5,9},{6,10},{7,11},{8,4},{9,5},... | collective-permute-start | bytes 368648 | tf_op jit(solution)/shard_map/ppermute | solution.py:63
  226.2 27.1 %collective-permute-start.44 = (bf16[96,1024]{1,0:T(8,128)(2,1)S(1)}, bf16[96,1024]{1,0:T(8,128)(2,1)S(1)}, u32[]{:S(2)}, u32[]{:S(2)}) collective-permute-start(bf16[96,1024]{1,0:T(8,128)(2,1)S(1)} %fusion.11.refs_0_.refs_6_), channel_id=1, source_target_pairs={{0,16},{1,17},{2,18},{3,19},{4,20},{5,21},{6,22},{7,23},{8,24},{9,... | collective-permute-start | bytes 589832 | tf_op jit(solution)/shard_map/ppermute | solution.py:51
  228.6 24.7 %collective-permute-start.43 = (bf16[176,384]{1,0:T(8,128)(2,1)S(1)}, bf16[176,384]{1,0:T(8,128)(2,1)S(1)}, u32[]{:S(2)}, u32[]{:S(2)}) collective-permute-start(bf16[176,384]{1,0:T(8,128)(2,1)S(1)} %fusion.15.refs_1_.refs_4_), channel_id=1, source_target_pairs={{0,16},{1,17},{2,18},{3,19},{4,20},{5,21},{6,22},{7,23},{8,24},{9,... | collective-permute-start | bytes 405512 | tf_op jit(solution)/shard_map/ppermute | solution.py:51
  230.5 22.8 %collective-permute-start.42 = (bf16[160,384]{1,0:T(8,128)(2,1)S(1)}, bf16[160,384]{1,0:T(8,128)(2,1)S(1)}, u32[]{:S(2)}, u32[]{:S(2)}) collective-permute-start(bf16[160,384]{1,0:T(8,128)(2,1)S(1)} %get-tuple-element.126.refs_2_), channel_id=1, source_target_pairs={{0,16},{1,17},{2,18},{3,19},{4,20},{5,21},{6,22},{7,23},{8,24},{9,... | collective-permute-start | bytes 368648 | tf_op jit(solution)/shard_map/ppermute | solution.py:51
  (49 other events, 342.4 us)
Sparse Core Ops, SparseCore 0:
  10.9 91.2 all-gather.1

commit v6 on v5

--- a/solution.py
+++ b/solution.py
@@ -74,7 +74,6 @@
 class Spread:
     def __init__(self, grid, part):
         self.grid, self.part = grid, part
-        self.half = grid.nz // 2
 
     def send_levels(self):
         self.levels = [self.grid.swap_z(self.part, k) for k in range(1, self.grid.nz)]
@@ -87,18 +86,16 @@
         self.across = self.grid.flip_y(self.column)
 
     def send_corners(self):
-        self.low = self.grid.flip_x(self.across[: self.half])
-        self.high = self.grid.flip_y(self.side[self.half :])
+        self.corner = self.grid.flip_x(self.across)
         self.most = jnp.concatenate([self.column, self.side, self.across])
         self.other_most = self.grid.flip_core(self.most)
 
     def finish(self):
-        self.rest = jnp.concatenate([self.low, self.high])
-        self.other_rest = self.grid.flip_core(self.rest)
+        self.other_rest = self.grid.flip_core(self.corner)
 
     @property
     def pieces(self):
-        return [self.most, self.rest, self.other_most, self.other_rest]
+        return [self.most, self.corner, self.other_most, self.other_rest]
 
 
 def piece_places(grid):
@@ -114,6 +111,9 @@
 
     def send_core(self):
         self.got = self.grid.flip_core(self.sent)
+
+    def split(self, array):
+        return array.reshape((2, self.grid.nz, 2) + array.shape[2:])
 
     def block(self, h, at_y):
         total = 0.0
@@ -435,45 +435,59 @@
             normed_t[...] = low.T
             total[...] = values
             d_normed[...] = jnp.zeros_like(d_normed)
-            wait_all(w_gate, sems.at[1])
-            wait_all(w_up, sems.at[2])
-            wait_all(w_down, sems.at[3])
-
-        columns = pl.ds(pl.multiple_of(step * chunk, chunk), chunk)
-        gate_w, up_w = (w[:, :, columns].reshape(width, chunk) for w in (w_gate, w_up))
-        down_w = w_down[columns]
-        e = e_ref[...]
-        gate, up = dot(normed[...], gate_w), dot(normed[...], up_w)
-        square = gate * gate
-        bend = jnp.tanh(0.7978845608 * (gate + 0.044715 * square * gate))
-        half_up = 0.5 * (1.0 + bend)
-        gelu = gate * half_up
-        slope = half_up + 0.5 * gate * (1.0 - bend * bend) * (
-            0.7978845608 * (1.0 + 3.0 * 0.044715 * square)
-        )
-        hidden = (gelu * up).astype(LOW)
-        total[...] += dot(hidden, down_w)
-        d_hidden = dot_nt(e, down_w)
-        d_gate = (d_hidden * up * slope).astype(LOW)
-        d_up = (d_hidden * gelu).astype(LOW)
-        g_down = dot_tn(hidden, e)
-        shards = chunk // down_rows
-        if grid.cube:
-            c = lax.rem(lax.axis_index("fsdp"), 2)
-            g_down = g_down.astype(LOW).reshape(shards // 2, 2, down_rows, width)
-            even, odd = g_down[:, 0], g_down[:, 1]
-            g_down = [jnp.where(c == 0, even, odd), jnp.where(c == 0, odd, even)]
-            lead = pl.ds(step * (shards // 2), shards // 2)
-        else:
-            g_down = [g_down.astype(LOW).reshape(shards, down_rows, width)]
-            lead = pl.ds(step * shards, shards)
-        for ref, value in zip(out_grads, g_down):
-            for h in range(2):
-                ref[h, lead, rows:] = value[:, :, h * (width // 2) : (h + 1) * (width // 2)]
-        everything = (0, slice(None))
-        store_grad(grid, in_grads, everything, 0, rows, dot(normed_t[...], d_gate))
-        store_grad(grid, in_grads, everything, rows, rows, dot(normed_t[...], d_up))
-        d_normed[...] += dot_nt(d_gate, gate_w) + dot_nt(d_up, up_w)
+
+        def one_chunk(first):
+            columns = pl.ds(pl.multiple_of(step * chunk, chunk), chunk)
+            if first:
+                wait_all(w_gate, sems.at[1])
+            gate_w = w_gate[:, :, columns].reshape(width, chunk)
+            gate = dot(normed[...], gate_w)
+            if first:
+                wait_all(w_up, sems.at[2])
+            up_w = w_up[:, :, columns].reshape(width, chunk)
+            up = dot(normed[...], up_w)
+            if first:
+                wait_all(w_down, sems.at[3])
+            down_w = w_down[columns]
+            e = e_ref[...]
+            square = gate * gate
+            bend = jnp.tanh(0.7978845608 * (gate + 0.044715 * square * gate))
+            half_up = 0.5 * (1.0 + bend)
+            gelu = gate * half_up
+            slope = half_up + 0.5 * gate * (1.0 - bend * bend) * (
+                0.7978845608 * (1.0 + 3.0 * 0.044715 * square)
+            )
+            hidden = (gelu * up).astype(LOW)
+            total[...] += dot(hidden, down_w)
+            d_hidden = dot_nt(e, down_w)
+            d_gate = (d_hidden * up * slope).astype(LOW)
+            d_up = (d_hidden * gelu).astype(LOW)
+            g_down = dot_tn(hidden, e)
+            shards = chunk // down_rows
+            if grid.cube:
+                c = lax.rem(lax.axis_index("fsdp"), 2)
+                g_down = g_down.astype(LOW).reshape(shards // 2, 2, down_rows, width)
+                even, odd = g_down[:, 0], g_down[:, 1]
+                g_down = [jnp.where(c == 0, even, odd), jnp.where(c == 0, odd, even)]
+                lead = pl.ds(step * (shards // 2), shards // 2)
+            else:
+                g_down = [g_down.astype(LOW).reshape(shards, down_rows, width)]
+                lead = pl.ds(step * shards, shards)
+            for ref, value in zip(out_grads, g_down):
+                for h in range(2):
+                    ref[h, lead, rows:] = value[:, :, h * (width // 2) : (h + 1) * (width // 2)]
+            everything = (0, slice(None))
+            store_grad(grid, in_grads, everything, 0, rows, dot(normed_t[...], d_gate))
+            store_grad(grid, in_grads, everything, rows, rows, dot(normed_t[...], d_up))
+            d_normed[...] += dot_nt(d_gate, gate_w) + dot_nt(d_up, up_w)
+
+        @pl.when(step == 0)
+        def _():
+            one_chunk(True)
+
+        @pl.when(step > 0)
+        def _():
+            one_chunk(False)
 
         @pl.when(step == steps - 1)
         def _():
@@ -586,44 +600,30 @@
     rows, columns = reduce.keep.shape[2:]
     half = grid.nz // 2
 
-    def level(i):
-        return jnp.where(i < half, 2 * i + 1, 2 * (i - half))
-
     def body(place_ref, keep_ref, got_ref, *refs):
-        sides, (leave_ref, rest_ref) = refs[:-2], refs[-2:]
         total = keep_ref[0, 0].astype(WIDE) + got_ref[0, 0].astype(WIDE)
-        for ref in sides:
+        for ref in refs[:-1]:
             total = total + ref[0].astype(WIDE)
-        total = total.astype(LOW)
-
-        @pl.when(pl.program_id(0) < half)
-        def _():
-            leave_ref[0] = total
-
-        @pl.when(pl.program_id(0) >= half)
-        def _():
-            rest_ref[0] = total
-
-    def own(i, place):
-        return place[0], (place[1] ^ level(i)) * 2 + place[2], 0, 0
+        refs[-1][0] = total.astype(LOW)
+
+    def level(i, place):
+        return place[1] ^ (2 * i + 1)
 
     block = (1, rows, columns)
-    whole = pl.BlockSpec((1,) + block, own)
-    side = pl.BlockSpec(block, lambda i, place: (place[1] ^ level(i), 0, 0))
-    shape = jax.ShapeDtypeStruct((half, rows, columns), LOW)
+    whole = pl.BlockSpec(
+        (1,) + block, lambda i, place: (place[0], level(i, place) * 2 + place[2], 0, 0)
+    )
+    side = pl.BlockSpec(block, lambda i, place: (level(i, place), 0, 0))
     x, z, y, _ = grid.place()
     return pl.pallas_call(
         body,
         grid_spec=pltpu.PrefetchScalarGridSpec(
             num_scalar_prefetch=1,
-            grid=(grid.nz,),
+            grid=(half,),
             in_specs=[whole, whole] + [side] * len(reduce.sides),
-            out_specs=[
-                pl.BlockSpec(block, lambda i, place: (jnp.minimum(i, half - 1), 0, 0)),
-                pl.BlockSpec(block, lambda i, place: (jnp.maximum(i - half, 0), 0, 0)),
-            ],
+            out_specs=pl.BlockSpec(block, lambda i, place: (i, 0, 0)),
         ),
-        out_shape=[shape, shape],
+        out_shape=jax.ShapeDtypeStruct((half, rows, columns), LOW),
         compiler_params=params(16, ("arbitrary",)),
         cost_estimate=cost(6e7),
         name="fold_column",
@@ -825,7 +825,7 @@
             arrived = grid.swap_z(leave, 1 << bit)
         one = Reduce(grid, *grads)
         one.send_core()
-        leave, rest = fold_column(three)
+        leave = fold_column(three)
         in_three = grid.swap_z(leave, 1)
         leave, one.got = after(leave, one.got)
         sides = one.load_sides()
@@ -833,7 +833,11 @@
         _, (arrived, in_three) = after(sides, (arrived, in_three))
         two.parts.append(arrived)
         arrived = grid.flip_y(two.leave(1, y))
-        three = Fold(grid, [rest, in_three])
+        rest = [z ^ k for k in range(0, grid.nz, 2)]
+        kept = [lax.dynamic_index_in_dim(three.split(v), x, 0, False) for v in (three.keep, three.got)]
+        kept = [lax.dynamic_index_in_dim(v, y, 1, False) for v in kept] + three.sides
+        kept = [jnp.stack([lax.dynamic_index_in_dim(v, k, 0, False) for k in rest]) for v in kept]
+        three = Fold(grid, kept + [in_three])
         bits = three.by_bits(0)
         for bit in range(1, bits + 1):
             in_three = grid.swap_z(three.leave(bits - bit, 0), 1 << bit)

time: 269 us -> 264 us (0.981)
  waiting for transfers between devices: 82 us -> 77.5 us
    ppermute x8 -> x6, waiting for transfers between devices: 22 us -> 5.99 us  [flip_y(): lax.ppermute(v, EVERY, self.move(lambda x, z, y, c: (x, z, 1 - y, c)))]
    ppermute x11, waiting for transfers between devices: 13.1 us -> 23.9 us  [flip_x(): lax.ppermute(v, EVERY, self.move(lambda x, z, y, c: (1 - x, z, y, c)))]
    ppermute x8 -> x6, starting transfers between devices: 10.3 us -> 9.58 us  [flip_y(): lax.ppermute(v, EVERY, self.move(lambda x, z, y, c: (x, z, 1 - y, c)))]
  transfers between devices with their start and end apart: 46 -> 44, of which waited for: 22 -> 20; matrix products, arithmetic and copies ran while one was open for 8% -> 8% of each run, Pallas kernels for 15% -> 15%
where the time goes in v6:
time: 264 us; the launch traced here: 263 us
  waiting for transfers between devices  77.5 us (29%)
  Pallas kernels  72.7 us (28%)
  starting transfers between devices  58.1 us (22%)
  other arithmetic  22.5 us (9%)
  between operations  20.7 us (8%)
  local copies, waits for them, and re-layouts  11.7 us (4%)
    ppermute x16, waiting for transfers between devices, swap_z(): lax.ppermute(v, EVERY, self.move(lambda x, z, y, c: (x, z ^ bit, y, c)))  42.2 us
    ppermute x16, starting transfers between devices, swap_z(): lax.ppermute(v, EVERY, self.move(lambda x, z, y, c: (x, z ^ bit, y, c)))  31.9 us
    pallas_call x1, Pallas kernels, feed_forward(): pl.pallas_call(body, grid=(steps,), out_shape=[jax.ShapeDtypeStruct((leng...  27.5 us
    ppermute x11, waiting for transfers between devices, flip_x(): lax.ppermute(v, EVERY, self.move(lambda x, z, y, c: (1 - x, z, y, c)))  23.9 us
    pallas_call x2, Pallas kernels, attend_back(): pl.pallas_call(body, grid=(width // pair,), out_shape=jax.ShapeDtypeStruc...  15.2 us
    ppermute x11, starting transfers between devices, flip_x(): lax.ppermute(v, EVERY, self.move(lambda x, z, y, c: (1 - x, z, y, c)))  14 us
    unnamed x81, local copies, waits for them, and re-layouts  10.3 us
    ppermute x6, starting transfers between devices, flip_y(): lax.ppermute(v, EVERY, self.move(lambda x, z, y, c: (x, z, 1 - y, c)))  9.58 us
  transfers between devices with their start and end apart: 44, of which 20 were waited for; matrix products, arithmetic and copies ran while one was open for 8% of the time, Pallas kernels for 15%

profile of v6, /device:TPU:0, one launch (start us, length us, event | category | flops | bytes accessed | tf_op | source)
XLA Modules:
  0.0 263.3 jit_solution(12122390276319728936)
XLA Ops:
  10.3 3.1 %collective-permute-start = (bf16[160,384]{1,0:T(8,128)(2,1)S(1)}, bf16[160,384]{1,0:T(8,128)(2,1)S(1)}, u32[]{:S(2)}, u32[]{:S(2)}) collective-permute-start(bf16[160,384]{1,0:T(8,128)(2,1)S(1)} %bitcast.190), channel_id=1, source_target_pairs={{0,4},{1,5},{2,6},{3,7},{4,0},{5,1},{6,2},{7,3},{8,12},{9,13},{10,... | collective-permute-start | bytes 368648 | tf_op jit(solution)/shard_map/ppermute | solution.py:63
  13.4 2.6 collective-permute-start.1
  18.1 7.7 %collective-permute-done.1 = bf16[160,384]{1,0:T(8,128)(2,1)S(1)} collective-permute-done((bf16[160,384]{1,0:T(8,128)(2,1)S(1)}, bf16[160,384]{1,0:T(8,128)(2,1)S(1)}, u32[]{:S(2)}, u32[]{:S(2)}) %collective-permute-start.1) | collective-permute-done | bytes 122912 | tf_op jit(solution)/shard_map/ppermute | solution.py:63
  29.0 8.4 %collective-permute-start.5 = (bf16[176,384]{1,0:T(8,128)(2,1)S(1)}, bf16[176,384]{1,0:T(8,128)(2,1)S(1)}, u32[]{:S(2)}, u32[]{:S(2)}) collective-permute-start(bf16[176,384]{1,0:T(8,128)(2,1)S(1)} %fusion.23), channel_id=1, source_target_pairs={{0,4},{1,5},{2,6},{3,7},{4,0},{5,1},{6,2},{7,3},{8,12},{9,13},{10,... | collective-permute-start | bytes 405512 | tf_op jit(solution)/shard_map/ppermute | solution.py:63
  37.4 2.3 collective-permute-start.6
  41.3 2.0 collective-permute-done.5
  43.3 6.5 %collective-permute-done.6 = bf16[176,384]{1,0:T(8,128)(2,1)S(1)} collective-permute-done((bf16[176,384]{1,0:T(8,128)(2,1)S(1)}, bf16[176,384]{1,0:T(8,128)(2,1)S(1)}, u32[]{:S(2)}, u32[]{:S(2)}) %collective-permute-start.6) | collective-permute-done | bytes 135200 | tf_op jit(solution)/shard_map/ppermute | solution.py:63
  54.4 9.8 %collective-permute-done.8.refs_3_.refs_8_ = bf16[4,160,384]{2,1,0:T(8,128)(2,1)S(1)} collective-permute-done((bf16[4,160,384]{2,1,0:T(8,128)(2,1)S(1)}, bf16[4,160,384]{2,1,0:T(8,128)(2,1)S(1)}, u32[]{:S(2)}, u32[]{:S(2)}) %collective-permute-start.8) | collective-permute-done | bytes 491552 | tf_op jit(solution)/shard_map/ppermute | solution.py:51
  66.1 4.8 %project_in.1 = (bf16[512,768]{1,0:T(8,128)(2,1)S(1)}, bf16[3,512,768]{2,1,0:T(8,128)(2,1)S(1)}, f32[16,768]{1,0:T(8,128)S(1)}) custom-call(bf16[512,768]{1,0:T(8,128)(2,1)S(1)} %bitcast.169, f32[16,768]{1,0:T(8,128)S(1)} %broadcast_in_dim.21.refs_1_, bf16[12,160,384]{2,1,0:T(8,128)(2,1)S(1)} %constant_dynamic-update-slice_fusion.refs_2_.refs_7_, ...), custom_call_target="tpu_custom_call" | custom-call | flops 8000000 | tf_op jit(solution)/shard_map/project_in/pallas_call | solution.py:309
  70.9 7.3 %attend.1.refs_2_ = bf16[512,768]{1,0:T(8,128)(2,1)S(1)} custom-call(s32[1]{0:T(128)S(6)} %copy.77.counts_ref.refs_0_, bf16[3,512,768]{2,1,0:T(8,128)(2,1)S(1)} %get-tuple-element.81.qkv_ref), custom_call_target="tpu_custom_call" | custom-call | flops 9000000 | tf_op jit(solution)/shard_map/attend/pallas_call | solution.py:347
  82.0 13.2 %collective-permute-done.13.refs_6_ = bf16[4,176,384]{2,1,0:T(8,128)(2,1)S(1)} collective-permute-done((bf16[4,176,384]{2,1,0:T(8,128)(2,1)S(1)}, bf16[4,176,384]{2,1,0:T(8,128)(2,1)S(1)}, u32[]{:S(2)}, u32[]{:S(2)}) %collective-permute-start.13) | collective-permute-done | bytes 540704 | tf_op jit(solution)/shard_map/ppermute | solution.py:51
  95.2 2.0 collective-permute-done.15.refs_8_
  98.0 27.5 %feed_forward.1 = (bf16[512,768]{1,0:T(8,128)(2,1)}, f32[512,768]{1,0:T(8,128)}, bf16[512,768]{1,0:T(8,128)(2,1)}, f32[8,768]{1,0:T(8,128)}, bf16[2,8,176,384]{3...) custom-call(s32[1]{0:T(128)S(6)} %copy.77.counts_ref.refs_0_, ...), custom_call_target="tpu_custom_call" | custom-call | flops 28000000 | tf_op jit(solution)/shard_map/feed_forward/pallas_call | solution.py:513
  127.2 5.1 %attend_back.2.refs_5_ = bf16[3,512,256]{2,1,0:T(8,128)(2,1)S(1)} custom-call(s32[1]{0:T(128)S(6)} %copy.77.counts_ref.refs_0_, bf16[3,512,768]{2,1,0:T(8,128)(2,1)S(1)} %get-tuple-element.81.qkv_ref, bf16[512,768]{1,0:T(8,128)(2,1)S(1)} %copy-done.6), custom_call_target="tpu_custom_call" | custom-call | flops 6600000 | tf_op jit(solution)/shard_map/attend_back/pallas_call | solution.py:385
  133.2 3.9 %fusion.4 = (bf16[4,96,1024]{2,1,0:T(8,128)(2,1)}, bf16[4,96,1024]{2,1,0:T(8,128)(2,1)}, bf16[4,96,1024]{2,1,0:T(8,128)(2,1)}) fusion(bf16[2,4,2,96,1024]{4,3,2,1,0:T(8,128)(2,1)} %bitcast.23, s32[]{:T(128)S(6)} %select_n.176, s32[]{:T(128)S(6)} %select_n.182, bf16[2,4,2,96,1024]{4,3,2,1,0:T(8,128)(2,1)S(1)} %bitcast.171, s32[]{:T(128)S(6)} %select_n.180, ...), kind=kLoop, calls=%fused_computation.21 | loop fusion | flops 4718592 | bytes 7077904 | tf_op jit(solution)/shard_map/convert_element_type | solution.py:129
  143.2 2.0 collective-permute-start.18
  145.4 10.1 %attend_back.3.refs_6_ = bf16[3,512,512]{2,1,0:T(8,128)(2,1)S(1)} custom-call(s32[1]{0:T(128)S(6)} %copy.77.counts_ref.refs_0_, bf16[3,512,768]{2,1,0:T(8,128)(2,1)S(1)} %get-tuple-element.81.qkv_ref, bf16[512,768]{1,0:T(8,128)(2,1)S(1)} %copy-done.7), custom_call_target="tpu_custom_call" | custom-call | flops 11200000 | tf_op jit(solution)/shard_map/attend_back/pallas_call | solution.py:385
  160.2 8.1 %project_back.1 = (bf16[512,768]{1,0:T(8,128)(2,1)}, bf16[2,8,160,384]{3,2,1,0:T(8,128)(2,1)S(1)}, bf16[2,8,160,384]{3,2,1,0:T(8,128)(2,1)}) custom-call(bf16[512,768]{1,0:T(8,128)(2,1)S(1)} %bitcast.170, bf16[512,768]{1,0:T(8,128)(2,1)S(1)} %copy-done.22, f32[512,768]{1,0:T(8,128)S(1)} %copy-done.19, f32[16,768]{1,0:T(8,128)S(1)} %copy-done.24, ...), custom_call_target="tpu_custom_call" | custom-call | flops 11000000 | tf_op jit(solution)/shard_map/project_back/pallas_call | solution.py:582
  168.8 2.4 fusion
  171.3 3.6 %collective-permute-done.21.refs_1_ = bf16[4,96,1024]{2,1,0:T(8,128)(2,1)} collective-permute-done((bf16[4,96,1024]{2,1,0:T(8,128)(2,1)}, bf16[4,96,1024]{2,1,0:T(8,128)(2,1)}, u32[]{:S(2)}, u32[]{:S(2)}) %collective-permute-start.21) | collective-permute-done | bytes 786464 | tf_op jit(solution)/shard_map/ppermute | solution.py:54
  174.9 3.2 %collective-permute-start.24 = (bf16[2,2,176,384]{3,2,1,0:T(8,128)(2,1)}, bf16[2,2,176,384]{3,2,1,0:T(8,128)(2,1)}, u32[]{:S(2)}, u32[]{:S(2)}) collective-permute-start(bf16[2,2,176,384]{3,2,1,0:T(8,128)(2,1)} %fusion), channel_id=1, source_target_pairs={{0,8},{1,9},{2,10},{3,11},{4,12},{5,13},{6,14},{7,15},{8,0},{9,1},... | collective-permute-start | bytes 1622024 | tf_op jit(solution)/shard_map/ppermute | solution.py:63
  178.1 2.4 fold_column.1
  180.7 2.6 %fusion.7 = (bf16[4,160,384]{2,1,0:T(8,128)(2,1)}, bf16[4,160,384]{2,1,0:T(8,128)(2,1)}, bf16[4,160,384]{2,1,0:T(8,128)(2,1)}) fusion(bf16[2,4,2,160,384]{4,3,2,1,0:T(8,128)(2,1)} %bitcast.45, s32[]{:T(128)S(6)} %select_n.176, s32[]{:T(128)S(6)} %select_n.179, bf16[2,4,2,160,384]{4,3,2,1,0:T(8,128)(2,1)S(1)} %bitcast.174, s32[]{:T(128)S(6)} %select_n.182, ...), kind=kLoop, calls=%fused_computation.30 | loop fusion | flops 2949120 | bytes 4423696 | tf_op jit(solution)/shard_map/convert_element_type | solution.py:129
  186.8 10.8 %collective-permute-done.25 = bf16[2,96,1024]{2,1,0:T(8,128)(2,1)} collective-permute-done((bf16[2,96,1024]{2,1,0:T(8,128)(2,1)S(1)}, bf16[2,96,1024]{2,1,0:T(8,128)(2,1)}, u32[]{:S(2)}, u32[]{:S(2)}) %collective-permute-start.25) | collective-permute-done | bytes 393248 | tf_op jit(solution)/shard_map/ppermute | solution.py:63
  197.7 4.0 %collective-permute-done.24 = bf16[2,2,176,384]{3,2,1,0:T(8,128)(2,1)} collective-permute-done((bf16[2,2,176,384]{3,2,1,0:T(8,128)(2,1)}, bf16[2,2,176,384]{3,2,1,0:T(8,128)(2,1)}, u32[]{:S(2)}, u32[]{:S(2)}) %collective-permute-start.24) | collective-permute-done | bytes 540704 | tf_op jit(solution)/shard_map/ppermute | solution.py:63
  211.6 2.4 collective-permute-start.34
  215.9 4.8 %collective-permute-done.30 = bf16[96,1024]{1,0:T(8,128)(2,1)S(1)} collective-permute-done((bf16[96,1024]{1,0:T(8,128)(2,1)S(1)}, bf16[96,1024]{1,0:T(8,128)(2,1)S(1)}, u32[]{:S(2)}, u32[]{:S(2)}) %collective-permute-start.30) | collective-permute-done | bytes 196640 | tf_op jit(solution)/shard_map/ppermute | solution.py:63
  230.0 2.6 collective-permute-start.36
  234.2 2.6 %collective-permute-start.37 = (f32[]{:T(128)}, f32[]{:T(128)}, u32[]{:S(2)}, u32[]{:S(2)}) collective-permute-start(f32[]{:T(128)} %add.545), channel_id=1, source_target_pairs={{0,2},{1,3},{2,0},{3,1},{4,6},{5,7},{6,4},{7,5},{8,10},{9,11},{10,... | collective-permute-start | bytes 20 | tf_op jit(solution)/shard_map/ppermute | solution.py:54
  240.0 2.0 collective-permute-done.38
  242.7 2.6 %collective-permute-start.39 = (f32[]{:T(128)}, f32[]{:T(128)}, u32[]{:S(2)}, u32[]{:S(2)}) collective-permute-start(f32[]{:T(128)} %add.547), channel_id=1, source_target_pairs={{0,8},{1,9},{2,10},{3,11},{4,12},{5,13},{6,14},{7,15},{8,0},{9,1},... | collective-permute-start | bytes 20 | tf_op jit(solution)/shard_map/ppermute | solution.py:63
  248.7 6.6 %update.1 = (f32[4,48,768]{2,1,0:T(8,128)}, f32[2,48,2048]{2,1,0:T(8,128)}, f32[128,768]{1,0:T(8,128)}, f32[2,48]{1,0:T(2,128)}, f32[4,48,768]{2,1,0:T(8,128)}, ...) custom-call(f32[1]{0:T(128)} %bitcast.72.refs_0_, ...), custom_call_target="tpu_custom_call" | custom-call | flops 4000000 | tf_op jit(solution)/shard_map/update/pallas_call | solution.py:718
  (179 shorter events, 63.3 us)
Async XLA Ops:
  7.2 90.3 %all-gather.2.cloned.1.call-start = ((), (), s32[]{:S(2)}) async-start(), calls=%async_computation | async-start | bytes 6684672 | tf_op jit(solution)/shard_map/all_gather | solution.py:770
  13.4 12.4 %collective-permute-start.1 = (bf16[160,384]{1,0:T(8,128)(2,1)S(1)}, bf16[160,384]{1,0:T(8,128)(2,1)S(1)}, u32[]{:S(2)}, u32[]{:S(2)}) collective-permute-start(bf16[160,384]{1,0:T(8,128)(2,1)S(1)} %bitcast.191), channel_id=1, source_target_pairs={{0,8},{1,9},{2,10},{3,11},{4,12},{5,13},{6,14},{7,15},{8,0},{9,1},... | collective-permute-start | bytes 368648 | tf_op jit(solution)/shard_map/ppermute | solution.py:63
  25.9 24.0 %collective-permute-start.3 = (bf16[4,160,384]{2,1,0:T(8,128)(2,1)S(1)}, bf16[4,160,384]{2,1,0:T(8,128)(2,1)S(1)}, u32[]{:S(2)}, u32[]{:S(2)}) collective-permute-start(bf16[4,160,384]{2,1,0:T(8,128)(2,1)S(1)} %pad_maximum_fusion.1), channel_id=1, source_target_pairs={{0,16},{1,17},{2,18},{3,19},{4,20},{5,21},{6,22},{7,23},{8,24},{9,... | collective-permute-start | bytes 1474568 | tf_op jit(solution)/shard_map/ppermute | solution.py:51
  27.4 22.4 %collective-permute-start.4 = (bf16[4,160,384]{2,1,0:T(8,128)(2,1)S(1)}, bf16[4,160,384]{2,1,0:T(8,128)(2,1)S(1)}, u32[]{:S(2)}, u32[]{:S(2)}) collective-permute-start(bf16[4,160,384]{2,1,0:T(8,128)(2,1)S(1)} %pad_maximum_fusion.1), channel_id=1, source_target_pairs={{0,2},{1,3},{2,0},{3,1},{4,6},{5,7},{6,4},{7,5},{8,10},{9,11},{10,... | collective-permute-start | bytes 1474568 | tf_op jit(solution)/shard_map/ppermute | solution.py:54
  29.0 14.3 %collective-permute-start.5 = (bf16[176,384]{1,0:T(8,128)(2,1)S(1)}, bf16[176,384]{1,0:T(8,128)(2,1)S(1)}, u32[]{:S(2)}, u32[]{:S(2)}) collective-permute-start(bf16[176,384]{1,0:T(8,128)(2,1)S(1)} %fusion.23), channel_id=1, source_target_pairs={{0,4},{1,5},{2,6},{3,7},{4,0},{5,1},{6,2},{7,3},{8,12},{9,13},{10,... | collective-permute-start | bytes 405512 | tf_op jit(solution)/shard_map/ppermute | solution.py:63
  37.4 12.4 %collective-permute-start.6 = (bf16[176,384]{1,0:T(8,128)(2,1)S(1)}, bf16[176,384]{1,0:T(8,128)(2,1)S(1)}, u32[]{:S(2)}, u32[]{:S(2)}) collective-permute-start(bf16[176,384]{1,0:T(8,128)(2,1)S(1)} %fusion.23), channel_id=1, source_target_pairs={{0,8},{1,9},{2,10},{3,11},{4,12},{5,13},{6,14},{7,15},{8,0},{9,1},... | collective-permute-start | bytes 405512 | tf_op jit(solution)/shard_map/ppermute | solution.py:63
  50.0 16.0 %collective-permute-start.9 = (bf16[12,160,384]{2,1,0:T(8,128)(2,1)S(1)}, bf16[12,160,384]{2,1,0:T(8,128)(2,1)S(1)}, u32[]{:S(2)}, u32[]{:S(2)}) collective-permute-start(bf16[12,160,384]{2,1,0:T(8,128)(2,1)S(1)} %constant_dynamic-update-slice_fusion.refs_2_.refs_7_), channel_id=1, source_target_pairs={{0,1},{1,0},{2,3},{3,2},{4,5},{5,4},{6,7},{7,6},{8,9},{9,8},{10,11... | collective-permute-start | bytes 4423688 | tf_op jit(solution)/shard_map/ppermute | solution.py:60
  50.1 14.1 %collective-permute-start.8 = (bf16[4,160,384]{2,1,0:T(8,128)(2,1)S(1)}, bf16[4,160,384]{2,1,0:T(8,128)(2,1)S(1)}, u32[]{:S(2)}, u32[]{:S(2)}) collective-permute-start(bf16[4,160,384]{2,1,0:T(8,128)(2,1)S(1)} %collective-permute-done.4), channel_id=1, source_target_pairs={{0,16},{1,17},{2,18},{3,19},{4,20},{5,21},{6,22},{7,23},{8,24},{9,... | collective-permute-start | bytes 1474568 | tf_op jit(solution)/shard_map/ppermute | solution.py:51
  52.3 26.8 %collective-permute-start.11 = (bf16[4,176,384]{2,1,0:T(8,128)(2,1)S(1)}, bf16[4,176,384]{2,1,0:T(8,128)(2,1)S(1)}, u32[]{:S(2)}, u32[]{:S(2)}) collective-permute-start(bf16[4,176,384]{2,1,0:T(8,128)(2,1)S(1)} %pad_maximum_fusion), channel_id=1, source_target_pairs={{0,16},{1,17},{2,18},{3,19},{4,20},{5,21},{6,22},{7,23},{8,24},{9,... | collective-permute-start | bytes 1622024 | tf_op jit(solution)/shard_map/ppermute | solution.py:51
  53.0 26.1 %collective-permute-start.12 = (bf16[4,176,384]{2,1,0:T(8,128)(2,1)S(1)}, bf16[4,176,384]{2,1,0:T(8,128)(2,1)S(1)}, u32[]{:S(2)}, u32[]{:S(2)}) collective-permute-start(bf16[4,176,384]{2,1,0:T(8,128)(2,1)S(1)} %pad_maximum_fusion), channel_id=1, source_target_pairs={{0,2},{1,3},{2,0},{3,1},{4,6},{5,7},{6,4},{7,5},{8,10},{9,11},{10,... | collective-permute-start | bytes 1622024 | tf_op jit(solution)/shard_map/ppermute | solution.py:54
  80.5 16.7 %collective-permute-start.14 = (bf16[12,176,384]{2,1,0:T(8,128)(2,1)S(1)}, bf16[12,176,384]{2,1,0:T(8,128)(2,1)}, u32[]{:S(2)}, u32[]{:S(2)}) collective-permute-start(bf16[12,176,384]{2,1,0:T(8,128)(2,1)S(1)} %constant_dynamic-update-slice_fusion.6.refs_5_), channel_id=1, source_target_pairs={{0,1},{1,0},{2,3},{3,2},{4,5},{5,4},{6,7},{7,6},{8,9},{9,8},{10,11... | collective-permute-start | bytes 4866056 | tf_op jit(solution)/shard_map/ppermute | solution.py:60
  80.6 14.6 %collective-permute-start.13 = (bf16[4,176,384]{2,1,0:T(8,128)(2,1)S(1)}, bf16[4,176,384]{2,1,0:T(8,128)(2,1)S(1)}, u32[]{:S(2)}, u32[]{:S(2)}) collective-permute-start(bf16[4,176,384]{2,1,0:T(8,128)(2,1)S(1)} %collective-permute-done.12), channel_id=1, source_target_pairs={{0,16},{1,17},{2,18},{3,19},{4,20},{5,21},{6,22},{7,23},{8,24},{9,... | collective-permute-start | bytes 1622024 | tf_op jit(solution)/shard_map/ppermute | solution.py:51
  125.7 14.9 %collective-permute-start.17 = (bf16[2,8,176,384]{3,2,1,0:T(8,128)(2,1)}, bf16[2,8,176,384]{3,2,1,0:T(8,128)(2,1)}, u32[]{:S(2)}, u32[]{:S(2)}) collective-permute-start(bf16[2,8,176,384]{3,2,1,0:T(8,128)(2,1)} %get-tuple-element.99), channel_id=1, source_target_pairs={{0,1},{1,0},{2,3},{3,2},{4,5},{5,4},{6,7},{7,6},{8,9},{9,8},{10,11... | collective-permute-start | bytes 6488072 | tf_op jit(solution)/shard_map/ppermute | solution.py:60
  137.1 34.2 %collective-permute-start.20 = (bf16[4,96,1024]{2,1,0:T(8,128)(2,1)}, bf16[4,96,1024]{2,1,0:T(8,128)(2,1)}, u32[]{:S(2)}, u32[]{:S(2)}) collective-permute-start(bf16[4,96,1024]{2,1,0:T(8,128)(2,1)} %get-tuple-element.139), channel_id=1, source_target_pairs={{0,16},{1,17},{2,18},{3,19},{4,20},{5,21},{6,22},{7,23},{8,24},{9,... | collective-permute-start | bytes 2359304 | tf_op jit(solution)/shard_map/ppermute | solution.py:51
  138.4 36.5 %collective-permute-start.21 = (bf16[4,96,1024]{2,1,0:T(8,128)(2,1)}, bf16[4,96,1024]{2,1,0:T(8,128)(2,1)}, u32[]{:S(2)}, u32[]{:S(2)}) collective-permute-start(bf16[4,96,1024]{2,1,0:T(8,128)(2,1)} %get-tuple-element.138), channel_id=1, source_target_pairs={{0,2},{1,3},{2,0},{3,1},{4,6},{5,7},{6,4},{7,5},{8,10},{9,11},{10,... | collective-permute-start | bytes 2359304 | tf_op jit(solution)/shard_map/ppermute | solution.py:54
  140.1 34.9 %collective-permute-start.22 = (bf16[4,96,1024]{2,1,0:T(8,128)(2,1)}, bf16[4,96,1024]{2,1,0:T(8,128)(2,1)}, u32[]{:S(2)}, u32[]{:S(2)}) collective-permute-start(bf16[4,96,1024]{2,1,0:T(8,128)(2,1)} %get-tuple-element.137), channel_id=1, source_target_pairs={{0,18},{1,19},{2,16},{3,17},{4,22},{5,23},{6,20},{7,21},{8,26},{9,... | collective-permute-start | bytes 2359304 | tf_op jit(solution)/shard_map/ppermute | solution.py:57
  143.2 25.0 %collective-permute-start.18 = (bf16[2,2,176,384]{3,2,1,0:T(8,128)(2,1)}, bf16[2,2,176,384]{3,2,1,0:T(8,128)(2,1)}, u32[]{:S(2)}, u32[]{:S(2)}) collective-permute-start(bf16[2,2,176,384]{3,2,1,0:T(8,128)(2,1)} %get-tuple-element.106), channel_id=1, source_target_pairs={{0,4},{1,5},{2,6},{3,7},{4,0},{5,1},{6,2},{7,3},{8,12},{9,13},{10,... | collective-permute-start | bytes 1622024 | tf_op jit(solution)/shard_map/ppermute | solution.py:63
  145.2 23.6 %collective-permute-start.19 = (bf16[2,2,176,384]{3,2,1,0:T(8,128)(2,1)}, bf16[2,2,176,384]{3,2,1,0:T(8,128)(2,1)}, u32[]{:S(2)}, u32[]{:S(2)}) collective-permute-start(bf16[2,2,176,384]{3,2,1,0:T(8,128)(2,1)} %get-tuple-element.107), channel_id=1, source_target_pairs={{0,4},{1,5},{2,6},{3,7},{4,0},{5,1},{6,2},{7,3},{8,12},{9,13},{10,... | collective-permute-start | bytes 1622024 | tf_op jit(solution)/shard_map/ppermute | solution.py:63
  168.8 11.8 %collective-permute-start.23 = (bf16[2,8,160,384]{3,2,1,0:T(8,128)(2,1)}, bf16[2,8,160,384]{3,2,1,0:T(8,128)(2,1)}, u32[]{:S(2)}, u32[]{:S(2)}) collective-permute-start(bf16[2,8,160,384]{3,2,1,0:T(8,128)(2,1)} %get-tuple-element.114), channel_id=1, source_target_pairs={{0,1},{1,0},{2,3},{3,2},{4,5},{5,4},{6,7},{7,6},{8,9},{9,8},{10,11... | collective-permute-start | bytes 5898248 | tf_op jit(solution)/shard_map/ppermute | solution.py:60
  174.9 26.7 %collective-permute-start.24 = (bf16[2,2,176,384]{3,2,1,0:T(8,128)(2,1)}, bf16[2,2,176,384]{3,2,1,0:T(8,128)(2,1)}, u32[]{:S(2)}, u32[]{:S(2)}) collective-permute-start(bf16[2,2,176,384]{3,2,1,0:T(8,128)(2,1)} %fusion), channel_id=1, source_target_pairs={{0,8},{1,9},{2,10},{3,11},{4,12},{5,13},{6,14},{7,15},{8,0},{9,1},... | collective-permute-start | bytes 1622024 | tf_op jit(solution)/shard_map/ppermute | solution.py:63
  180.6 17.1 %collective-permute-start.25 = (bf16[2,96,1024]{2,1,0:T(8,128)(2,1)S(1)}, bf16[2,96,1024]{2,1,0:T(8,128)(2,1)}, u32[]{:S(2)}, u32[]{:S(2)}) collective-permute-start(bf16[2,96,1024]{2,1,0:T(8,128)(2,1)S(1)} %fold_column.1), channel_id=1, source_target_pairs={{0,4},{1,5},{2,6},{3,7},{4,0},{5,1},{6,2},{7,3},{8,12},{9,13},{10,... | collective-permute-start | bytes 1179656 | tf_op jit(solution)/shard_map/ppermute | solution.py:63
  183.3 22.8 %collective-permute-start.26 = (bf16[4,160,384]{2,1,0:T(8,128)(2,1)}, bf16[4,160,384]{2,1,0:T(8,128)(2,1)}, u32[]{:S(2)}, u32[]{:S(2)}) collective-permute-start(bf16[4,160,384]{2,1,0:T(8,128)(2,1)} %get-tuple-element.140), channel_id=1, source_target_pairs={{0,16},{1,17},{2,18},{3,19},{4,20},{5,21},{6,22},{7,23},{8,24},{9,... | collective-permute-start | bytes 1474568 | tf_op jit(solution)/shard_map/ppermute | solution.py:51
  184.7 22.9 %collective-permute-start.27 = (bf16[4,160,384]{2,1,0:T(8,128)(2,1)}, bf16[4,160,384]{2,1,0:T(8,128)(2,1)}, u32[]{:S(2)}, u32[]{:S(2)}) collective-permute-start(bf16[4,160,384]{2,1,0:T(8,128)(2,1)} %get-tuple-element.142), channel_id=1, source_target_pairs={{0,2},{1,3},{2,0},{3,1},{4,6},{5,7},{6,4},{7,5},{8,10},{9,11},{10,... | collective-permute-start | bytes 1474568 | tf_op jit(solution)/shard_map/ppermute | solution.py:54
  185.5 22.1 %collective-permute-start.28 = (bf16[4,160,384]{2,1,0:T(8,128)(2,1)}, bf16[4,160,384]{2,1,0:T(8,128)(2,1)}, u32[]{:S(2)}, u32[]{:S(2)}) collective-permute-start(bf16[4,160,384]{2,1,0:T(8,128)(2,1)} %get-tuple-element.141), channel_id=1, source_target_pairs={{0,18},{1,19},{2,16},{3,17},{4,22},{5,23},{6,20},{7,21},{8,26},{9,... | collective-permute-start | bytes 1474568 | tf_op jit(solution)/shard_map/ppermute | solution.py:57
  203.0 11.0 %collective-permute-start.29 = (bf16[2,176,384]{2,1,0:T(8,128)(2,1)S(1)}, bf16[2,176,384]{2,1,0:T(8,128)(2,1)S(1)}, u32[]{:S(2)}, u32[]{:S(2)}) collective-permute-start(bf16[2,176,384]{2,1,0:T(8,128)(2,1)S(1)} %fusion.6), channel_id=1, source_target_pairs={{0,2},{1,3},{2,0},{3,1},{4,6},{5,7},{6,4},{7,5},{8,10},{9,11},{10,... | collective-permute-start | bytes 811016 | tf_op jit(solution)/shard_map/ppermute | solution.py:54
  206.0 14.7 %collective-permute-start.30 = (bf16[96,1024]{1,0:T(8,128)(2,1)S(1)}, bf16[96,1024]{1,0:T(8,128)(2,1)S(1)}, u32[]{:S(2)}, u32[]{:S(2)}) collective-permute-start(bf16[96,1024]{1,0:T(8,128)(2,1)S(1)} %fusion.11), channel_id=1, source_target_pairs={{0,8},{1,9},{2,10},{3,11},{4,12},{5,13},{6,14},{7,15},{8,0},{9,1},... | collective-permute-start | bytes 589832 | tf_op jit(solution)/shard_map/ppermute | solution.py:63
  209.5 16.1 %collective-permute-start.32 = (bf16[160,384]{1,0:T(8,128)(2,1)S(1)}, bf16[160,384]{1,0:T(8,128)(2,1)S(1)}, u32[]{:S(2)}, u32[]{:S(2)}) collective-permute-start(bf16[160,384]{1,0:T(8,128)(2,1)S(1)} %get-tuple-element.148), channel_id=1, source_target_pairs={{0,4},{1,5},{2,6},{3,7},{4,0},{5,1},{6,2},{7,3},{8,12},{9,13},{10,... | collective-permute-start | bytes 368648 | tf_op jit(solution)/shard_map/ppermute | solution.py:63
  211.3 14.3 %collective-permute-start.33 = (bf16[160,384]{1,0:T(8,128)(2,1)S(1)}, bf16[160,384]{1,0:T(8,128)(2,1)S(1)}, u32[]{:S(2)}, u32[]{:S(2)}) collective-permute-start(bf16[160,384]{1,0:T(8,128)(2,1)S(1)} %get-tuple-element.147), channel_id=1, source_target_pairs={{0,8},{1,9},{2,10},{3,11},{4,12},{5,13},{6,14},{7,15},{8,0},{9,1},... | collective-permute-start | bytes 368648 | tf_op jit(solution)/shard_map/ppermute | solution.py:63
  211.6 14.1 %collective-permute-start.34 = (bf16[160,384]{1,0:T(8,128)(2,1)S(1)}, bf16[160,384]{1,0:T(8,128)(2,1)S(1)}, u32[]{:S(2)}, u32[]{:S(2)}) collective-permute-start(bf16[160,384]{1,0:T(8,128)(2,1)S(1)} %get-tuple-element.146), channel_id=1, source_target_pairs={{0,12},{1,13},{2,14},{3,15},{4,8},{5,9},{6,10},{7,11},{8,4},{9,5},... | collective-permute-start | bytes 368648 | tf_op jit(solution)/shard_map/ppermute | solution.py:63
  222.2 25.7 %collective-permute-start.42 = (bf16[96,1024]{1,0:T(8,128)(2,1)S(1)}, bf16[96,1024]{1,0:T(8,128)(2,1)S(1)}, u32[]{:S(2)}, u32[]{:S(2)}) collective-permute-start(bf16[96,1024]{1,0:T(8,128)(2,1)S(1)} %fusion.13.refs_0_.refs_6_), channel_id=1, source_target_pairs={{0,16},{1,17},{2,18},{3,19},{4,20},{5,21},{6,22},{7,23},{8,24},{9,... | collective-permute-start | bytes 589832 | tf_op jit(solution)/shard_map/ppermute | solution.py:51
  224.4 23.6 %collective-permute-start.41 = (bf16[176,384]{1,0:T(8,128)(2,1)S(1)}, bf16[176,384]{1,0:T(8,128)(2,1)S(1)}, u32[]{:S(2)}, u32[]{:S(2)}) collective-permute-start(bf16[176,384]{1,0:T(8,128)(2,1)S(1)} %fusion.17.refs_1_.refs_4_), channel_id=1, source_target_pairs={{0,16},{1,17},{2,18},{3,19},{4,20},{5,21},{6,22},{7,23},{8,24},{9,... | collective-permute-start | bytes 405512 | tf_op jit(solution)/shard_map/ppermute | solution.py:51
  226.5 21.4 %collective-permute-start.40 = (bf16[160,384]{1,0:T(8,128)(2,1)S(1)}, bf16[160,384]{1,0:T(8,128)(2,1)S(1)}, u32[]{:S(2)}, u32[]{:S(2)}) collective-permute-start(bf16[160,384]{1,0:T(8,128)(2,1)S(1)} %get-tuple-element.122.refs_2_), channel_id=1, source_target_pairs={{0,16},{1,17},{2,18},{3,19},{4,20},{5,21},{6,22},{7,23},{8,24},{9,... | collective-permute-start | bytes 368648 | tf_op jit(solution)/shard_map/ppermute | solution.py:51
  (48 other events, 334.9 us)
Sparse Core Ops, SparseCore 0:
  10.9 86.5 all-gather.1

commit v7 on v6

--- a/solution.py
+++ b/solution.py
@@ -801,7 +801,7 @@
         three.send_core()
         two_keep, two_sent = out_grads
         two_got = grid.flip_core(two_sent)
-        cut = pairs // 3
+        cut = max(1, pairs // 6)
         d_qkv = [attend_back(qkv, d_context, counts, 0, cut)]
         three.got, d_qkv = after(three.got, d_qkv)
         sides = three.load_sides()

time: 264 us -> 262 us (level)
  local copies, waits for them, and re-layouts: 11.7 us -> 8.78 us
    unnamed x81 -> x77, local copies, waits for them, and re-layouts: 10.3 us -> 7.32 us
  transfers between devices with their start and end apart: 44 -> 44, of which waited for: 20 -> 20; matrix products, arithmetic and copies ran while one was open for 8% -> 9% of each run, Pallas kernels for 15% -> 15%
where the time goes in v7:
time: 262 us
  waiting for transfers between devices  79.3 us (30%)
  Pallas kernels  72.5 us (28%)
  starting transfers between devices  58.1 us (22%)
  other arithmetic  23 us (9%)
  between operations  20.1 us (8%)
  local copies, waits for them, and re-layouts  8.78 us (3%)
    ppermute x16, waiting for transfers between devices, swap_z(): lax.ppermute(v, EVERY, self.move(lambda x, z, y, c: (x, z ^ bit, y, c)))  42.4 us
    ppermute x16, starting transfers between devices, swap_z(): lax.ppermute(v, EVERY, self.move(lambda x, z, y, c: (x, z ^ bit, y, c)))  31.9 us
    pallas_call x1, Pallas kernels, feed_forward(): pl.pallas_call(body, grid=(steps,), out_shape=[jax.ShapeDtypeStruct((leng...  27.5 us
    ppermute x11, waiting for transfers between devices, flip_x(): lax.ppermute(v, EVERY, self.move(lambda x, z, y, c: (1 - x, z, y, c)))  24.1 us
    pallas_call x2, Pallas kernels, attend_back(): pl.pallas_call(body, grid=(width // pair,), out_shape=jax.ShapeDtypeStruc...  15 us
    ppermute x11, starting transfers between devices, flip_x(): lax.ppermute(v, EVERY, self.move(lambda x, z, y, c: (1 - x, z, y, c)))  14 us
    ppermute x6, starting transfers between devices, flip_y(): lax.ppermute(v, EVERY, self.move(lambda x, z, y, c: (x, z, 1 - y, c)))  9.41 us
    convert_element_type x5, other arithmetic, leave(): return leave.astype(LOW)  8.57 us
  transfers between devices with their start and end apart: 44, of which 20 were waited for; matrix products, arithmetic and copies ran while one was open for 9% of the time, Pallas kernels for 15%

profile of v7, /device:TPU:0, one launch (start us, length us, event | category | flops | bytes accessed | tf_op | source)
XLA Modules:
  0.0 261.8 jit_solution(854271399161684673)
XLA Ops:
  7.2 2.0 convert_element_type.307
  10.3 3.1 %collective-permute-start = (bf16[160,384]{1,0:T(8,128)(2,1)S(1)}, bf16[160,384]{1,0:T(8,128)(2,1)S(1)}, u32[]{:S(2)}, u32[]{:S(2)}) collective-permute-start(bf16[160,384]{1,0:T(8,128)(2,1)S(1)} %bitcast.190), channel_id=1, source_target_pairs={{0,4},{1,5},{2,6},{3,7},{4,0},{5,1},{6,2},{7,3},{8,12},{9,13},{10,... | collective-permute-start | bytes 368648 | tf_op jit(solution)/shard_map/ppermute | solution.py:63
  13.4 2.6 collective-permute-start.1
  18.1 7.7 %collective-permute-done.1 = bf16[160,384]{1,0:T(8,128)(2,1)S(1)} collective-permute-done((bf16[160,384]{1,0:T(8,128)(2,1)S(1)}, bf16[160,384]{1,0:T(8,128)(2,1)S(1)}, u32[]{:S(2)}, u32[]{:S(2)}) %collective-permute-start.1) | collective-permute-done | bytes 122912 | tf_op jit(solution)/shard_map/ppermute | solution.py:63
  29.0 8.4 %collective-permute-start.5 = (bf16[176,384]{1,0:T(8,128)(2,1)S(1)}, bf16[176,384]{1,0:T(8,128)(2,1)S(1)}, u32[]{:S(2)}, u32[]{:S(2)}) collective-permute-start(bf16[176,384]{1,0:T(8,128)(2,1)S(1)} %fusion.23), channel_id=1, source_target_pairs={{0,4},{1,5},{2,6},{3,7},{4,0},{5,1},{6,2},{7,3},{8,12},{9,13},{10,... | collective-permute-start | bytes 405512 | tf_op jit(solution)/shard_map/ppermute | solution.py:63
  37.4 2.3 collective-permute-start.6
  41.3 2.0 collective-permute-done.5
  43.3 6.5 %collective-permute-done.6 = bf16[176,384]{1,0:T(8,128)(2,1)S(1)} collective-permute-done((bf16[176,384]{1,0:T(8,128)(2,1)S(1)}, bf16[176,384]{1,0:T(8,128)(2,1)S(1)}, u32[]{:S(2)}, u32[]{:S(2)}) %collective-permute-start.6) | collective-permute-done | bytes 135200 | tf_op jit(solution)/shard_map/ppermute | solution.py:63
  54.4 9.8 %collective-permute-done.8.refs_3_.refs_8_ = bf16[4,160,384]{2,1,0:T(8,128)(2,1)S(1)} collective-permute-done((bf16[4,160,384]{2,1,0:T(8,128)(2,1)S(1)}, bf16[4,160,384]{2,1,0:T(8,128)(2,1)S(1)}, u32[]{:S(2)}, u32[]{:S(2)}) %collective-permute-start.8) | collective-permute-done | bytes 491552 | tf_op jit(solution)/shard_map/ppermute | solution.py:51
  66.1 4.8 %project_in.1 = (bf16[512,768]{1,0:T(8,128)(2,1)S(1)}, bf16[3,512,768]{2,1,0:T(8,128)(2,1)S(1)}, f32[16,768]{1,0:T(8,128)S(1)}) custom-call(bf16[512,768]{1,0:T(8,128)(2,1)S(1)} %bitcast.169, f32[16,768]{1,0:T(8,128)S(1)} %broadcast_in_dim.21.refs_1_, bf16[12,160,384]{2,1,0:T(8,128)(2,1)S(1)} %constant_dynamic-update-slice_fusion.refs_2_.refs_7_, ...), custom_call_target="tpu_custom_call" | custom-call | flops 8000000 | tf_op jit(solution)/shard_map/project_in/pallas_call | solution.py:309
  70.9 7.3 %attend.1.refs_2_ = bf16[512,768]{1,0:T(8,128)(2,1)S(1)} custom-call(s32[1]{0:T(128)S(6)} %copy.77.counts_ref.refs_0_, bf16[3,512,768]{2,1,0:T(8,128)(2,1)S(1)} %get-tuple-element.81.qkv_ref), custom_call_target="tpu_custom_call" | custom-call | flops 9000000 | tf_op jit(solution)/shard_map/attend/pallas_call | solution.py:347
  82.0 13.2 %collective-permute-done.13.refs_6_ = bf16[4,176,384]{2,1,0:T(8,128)(2,1)S(1)} collective-permute-done((bf16[4,176,384]{2,1,0:T(8,128)(2,1)S(1)}, bf16[4,176,384]{2,1,0:T(8,128)(2,1)S(1)}, u32[]{:S(2)}, u32[]{:S(2)}) %collective-permute-start.13) | collective-permute-done | bytes 540704 | tf_op jit(solution)/shard_map/ppermute | solution.py:51
  95.2 2.0 collective-permute-done.15.refs_8_
  98.0 27.5 %feed_forward.1 = (bf16[512,768]{1,0:T(8,128)(2,1)}, f32[512,768]{1,0:T(8,128)}, bf16[512,768]{1,0:T(8,128)(2,1)}, f32[8,768]{1,0:T(8,128)}, bf16[2,8,176,384]{3...) custom-call(s32[1]{0:T(128)S(6)} %copy.77.counts_ref.refs_0_, ...), custom_call_target="tpu_custom_call" | custom-call | flops 28000000 | tf_op jit(solution)/shard_map/feed_forward/pallas_call | solution.py:513
  127.3 2.4 attend_back.2.refs_5_
  131.6 3.9 %fusion.4 = (bf16[4,96,1024]{2,1,0:T(8,128)(2,1)}, bf16[4,96,1024]{2,1,0:T(8,128)(2,1)}, bf16[4,96,1024]{2,1,0:T(8,128)(2,1)}) fusion(bf16[2,4,2,96,1024]{4,3,2,1,0:T(8,128)(2,1)} %bitcast.23, s32[]{:T(128)S(6)} %select_n.176, s32[]{:T(128)S(6)} %select_n.182, bf16[2,4,2,96,1024]{4,3,2,1,0:T(8,128)(2,1)S(1)} %bitcast.171, s32[]{:T(128)S(6)} %select_n.180, ...), kind=kLoop, calls=%fused_computation.21 | loop fusion | flops 4718592 | bytes 7077904 | tf_op jit(solution)/shard_map/convert_element_type | solution.py:129
  143.8 12.6 %attend_back.3.refs_6_ = bf16[3,512,640]{2,1,0:T(8,128)(2,1)S(1)} custom-call(s32[1]{0:T(128)S(6)} %copy.77.counts_ref.refs_0_, bf16[3,512,768]{2,1,0:T(8,128)(2,1)S(1)} %get-tuple-element.81.qkv_ref, bf16[512,768]{1,0:T(8,128)(2,1)S(1)} %copy-done.8), custom_call_target="tpu_custom_call" | custom-call | flops 13500000 | tf_op jit(solution)/shard_map/attend_back/pallas_call | solution.py:385
  159.0 8.3 %project_back.1 = (bf16[512,768]{1,0:T(8,128)(2,1)}, bf16[2,8,160,384]{3,2,1,0:T(8,128)(2,1)S(1)}, bf16[2,8,160,384]{3,2,1,0:T(8,128)(2,1)}) custom-call(bf16[512,768]{1,0:T(8,128)(2,1)S(1)} %bitcast.170, bf16[512,768]{1,0:T(8,128)(2,1)S(1)} %copy-done.20, f32[512,768]{1,0:T(8,128)S(1)} %copy-done.17, f32[16,768]{1,0:T(8,128)S(1)} %copy-done.22, ...), custom_call_target="tpu_custom_call" | custom-call | flops 11000000 | tf_op jit(solution)/shard_map/project_back/pallas_call | solution.py:582
  167.5 3.0 %fusion = bf16[2,2,176,384]{3,2,1,0:T(8,128)(2,1)} fusion(bf16[2,2,2,2,176,384]{5,4,3,2,1,0:T(8,128)(2,1)} %bitcast.27, s32[]{:T(128)S(6)} %select_n.186, s32[]{:T(128)S(6)} %select_n.188, bf16[2,2,2,2,176,384]{5,4,3,2,1,0:T(8,128)(2,1)} %bitcast.176, s32[]{:T(128)S(6)} %select_n.185, bf16[1,2,2,176,384]{4,3,0,2,1:T(8,128)(2,1)} %bitcast.34, ...), kind=kLoop, calls=%fused_computation.13 | loop fusion | flops 1892352 | bytes 2703372 | tf_op jit(solution)/shard_map/convert_element_type | solution.py:166
  170.5 2.9 %collective-permute-done.21.refs_1_ = bf16[4,96,1024]{2,1,0:T(8,128)(2,1)} collective-permute-done((bf16[4,96,1024]{2,1,0:T(8,128)(2,1)}, bf16[4,96,1024]{2,1,0:T(8,128)(2,1)}, u32[]{:S(2)}, u32[]{:S(2)}) %collective-permute-start.21) | collective-permute-done | bytes 786464 | tf_op jit(solution)/shard_map/ppermute | solution.py:54
  173.3 3.2 %collective-permute-start.24 = (bf16[2,2,176,384]{3,2,1,0:T(8,128)(2,1)}, bf16[2,2,176,384]{3,2,1,0:T(8,128)(2,1)}, u32[]{:S(2)}, u32[]{:S(2)}) collective-permute-start(bf16[2,2,176,384]{3,2,1,0:T(8,128)(2,1)} %fusion), channel_id=1, source_target_pairs={{0,8},{1,9},{2,10},{3,11},{4,12},{5,13},{6,14},{7,15},{8,0},{9,1},... | collective-permute-start | bytes 1622024 | tf_op jit(solution)/shard_map/ppermute | solution.py:63
  176.5 2.2 fold_column.1
  178.8 2.6 %fusion.7 = (bf16[4,160,384]{2,1,0:T(8,128)(2,1)}, bf16[4,160,384]{2,1,0:T(8,128)(2,1)}, bf16[4,160,384]{2,1,0:T(8,128)(2,1)}) fusion(bf16[2,4,2,160,384]{4,3,2,1,0:T(8,128)(2,1)} %bitcast.45, s32[]{:T(128)S(6)} %select_n.176, s32[]{:T(128)S(6)} %select_n.179, bf16[2,4,2,160,384]{4,3,2,1,0:T(8,128)(2,1)S(1)} %bitcast.174, s32[]{:T(128)S(6)} %select_n.182, ...), kind=kLoop, calls=%fused_computation.30 | loop fusion | flops 2949120 | bytes 4423696 | tf_op jit(solution)/shard_map/convert_element_type | solution.py:129
  184.9 11.2 %collective-permute-done.25 = bf16[2,96,1024]{2,1,0:T(8,128)(2,1)} collective-permute-done((bf16[2,96,1024]{2,1,0:T(8,128)(2,1)S(1)}, bf16[2,96,1024]{2,1,0:T(8,128)(2,1)}, u32[]{:S(2)}, u32[]{:S(2)}) %collective-permute-start.25) | collective-permute-done | bytes 393248 | tf_op jit(solution)/shard_map/ppermute | solution.py:63
  196.1 4.0 %collective-permute-done.24 = bf16[2,2,176,384]{3,2,1,0:T(8,128)(2,1)} collective-permute-done((bf16[2,2,176,384]{3,2,1,0:T(8,128)(2,1)}, bf16[2,2,176,384]{3,2,1,0:T(8,128)(2,1)}, u32[]{:S(2)}, u32[]{:S(2)}) %collective-permute-start.24) | collective-permute-done | bytes 540704 | tf_op jit(solution)/shard_map/ppermute | solution.py:63
  209.7 2.4 collective-permute-start.34
  214.1 5.0 %collective-permute-done.30 = bf16[96,1024]{1,0:T(8,128)(2,1)S(1)} collective-permute-done((bf16[96,1024]{1,0:T(8,128)(2,1)S(1)}, bf16[96,1024]{1,0:T(8,128)(2,1)S(1)}, u32[]{:S(2)}, u32[]{:S(2)}) %collective-permute-start.30) | collective-permute-done | bytes 196640 | tf_op jit(solution)/shard_map/ppermute | solution.py:63
  228.4 2.6 collective-permute-start.36
  232.7 2.5 collective-permute-start.37
  238.5 2.2 collective-permute-done.38
  241.3 2.7 %collective-permute-start.39 = (f32[]{:T(128)}, f32[]{:T(128)}, u32[]{:S(2)}, u32[]{:S(2)}) collective-permute-start(f32[]{:T(128)} %add.547), channel_id=1, source_target_pairs={{0,8},{1,9},{2,10},{3,11},{4,12},{5,13},{6,14},{7,15},{8,0},{9,1},... | collective-permute-start | bytes 20 | tf_op jit(solution)/shard_map/ppermute | solution.py:63
  247.3 6.6 %update.1 = (f32[4,48,768]{2,1,0:T(8,128)}, f32[2,48,2048]{2,1,0:T(8,128)}, f32[128,768]{1,0:T(8,128)}, f32[2,48]{1,0:T(2,128)}, f32[4,48,768]{2,1,0:T(8,128)}, ...) custom-call(f32[1]{0:T(128)} %bitcast.72.refs_0_, ...), custom_call_target="tpu_custom_call" | custom-call | flops 4000000 | tf_op jit(solution)/shard_map/update/pallas_call | solution.py:718
  (175 shorter events, 62.4 us)
Async XLA Ops:
  7.2 90.3 %all-gather.2.cloned.1.call-start = ((), (), s32[]{:S(2)}) async-start(), calls=%async_computation | async-start | bytes 6684672 | tf_op jit(solution)/shard_map/all_gather | solution.py:770
  13.4 12.4 %collective-permute-start.1 = (bf16[160,384]{1,0:T(8,128)(2,1)S(1)}, bf16[160,384]{1,0:T(8,128)(2,1)S(1)}, u32[]{:S(2)}, u32[]{:S(2)}) collective-permute-start(bf16[160,384]{1,0:T(8,128)(2,1)S(1)} %bitcast.191), channel_id=1, source_target_pairs={{0,8},{1,9},{2,10},{3,11},{4,12},{5,13},{6,14},{7,15},{8,0},{9,1},... | collective-permute-start | bytes 368648 | tf_op jit(solution)/shard_map/ppermute | solution.py:63
  25.9 24.0 %collective-permute-start.3 = (bf16[4,160,384]{2,1,0:T(8,128)(2,1)S(1)}, bf16[4,160,384]{2,1,0:T(8,128)(2,1)S(1)}, u32[]{:S(2)}, u32[]{:S(2)}) collective-permute-start(bf16[4,160,384]{2,1,0:T(8,128)(2,1)S(1)} %pad_maximum_fusion.1), channel_id=1, source_target_pairs={{0,16},{1,17},{2,18},{3,19},{4,20},{5,21},{6,22},{7,23},{8,24},{9,... | collective-permute-start | bytes 1474568 | tf_op jit(solution)/shard_map/ppermute | solution.py:51
  27.4 22.4 %collective-permute-start.4 = (bf16[4,160,384]{2,1,0:T(8,128)(2,1)S(1)}, bf16[4,160,384]{2,1,0:T(8,128)(2,1)S(1)}, u32[]{:S(2)}, u32[]{:S(2)}) collective-permute-start(bf16[4,160,384]{2,1,0:T(8,128)(2,1)S(1)} %pad_maximum_fusion.1), channel_id=1, source_target_pairs={{0,2},{1,3},{2,0},{3,1},{4,6},{5,7},{6,4},{7,5},{8,10},{9,11},{10,... | collective-permute-start | bytes 1474568 | tf_op jit(solution)/shard_map/ppermute | solution.py:54
  29.0 14.3 %collective-permute-start.5 = (bf16[176,384]{1,0:T(8,128)(2,1)S(1)}, bf16[176,384]{1,0:T(8,128)(2,1)S(1)}, u32[]{:S(2)}, u32[]{:S(2)}) collective-permute-start(bf16[176,384]{1,0:T(8,128)(2,1)S(1)} %fusion.23), channel_id=1, source_target_pairs={{0,4},{1,5},{2,6},{3,7},{4,0},{5,1},{6,2},{7,3},{8,12},{9,13},{10,... | collective-permute-start | bytes 405512 | tf_op jit(solution)/shard_map/ppermute | solution.py:63
  37.4 12.4 %collective-permute-start.6 = (bf16[176,384]{1,0:T(8,128)(2,1)S(1)}, bf16[176,384]{1,0:T(8,128)(2,1)S(1)}, u32[]{:S(2)}, u32[]{:S(2)}) collective-permute-start(bf16[176,384]{1,0:T(8,128)(2,1)S(1)} %fusion.23), channel_id=1, source_target_pairs={{0,8},{1,9},{2,10},{3,11},{4,12},{5,13},{6,14},{7,15},{8,0},{9,1},... | collective-permute-start | bytes 405512 | tf_op jit(solution)/shard_map/ppermute | solution.py:63
  50.0 16.0 %collective-permute-start.9 = (bf16[12,160,384]{2,1,0:T(8,128)(2,1)S(1)}, bf16[12,160,384]{2,1,0:T(8,128)(2,1)S(1)}, u32[]{:S(2)}, u32[]{:S(2)}) collective-permute-start(bf16[12,160,384]{2,1,0:T(8,128)(2,1)S(1)} %constant_dynamic-update-slice_fusion.refs_2_.refs_7_), channel_id=1, source_target_pairs={{0,1},{1,0},{2,3},{3,2},{4,5},{5,4},{6,7},{7,6},{8,9},{9,8},{10,11... | collective-permute-start | bytes 4423688 | tf_op jit(solution)/shard_map/ppermute | solution.py:60
  50.1 14.1 %collective-permute-start.8 = (bf16[4,160,384]{2,1,0:T(8,128)(2,1)S(1)}, bf16[4,160,384]{2,1,0:T(8,128)(2,1)S(1)}, u32[]{:S(2)}, u32[]{:S(2)}) collective-permute-start(bf16[4,160,384]{2,1,0:T(8,128)(2,1)S(1)} %collective-permute-done.4), channel_id=1, source_target_pairs={{0,16},{1,17},{2,18},{3,19},{4,20},{5,21},{6,22},{7,23},{8,24},{9,... | collective-permute-start | bytes 1474568 | tf_op jit(solution)/shard_map/ppermute | solution.py:51
  52.3 26.8 %collective-permute-start.11 = (bf16[4,176,384]{2,1,0:T(8,128)(2,1)S(1)}, bf16[4,176,384]{2,1,0:T(8,128)(2,1)S(1)}, u32[]{:S(2)}, u32[]{:S(2)}) collective-permute-start(bf16[4,176,384]{2,1,0:T(8,128)(2,1)S(1)} %pad_maximum_fusion), channel_id=1, source_target_pairs={{0,16},{1,17},{2,18},{3,19},{4,20},{5,21},{6,22},{7,23},{8,24},{9,... | collective-permute-start | bytes 1622024 | tf_op jit(solution)/shard_map/ppermute | solution.py:51
  53.0 26.1 %collective-permute-start.12 = (bf16[4,176,384]{2,1,0:T(8,128)(2,1)S(1)}, bf16[4,176,384]{2,1,0:T(8,128)(2,1)S(1)}, u32[]{:S(2)}, u32[]{:S(2)}) collective-permute-start(bf16[4,176,384]{2,1,0:T(8,128)(2,1)S(1)} %pad_maximum_fusion), channel_id=1, source_target_pairs={{0,2},{1,3},{2,0},{3,1},{4,6},{5,7},{6,4},{7,5},{8,10},{9,11},{10,... | collective-permute-start | bytes 1622024 | tf_op jit(solution)/shard_map/ppermute | solution.py:54
  80.5 16.7 %collective-permute-start.14 = (bf16[12,176,384]{2,1,0:T(8,128)(2,1)S(1)}, bf16[12,176,384]{2,1,0:T(8,128)(2,1)}, u32[]{:S(2)}, u32[]{:S(2)}) collective-permute-start(bf16[12,176,384]{2,1,0:T(8,128)(2,1)S(1)} %constant_dynamic-update-slice_fusion.6.refs_5_), channel_id=1, source_target_pairs={{0,1},{1,0},{2,3},{3,2},{4,5},{5,4},{6,7},{7,6},{8,9},{9,8},{10,11... | collective-permute-start | bytes 4866056 | tf_op jit(solution)/shard_map/ppermute | solution.py:60
  80.6 14.6 %collective-permute-start.13 = (bf16[4,176,384]{2,1,0:T(8,128)(2,1)S(1)}, bf16[4,176,384]{2,1,0:T(8,128)(2,1)S(1)}, u32[]{:S(2)}, u32[]{:S(2)}) collective-permute-start(bf16[4,176,384]{2,1,0:T(8,128)(2,1)S(1)} %collective-permute-done.12), channel_id=1, source_target_pairs={{0,16},{1,17},{2,18},{3,19},{4,20},{5,21},{6,22},{7,23},{8,24},{9,... | collective-permute-start | bytes 1622024 | tf_op jit(solution)/shard_map/ppermute | solution.py:51
  125.8 13.2 %collective-permute-start.17 = (bf16[2,8,176,384]{3,2,1,0:T(8,128)(2,1)}, bf16[2,8,176,384]{3,2,1,0:T(8,128)(2,1)}, u32[]{:S(2)}, u32[]{:S(2)}) collective-permute-start(bf16[2,8,176,384]{3,2,1,0:T(8,128)(2,1)} %get-tuple-element.99), channel_id=1, source_target_pairs={{0,1},{1,0},{2,3},{3,2},{4,5},{5,4},{6,7},{7,6},{8,9},{9,8},{10,11... | collective-permute-start | bytes 6488072 | tf_op jit(solution)/shard_map/ppermute | solution.py:60
  135.5 35.0 %collective-permute-start.20 = (bf16[4,96,1024]{2,1,0:T(8,128)(2,1)}, bf16[4,96,1024]{2,1,0:T(8,128)(2,1)}, u32[]{:S(2)}, u32[]{:S(2)}) collective-permute-start(bf16[4,96,1024]{2,1,0:T(8,128)(2,1)} %get-tuple-element.139), channel_id=1, source_target_pairs={{0,16},{1,17},{2,18},{3,19},{4,20},{5,21},{6,22},{7,23},{8,24},{9,... | collective-permute-start | bytes 2359304 | tf_op jit(solution)/shard_map/ppermute | solution.py:51
  136.8 36.6 %collective-permute-start.21 = (bf16[4,96,1024]{2,1,0:T(8,128)(2,1)}, bf16[4,96,1024]{2,1,0:T(8,128)(2,1)}, u32[]{:S(2)}, u32[]{:S(2)}) collective-permute-start(bf16[4,96,1024]{2,1,0:T(8,128)(2,1)} %get-tuple-element.138), channel_id=1, source_target_pairs={{0,2},{1,3},{2,0},{3,1},{4,6},{5,7},{6,4},{7,5},{8,10},{9,11},{10,... | collective-permute-start | bytes 2359304 | tf_op jit(solution)/shard_map/ppermute | solution.py:54
  138.5 34.9 %collective-permute-start.22 = (bf16[4,96,1024]{2,1,0:T(8,128)(2,1)}, bf16[4,96,1024]{2,1,0:T(8,128)(2,1)}, u32[]{:S(2)}, u32[]{:S(2)}) collective-permute-start(bf16[4,96,1024]{2,1,0:T(8,128)(2,1)} %get-tuple-element.137), channel_id=1, source_target_pairs={{0,18},{1,19},{2,16},{3,17},{4,22},{5,23},{6,20},{7,21},{8,26},{9,... | collective-permute-start | bytes 2359304 | tf_op jit(solution)/shard_map/ppermute | solution.py:57
  141.6 25.8 %collective-permute-start.18 = (bf16[2,2,176,384]{3,2,1,0:T(8,128)(2,1)}, bf16[2,2,176,384]{3,2,1,0:T(8,128)(2,1)}, u32[]{:S(2)}, u32[]{:S(2)}) collective-permute-start(bf16[2,2,176,384]{3,2,1,0:T(8,128)(2,1)} %get-tuple-element.106), channel_id=1, source_target_pairs={{0,4},{1,5},{2,6},{3,7},{4,0},{5,1},{6,2},{7,3},{8,12},{9,13},{10,... | collective-permute-start | bytes 1622024 | tf_op jit(solution)/shard_map/ppermute | solution.py:63
  143.6 23.8 %collective-permute-start.19 = (bf16[2,2,176,384]{3,2,1,0:T(8,128)(2,1)}, bf16[2,2,176,384]{3,2,1,0:T(8,128)(2,1)}, u32[]{:S(2)}, u32[]{:S(2)}) collective-permute-start(bf16[2,2,176,384]{3,2,1,0:T(8,128)(2,1)} %get-tuple-element.107), channel_id=1, source_target_pairs={{0,4},{1,5},{2,6},{3,7},{4,0},{5,1},{6,2},{7,3},{8,12},{9,13},{10,... | collective-permute-start | bytes 1622024 | tf_op jit(solution)/shard_map/ppermute | solution.py:63
  167.4 11.4 %collective-permute-start.23 = (bf16[2,8,160,384]{3,2,1,0:T(8,128)(2,1)}, bf16[2,8,160,384]{3,2,1,0:T(8,128)(2,1)}, u32[]{:S(2)}, u32[]{:S(2)}) collective-permute-start(bf16[2,8,160,384]{3,2,1,0:T(8,128)(2,1)} %get-tuple-element.114), channel_id=1, source_target_pairs={{0,1},{1,0},{2,3},{3,2},{4,5},{5,4},{6,7},{7,6},{8,9},{9,8},{10,11... | collective-permute-start | bytes 5898248 | tf_op jit(solution)/shard_map/ppermute | solution.py:60
  173.3 26.7 %collective-permute-start.24 = (bf16[2,2,176,384]{3,2,1,0:T(8,128)(2,1)}, bf16[2,2,176,384]{3,2,1,0:T(8,128)(2,1)}, u32[]{:S(2)}, u32[]{:S(2)}) collective-permute-start(bf16[2,2,176,384]{3,2,1,0:T(8,128)(2,1)} %fusion), channel_id=1, source_target_pairs={{0,8},{1,9},{2,10},{3,11},{4,12},{5,13},{6,14},{7,15},{8,0},{9,1},... | collective-permute-start | bytes 1622024 | tf_op jit(solution)/shard_map/ppermute | solution.py:63
  178.7 17.4 %collective-permute-start.25 = (bf16[2,96,1024]{2,1,0:T(8,128)(2,1)S(1)}, bf16[2,96,1024]{2,1,0:T(8,128)(2,1)}, u32[]{:S(2)}, u32[]{:S(2)}) collective-permute-start(bf16[2,96,1024]{2,1,0:T(8,128)(2,1)S(1)} %fold_column.1), channel_id=1, source_target_pairs={{0,4},{1,5},{2,6},{3,7},{4,0},{5,1},{6,2},{7,3},{8,12},{9,13},{10,... | collective-permute-start | bytes 1179656 | tf_op jit(solution)/shard_map/ppermute | solution.py:63
  181.4 23.0 %collective-permute-start.26 = (bf16[4,160,384]{2,1,0:T(8,128)(2,1)}, bf16[4,160,384]{2,1,0:T(8,128)(2,1)}, u32[]{:S(2)}, u32[]{:S(2)}) collective-permute-start(bf16[4,160,384]{2,1,0:T(8,128)(2,1)} %get-tuple-element.140), channel_id=1, source_target_pairs={{0,16},{1,17},{2,18},{3,19},{4,20},{5,21},{6,22},{7,23},{8,24},{9,... | collective-permute-start | bytes 1474568 | tf_op jit(solution)/shard_map/ppermute | solution.py:51
  182.8 22.9 %collective-permute-start.27 = (bf16[4,160,384]{2,1,0:T(8,128)(2,1)}, bf16[4,160,384]{2,1,0:T(8,128)(2,1)}, u32[]{:S(2)}, u32[]{:S(2)}) collective-permute-start(bf16[4,160,384]{2,1,0:T(8,128)(2,1)} %get-tuple-element.142), channel_id=1, source_target_pairs={{0,2},{1,3},{2,0},{3,1},{4,6},{5,7},{6,4},{7,5},{8,10},{9,11},{10,... | collective-permute-start | bytes 1474568 | tf_op jit(solution)/shard_map/ppermute | solution.py:54
  183.6 22.1 %collective-permute-start.28 = (bf16[4,160,384]{2,1,0:T(8,128)(2,1)}, bf16[4,160,384]{2,1,0:T(8,128)(2,1)}, u32[]{:S(2)}, u32[]{:S(2)}) collective-permute-start(bf16[4,160,384]{2,1,0:T(8,128)(2,1)} %get-tuple-element.141), channel_id=1, source_target_pairs={{0,18},{1,19},{2,16},{3,17},{4,22},{5,23},{6,20},{7,21},{8,26},{9,... | collective-permute-start | bytes 1474568 | tf_op jit(solution)/shard_map/ppermute | solution.py:57
  201.4 10.7 %collective-permute-start.29 = (bf16[2,176,384]{2,1,0:T(8,128)(2,1)S(1)}, bf16[2,176,384]{2,1,0:T(8,128)(2,1)S(1)}, u32[]{:S(2)}, u32[]{:S(2)}) collective-permute-start(bf16[2,176,384]{2,1,0:T(8,128)(2,1)S(1)} %fusion.6), channel_id=1, source_target_pairs={{0,2},{1,3},{2,0},{3,1},{4,6},{5,7},{6,4},{7,5},{8,10},{9,11},{10,... | collective-permute-start | bytes 811016 | tf_op jit(solution)/shard_map/ppermute | solution.py:54
  204.4 14.7 %collective-permute-start.30 = (bf16[96,1024]{1,0:T(8,128)(2,1)S(1)}, bf16[96,1024]{1,0:T(8,128)(2,1)S(1)}, u32[]{:S(2)}, u32[]{:S(2)}) collective-permute-start(bf16[96,1024]{1,0:T(8,128)(2,1)S(1)} %fusion.11), channel_id=1, source_target_pairs={{0,8},{1,9},{2,10},{3,11},{4,12},{5,13},{6,14},{7,15},{8,0},{9,1},... | collective-permute-start | bytes 589832 | tf_op jit(solution)/shard_map/ppermute | solution.py:63
  207.7 16.4 %collective-permute-start.32 = (bf16[160,384]{1,0:T(8,128)(2,1)S(1)}, bf16[160,384]{1,0:T(8,128)(2,1)S(1)}, u32[]{:S(2)}, u32[]{:S(2)}) collective-permute-start(bf16[160,384]{1,0:T(8,128)(2,1)S(1)} %get-tuple-element.148), channel_id=1, source_target_pairs={{0,4},{1,5},{2,6},{3,7},{4,0},{5,1},{6,2},{7,3},{8,12},{9,13},{10,... | collective-permute-start | bytes 368648 | tf_op jit(solution)/shard_map/ppermute | solution.py:63
  209.4 14.6 %collective-permute-start.33 = (bf16[160,384]{1,0:T(8,128)(2,1)S(1)}, bf16[160,384]{1,0:T(8,128)(2,1)S(1)}, u32[]{:S(2)}, u32[]{:S(2)}) collective-permute-start(bf16[160,384]{1,0:T(8,128)(2,1)S(1)} %get-tuple-element.147), channel_id=1, source_target_pairs={{0,8},{1,9},{2,10},{3,11},{4,12},{5,13},{6,14},{7,15},{8,0},{9,1},... | collective-permute-start | bytes 368648 | tf_op jit(solution)/shard_map/ppermute | solution.py:63
  209.7 14.3 %collective-permute-start.34 = (bf16[160,384]{1,0:T(8,128)(2,1)S(1)}, bf16[160,384]{1,0:T(8,128)(2,1)S(1)}, u32[]{:S(2)}, u32[]{:S(2)}) collective-permute-start(bf16[160,384]{1,0:T(8,128)(2,1)S(1)} %get-tuple-element.146), channel_id=1, source_target_pairs={{0,12},{1,13},{2,14},{3,15},{4,8},{5,9},{6,10},{7,11},{8,4},{9,5},... | collective-permute-start | bytes 368648 | tf_op jit(solution)/shard_map/ppermute | solution.py:63
  220.6 25.9 %collective-permute-start.42 = (bf16[96,1024]{1,0:T(8,128)(2,1)S(1)}, bf16[96,1024]{1,0:T(8,128)(2,1)S(1)}, u32[]{:S(2)}, u32[]{:S(2)}) collective-permute-start(bf16[96,1024]{1,0:T(8,128)(2,1)S(1)} %fusion.13.refs_0_.refs_6_), channel_id=1, source_target_pairs={{0,16},{1,17},{2,18},{3,19},{4,20},{5,21},{6,22},{7,23},{8,24},{9,... | collective-permute-start | bytes 589832 | tf_op jit(solution)/shard_map/ppermute | solution.py:51
  222.7 23.8 %collective-permute-start.41 = (bf16[176,384]{1,0:T(8,128)(2,1)S(1)}, bf16[176,384]{1,0:T(8,128)(2,1)S(1)}, u32[]{:S(2)}, u32[]{:S(2)}) collective-permute-start(bf16[176,384]{1,0:T(8,128)(2,1)S(1)} %fusion.17.refs_1_.refs_4_), channel_id=1, source_target_pairs={{0,16},{1,17},{2,18},{3,19},{4,20},{5,21},{6,22},{7,23},{8,24},{9,... | collective-permute-start | bytes 405512 | tf_op jit(solution)/shard_map/ppermute | solution.py:51
  224.9 21.6 %collective-permute-start.40 = (bf16[160,384]{1,0:T(8,128)(2,1)S(1)}, bf16[160,384]{1,0:T(8,128)(2,1)S(1)}, u32[]{:S(2)}, u32[]{:S(2)}) collective-permute-start(bf16[160,384]{1,0:T(8,128)(2,1)S(1)} %get-tuple-element.122.refs_2_), channel_id=1, source_target_pairs={{0,16},{1,17},{2,18},{3,19},{4,20},{5,21},{6,22},{7,23},{8,24},{9,... | collective-permute-start | bytes 368648 | tf_op jit(solution)/shard_map/ppermute | solution.py:51
  (46 other events, 356.7 us)
Sparse Core Ops, SparseCore 0:
  10.9 86.5 all-gather.1

commit v8 on v7

--- a/solution.py
+++ b/solution.py
@@ -852,11 +852,11 @@
         _, in_three = after(leave, in_three)
         three.parts[-1] = in_three
         three.total = three.total()
-        three.other = grid.flip_x(three.total)
         two.total = two.total()
-        two.other = grid.flip_x(two.total)
         totals = (three.total, two.total)
         one.total, squared = finish(grid, one.own, one.arrive, totals, SLAB)
+        _, totals = after(squared, totals)
+        three.other, two.other = (grid.flip_x(v) for v in totals)
         one.send_total()
         grad_norm = jnp.sqrt(total_of(grid, squared[0]))
         reduced = [(g.total, g.other) for g in (one, two, three)]

time: 262 us -> 265 us (1.011)
  starting transfers between devices: 58.1 us -> 64.5 us
  waiting for transfers between devices: 79.3 us -> 75.6 us
    ppermute x16, starting transfers between devices: 31.9 us -> 36.9 us  [swap_z(): lax.ppermute(v, EVERY, self.move(lambda x, z, y, c: (x, z ^ bit, y, c)))]
    ppermute x16, waiting for transfers between devices: 42.4 us -> 38.9 us  [swap_z(): lax.ppermute(v, EVERY, self.move(lambda x, z, y, c: (x, z ^ bit, y, c)))]
  transfers between devices with their start and end apart: 44 -> 44, of which waited for: 20 -> 20; matrix products, arithmetic and copies ran while one was open for 9% -> 9% of each run, Pallas kernels for 15% -> 14%
where the time goes in v8:
time: 265 us
  waiting for transfers between devices  75.6 us (29%)
  Pallas kernels  72.5 us (27%)
  starting transfers between devices  64.5 us (24%)
  other arithmetic  23.1 us (9%)
  between operations  20.1 us (8%)
  local copies, waits for them, and re-layouts  8.78 us (3%)
    ppermute x16, waiting for transfers between devices, swap_z(): lax.ppermute(v, EVERY, self.move(lambda x, z, y, c: (x, z ^ bit, y, c)))  38.9 us
    ppermute x16, starting transfers between devices, swap_z(): lax.ppermute(v, EVERY, self.move(lambda x, z, y, c: (x, z ^ bit, y, c)))  36.9 us
    pallas_call x1, Pallas kernels, feed_forward(): pl.pallas_call(body, grid=(steps,), out_shape=[jax.ShapeDtypeStruct((leng...  27.5 us
    ppermute x11, waiting for transfers between devices, flip_x(): lax.ppermute(v, EVERY, self.move(lambda x, z, y, c: (1 - x, z, y, c)))  24.1 us
    ppermute x11, starting transfers between devices, flip_x(): lax.ppermute(v, EVERY, self.move(lambda x, z, y, c: (1 - x, z, y, c)))  15.3 us
    pallas_call x2, Pallas kernels, attend_back(): pl.pallas_call(body, grid=(width // pair,), out_shape=jax.ShapeDtypeStruc...  15 us
    ppermute x6, starting transfers between devices, flip_y(): lax.ppermute(v, EVERY, self.move(lambda x, z, y, c: (x, z, 1 - y, c)))  9.58 us
    convert_element_type x5, other arithmetic, leave(): return leave.astype(LOW)  8.57 us
  transfers between devices with their start and end apart: 44, of which 20 were waited for; matrix products, arithmetic and copies ran while one was open for 9% of the time, Pallas kernels for 14%

profile of v8, /device:TPU:0, one launch (start us, length us, event | category | flops | bytes accessed | tf_op | source)
XLA Modules:
  0.0 264.7 jit_solution(3427474730819736769)
XLA Ops:
  7.2 2.0 convert_element_type.307
  10.3 3.1 %collective-permute-start = (bf16[160,384]{1,0:T(8,128)(2,1)S(1)}, bf16[160,384]{1,0:T(8,128)(2,1)S(1)}, u32[]{:S(2)}, u32[]{:S(2)}) collective-permute-start(bf16[160,384]{1,0:T(8,128)(2,1)S(1)} %bitcast.190), channel_id=1, source_target_pairs={{0,4},{1,5},{2,6},{3,7},{4,0},{5,1},{6,2},{7,3},{8,12},{9,13},{10,... | collective-permute-start | bytes 368648 | tf_op jit(solution)/shard_map/ppermute | solution.py:63
  13.4 2.6 collective-permute-start.1
  18.1 7.7 %collective-permute-done.1 = bf16[160,384]{1,0:T(8,128)(2,1)S(1)} collective-permute-done((bf16[160,384]{1,0:T(8,128)(2,1)S(1)}, bf16[160,384]{1,0:T(8,128)(2,1)S(1)}, u32[]{:S(2)}, u32[]{:S(2)}) %collective-permute-start.1) | collective-permute-done | bytes 122912 | tf_op jit(solution)/shard_map/ppermute | solution.py:63
  29.0 8.4 %collective-permute-start.5 = (bf16[176,384]{1,0:T(8,128)(2,1)S(1)}, bf16[176,384]{1,0:T(8,128)(2,1)S(1)}, u32[]{:S(2)}, u32[]{:S(2)}) collective-permute-start(bf16[176,384]{1,0:T(8,128)(2,1)S(1)} %fusion.23), channel_id=1, source_target_pairs={{0,4},{1,5},{2,6},{3,7},{4,0},{5,1},{6,2},{7,3},{8,12},{9,13},{10,... | collective-permute-start | bytes 405512 | tf_op jit(solution)/shard_map/ppermute | solution.py:63
  37.4 2.3 collective-permute-start.6
  41.3 2.0 collective-permute-done.5
  43.3 6.5 %collective-permute-done.6 = bf16[176,384]{1,0:T(8,128)(2,1)S(1)} collective-permute-done((bf16[176,384]{1,0:T(8,128)(2,1)S(1)}, bf16[176,384]{1,0:T(8,128)(2,1)S(1)}, u32[]{:S(2)}, u32[]{:S(2)}) %collective-permute-start.6) | collective-permute-done | bytes 135200 | tf_op jit(solution)/shard_map/ppermute | solution.py:63
  54.4 9.8 %collective-permute-done.8.refs_3_.refs_8_ = bf16[4,160,384]{2,1,0:T(8,128)(2,1)S(1)} collective-permute-done((bf16[4,160,384]{2,1,0:T(8,128)(2,1)S(1)}, bf16[4,160,384]{2,1,0:T(8,128)(2,1)S(1)}, u32[]{:S(2)}, u32[]{:S(2)}) %collective-permute-start.8) | collective-permute-done | bytes 491552 | tf_op jit(solution)/shard_map/ppermute | solution.py:51
  66.1 4.8 %project_in.1 = (bf16[512,768]{1,0:T(8,128)(2,1)S(1)}, bf16[3,512,768]{2,1,0:T(8,128)(2,1)S(1)}, f32[16,768]{1,0:T(8,128)S(1)}) custom-call(bf16[512,768]{1,0:T(8,128)(2,1)S(1)} %bitcast.169, f32[16,768]{1,0:T(8,128)S(1)} %broadcast_in_dim.21.refs_1_, bf16[12,160,384]{2,1,0:T(8,128)(2,1)S(1)} %constant_dynamic-update-slice_fusion.refs_2_.refs_7_, ...), custom_call_target="tpu_custom_call" | custom-call | flops 8000000 | tf_op jit(solution)/shard_map/project_in/pallas_call | solution.py:309
  70.9 7.3 %attend.1.refs_2_ = bf16[512,768]{1,0:T(8,128)(2,1)S(1)} custom-call(s32[1]{0:T(128)S(6)} %copy.77.counts_ref.refs_0_, bf16[3,512,768]{2,1,0:T(8,128)(2,1)S(1)} %get-tuple-element.83.qkv_ref), custom_call_target="tpu_custom_call" | custom-call | flops 9000000 | tf_op jit(solution)/shard_map/attend/pallas_call | solution.py:347
  82.0 13.2 %collective-permute-done.13.refs_6_ = bf16[4,176,384]{2,1,0:T(8,128)(2,1)S(1)} collective-permute-done((bf16[4,176,384]{2,1,0:T(8,128)(2,1)S(1)}, bf16[4,176,384]{2,1,0:T(8,128)(2,1)S(1)}, u32[]{:S(2)}, u32[]{:S(2)}) %collective-permute-start.13) | collective-permute-done | bytes 540704 | tf_op jit(solution)/shard_map/ppermute | solution.py:51
  95.2 2.0 collective-permute-done.15.refs_8_
  98.0 27.5 %feed_forward.1 = (bf16[512,768]{1,0:T(8,128)(2,1)}, f32[512,768]{1,0:T(8,128)}, bf16[512,768]{1,0:T(8,128)(2,1)}, f32[8,768]{1,0:T(8,128)}, bf16[2,8,176,384]{3...) custom-call(s32[1]{0:T(128)S(6)} %copy.77.counts_ref.refs_0_, ...), custom_call_target="tpu_custom_call" | custom-call | flops 28000000 | tf_op jit(solution)/shard_map/feed_forward/pallas_call | solution.py:513
  127.3 2.4 attend_back.2.refs_5_
  131.6 3.9 %fusion.4 = (bf16[4,96,1024]{2,1,0:T(8,128)(2,1)}, bf16[4,96,1024]{2,1,0:T(8,128)(2,1)}, bf16[4,96,1024]{2,1,0:T(8,128)(2,1)}) fusion(bf16[2,4,2,96,1024]{4,3,2,1,0:T(8,128)(2,1)} %bitcast.23, s32[]{:T(128)S(6)} %select_n.176, s32[]{:T(128)S(6)} %select_n.182, bf16[2,4,2,96,1024]{4,3,2,1,0:T(8,128)(2,1)S(1)} %bitcast.171, s32[]{:T(128)S(6)} %select_n.180, ...), kind=kLoop, calls=%fused_computation.21 | loop fusion | flops 4718592 | bytes 7077904 | tf_op jit(solution)/shard_map/convert_element_type | solution.py:129
  143.8 12.6 %attend_back.3.refs_6_ = bf16[3,512,640]{2,1,0:T(8,128)(2,1)S(1)} custom-call(s32[1]{0:T(128)S(6)} %copy.77.counts_ref.refs_0_, bf16[3,512,768]{2,1,0:T(8,128)(2,1)S(1)} %get-tuple-element.83.qkv_ref, bf16[512,768]{1,0:T(8,128)(2,1)S(1)} %copy-done.8), custom_call_target="tpu_custom_call" | custom-call | flops 13500000 | tf_op jit(solution)/shard_map/attend_back/pallas_call | solution.py:385
  159.0 8.3 %project_back.1 = (bf16[512,768]{1,0:T(8,128)(2,1)}, bf16[2,8,160,384]{3,2,1,0:T(8,128)(2,1)S(1)}, bf16[2,8,160,384]{3,2,1,0:T(8,128)(2,1)}) custom-call(bf16[512,768]{1,0:T(8,128)(2,1)S(1)} %bitcast.170, bf16[512,768]{1,0:T(8,128)(2,1)S(1)} %copy-done.20, f32[512,768]{1,0:T(8,128)S(1)} %copy-done.17, f32[16,768]{1,0:T(8,128)S(1)} %copy-done.22, ...), custom_call_target="tpu_custom_call" | custom-call | flops 11000000 | tf_op jit(solution)/shard_map/project_back/pallas_call | solution.py:582
  167.5 3.0 %fusion = bf16[2,2,176,384]{3,2,1,0:T(8,128)(2,1)} fusion(bf16[2,2,2,2,176,384]{5,4,3,2,1,0:T(8,128)(2,1)} %bitcast.27, s32[]{:T(128)S(6)} %select_n.186, s32[]{:T(128)S(6)} %select_n.188, bf16[2,2,2,2,176,384]{5,4,3,2,1,0:T(8,128)(2,1)} %bitcast.176, s32[]{:T(128)S(6)} %select_n.185, bf16[1,2,2,176,384]{4,3,0,2,1:T(8,128)(2,1)} %bitcast.34, ...), kind=kLoop, calls=%fused_computation.13 | loop fusion | flops 1892352 | bytes 2703372 | tf_op jit(solution)/shard_map/convert_element_type | solution.py:166
  170.5 2.9 %collective-permute-done.21.refs_1_ = bf16[4,96,1024]{2,1,0:T(8,128)(2,1)} collective-permute-done((bf16[4,96,1024]{2,1,0:T(8,128)(2,1)}, bf16[4,96,1024]{2,1,0:T(8,128)(2,1)}, u32[]{:S(2)}, u32[]{:S(2)}) %collective-permute-start.21) | collective-permute-done | bytes 786464 | tf_op jit(solution)/shard_map/ppermute | solution.py:54
  173.3 3.2 %collective-permute-start.24 = (bf16[2,2,176,384]{3,2,1,0:T(8,128)(2,1)}, bf16[2,2,176,384]{3,2,1,0:T(8,128)(2,1)}, u32[]{:S(2)}, u32[]{:S(2)}) collective-permute-start(bf16[2,2,176,384]{3,2,1,0:T(8,128)(2,1)} %fusion), channel_id=1, source_target_pairs={{0,8},{1,9},{2,10},{3,11},{4,12},{5,13},{6,14},{7,15},{8,0},{9,1},... | collective-permute-start | bytes 1622024 | tf_op jit(solution)/shard_map/ppermute | solution.py:63
  176.5 2.2 fold_column.1
  178.8 2.6 %fusion.7 = (bf16[4,160,384]{2,1,0:T(8,128)(2,1)}, bf16[4,160,384]{2,1,0:T(8,128)(2,1)}, bf16[4,160,384]{2,1,0:T(8,128)(2,1)}) fusion(bf16[2,4,2,160,384]{4,3,2,1,0:T(8,128)(2,1)} %bitcast.45, s32[]{:T(128)S(6)} %select_n.176, s32[]{:T(128)S(6)} %select_n.179, bf16[2,4,2,160,384]{4,3,2,1,0:T(8,128)(2,1)S(1)} %bitcast.174, s32[]{:T(128)S(6)} %select_n.182, ...), kind=kLoop, calls=%fused_computation.30 | loop fusion | flops 2949120 | bytes 4423696 | tf_op jit(solution)/shard_map/convert_element_type | solution.py:129
  184.9 11.2 %collective-permute-done.25 = bf16[2,96,1024]{2,1,0:T(8,128)(2,1)} collective-permute-done((bf16[2,96,1024]{2,1,0:T(8,128)(2,1)S(1)}, bf16[2,96,1024]{2,1,0:T(8,128)(2,1)}, u32[]{:S(2)}, u32[]{:S(2)}) %collective-permute-start.25) | collective-permute-done | bytes 393248 | tf_op jit(solution)/shard_map/ppermute | solution.py:63
  196.1 4.0 %collective-permute-done.24 = bf16[2,2,176,384]{3,2,1,0:T(8,128)(2,1)} collective-permute-done((bf16[2,2,176,384]{3,2,1,0:T(8,128)(2,1)}, bf16[2,2,176,384]{3,2,1,0:T(8,128)(2,1)}, u32[]{:S(2)}, u32[]{:S(2)}) %collective-permute-start.24) | collective-permute-done | bytes 540704 | tf_op jit(solution)/shard_map/ppermute | solution.py:63
  209.7 2.4 collective-permute-start.34
  214.1 5.0 %collective-permute-done.30 = bf16[96,1024]{1,0:T(8,128)(2,1)S(1)} collective-permute-done((bf16[96,1024]{1,0:T(8,128)(2,1)S(1)}, bf16[96,1024]{1,0:T(8,128)(2,1)S(1)}, u32[]{:S(2)}, u32[]{:S(2)}) %collective-permute-start.30) | collective-permute-done | bytes 196640 | tf_op jit(solution)/shard_map/ppermute | solution.py:63
  228.4 4.0 %collective-permute-start.36 = (f32[]{:T(128)}, f32[]{:T(128)}, u32[]{:S(2)}, u32[]{:S(2)}) collective-permute-start(f32[]{:T(128)} %add.544), channel_id=1, source_target_pairs={{0,16},{1,17},{2,18},{3,19},{4,20},{5,21},{6,22},{7,23},{8,24},{9,... | collective-permute-start | bytes 20 | tf_op jit(solution)/shard_map/ppermute | solution.py:51
  234.0 2.7 %collective-permute-start.37 = (f32[]{:T(128)}, f32[]{:T(128)}, u32[]{:S(2)}, u32[]{:S(2)}) collective-permute-start(f32[]{:T(128)} %add.545), channel_id=1, source_target_pairs={{0,2},{1,3},{2,0},{3,1},{4,6},{5,7},{6,4},{7,5},{8,10},{9,11},{10,... | collective-permute-start | bytes 20 | tf_op jit(solution)/shard_map/ppermute | solution.py:54
  238.3 4.6 %collective-permute-start.38 = (f32[]{:T(128)}, f32[]{:T(128)}, u32[]{:S(2)}, u32[]{:S(2)}) collective-permute-start(f32[]{:T(128)} %add.546), channel_id=1, source_target_pairs={{0,4},{1,5},{2,6},{3,7},{4,0},{5,1},{6,2},{7,3},{8,12},{9,13},{10,... | collective-permute-start | bytes 20 | tf_op jit(solution)/shard_map/ppermute | solution.py:63
  243.7 4.6 %collective-permute-start.39 = (f32[]{:T(128)}, f32[]{:T(128)}, u32[]{:S(2)}, u32[]{:S(2)}) collective-permute-start(f32[]{:T(128)} %add.547), channel_id=1, source_target_pairs={{0,8},{1,9},{2,10},{3,11},{4,12},{5,13},{6,14},{7,15},{8,0},{9,1},... | collective-permute-start | bytes 20 | tf_op jit(solution)/shard_map/ppermute | solution.py:63
  250.1 6.6 %update.1 = (f32[4,48,768]{2,1,0:T(8,128)}, f32[2,48,2048]{2,1,0:T(8,128)}, f32[128,768]{1,0:T(8,128)}, f32[2,48]{1,0:T(2,128)}, f32[4,48,768]{2,1,0:T(8,128)}, ...) custom-call(f32[1]{0:T(128)} %bitcast.72.refs_0_, ...), custom_call_target="tpu_custom_call" | custom-call | flops 4000000 | tf_op jit(solution)/shard_map/update/pallas_call | solution.py:718
  (175 shorter events, 59.3 us)
Async XLA Ops:
  7.2 90.3 %all-gather.2.cloned.1.call-start = ((), (), s32[]{:S(2)}) async-start(), calls=%async_computation | async-start | bytes 6684672 | tf_op jit(solution)/shard_map/all_gather | solution.py:770
  13.4 12.4 %collective-permute-start.1 = (bf16[160,384]{1,0:T(8,128)(2,1)S(1)}, bf16[160,384]{1,0:T(8,128)(2,1)S(1)}, u32[]{:S(2)}, u32[]{:S(2)}) collective-permute-start(bf16[160,384]{1,0:T(8,128)(2,1)S(1)} %bitcast.191), channel_id=1, source_target_pairs={{0,8},{1,9},{2,10},{3,11},{4,12},{5,13},{6,14},{7,15},{8,0},{9,1},... | collective-permute-start | bytes 368648 | tf_op jit(solution)/shard_map/ppermute | solution.py:63
  25.9 24.0 %collective-permute-start.3 = (bf16[4,160,384]{2,1,0:T(8,128)(2,1)S(1)}, bf16[4,160,384]{2,1,0:T(8,128)(2,1)S(1)}, u32[]{:S(2)}, u32[]{:S(2)}) collective-permute-start(bf16[4,160,384]{2,1,0:T(8,128)(2,1)S(1)} %pad_maximum_fusion.1), channel_id=1, source_target_pairs={{0,16},{1,17},{2,18},{3,19},{4,20},{5,21},{6,22},{7,23},{8,24},{9,... | collective-permute-start | bytes 1474568 | tf_op jit(solution)/shard_map/ppermute | solution.py:51
  27.4 22.4 %collective-permute-start.4 = (bf16[4,160,384]{2,1,0:T(8,128)(2,1)S(1)}, bf16[4,160,384]{2,1,0:T(8,128)(2,1)S(1)}, u32[]{:S(2)}, u32[]{:S(2)}) collective-permute-start(bf16[4,160,384]{2,1,0:T(8,128)(2,1)S(1)} %pad_maximum_fusion.1), channel_id=1, source_target_pairs={{0,2},{1,3},{2,0},{3,1},{4,6},{5,7},{6,4},{7,5},{8,10},{9,11},{10,... | collective-permute-start | bytes 1474568 | tf_op jit(solution)/shard_map/ppermute | solution.py:54
  29.0 14.3 %collective-permute-start.5 = (bf16[176,384]{1,0:T(8,128)(2,1)S(1)}, bf16[176,384]{1,0:T(8,128)(2,1)S(1)}, u32[]{:S(2)}, u32[]{:S(2)}) collective-permute-start(bf16[176,384]{1,0:T(8,128)(2,1)S(1)} %fusion.23), channel_id=1, source_target_pairs={{0,4},{1,5},{2,6},{3,7},{4,0},{5,1},{6,2},{7,3},{8,12},{9,13},{10,... | collective-permute-start | bytes 405512 | tf_op jit(solution)/shard_map/ppermute | solution.py:63
  37.4 12.4 %collective-permute-start.6 = (bf16[176,384]{1,0:T(8,128)(2,1)S(1)}, bf16[176,384]{1,0:T(8,128)(2,1)S(1)}, u32[]{:S(2)}, u32[]{:S(2)}) collective-permute-start(bf16[176,384]{1,0:T(8,128)(2,1)S(1)} %fusion.23), channel_id=1, source_target_pairs={{0,8},{1,9},{2,10},{3,11},{4,12},{5,13},{6,14},{7,15},{8,0},{9,1},... | collective-permute-start | bytes 405512 | tf_op jit(solution)/shard_map/ppermute | solution.py:63
  50.0 16.0 %collective-permute-start.9 = (bf16[12,160,384]{2,1,0:T(8,128)(2,1)S(1)}, bf16[12,160,384]{2,1,0:T(8,128)(2,1)S(1)}, u32[]{:S(2)}, u32[]{:S(2)}) collective-permute-start(bf16[12,160,384]{2,1,0:T(8,128)(2,1)S(1)} %constant_dynamic-update-slice_fusion.refs_2_.refs_7_), channel_id=1, source_target_pairs={{0,1},{1,0},{2,3},{3,2},{4,5},{5,4},{6,7},{7,6},{8,9},{9,8},{10,11... | collective-permute-start | bytes 4423688 | tf_op jit(solution)/shard_map/ppermute | solution.py:60
  50.1 14.1 %collective-permute-start.8 = (bf16[4,160,384]{2,1,0:T(8,128)(2,1)S(1)}, bf16[4,160,384]{2,1,0:T(8,128)(2,1)S(1)}, u32[]{:S(2)}, u32[]{:S(2)}) collective-permute-start(bf16[4,160,384]{2,1,0:T(8,128)(2,1)S(1)} %collective-permute-done.4), channel_id=1, source_target_pairs={{0,16},{1,17},{2,18},{3,19},{4,20},{5,21},{6,22},{7,23},{8,24},{9,... | collective-permute-start | bytes 1474568 | tf_op jit(solution)/shard_map/ppermute | solution.py:51
  52.3 26.8 %collective-permute-start.11 = (bf16[4,176,384]{2,1,0:T(8,128)(2,1)S(1)}, bf16[4,176,384]{2,1,0:T(8,128)(2,1)S(1)}, u32[]{:S(2)}, u32[]{:S(2)}) collective-permute-start(bf16[4,176,384]{2,1,0:T(8,128)(2,1)S(1)} %pad_maximum_fusion), channel_id=1, source_target_pairs={{0,16},{1,17},{2,18},{3,19},{4,20},{5,21},{6,22},{7,23},{8,24},{9,... | collective-permute-start | bytes 1622024 | tf_op jit(solution)/shard_map/ppermute | solution.py:51
  53.0 26.1 %collective-permute-start.12 = (bf16[4,176,384]{2,1,0:T(8,128)(2,1)S(1)}, bf16[4,176,384]{2,1,0:T(8,128)(2,1)S(1)}, u32[]{:S(2)}, u32[]{:S(2)}) collective-permute-start(bf16[4,176,384]{2,1,0:T(8,128)(2,1)S(1)} %pad_maximum_fusion), channel_id=1, source_target_pairs={{0,2},{1,3},{2,0},{3,1},{4,6},{5,7},{6,4},{7,5},{8,10},{9,11},{10,... | collective-permute-start | bytes 1622024 | tf_op jit(solution)/shard_map/ppermute | solution.py:54
  80.5 16.7 %collective-permute-start.14 = (bf16[12,176,384]{2,1,0:T(8,128)(2,1)S(1)}, bf16[12,176,384]{2,1,0:T(8,128)(2,1)}, u32[]{:S(2)}, u32[]{:S(2)}) collective-permute-start(bf16[12,176,384]{2,1,0:T(8,128)(2,1)S(1)} %constant_dynamic-update-slice_fusion.6.refs_5_), channel_id=1, source_target_pairs={{0,1},{1,0},{2,3},{3,2},{4,5},{5,4},{6,7},{7,6},{8,9},{9,8},{10,11... | collective-permute-start | bytes 4866056 | tf_op jit(solution)/shard_map/ppermute | solution.py:60
  80.6 14.6 %collective-permute-start.13 = (bf16[4,176,384]{2,1,0:T(8,128)(2,1)S(1)}, bf16[4,176,384]{2,1,0:T(8,128)(2,1)S(1)}, u32[]{:S(2)}, u32[]{:S(2)}) collective-permute-start(bf16[4,176,384]{2,1,0:T(8,128)(2,1)S(1)} %collective-permute-done.12), channel_id=1, source_target_pairs={{0,16},{1,17},{2,18},{3,19},{4,20},{5,21},{6,22},{7,23},{8,24},{9,... | collective-permute-start | bytes 1622024 | tf_op jit(solution)/shard_map/ppermute | solution.py:51
  125.8 13.2 %collective-permute-start.17 = (bf16[2,8,176,384]{3,2,1,0:T(8,128)(2,1)}, bf16[2,8,176,384]{3,2,1,0:T(8,128)(2,1)}, u32[]{:S(2)}, u32[]{:S(2)}) collective-permute-start(bf16[2,8,176,384]{3,2,1,0:T(8,128)(2,1)} %get-tuple-element.101), channel_id=1, source_target_pairs={{0,1},{1,0},{2,3},{3,2},{4,5},{5,4},{6,7},{7,6},{8,9},{9,8},{10,11... | collective-permute-start | bytes 6488072 | tf_op jit(solution)/shard_map/ppermute | solution.py:60
  135.5 35.0 %collective-permute-start.20 = (bf16[4,96,1024]{2,1,0:T(8,128)(2,1)}, bf16[4,96,1024]{2,1,0:T(8,128)(2,1)}, u32[]{:S(2)}, u32[]{:S(2)}) collective-permute-start(bf16[4,96,1024]{2,1,0:T(8,128)(2,1)} %get-tuple-element.143), channel_id=1, source_target_pairs={{0,16},{1,17},{2,18},{3,19},{4,20},{5,21},{6,22},{7,23},{8,24},{9,... | collective-permute-start | bytes 2359304 | tf_op jit(solution)/shard_map/ppermute | solution.py:51
  136.8 36.6 %collective-permute-start.21 = (bf16[4,96,1024]{2,1,0:T(8,128)(2,1)}, bf16[4,96,1024]{2,1,0:T(8,128)(2,1)}, u32[]{:S(2)}, u32[]{:S(2)}) collective-permute-start(bf16[4,96,1024]{2,1,0:T(8,128)(2,1)} %get-tuple-element.142), channel_id=1, source_target_pairs={{0,2},{1,3},{2,0},{3,1},{4,6},{5,7},{6,4},{7,5},{8,10},{9,11},{10,... | collective-permute-start | bytes 2359304 | tf_op jit(solution)/shard_map/ppermute | solution.py:54
  138.5 34.9 %collective-permute-start.22 = (bf16[4,96,1024]{2,1,0:T(8,128)(2,1)}, bf16[4,96,1024]{2,1,0:T(8,128)(2,1)}, u32[]{:S(2)}, u32[]{:S(2)}) collective-permute-start(bf16[4,96,1024]{2,1,0:T(8,128)(2,1)} %get-tuple-element.141), channel_id=1, source_target_pairs={{0,18},{1,19},{2,16},{3,17},{4,22},{5,23},{6,20},{7,21},{8,26},{9,... | collective-permute-start | bytes 2359304 | tf_op jit(solution)/shard_map/ppermute | solution.py:57
  141.6 25.8 %collective-permute-start.18 = (bf16[2,2,176,384]{3,2,1,0:T(8,128)(2,1)}, bf16[2,2,176,384]{3,2,1,0:T(8,128)(2,1)}, u32[]{:S(2)}, u32[]{:S(2)}) collective-permute-start(bf16[2,2,176,384]{3,2,1,0:T(8,128)(2,1)} %get-tuple-element.108), channel_id=1, source_target_pairs={{0,4},{1,5},{2,6},{3,7},{4,0},{5,1},{6,2},{7,3},{8,12},{9,13},{10,... | collective-permute-start | bytes 1622024 | tf_op jit(solution)/shard_map/ppermute | solution.py:63
  143.6 23.8 %collective-permute-start.19 = (bf16[2,2,176,384]{3,2,1,0:T(8,128)(2,1)}, bf16[2,2,176,384]{3,2,1,0:T(8,128)(2,1)}, u32[]{:S(2)}, u32[]{:S(2)}) collective-permute-start(bf16[2,2,176,384]{3,2,1,0:T(8,128)(2,1)} %get-tuple-element.109), channel_id=1, source_target_pairs={{0,4},{1,5},{2,6},{3,7},{4,0},{5,1},{6,2},{7,3},{8,12},{9,13},{10,... | collective-permute-start | bytes 1622024 | tf_op jit(solution)/shard_map/ppermute | solution.py:63
  167.4 11.4 %collective-permute-start.23 = (bf16[2,8,160,384]{3,2,1,0:T(8,128)(2,1)}, bf16[2,8,160,384]{3,2,1,0:T(8,128)(2,1)}, u32[]{:S(2)}, u32[]{:S(2)}) collective-permute-start(bf16[2,8,160,384]{3,2,1,0:T(8,128)(2,1)} %get-tuple-element.116), channel_id=1, source_target_pairs={{0,1},{1,0},{2,3},{3,2},{4,5},{5,4},{6,7},{7,6},{8,9},{9,8},{10,11... | collective-permute-start | bytes 5898248 | tf_op jit(solution)/shard_map/ppermute | solution.py:60
  173.3 26.7 %collective-permute-start.24 = (bf16[2,2,176,384]{3,2,1,0:T(8,128)(2,1)}, bf16[2,2,176,384]{3,2,1,0:T(8,128)(2,1)}, u32[]{:S(2)}, u32[]{:S(2)}) collective-permute-start(bf16[2,2,176,384]{3,2,1,0:T(8,128)(2,1)} %fusion), channel_id=1, source_target_pairs={{0,8},{1,9},{2,10},{3,11},{4,12},{5,13},{6,14},{7,15},{8,0},{9,1},... | collective-permute-start | bytes 1622024 | tf_op jit(solution)/shard_map/ppermute | solution.py:63
  178.7 17.4 %collective-permute-start.25 = (bf16[2,96,1024]{2,1,0:T(8,128)(2,1)S(1)}, bf16[2,96,1024]{2,1,0:T(8,128)(2,1)}, u32[]{:S(2)}, u32[]{:S(2)}) collective-permute-start(bf16[2,96,1024]{2,1,0:T(8,128)(2,1)S(1)} %fold_column.1), channel_id=1, source_target_pairs={{0,4},{1,5},{2,6},{3,7},{4,0},{5,1},{6,2},{7,3},{8,12},{9,13},{10,... | collective-permute-start | bytes 1179656 | tf_op jit(solution)/shard_map/ppermute | solution.py:63
  181.4 23.0 %collective-permute-start.26 = (bf16[4,160,384]{2,1,0:T(8,128)(2,1)}, bf16[4,160,384]{2,1,0:T(8,128)(2,1)}, u32[]{:S(2)}, u32[]{:S(2)}) collective-permute-start(bf16[4,160,384]{2,1,0:T(8,128)(2,1)} %get-tuple-element.144), channel_id=1, source_target_pairs={{0,16},{1,17},{2,18},{3,19},{4,20},{5,21},{6,22},{7,23},{8,24},{9,... | collective-permute-start | bytes 1474568 | tf_op jit(solution)/shard_map/ppermute | solution.py:51
  182.8 22.9 %collective-permute-start.27 = (bf16[4,160,384]{2,1,0:T(8,128)(2,1)}, bf16[4,160,384]{2,1,0:T(8,128)(2,1)}, u32[]{:S(2)}, u32[]{:S(2)}) collective-permute-start(bf16[4,160,384]{2,1,0:T(8,128)(2,1)} %get-tuple-element.146), channel_id=1, source_target_pairs={{0,2},{1,3},{2,0},{3,1},{4,6},{5,7},{6,4},{7,5},{8,10},{9,11},{10,... | collective-permute-start | bytes 1474568 | tf_op jit(solution)/shard_map/ppermute | solution.py:54
  183.6 22.1 %collective-permute-start.28 = (bf16[4,160,384]{2,1,0:T(8,128)(2,1)}, bf16[4,160,384]{2,1,0:T(8,128)(2,1)}, u32[]{:S(2)}, u32[]{:S(2)}) collective-permute-start(bf16[4,160,384]{2,1,0:T(8,128)(2,1)} %get-tuple-element.145), channel_id=1, source_target_pairs={{0,18},{1,19},{2,16},{3,17},{4,22},{5,23},{6,20},{7,21},{8,26},{9,... | collective-permute-start | bytes 1474568 | tf_op jit(solution)/shard_map/ppermute | solution.py:57
  201.4 10.7 %collective-permute-start.29 = (bf16[2,176,384]{2,1,0:T(8,128)(2,1)S(1)}, bf16[2,176,384]{2,1,0:T(8,128)(2,1)S(1)}, u32[]{:S(2)}, u32[]{:S(2)}) collective-permute-start(bf16[2,176,384]{2,1,0:T(8,128)(2,1)S(1)} %fusion.6), channel_id=1, source_target_pairs={{0,2},{1,3},{2,0},{3,1},{4,6},{5,7},{6,4},{7,5},{8,10},{9,11},{10,... | collective-permute-start | bytes 811016 | tf_op jit(solution)/shard_map/ppermute | solution.py:54
  204.4 14.7 %collective-permute-start.30 = (bf16[96,1024]{1,0:T(8,128)(2,1)S(1)}, bf16[96,1024]{1,0:T(8,128)(2,1)S(1)}, u32[]{:S(2)}, u32[]{:S(2)}) collective-permute-start(bf16[96,1024]{1,0:T(8,128)(2,1)S(1)} %fusion.11), channel_id=1, source_target_pairs={{0,8},{1,9},{2,10},{3,11},{4,12},{5,13},{6,14},{7,15},{8,0},{9,1},... | collective-permute-start | bytes 589832 | tf_op jit(solution)/shard_map/ppermute | solution.py:63
  207.7 14.3 %collective-permute-start.32 = (bf16[160,384]{1,0:T(8,128)(2,1)S(1)}, bf16[160,384]{1,0:T(8,128)(2,1)S(1)}, u32[]{:S(2)}, u32[]{:S(2)}) collective-permute-start(bf16[160,384]{1,0:T(8,128)(2,1)S(1)} %get-tuple-element.152), channel_id=1, source_target_pairs={{0,4},{1,5},{2,6},{3,7},{4,0},{5,1},{6,2},{7,3},{8,12},{9,13},{10,... | collective-permute-start | bytes 368648 | tf_op jit(solution)/shard_map/ppermute | solution.py:63
  209.4 12.5 %collective-permute-start.33 = (bf16[160,384]{1,0:T(8,128)(2,1)S(1)}, bf16[160,384]{1,0:T(8,128)(2,1)S(1)}, u32[]{:S(2)}, u32[]{:S(2)}) collective-permute-start(bf16[160,384]{1,0:T(8,128)(2,1)S(1)} %get-tuple-element.151), channel_id=1, source_target_pairs={{0,8},{1,9},{2,10},{3,11},{4,12},{5,13},{6,14},{7,15},{8,0},{9,1},... | collective-permute-start | bytes 368648 | tf_op jit(solution)/shard_map/ppermute | solution.py:63
  209.7 12.2 %collective-permute-start.34 = (bf16[160,384]{1,0:T(8,128)(2,1)S(1)}, bf16[160,384]{1,0:T(8,128)(2,1)S(1)}, u32[]{:S(2)}, u32[]{:S(2)}) collective-permute-start(bf16[160,384]{1,0:T(8,128)(2,1)S(1)} %get-tuple-element.150), channel_id=1, source_target_pairs={{0,12},{1,13},{2,14},{3,15},{4,8},{5,9},{6,10},{7,11},{8,4},{9,5},... | collective-permute-start | bytes 368648 | tf_op jit(solution)/shard_map/ppermute | solution.py:63
  222.8 26.5 %collective-permute-start.42 = (bf16[96,1024]{1,0:T(8,128)(2,1)S(1)}, bf16[96,1024]{1,0:T(8,128)(2,1)S(1)}, u32[]{:S(2)}, u32[]{:S(2)}) collective-permute-start(bf16[96,1024]{1,0:T(8,128)(2,1)S(1)} %fusion.13.refs_0_.refs_6_), channel_id=1, source_target_pairs={{0,16},{1,17},{2,18},{3,19},{4,20},{5,21},{6,22},{7,23},{8,24},{9,... | collective-permute-start | bytes 589832 | tf_op jit(solution)/shard_map/ppermute | solution.py:51
  223.7 25.6 %collective-permute-start.41 = (bf16[176,384]{1,0:T(8,128)(2,1)S(1)}, bf16[176,384]{1,0:T(8,128)(2,1)S(1)}, u32[]{:S(2)}, u32[]{:S(2)}) collective-permute-start(bf16[176,384]{1,0:T(8,128)(2,1)S(1)} %fusion.17.refs_1_.refs_4_), channel_id=1, source_target_pairs={{0,16},{1,17},{2,18},{3,19},{4,20},{5,21},{6,22},{7,23},{8,24},{9,... | collective-permute-start | bytes 405512 | tf_op jit(solution)/shard_map/ppermute | solution.py:51
  224.9 24.4 %collective-permute-start.40 = (bf16[160,384]{1,0:T(8,128)(2,1)S(1)}, bf16[160,384]{1,0:T(8,128)(2,1)S(1)}, u32[]{:S(2)}, u32[]{:S(2)}) collective-permute-start(bf16[160,384]{1,0:T(8,128)(2,1)S(1)} %get-tuple-element.124.refs_2_), channel_id=1, source_target_pairs={{0,16},{1,17},{2,18},{3,19},{4,20},{5,21},{6,22},{7,23},{8,24},{9,... | collective-permute-start | bytes 368648 | tf_op jit(solution)/shard_map/ppermute | solution.py:51
  (46 other events, 370.1 us)
Sparse Core Ops, SparseCore 0:
  10.9 86.5 all-gather.1
